TPU v7x, 32 devices: a whole 2x2x4 slice. The times are simulated.
32 devices in a mesh: section: 4 (over x, core), feat: 8 (over z, y).
Axes of the slice: x: 2, y: 2, z: 4, core: 2. Of those that a mesh axis runs over, the one named last changes fastest.
Arguments:
- inputs: bfloat16 [4, 128, 8192], P('section', None, 'feat'), may hold values from -6 to 6
- targets: bfloat16 [4, 128, 8192], P('section', None, 'feat'), may hold values from -6 to 6
- enc_w: bfloat16 [4, 4096, 8192], P('section', 'feat'), may hold values from -0.0625 to 0.0625
- enc_b: float32 [4, 4096], P('section', 'feat'), may hold values from -3 to 3
- dec_w: bfloat16 [4, 2, 8192, 4096], P('section', None, 'feat'), may hold values from -0.125 to 0.125
- dec_b: float32 [4, 8192], P('section', 'feat'), may hold values from -3 to 3
Outputs:
- enc_grad: bfloat16 [4, 4096, 8192], P('section', 'feat')
- dec_grad: bfloat16 [4, 2, 8192, 4096], P('section', None, 'feat')
All inputs are finite; a program needn't handle non-finite values.
Results may differ from a plain program's by a relative error of at most 0.0058.
Values may be sent and summed in bfloat16 or wider, within the bound.
No kernel may reach another device: no remote copies, remote signals or barrier semaphores. Data moves between devices by JAX's collectives and lax.ppermute only.
A program may use at most 128 MiB of HBM per device.

v0:
```python
import jax
import jax.numpy as jnp
from jax import lax
from jax.sharding import PartitionSpec as P


def from_behind(value, axis, steps):
    count = lax.axis_size(axis)
    initial, last = (max(0, -steps), min(count, count - steps))
    return lax.ppermute(value, axis, [(source, source + steps) for source in range(initial, last)])


def transposed(left, right):
    return lax.dot_general(
        left, right, (((0,), (0,)), ((), ())), preferred_element_type=jnp.float32
    )


def against(left, right):
    return lax.dot_general(
        left, right, (((1,), (1,)), ((), ())), preferred_element_type=jnp.float32
    )


def on_device(inputs, targets, enc_w, enc_b, dec_w, dec_b):
    scale = inputs.shape[1] ** (-0.5)
    reach = dec_w.shape[1]
    gathered = lax.all_gather(inputs[0], "feat", axis=1, tiled=True)
    pre = against(gathered, enc_w[0]) + enc_b[0]
    active = jnp.maximum(pre, 0.0)
    codes = (active * active).astype(jnp.bfloat16)
    own_codes = lax.all_gather(codes, "feat", axis=1, tiled=True)
    target = targets[0].astype(jnp.float32)
    weights = dec_w[0]
    code_grad = None
    sources = [own_codes]
    previous = own_codes
    previous = from_behind(previous, "section", 1)
    sources.append(previous)
    total = dec_b[0] + against(sources[0], weights[0])
    offset = 1
    total = total + against(sources[offset], weights[offset])
    error = ((total - target) * scale).astype(jnp.bfloat16)
    slots = [transposed(error, sources[offset]).astype(jnp.bfloat16) for offset in range(reach)]
    code_grad = jnp.dot(error, weights[0], preferred_element_type=jnp.float32)
    held_error = error
    held_weights = weights[1:]
    held_error, held_weights = from_behind((held_error, held_weights), "section", -1)
    code_grad = code_grad + jnp.dot(held_error, held_weights[0], preferred_element_type=jnp.float32)
    mine = lax.psum_scatter(code_grad, "feat", scatter_dimension=1, tiled=True)
    pre_grad = (mine * 2.0 * active).astype(jnp.bfloat16)
    enc_grad = transposed(pre_grad, gathered).astype(jnp.bfloat16)[None]
    dec_grad = jnp.stack(slots)[None]
    return (enc_grad, dec_grad)


def solution(mesh):
    return jax.shard_map(
        on_device,
        mesh=mesh,
        in_specs=(
            P("section", None, "feat"),
            P("section", None, "feat"),
            P("section", "feat", None),
            P("section", "feat"),
            P("section", None, "feat", None),
            P("section", "feat"),
        ),
        out_specs=(P("section", "feat", None), P("section", None, "feat", None)),
        check_vma=False,
    )
```

profile of v0, /device:TPU:1, one launch (start us, length us, event | category | flops | bytes accessed | tf_op | source)
XLA Modules:
  0.0 221.8 jit_solution(1825936971229578894)
XLA Ops:
  7.2 0.0 all-gather.6.cloned.1.call-start
  7.2 0.7 all-gather.6.cloned.1.call-update
  7.9 0.0 copy-start.2
  7.9 0.0 all-gather.4.cloned.1.call-start
  8.0 7.9 %slice_bitcast_fusion = bf16[1,1024,4096]{2,1,0:T(8,128)(2,1)} fusion(bf16[1,2,1024,4096]{3,2,1,0:T(8,128)(2,1)} %param.10), kind=kLoop, calls=%fused_computation.15 | loop fusion | bytes 16777216 | tf_op jit(solution)/shard_map/slice | solution.py:42
  15.8 0.0 copy-start.4
  15.8 2.1 collective-permute-start.2
  17.9 42.5 %all-gather.6.cloned.1.call-done = bf16[1,128,8192]{2,1,0:T(8,128)(2,1)} async-done(((bf16[1,128,1024]{2,1,0:T(8,128)(2,1)}), bf16[1,128,8192]{2,1,0:T(8,128)(2,1)}) %all-gather.6.cloned.1.call-update) | async-done | bytes 2097168 | tf_op jit(solution)/shard_map/all_gather | solution.py:28
  60.5 0.0 copy-done.2
  60.5 7.6 %multiply_convert_fusion.1 = (bf16[128,512]{1,0:T(8,128)(2,1)}, f32[128,512]{1,0:T(8,128)S(1)}) fusion(f32[512]{0:T(512)S(1)} %bitcast.66, bf16[1,512,8192]{2,1,0:T(8,128)(2,1)} %param.8, bf16[1,128,8192]{2,1,0:T(8,128)(2,1)} %all-gather.6.cloned.1.call-done), kind=kOutput, calls=%fused_computation.30 | convolution fusion | flops 1074003968 | bytes 10881024 | tf_op jit(solution)/shard_map/dot_general | solution.py:20
  68.1 0.0 copy-start.3
  68.1 0.0 all-gather.4.cloned.1.call-update
  68.1 0.0 reduce-scatter.2.cloned.1.call-start
  68.1 36.8 %all-gather.4.cloned.1.call-done = bf16[128,4096]{1,0:T(8,128)(2,1)} async-done(((bf16[128,512]{1,0:T(8,128)(2,1)}), bf16[128,4096]{1,0:T(8,128)(2,1)}) %all-gather.4.cloned.1.call-update) | async-done | bytes 1048592 | tf_op jit(solution)/shard_map/all_gather | solution.py:32
  104.9 6.1 %collective-permute-start = (bf16[128,4096]{1,0:T(8,128)(2,1)}, bf16[128,4096]{1,0:T(8,128)(2,1)S(1)}, u32[]{:S(2)}, u32[]{:S(2)}) collective-permute-start(bf16[128,4096]{1,0:T(8,128)(2,1)} %all-gather.4.cloned.1.call-done), channel_id=1, source_target_pairs={{0,8},{8,16},{16,24},{1,9},{9,17},{17,25},{2,10},{10,18},{18,26},{... | collective-permute-start | bytes 3145736 | tf_op jit(solution)/shard_map/ppermute | solution.py:10
  111.1 0.0 copy-done.4
  111.1 6.6 %fusion.19 = f32[128,1024]{1,0:T(8,128)S(1)} fusion(bf16[128,4096]{1,0:T(8,128)(2,1)} %all-gather.4.cloned.1.call-done, bf16[1,2,1024,4096]{3,2,1,0:T(8,128)(2,1)} %param.10, f32[1024]{0:T(1024)S(1)} %bitcast.67), kind=kOutput, calls=%fused_computation.22 | convolution fusion | flops 1073872896 | bytes 9965568 | tf_op jit(solution)/shard_map/dot_general | solution.py:20
  117.7 5.4 %collective-permute-done = bf16[128,4096]{1,0:T(8,128)(2,1)S(1)} collective-permute-done((bf16[128,4096]{1,0:T(8,128)(2,1)}, bf16[128,4096]{1,0:T(8,128)(2,1)S(1)}, u32[]{:S(2)}, u32[]{:S(2)}) %collective-permute-start) | collective-permute-done | bytes 1048608 | tf_op jit(solution)/shard_map/ppermute | solution.py:10
  123.1 0.0 copy-done.3
  123.1 6.3 %fusion.31 = bf16[128,1024]{1,0:T(8,128)(2,1)S(1)} fusion(f32[128,1024]{1,0:T(8,128)S(1)} %fusion.19, bf16[128,4096]{1,0:T(8,128)(2,1)S(1)} %collective-permute-done, bf16[1,2,1024,4096]{3,2,1,0:T(8,128)(2,1)} %param.10, bf16[1,128,1024]{2,1,0:T(8,128)(2,1)S(1)} %copy-done.3), kind=kOutput, calls=%fused_computation.26 | convolution fusion | flops 1074397184 | bytes 10485760 | tf_op jit(solution)/shard_map/dot_general | solution.py:20
  129.4 2.1 collective-permute-start.1
  131.5 4.6 %fusion.5 = f32[128,4096]{1,0:T(8,128)S(1)} fusion(bf16[128,1024]{1,0:T(8,128)(2,1)S(1)} %fusion.31, bf16[1,2,1024,4096]{3,2,1,0:T(8,128)(2,1)} %param.10), kind=kOutput, calls=%fused_computation.7 | convolution fusion | flops 1073741824 | bytes 10747904 | tf_op jit(solution)/shard_map/dot_general | solution.py:45
  136.2 1.6 collective-permute-done.1
  137.7 0.0 collective-permute-done.2
  137.7 6.1 %fusion.14 = f32[128,4096]{1,0:T(8,128)} fusion(f32[128,4096]{1,0:T(8,128)S(1)} %fusion.5, bf16[128,1024]{1,0:T(8,128)(2,1)S(1)} %collective-permute-done.1, bf16[1,1024,4096]{2,1,0:T(8,128)(2,1)} %collective-permute-done.2), kind=kOutput, calls=%fused_computation.19 | convolution fusion | flops 1074266112 | bytes 12845056 | tf_op jit(solution)/shard_map/dot_general | solution.py:49
  143.8 0.0 copy-start.1
  143.8 0.0 reduce-scatter.2.cloned.1.call-update
  143.9 2.4 %convert_bitcast_fusion = bf16[1,1024,4096]{2,1,0:T(8,128)(2,1)S(1)} fusion(bf16[128,1024]{1,0:T(8,128)(2,1)S(1)} %fusion.31, bf16[128,4096]{1,0:T(8,128)(2,1)S(1)} %collective-permute-done), kind=kOutput, calls=%fused_computation.13 | convolution fusion | flops 1077936128 | bytes 9699328 | tf_op jit(solution)/shard_map/dot_general | solution.py:14
  146.2 0.0 copy-done.1
  146.2 2.4 %convert_bitcast_fusion.1 = bf16[1,1024,4096]{2,1,0:T(8,128)(2,1)S(1)} fusion(bf16[128,1024]{1,0:T(8,128)(2,1)S(1)} %fusion.31, bf16[128,4096]{1,0:T(8,128)(2,1)S(1)} %copy-done.1), kind=kOutput, calls=%fused_computation.14 | convolution fusion | flops 1077936128 | bytes 9699328 | tf_op jit(solution)/shard_map/dot_general | solution.py:14
  148.6 0.0 copy-start
  148.6 6.8 %maximum_bitcast_fusion = bf16[1,2,1024,4096]{3,2,1,0:T(8,128)(2,1)} fusion(bf16[1,1024,4096]{2,1,0:T(8,128)(2,1)S(1)} %convert_bitcast_fusion, bf16[1,1024,4096]{2,1,0:T(8,128)(2,1)S(1)} %convert_bitcast_fusion.1), kind=kLoop, calls=%fused_computation | loop fusion | flops 8388608 | bytes 33554432 | tf_op jit(solution)/shard_map/broadcast_in_dim | solution.py:53
  155.4 53.2 %reduce-scatter.2.cloned.1.call-done = f32[128,512]{1,0:T(8,128)} async-done(((f32[128,4096]{1,0:T(8,128)}), f32[128,512]{1,0:T(8,128)}) %reduce-scatter.2.cloned.1.call-update) | async-done | bytes 262160 | tf_op jit(solution)/shard_map/reduce_scatter | solution.py:50
  208.6 0.0 copy-done
  208.6 6.7 %fusion = bf16[1,512,8192]{2,1,0:T(8,128)(2,1)} fusion(bf16[1,128,8192]{2,1,0:T(8,128)(2,1)S(1)} %copy-done, f32[128,512]{1,0:T(8,128)S(1)} %get-tuple-element.3, f32[128,512]{1,0:T(8,128)} %reduce-scatter.2.cloned.1.call-done), kind=kOutput, calls=%fused_computation.2 | convolution fusion | flops 1078132736 | bytes 11010048 | tf_op jit(solution)/shard_map/dot_general | solution.py:14
Async XLA Ops:
  7.2 53.3 %all-gather.6.cloned.1.call-start = ((), (), s32[]{:S(2)}) async-start(), calls=%async_computation.3 | async-start | bytes 2359296 | tf_op jit(solution)/shard_map/all_gather | solution.py:28
  7.9 52.6 %copy-start.2 = (f32[1,512]{1,0:T(1,128)S(1)}, f32[1,512]{1,0:T(1,128)}, u32[]{:S(2)}) copy-start(f32[1,512]{1,0:T(1,128)} %param.9) | copy-start | bytes 6148
  7.9 97.0 %all-gather.4.cloned.1.call-start = ((), (), s32[]{:S(2)}) async-start(), calls=%async_computation.1 | async-start | bytes 1179648 | tf_op jit(solution)/shard_map/all_gather | solution.py:32
  15.8 95.2 %copy-start.4 = (f32[1,1024]{1,0:T(1,128)S(1)}, f32[1,1024]{1,0:T(1,128)}, u32[]{:S(2)}) copy-start(f32[1,1024]{1,0:T(1,128)} %param.11) | copy-start | bytes 12292
  15.8 121.9 %collective-permute-start.2 = (bf16[1,1024,4096]{2,1,0:T(8,128)(2,1)}, bf16[1,1024,4096]{2,1,0:T(8,128)(2,1)}, u32[]{:S(2)}, u32[]{:S(2)}) collective-permute-start(bf16[1,1024,4096]{2,1,0:T(8,128)(2,1)} %slice_bitcast_fusion), channel_id=1, source_target_pairs={{8,0},{16,8},{24,16},{9,1},{17,9},{25,17},{10,2},{18,10},{26,18},{... | collective-permute-start | bytes 25165832 | tf_op jit(solution)/shard_map/ppermute | solution.py:10
  68.1 55.1 %copy-start.3 = (bf16[1,128,1024]{2,1,0:T(8,128)(2,1)S(1)}, bf16[1,128,1024]{2,1,0:T(8,128)(2,1)}, u32[]{:S(2)}) copy-start(bf16[1,128,1024]{2,1,0:T(8,128)(2,1)} %param.7) | copy-start | bytes 786436
  68.1 140.5 %reduce-scatter.2.cloned.1.call-start = ((), (), s32[]{:S(2)}) async-start(), calls=%async_computation.2 | async-start | bytes 2359296 | tf_op jit(solution)/shard_map/reduce_scatter | solution.py:50
  104.9 18.2 %collective-permute-start = (bf16[128,4096]{1,0:T(8,128)(2,1)}, bf16[128,4096]{1,0:T(8,128)(2,1)S(1)}, u32[]{:S(2)}, u32[]{:S(2)}) collective-permute-start(bf16[128,4096]{1,0:T(8,128)(2,1)} %all-gather.4.cloned.1.call-done), channel_id=1, source_target_pairs={{0,8},{8,16},{16,24},{1,9},{9,17},{17,25},{2,10},{10,18},{18,26},{... | collective-permute-start | bytes 3145736 | tf_op jit(solution)/shard_map/ppermute | solution.py:10
  129.4 8.3 %collective-permute-start.1 = (bf16[128,1024]{1,0:T(8,128)(2,1)S(1)}, bf16[128,1024]{1,0:T(8,128)(2,1)S(1)}, u32[]{:S(2)}, u32[]{:S(2)}) collective-permute-start(bf16[128,1024]{1,0:T(8,128)(2,1)S(1)} %fusion.31), channel_id=1, source_target_pairs={{8,0},{16,8},{24,16},{9,1},{17,9},{25,17},{10,2},{18,10},{26,18},{... | collective-permute-start | bytes 786440 | tf_op jit(solution)/shard_map/ppermute | solution.py:10
  143.8 2.4 %copy-start.1 = (bf16[128,4096]{1,0:T(8,128)(2,1)S(1)}, bf16[128,4096]{1,0:T(8,128)(2,1)}, u32[]{:S(2)}) copy-start(bf16[128,4096]{1,0:T(8,128)(2,1)} %all-gather.4.cloned.1.call-done) | copy-start | bytes 3145732
  148.6 59.9 %copy-start = (bf16[1,128,8192]{2,1,0:T(8,128)(2,1)S(1)}, bf16[1,128,8192]{2,1,0:T(8,128)(2,1)}, u32[]{:S(2)}) copy-start(bf16[1,128,8192]{2,1,0:T(8,128)(2,1)} %all-gather.6.cloned.1.call-done) | copy-start | bytes 6291460
Sparse Core Ops, SparseCore 0:
  10.2 50.2 all-gather.5
  68.2 36.6 all-gather.3
  144.0 64.5 reduce-scatter.1
where the time goes:
time: 225 us; the launch traced here: 222 us
  waiting for transfers between devices  140 us (62%)
  matrix products  42.7 us (19%)
  between operations  13.8 us (6%)
  starting transfers between devices  10.4 us (5%)
  local copies, waits for them, and re-layouts  7.91 us (4%)
  other arithmetic  6.75 us (3%)
    reduce_scatter x1, waiting for transfers between devices, on_device(): mine = lax.psum_scatter(code_grad, 'feat', scatter_dimension=1, tiled=True)  53.2 us
    all_gather x1, waiting for transfers between devices, on_device(): gathered = lax.all_gather(inputs[0], 'feat', axis=1, tiled=True)  42.5 us
    all_gather x1, waiting for transfers between devices, on_device(): own_codes = lax.all_gather(codes, 'feat', axis=1, tiled=True)  36.8 us
    dot_general x3, matrix products, against(): lax.dot_general(left, right, (((1,), (1,)), ((), ())), preferred_element_...  20.5 us
    dot_general x3, matrix products, transposed(): lax.dot_general(left, right, (((0,), (0,)), ((), ())), preferred_element_...  11.5 us
    ppermute x3, starting transfers between devices, from_behind(): lax.ppermute(value, axis, [(source, source + steps) for source in range(i...  10.3 us
    slice x1, local copies, waits for them, and re-layouts, on_device(): total = total + against(sources[offset], weights[offset])  7.89 us
    ppermute x3, waiting for transfers between devices, from_behind(): lax.ppermute(value, axis, [(source, source + steps) for source in range(i...  6.98 us
  transfers between devices with their start and end apart: 6, of which 5 were waited for; matrix products, arithmetic and copies ran while one was open for 20% of the time, Pallas kernels for 0%

commit v1 on v0

v1 whole, which is shorter than its diff:
```python
import functools

import jax
import jax.numpy as jnp
from jax import lax
from jax.experimental import pallas as pl
from jax.experimental.pallas import tpu as pltpu
from jax.sharding import PartitionSpec as P

LANES = 128
MIB = 1024 * 1024
BF16 = jnp.bfloat16
F32 = jnp.float32


def from_behind(value, axis, steps):
    count = lax.axis_size(axis)
    initial, last = (max(0, -steps), min(count, count - steps))
    return lax.ppermute(value, axis, [(source, source + steps) for source in range(initial, last)])


def transposed(left, right):
    return lax.dot_general(left, right, (((0,), (0,)), ((), ())), preferred_element_type=F32)


def against(left, right):
    return lax.dot_general(left, right, (((1,), (1,)), ((), ())), preferred_element_type=F32)


def shifted(value, by):
    count = lax.axis_size("feat")
    return lax.ppermute(value, "feat", [(i, (i + by) % count) for i in range(count)])


def swapped(value):
    count = lax.axis_size("feat")
    return lax.ppermute(value, "feat", [(i, i ^ 1) for i in range(count)])


def gather_parts(own):
    pairs = lax.axis_size("feat") // 2
    own_swapped = swapped(own)
    lines = [shifted(own, 2 * k) for k in range(1, pairs)]
    return [own, *lines, own_swapped, *[swapped(part) for part in lines]]


def owners():
    count = lax.axis_size("feat")
    me = lax.axis_index("feat")
    partner = me + 1 - 2 * lax.rem(me, 2)
    pairs = count // 2
    return [lax.rem(base - 2 * k + count, count) for base in (me, partner) for k in range(pairs)]


def columns(owner, width):
    return pl.ds(pl.multiple_of(owner * width, width), width)


def vmem(count):
    return [pl.BlockSpec(memory_space=pltpu.VMEM)] * count


def params(mib):
    return pltpu.CompilerParams(vmem_limit_bytes=mib * MIB)


def fetch_kernel(enc_ref, dec_ref, enc_out, dec_out, sems):
    copies = [
        pltpu.make_async_copy(enc_ref, enc_out, sems.at[0]),
        pltpu.make_async_copy(dec_ref.at[0], dec_out.at[0], sems.at[1]),
        pltpu.make_async_copy(dec_ref.at[1], dec_out.at[1], sems.at[2]),
    ]
    for copy in copies:
        copy.start()
    for copy in copies:
        copy.wait()


def pre_kernel(count, *refs):
    parts, (w_ref, b_ref, codes_ref, active_ref) = refs[:count], refs[count:]
    width = parts[0].shape[1]
    total = None
    for part, owner in zip(parts, owners()):
        term = against(part[...], w_ref[:, columns(owner, width)])
        total = term if total is None else total + term
    active = jnp.maximum(total + b_ref[...], 0.0)
    active_ref[...] = active
    codes_ref[...] = (active * active).astype(BF16)


def recon_kernel(count, scale, *refs):
    own, previous = refs[:count], refs[count : 2 * count]
    w_ref, b_ref, target_ref, error_ref, sent_ref = refs[2 * count :]
    width = own[0].shape[1]
    rows = w_ref.shape[1]
    tile = 256 if rows % 256 == 0 else LANES
    places = owners()

    @pl.loop(0, rows // tile)
    def _(j):
        here = pl.ds(pl.multiple_of(j * tile, tile), tile)
        total = b_ref[:, here]
        for slot, parts in enumerate((own, previous)):
            for part, owner in zip(parts, places):
                total = total + against(part[...], w_ref[slot, here, columns(owner, width)])
        error_ref[:, here] = ((total - target_ref[:, here].astype(F32)) * scale).astype(BF16)

    features = w_ref.shape[2]
    wide = 512 if features % 512 == 0 else LANES

    @pl.loop(0, features // wide)
    def _(j):
        here = pl.ds(pl.multiple_of(j * wide, wide), wide)
        sent_ref[:, here] = jnp.dot(
            error_ref[...], w_ref[1, :, here], preferred_element_type=F32
        ).astype(BF16)


def own_grad_kernel(error_ref, w_ref, own_ref):
    features = w_ref.shape[2]
    wide = 512 if features % 512 == 0 else LANES

    @pl.loop(0, features // wide)
    def _(j):
        here = pl.ds(pl.multiple_of(j * wide, wide), wide)
        own_ref[:, here] = jnp.dot(error_ref[...], w_ref[0, :, here], preferred_element_type=F32)


def dec_grad_kernel(count, *refs):
    error_ref, parts, out_ref = refs[0], refs[1:-1], refs[-1]
    width = parts[0].shape[1]
    places = owners()
    for slot in range(2):

        @pl.when(pl.program_id(0) == slot)
        def _(slot=slot):
            for k in range(count):
                out_ref[0, 0, :, columns(places[k], width)] = transposed(
                    error_ref[...], parts[slot * count + k][...]
                ).astype(BF16)


def sum_kernel(count, own_ref, arrived_ref, *outs):
    me = lax.axis_index("feat")
    width = outs[0].shape[1]
    for k in range(count):
        here = columns(lax.rem(me + k, count), width)
        total = own_ref[:, here] + arrived_ref[:, here].astype(F32)
        outs[k][...] = total.astype(outs[k].dtype)


def enc_grad_kernel(count, *refs):
    grads, parts = refs[:count], refs[count : 2 * count]
    active_ref, out_ref = refs[2 * count :]
    width = parts[0].shape[1]
    total = grads[0][...]
    for grad in grads[1:]:
        total = total + grad[...].astype(F32)
    pre_grad = (total * 2.0 * active_ref[...]).astype(BF16)
    for part, owner in zip(parts, owners()):
        out_ref[0, :, columns(owner, width)] = transposed(pre_grad, part[...]).astype(BF16)


def on_device(inputs, targets, enc_w, enc_b, dec_w, dec_b):
    count = lax.axis_size("feat")
    tok, width = inputs.shape[1:]
    own_features, model = enc_w.shape[1:]
    features = dec_w.shape[3]
    scale = tok ** (-0.5)

    parts = gather_parts(inputs[0])
    enc_weights, weights = pl.pallas_call(
        fetch_kernel,
        name="fetch",
        out_shape=(pltpu.VMEM(enc_w.shape[1:], BF16), pltpu.VMEM(dec_w.shape[1:], BF16)),
        in_specs=[pl.BlockSpec(memory_space=pltpu.HBM)] * 2,
        out_specs=tuple(vmem(2)),
        scratch_shapes=[pltpu.SemaphoreType.DMA((3,))],
        compiler_params=params(1),
        cost_estimate=pl.CostEstimate(
            flops=0, bytes_accessed=2 * (own_features * model + 2 * width * features), transcendentals=0
        ),
    )(*[pltpu.with_memory_space_constraint(w[0], pltpu.HBM) for w in (enc_w, dec_w)])
    codes, active = pl.pallas_call(
        functools.partial(pre_kernel, count),
        name="pre",
        out_shape=(
            jax.ShapeDtypeStruct((tok, own_features), BF16),
            jax.ShapeDtypeStruct((tok, own_features), F32),
        ),
        in_specs=vmem(count + 2),
        out_specs=tuple(vmem(2)),
        compiler_params=params(16),
        cost_estimate=pl.CostEstimate(
            flops=2 * tok * own_features * model, bytes_accessed=4 * MIB, transcendentals=0
        ),
    )(*parts, enc_weights, enc_b)

    own = gather_parts(codes)
    previous = [from_behind(part, "section", 1) for part in own]

    error, sent = pl.pallas_call(
        functools.partial(recon_kernel, count, scale),
        name="recon",
        out_shape=(
            jax.ShapeDtypeStruct((tok, width), BF16),
            jax.ShapeDtypeStruct((tok, features), BF16),
        ),
        in_specs=vmem(2 * count + 3),
        out_specs=tuple(vmem(2)),
        compiler_params=params(16),
        cost_estimate=pl.CostEstimate(
            flops=6 * tok * width * features, bytes_accessed=4 * MIB, transcendentals=0
        ),
    )(*own, *previous, weights, dec_b, targets[0])

    arrived = from_behind(sent, "section", -1)

    own_grad = pl.pallas_call(
        own_grad_kernel,
        name="own_grad",
        out_shape=jax.ShapeDtypeStruct((tok, features), F32),
        in_specs=vmem(2),
        out_specs=vmem(1)[0],
        compiler_params=params(16),
        cost_estimate=pl.CostEstimate(
            flops=2 * tok * width * features, bytes_accessed=4 * MIB, transcendentals=0
        ),
    )(error, weights)

    rows = 256 if width % 256 == 0 else LANES
    dec_grad = pl.pallas_call(
        functools.partial(dec_grad_kernel, count),
        name="dec_grad",
        grid=(2, width // rows),
        out_shape=jax.ShapeDtypeStruct(dec_w.shape, BF16),
        in_specs=[
            pl.BlockSpec((tok, rows), lambda slot, j: (0, j)),
            *[pl.BlockSpec((tok, own_features), lambda slot, j: (0, 0))] * (2 * count),
        ],
        out_specs=pl.BlockSpec((1, 1, rows, features), lambda slot, j: (0, slot, j, 0)),
        compiler_params=params(20),
        cost_estimate=pl.CostEstimate(
            flops=4 * tok * width * features, bytes_accessed=4 * width * features, transcendentals=0
        ),
    )(error, *own, *previous)

    pieces = pl.pallas_call(
        functools.partial(sum_kernel, count),
        name="sum",
        out_shape=tuple(
            jax.ShapeDtypeStruct((tok, own_features), F32 if k == 0 else BF16) for k in range(count)
        ),
        in_specs=vmem(2),
        out_specs=tuple(vmem(count)),
        compiler_params=params(16),
        cost_estimate=pl.CostEstimate(
            flops=2 * tok * features, bytes_accessed=4 * MIB, transcendentals=0
        ),
    )(own_grad, arrived)
    grads = [pieces[0], *[shifted(pieces[k], k) for k in range(1, count)]]

    block = 128 if own_features % 128 == 0 else own_features
    enc_grad = pl.pallas_call(
        functools.partial(enc_grad_kernel, count),
        name="enc_grad",
        grid=(own_features // block,),
        out_shape=jax.ShapeDtypeStruct(enc_w.shape, BF16),
        in_specs=[
            *[pl.BlockSpec((tok, block), lambda j: (0, j))] * count,
            *[pl.BlockSpec((tok, width), lambda j: (0, 0))] * count,
            pl.BlockSpec((tok, block), lambda j: (0, j)),
        ],
        out_specs=pl.BlockSpec((1, block, model), lambda j: (0, j, 0)),
        compiler_params=params(20),
        cost_estimate=pl.CostEstimate(
            flops=2 * tok * own_features * model, bytes_accessed=2 * own_features * model, transcendentals=0
        ),
    )(*grads, *parts, active)
    return enc_grad, dec_grad


def plain(inputs, targets, enc_w, enc_b, dec_w, dec_b):
    scale = inputs.shape[1] ** (-0.5)
    gathered = lax.all_gather(inputs[0], "feat", axis=1, tiled=True)
    active = jnp.maximum(against(gathered, enc_w[0]) + enc_b[0], 0.0)
    codes = (active * active).astype(BF16)
    own = lax.all_gather(codes, "feat", axis=1, tiled=True)
    previous = from_behind(own, "section", 1)
    weights = dec_w[0]
    total = dec_b[0] + against(own, weights[0]) + against(previous, weights[1])
    error = ((total - targets[0].astype(F32)) * scale).astype(BF16)
    sent = jnp.dot(error, weights[1], preferred_element_type=F32)
    code_grad = jnp.dot(error, weights[0], preferred_element_type=F32) + from_behind(sent, "section", -1)
    mine = lax.psum_scatter(code_grad, "feat", scatter_dimension=1, tiled=True)
    pre_grad = (mine * 2.0 * active).astype(BF16)
    enc_grad = transposed(pre_grad, gathered).astype(BF16)[None]
    dec_grad = jnp.stack([transposed(error, source).astype(BF16) for source in (own, previous)])[None]
    return enc_grad, dec_grad


def chosen(inputs, targets, enc_w, enc_b, dec_w, dec_b):
    aligned = inputs.shape[2] % LANES == 0 and enc_w.shape[1] % LANES == 0
    small = lax.axis_size("feat") % 2 == 0 and lax.axis_size("feat") <= 16
    body = on_device if aligned and small else plain
    return body(inputs, targets, enc_w, enc_b, dec_w, dec_b)


def solution(mesh):
    return jax.shard_map(
        chosen,
        mesh=mesh,
        in_specs=(
            P("section", None, "feat"),
            P("section", None, "feat"),
            P("section", "feat", None),
            P("section", "feat"),
            P("section", None, "feat", None),
            P("section", "feat"),
        ),
        out_specs=(P("section", "feat", None), P("section", None, "feat", None)),
        check_vma=False,
    )
```

time: 225 us -> 122 us (0.54); the launches traced: 222 us -> 121 us
  waiting for transfers between devices: 140 us -> 41.7 us
  matrix products: 42.7 us -> 0 us
  Pallas kernels: 0 us -> 37.1 us
  starting transfers between devices: 10.4 us -> 41.5 us
  between operations: 13.8 us -> 0.92 us
  local copies, waits for them, and re-layouts: 7.91 us -> 0.02 us
  other arithmetic: 6.75 us -> 0 us
    all_gather x2 -> x0, waiting for transfers between devices: 79.3 us -> none  [the longest x1 42.5 us: on_device(): gathered = lax.all_gather(inputs[0], 'feat', axis=1, tiled=True)]
    reduce_scatter x1 -> x0, waiting for transfers between devices: 53.2 us -> none  [on_device(): mine = lax.psum_scatter(code_grad, 'feat', scatter_dimension=1, tiled=True)]
    dot_general x8 -> x0, matrix products: 42.7 us -> none  [the longest x3 20.5 us: against(): lax.dot_general(left, right, (((1,), (1,)), ((), ())), preferred_element_...]
    pallas_call x0 -> x7, Pallas kernels: none -> 37.1 us  [the longest x1 9.11 us: on_device(): pl.pallas_call(functools.partial(dec_grad_kernel, count), name='dec_grad'...]
    ppermute x0 -> x21, waiting for transfers between devices: none -> 27.2 us  [the longest x13 25 us: shifted(): lax.ppermute(value, 'feat', [(i, (i + by) % count) for i in range(count)])]
    ppermute x0 -> x21, starting transfers between devices: none -> 20.1 us  [the longest x13 12.7 us: shifted(): lax.ppermute(value, 'feat', [(i, (i + by) % count) for i in range(count)])]
    ppermute x3 -> x9, starting transfers between devices: 10.3 us -> 21.4 us  [from_behind(): lax.ppermute(value, axis, [(source, source + steps) for source in range(i...]
    slice x1 -> x0, local copies, waits for them, and re-layouts: 7.89 us -> none  [on_device(): total = total + against(sources[offset], weights[offset])]
  transfers between devices with their start and end apart: 6 -> 30, of which waited for: 5 -> 7; matrix products, arithmetic and copies ran while one was open for 20% -> 0% of each run, Pallas kernels for 0% -> 16%
where the time goes in v1:
time: 122 us; the launch traced here: 121 us
  waiting for transfers between devices  41.7 us (34%)
  starting transfers between devices  41.5 us (34%)
  Pallas kernels  37.1 us (30%)
    ppermute x13, waiting for transfers between devices, shifted(): lax.ppermute(value, 'feat', [(i, (i + by) % count) for i in range(count)])  25 us
    ppermute x9, starting transfers between devices, from_behind(): lax.ppermute(value, axis, [(source, source + steps) for source in range(i...  21.4 us
    ppermute x9, waiting for transfers between devices, from_behind(): lax.ppermute(value, axis, [(source, source + steps) for source in range(i...  14.5 us
    ppermute x13, starting transfers between devices, shifted(): lax.ppermute(value, 'feat', [(i, (i + by) % count) for i in range(count)])  12.7 us
    pallas_call x1, Pallas kernels, on_device(): pl.pallas_call(functools.partial(dec_grad_kernel, count), name='dec_grad'...  9.11 us
    pallas_call x1, Pallas kernels, on_device(): pl.pallas_call(functools.partial(recon_kernel, count, scale), name='recon...  8.8 us
    pallas_call x1, Pallas kernels, on_device(): pl.pallas_call(fetch_kernel, name='fetch', out_shape=(pltpu.VMEM(enc_w.sh...  8.22 us
    ppermute x8, starting transfers between devices, swapped(): return lax.ppermute(value, 'feat', [(i, i ^ 1) for i in range(count)])  7.39 us
  transfers between devices with their start and end apart: 30, of which 7 were waited for; matrix products, arithmetic and copies ran while one was open for 0% of the time, Pallas kernels for 16%

profile of v1, /device:TPU:1, one launch (start us, length us, event | category | flops | bytes accessed | tf_op | source)
XLA Modules:
  0.0 121.2 jit_solution(9054893571857749019)
XLA Ops:
  0.6 4.2 %collective-permute-start.2 = (bf16[128,1024]{1,0:T(8,128)(2,1)}, bf16[128,1024]{1,0:T(8,128)(2,1)S(1)}, u32[]{:S(2)}, u32[]{:S(2)}) collective-permute-start(bf16[128,1024]{1,0:T(8,128)(2,1)} %bitcast.4), channel_id=1, source_target_pairs={{0,6},{1,7},{2,0},{3,1},{4,2},{5,3},{6,4},{7,5},{8,14},{9,15},{10,... | collective-permute-start | bytes 786440 | tf_op jit(solution)/shard_map/ppermute | solution.py:32
  4.8 0.0 collective-permute-start.1
  4.8 0.5 collective-permute-start
  5.3 1.2 %collective-permute-start.3 = (bf16[128,1024]{1,0:T(8,128)(2,1)}, bf16[128,1024]{1,0:T(8,128)(2,1)S(1)}, u32[]{:S(2)}, u32[]{:S(2)}) collective-permute-start(bf16[128,1024]{1,0:T(8,128)(2,1)} %bitcast.7), channel_id=1, source_target_pairs={{0,1},{1,0},{2,3},{3,2},{4,5},{5,4},{6,7},{7,6},{8,9},{9,8},{10,11... | collective-permute-start | bytes 786440 | tf_op jit(solution)/shard_map/ppermute | solution.py:37
  6.5 3.7 %collective-permute-done.2.refs_3_.refs_11_ = bf16[128,1024]{1,0:T(8,128)(2,1)S(1)} collective-permute-done((bf16[128,1024]{1,0:T(8,128)(2,1)}, bf16[128,1024]{1,0:T(8,128)(2,1)S(1)}, u32[]{:S(2)}, u32[]{:S(2)}) %collective-permute-start.2) | collective-permute-done | bytes 262176 | tf_op jit(solution)/shard_map/ppermute | solution.py:32
  10.3 1.2 %collective-permute-start.6 = (bf16[128,1024]{1,0:T(8,128)(2,1)S(1)}, bf16[128,1024]{1,0:T(8,128)(2,1)S(1)}, u32[]{:S(2)}, u32[]{:S(2)}) collective-permute-start(bf16[128,1024]{1,0:T(8,128)(2,1)S(1)} %collective-permute-done.2.refs_3_.refs_11_), channel_id=1, source_target_pairs={{0,1},{1,0},{2,3},{3,2},{4,5},{5,4},{6,7},{7,6},{8,9},{9,8},{10,11... | collective-permute-start | bytes 786440 | tf_op jit(solution)/shard_map/ppermute | solution.py:37
  11.5 15.3 %collective-permute-done.1.refs_2_.refs_10_ = bf16[128,1024]{1,0:T(8,128)(2,1)S(1)} collective-permute-done((bf16[128,1024]{1,0:T(8,128)(2,1)}, bf16[128,1024]{1,0:T(8,128)(2,1)S(1)}, u32[]{:S(2)}, u32[]{:S(2)}) %collective-permute-start.1) | collective-permute-done | bytes 262176 | tf_op jit(solution)/shard_map/ppermute | solution.py:32
  26.8 1.2 %collective-permute-start.5 = (bf16[128,1024]{1,0:T(8,128)(2,1)S(1)}, bf16[128,1024]{1,0:T(8,128)(2,1)S(1)}, u32[]{:S(2)}, u32[]{:S(2)}) collective-permute-start(bf16[128,1024]{1,0:T(8,128)(2,1)S(1)} %collective-permute-done.1.refs_2_.refs_10_), channel_id=1, source_target_pairs={{0,1},{1,0},{2,3},{3,2},{4,5},{5,4},{6,7},{7,6},{8,9},{9,8},{10,11... | collective-permute-start | bytes 786440 | tf_op jit(solution)/shard_map/ppermute | solution.py:37
  28.0 0.0 collective-permute-done.refs_1_.refs_9_
  28.0 0.2 collective-permute-start.4
  28.2 8.2 %fetch.1 = (bf16[512,8192]{1,0:T(8,128)(2,1)S(1)}, bf16[2,1024,4096]{2,1,0:T(8,128)(2,1)S(1)}) custom-call(bf16[512,8192]{1,0:T(8,128)(2,1)} %bitcast.12, bf16[2,1024,4096]{2,1,0:T(8,128)(2,1)} %bitcast.11), custom_call_target="tpu_custom_call" | custom-call | bytes 25165824 | tf_op jit(solution)/shard_map/fetch/pallas_call | solution.py:172
  36.5 0.0 copy-start.1
  36.5 0.0 copy-start.2
  36.5 0.0 collective-permute-done.3.refs_4_.refs_12_
  36.5 0.0 collective-permute-done.6.refs_7_.refs_15_
  36.5 2.1 %collective-permute-done.4.refs_5_.refs_13_ = bf16[128,1024]{1,0:T(8,128)(2,1)S(1)} collective-permute-done((bf16[128,1024]{1,0:T(8,128)(2,1)S(1)}, bf16[128,1024]{1,0:T(8,128)(2,1)S(1)}, u32[]{:S(2)}, u32[]{:S(2)}) %collective-permute-start.4) | collective-permute-done | bytes 262176 | tf_op jit(solution)/shard_map/ppermute | solution.py:37
  38.6 2.9 %pre.1 = (bf16[128,512]{1,0:T(8,128)(2,1)S(1)}, f32[128,512]{1,0:T(8,128)S(1)}) custom-call(bf16[128,1024]{1,0:T(8,128)(2,1)S(1)} %bitcast.8, bf16[128,1024]{1,0:T(8,128)(2,1)S(1)} %collective-permute-done.refs_1_.refs_9_, bf16[128,1024]{1,0:T(8,128)(2,1)S(1)} %collective-permute-done.1.refs_2_.refs_10_, ...), custom_call_target="tpu_custom_call" | custom-call | flops 1073741824 | bytes 4194304 | tf_op jit(solution)/shard_map/pre/pallas_call | solution.py:184
  41.6 1.3 %collective-permute-start.10 = (bf16[128,512]{1,0:T(8,128)(2,1)S(1)}, bf16[128,512]{1,0:T(8,128)(2,1)S(1)}, u32[]{:S(2)}, u32[]{:S(2)}) collective-permute-start(bf16[128,512]{1,0:T(8,128)(2,1)S(1)} %get-tuple-element.17.refs_0_.refs_1_), channel_id=1, source_target_pairs={{0,1},{1,0},{2,3},{3,2},{4,5},{5,4},{6,7},{7,6},{8,9},{9,8},{10,11... | collective-permute-start | bytes 393224 | tf_op jit(solution)/shard_map/ppermute | solution.py:37
  42.9 5.7 %collective-permute-start.14 = (bf16[128,512]{1,0:T(8,128)(2,1)S(1)}, bf16[128,512]{1,0:T(8,128)(2,1)S(1)}, u32[]{:S(2)}, u32[]{:S(2)}) collective-permute-start(bf16[128,512]{1,0:T(8,128)(2,1)S(1)} %get-tuple-element.17.refs_0_.refs_1_), channel_id=1, source_target_pairs={{0,8},{8,16},{16,24},{1,9},{9,17},{17,25},{2,10},{10,18},{18,26},{... | collective-permute-start | bytes 393224 | tf_op jit(solution)/shard_map/ppermute | solution.py:19
  48.6 0.1 collective-permute-start.8
  48.7 1.8 %collective-permute-start.7 = (bf16[128,512]{1,0:T(8,128)(2,1)S(1)}, bf16[128,512]{1,0:T(8,128)(2,1)S(1)}, u32[]{:S(2)}, u32[]{:S(2)}) collective-permute-start(bf16[128,512]{1,0:T(8,128)(2,1)S(1)} %get-tuple-element.17.refs_0_.refs_1_), channel_id=1, source_target_pairs={{0,2},{1,3},{2,4},{3,5},{4,6},{5,7},{6,0},{7,1},{8,10},{9,11},{10,... | collective-permute-start | bytes 393224 | tf_op jit(solution)/shard_map/ppermute | solution.py:32
  50.5 2.2 %collective-permute-start.18 = (bf16[128,512]{1,0:T(8,128)(2,1)S(1)}, bf16[128,512]{1,0:T(8,128)(2,1)S(1)}, u32[]{:S(2)}, u32[]{:S(2)}) collective-permute-start(bf16[128,512]{1,0:T(8,128)(2,1)S(1)} %collective-permute-done.10.refs_4_.refs_5_), channel_id=1, source_target_pairs={{0,8},{8,16},{16,24},{1,9},{9,17},{17,25},{2,10},{10,18},{18,26},{... | collective-permute-start | bytes 393224 | tf_op jit(solution)/shard_map/ppermute | solution.py:19
  52.7 1.9 %collective-permute-start.17 = (bf16[128,512]{1,0:T(8,128)(2,1)S(1)}, bf16[128,512]{1,0:T(8,128)(2,1)S(1)}, u32[]{:S(2)}, u32[]{:S(2)}) collective-permute-start(bf16[128,512]{1,0:T(8,128)(2,1)S(1)} %collective-permute-done.9.refs_3_.refs_4_), channel_id=1, source_target_pairs={{0,8},{8,16},{16,24},{1,9},{9,17},{17,25},{2,10},{10,18},{18,26},{... | collective-permute-start | bytes 393224 | tf_op jit(solution)/shard_map/ppermute | solution.py:19
  54.6 0.7 collective-permute-start.13
  55.3 3.9 %collective-permute-done.8.refs_2_.refs_3_ = bf16[128,512]{1,0:T(8,128)(2,1)S(1)} collective-permute-done((bf16[128,512]{1,0:T(8,128)(2,1)S(1)}, bf16[128,512]{1,0:T(8,128)(2,1)S(1)}, u32[]{:S(2)}, u32[]{:S(2)}) %collective-permute-start.8) | collective-permute-done | bytes 131104 | tf_op jit(solution)/shard_map/ppermute | solution.py:32
  59.2 0.2 collective-permute-start.12
  59.4 1.2 %collective-permute-start.11 = (bf16[128,512]{1,0:T(8,128)(2,1)S(1)}, bf16[128,512]{1,0:T(8,128)(2,1)S(1)}, u32[]{:S(2)}, u32[]{:S(2)}) collective-permute-start(bf16[128,512]{1,0:T(8,128)(2,1)S(1)} %collective-permute-done.7.refs_1_.refs_2_), channel_id=1, source_target_pairs={{0,1},{1,0},{2,3},{3,2},{4,5},{5,4},{6,7},{7,6},{8,9},{9,8},{10,11... | collective-permute-start | bytes 393224 | tf_op jit(solution)/shard_map/ppermute | solution.py:37
  60.7 1.9 %collective-permute-start.16 = (bf16[128,512]{1,0:T(8,128)(2,1)S(1)}, bf16[128,512]{1,0:T(8,128)(2,1)S(1)}, u32[]{:S(2)}, u32[]{:S(2)}) collective-permute-start(bf16[128,512]{1,0:T(8,128)(2,1)S(1)} %collective-permute-done.8.refs_2_.refs_3_), channel_id=1, source_target_pairs={{0,8},{8,16},{16,24},{1,9},{9,17},{17,25},{2,10},{10,18},{18,26},{... | collective-permute-start | bytes 393224 | tf_op jit(solution)/shard_map/ppermute | solution.py:19
  62.6 1.9 %collective-permute-start.15 = (bf16[128,512]{1,0:T(8,128)(2,1)S(1)}, bf16[128,512]{1,0:T(8,128)(2,1)S(1)}, u32[]{:S(2)}, u32[]{:S(2)}) collective-permute-start(bf16[128,512]{1,0:T(8,128)(2,1)S(1)} %collective-permute-done.7.refs_1_.refs_2_), channel_id=1, source_target_pairs={{0,8},{8,16},{16,24},{1,9},{9,17},{17,25},{2,10},{10,18},{18,26},{... | collective-permute-start | bytes 393224 | tf_op jit(solution)/shard_map/ppermute | solution.py:19
  64.5 1.9 %collective-permute-start.21 = (bf16[128,512]{1,0:T(8,128)(2,1)S(1)}, bf16[128,512]{1,0:T(8,128)(2,1)S(1)}, u32[]{:S(2)}, u32[]{:S(2)}) collective-permute-start(bf16[128,512]{1,0:T(8,128)(2,1)S(1)} %collective-permute-done.13.refs_7_.refs_8_), channel_id=1, source_target_pairs={{0,8},{8,16},{16,24},{1,9},{9,17},{17,25},{2,10},{10,18},{18,26},{... | collective-permute-start | bytes 393224 | tf_op jit(solution)/shard_map/ppermute | solution.py:19
  66.5 1.9 %collective-permute-start.20 = (bf16[128,512]{1,0:T(8,128)(2,1)S(1)}, bf16[128,512]{1,0:T(8,128)(2,1)S(1)}, u32[]{:S(2)}, u32[]{:S(2)}) collective-permute-start(bf16[128,512]{1,0:T(8,128)(2,1)S(1)} %collective-permute-done.12.refs_6_.refs_7_), channel_id=1, source_target_pairs={{0,8},{8,16},{16,24},{1,9},{9,17},{17,25},{2,10},{10,18},{18,26},{... | collective-permute-start | bytes 393224 | tf_op jit(solution)/shard_map/ppermute | solution.py:19
  68.4 1.9 %collective-permute-start.19 = (bf16[128,512]{1,0:T(8,128)(2,1)S(1)}, bf16[128,512]{1,0:T(8,128)(2,1)S(1)}, u32[]{:S(2)}, u32[]{:S(2)}) collective-permute-start(bf16[128,512]{1,0:T(8,128)(2,1)S(1)} %collective-permute-done.11.refs_5_.refs_6_), channel_id=1, source_target_pairs={{0,8},{8,16},{16,24},{1,9},{9,17},{17,25},{2,10},{10,18},{18,26},{... | collective-permute-start | bytes 393224 | tf_op jit(solution)/shard_map/ppermute | solution.py:19
  70.4 1.9 %collective-permute-done.19.refs_13_.refs_14_ = bf16[128,512]{1,0:T(8,128)(2,1)S(1)} collective-permute-done((bf16[128,512]{1,0:T(8,128)(2,1)S(1)}, bf16[128,512]{1,0:T(8,128)(2,1)S(1)}, u32[]{:S(2)}, u32[]{:S(2)}) %collective-permute-start.19) | collective-permute-done | bytes 131104 | tf_op jit(solution)/shard_map/ppermute | solution.py:19
  72.3 8.8 %recon.1 = (bf16[128,1024]{1,0:T(8,128)(2,1)S(1)}, bf16[128,4096]{1,0:T(8,128)(2,1)S(1)}) custom-call(bf16[128,512]{1,0:T(8,128)(2,1)S(1)} %get-tuple-element.17.refs_0_.refs_1_, bf16[128,512]{1,0:T(8,128)(2,1)S(1)} %collective-permute-done.7.refs_1_.refs_2_, bf16[128,512]{1,0:T(8,128)(2,1)S(1)} %collective-permute-done.8.refs_2_.refs_3_, ...), custom_call_target="tpu_custom_call" | custom-call | flops 3221225472 | bytes 4194304 | tf_op jit(solution)/shard_map/recon/pallas_call | solution.py:202
  81.1 1.9 %collective-permute-start.22 = (bf16[128,4096]{1,0:T(8,128)(2,1)S(1)}, bf16[128,4096]{1,0:T(8,128)(2,1)S(1)}, u32[]{:S(2)}, u32[]{:S(2)}) collective-permute-start(bf16[128,4096]{1,0:T(8,128)(2,1)S(1)} %get-tuple-element.20), channel_id=1, source_target_pairs={{8,0},{16,8},{24,16},{9,1},{17,9},{25,17},{10,2},{18,10},{26,18},{... | collective-permute-start | bytes 3145736 | tf_op jit(solution)/shard_map/ppermute | solution.py:19
  83.0 2.6 %own_grad.1.own_ref = f32[128,4096]{1,0:T(8,128)S(1)} custom-call(bf16[128,1024]{1,0:T(8,128)(2,1)S(1)} %get-tuple-element.19.error_ref.refs_0_, bf16[2,1024,4096]{2,1,0:T(8,128)(2,1)S(1)} %get-tuple-element.18.refs_16_.w_ref), custom_call_target="tpu_custom_call" | custom-call | flops 1073741824 | bytes 4194304 | tf_op jit(solution)/shard_map/own_grad/pallas_call | solution.py:219
  85.6 12.6 %collective-permute-done.22.arrived_ref = bf16[128,4096]{1,0:T(8,128)(2,1)S(1)} collective-permute-done((bf16[128,4096]{1,0:T(8,128)(2,1)S(1)}, bf16[128,4096]{1,0:T(8,128)(2,1)S(1)}, u32[]{:S(2)}, u32[]{:S(2)}) %collective-permute-start.22) | collective-permute-done | bytes 1048608 | tf_op jit(solution)/shard_map/ppermute | solution.py:19
  98.2 0.2 sum.1
  98.4 0.1 collective-permute-start.23
  98.5 0.1 collective-permute-start.24
  98.6 1.3 %collective-permute-start.25 = (bf16[128,512]{1,0:T(8,128)(2,1)S(1)}, bf16[128,512]{1,0:T(8,128)(2,1)S(1)}, u32[]{:S(2)}, u32[]{:S(2)}) collective-permute-start(bf16[128,512]{1,0:T(8,128)(2,1)S(1)} %get-tuple-element.24), channel_id=1, source_target_pairs={{0,3},{1,4},{2,5},{3,6},{4,7},{5,0},{6,1},{7,2},{8,11},{9,12},{10,... | collective-permute-start | bytes 393224 | tf_op jit(solution)/shard_map/ppermute | solution.py:32
  99.9 3.1 %collective-permute-start.26 = (bf16[128,512]{1,0:T(8,128)(2,1)S(1)}, bf16[128,512]{1,0:T(8,128)(2,1)S(1)}, u32[]{:S(2)}, u32[]{:S(2)}) collective-permute-start(bf16[128,512]{1,0:T(8,128)(2,1)S(1)} %get-tuple-element.25), channel_id=1, source_target_pairs={{0,4},{1,5},{2,6},{3,7},{4,0},{5,1},{6,2},{7,3},{8,12},{9,13},{10,... | collective-permute-start | bytes 393224 | tf_op jit(solution)/shard_map/ppermute | solution.py:32
  102.9 0.0 collective-permute-start.27
  102.9 2.2 %collective-permute-done.23.refs_1_ = bf16[128,512]{1,0:T(8,128)(2,1)S(1)} collective-permute-done((bf16[128,512]{1,0:T(8,128)(2,1)S(1)}, bf16[128,512]{1,0:T(8,128)(2,1)S(1)}, u32[]{:S(2)}, u32[]{:S(2)}) %collective-permute-start.23) | collective-permute-done | bytes 131104 | tf_op jit(solution)/shard_map/ppermute | solution.py:32
  105.1 0.2 collective-permute-start.28
  105.3 1.5 %collective-permute-start.29 = (bf16[128,512]{1,0:T(8,128)(2,1)S(1)}, bf16[128,512]{1,0:T(8,128)(2,1)S(1)}, u32[]{:S(2)}, u32[]{:S(2)}) collective-permute-start(bf16[128,512]{1,0:T(8,128)(2,1)S(1)} %get-tuple-element.28), channel_id=1, source_target_pairs={{0,7},{1,0},{2,1},{3,2},{4,3},{5,4},{6,5},{7,6},{8,15},{9,8},{10,9... | collective-permute-start | bytes 393224 | tf_op jit(solution)/shard_map/ppermute | solution.py:32
  106.8 9.1 %dec_grad.1 = bf16[1,2,1024,4096]{3,2,1,0:T(8,128)(2,1)} custom-call(bf16[128,1024]{1,0:T(8,128)(2,1)S(1)} %get-tuple-element.19.error_ref.refs_0_, bf16[128,512]{1,0:T(8,128)(2,1)S(1)} %get-tuple-element.17.refs_0_.refs_1_, bf16[128,512]{1,0:T(8,128)(2,1)S(1)} %collective-permute-done.7.refs_1_.refs_2_, ...), custom_call_target="tpu_custom_call" | custom-call | flops 2147483648 | bytes 16777216 | tf_op jit(solution)/shard_map/dec_grad/pallas_call | solution.py:232
  115.9 5.3 %enc_grad.1 = bf16[1,512,8192]{2,1,0:T(8,128)(2,1)} custom-call(f32[128,512]{1,0:T(8,128)S(1)} %get-tuple-element.21.refs_0_, bf16[128,512]{1,0:T(8,128)(2,1)S(1)} %collective-permute-done.23.refs_1_, bf16[128,512]{1,0:T(8,128)(2,1)S(1)} %collective-permute-done.24.refs_2_, bf16[128,512]{1,0:T(8,128)(2,1)S(1)} %collective-permute-done.25.refs_3_, ...), custom_call_target="tpu_custom_call" | custom-call | flops 1073741824 | bytes 8388608 | tf_op jit(solution)/shard_map/enc_grad/pallas_call | solution.py:264
  (27 shorter events, 0.1 us)
Async XLA Ops:
  0.6 9.6 %collective-permute-start.2 = (bf16[128,1024]{1,0:T(8,128)(2,1)}, bf16[128,1024]{1,0:T(8,128)(2,1)S(1)}, u32[]{:S(2)}, u32[]{:S(2)}) collective-permute-start(bf16[128,1024]{1,0:T(8,128)(2,1)} %bitcast.4), channel_id=1, source_target_pairs={{0,6},{1,7},{2,0},{3,1},{4,2},{5,3},{6,4},{7,5},{8,14},{9,15},{10,... | collective-permute-start | bytes 786440 | tf_op jit(solution)/shard_map/ppermute | solution.py:32
  4.8 21.9 %collective-permute-start.1 = (bf16[128,1024]{1,0:T(8,128)(2,1)}, bf16[128,1024]{1,0:T(8,128)(2,1)S(1)}, u32[]{:S(2)}, u32[]{:S(2)}) collective-permute-start(bf16[128,1024]{1,0:T(8,128)(2,1)} %bitcast.5), channel_id=1, source_target_pairs={{0,4},{1,5},{2,6},{3,7},{4,0},{5,1},{6,2},{7,3},{8,12},{9,13},{10,... | collective-permute-start | bytes 786440 | tf_op jit(solution)/shard_map/ppermute | solution.py:32
  4.8 23.2 %collective-permute-start = (bf16[128,1024]{1,0:T(8,128)(2,1)}, bf16[128,1024]{1,0:T(8,128)(2,1)S(1)}, u32[]{:S(2)}, u32[]{:S(2)}) collective-permute-start(bf16[128,1024]{1,0:T(8,128)(2,1)} %bitcast.6), channel_id=1, source_target_pairs={{0,2},{1,3},{2,4},{3,5},{4,6},{5,7},{6,0},{7,1},{8,10},{9,11},{10,... | collective-permute-start | bytes 786440 | tf_op jit(solution)/shard_map/ppermute | solution.py:32
  5.3 31.2 %collective-permute-start.3 = (bf16[128,1024]{1,0:T(8,128)(2,1)}, bf16[128,1024]{1,0:T(8,128)(2,1)S(1)}, u32[]{:S(2)}, u32[]{:S(2)}) collective-permute-start(bf16[128,1024]{1,0:T(8,128)(2,1)} %bitcast.7), channel_id=1, source_target_pairs={{0,1},{1,0},{2,3},{3,2},{4,5},{5,4},{6,7},{7,6},{8,9},{9,8},{10,11... | collective-permute-start | bytes 786440 | tf_op jit(solution)/shard_map/ppermute | solution.py:37
  10.3 26.3 %collective-permute-start.6 = (bf16[128,1024]{1,0:T(8,128)(2,1)S(1)}, bf16[128,1024]{1,0:T(8,128)(2,1)S(1)}, u32[]{:S(2)}, u32[]{:S(2)}) collective-permute-start(bf16[128,1024]{1,0:T(8,128)(2,1)S(1)} %collective-permute-done.2.refs_3_.refs_11_), channel_id=1, source_target_pairs={{0,1},{1,0},{2,3},{3,2},{4,5},{5,4},{6,7},{7,6},{8,9},{9,8},{10,11... | collective-permute-start | bytes 786440 | tf_op jit(solution)/shard_map/ppermute | solution.py:37
  26.8 9.8 %collective-permute-start.5 = (bf16[128,1024]{1,0:T(8,128)(2,1)S(1)}, bf16[128,1024]{1,0:T(8,128)(2,1)S(1)}, u32[]{:S(2)}, u32[]{:S(2)}) collective-permute-start(bf16[128,1024]{1,0:T(8,128)(2,1)S(1)} %collective-permute-done.1.refs_2_.refs_10_), channel_id=1, source_target_pairs={{0,1},{1,0},{2,3},{3,2},{4,5},{5,4},{6,7},{7,6},{8,9},{9,8},{10,11... | collective-permute-start | bytes 786440 | tf_op jit(solution)/shard_map/ppermute | solution.py:37
  28.0 10.6 %collective-permute-start.4 = (bf16[128,1024]{1,0:T(8,128)(2,1)S(1)}, bf16[128,1024]{1,0:T(8,128)(2,1)S(1)}, u32[]{:S(2)}, u32[]{:S(2)}) collective-permute-start(bf16[128,1024]{1,0:T(8,128)(2,1)S(1)} %collective-permute-done.refs_1_.refs_9_), channel_id=1, source_target_pairs={{0,1},{1,0},{2,3},{3,2},{4,5},{5,4},{6,7},{7,6},{8,9},{9,8},{10,11... | collective-permute-start | bytes 786440 | tf_op jit(solution)/shard_map/ppermute | solution.py:37
  28.2 10.4 %copy-start = (bf16[1,128,1024]{2,1,0:T(8,128)(2,1)S(1)}, bf16[1,128,1024]{2,1,0:T(8,128)(2,1)}, u32[]{:S(2)}) copy-start(bf16[1,128,1024]{2,1,0:T(8,128)(2,1)} %param.6) | copy-start | bytes 786436
  28.2 10.4 %copy-start.3 = (f32[1,512]{1,0:T(1,128)S(1)}, f32[1,512]{1,0:T(1,128)}, u32[]{:S(2)}) copy-start(f32[1,512]{1,0:T(1,128)} %refs_9_.1) | copy-start | bytes 6148
  36.5 35.8 %copy-start.1 = (bf16[1,128,1024]{2,1,0:T(8,128)(2,1)S(1)}, bf16[1,128,1024]{2,1,0:T(8,128)(2,1)}, u32[]{:S(2)}) copy-start(bf16[1,128,1024]{2,1,0:T(8,128)(2,1)} %param.7) | copy-start | bytes 786436
  36.5 35.8 %copy-start.2 = (f32[1,1024]{1,0:T(1,128)S(1)}, f32[1,1024]{1,0:T(1,128)}, u32[]{:S(2)}) copy-start(f32[1,1024]{1,0:T(1,128)} %refs_17_.1) | copy-start | bytes 12292
  41.6 8.9 %collective-permute-start.10 = (bf16[128,512]{1,0:T(8,128)(2,1)S(1)}, bf16[128,512]{1,0:T(8,128)(2,1)S(1)}, u32[]{:S(2)}, u32[]{:S(2)}) collective-permute-start(bf16[128,512]{1,0:T(8,128)(2,1)S(1)} %get-tuple-element.17.refs_0_.refs_1_), channel_id=1, source_target_pairs={{0,1},{1,0},{2,3},{3,2},{4,5},{5,4},{6,7},{7,6},{8,9},{9,8},{10,11... | collective-permute-start | bytes 393224 | tf_op jit(solution)/shard_map/ppermute | solution.py:37
  42.9 9.8 %collective-permute-start.9 = (bf16[128,512]{1,0:T(8,128)(2,1)S(1)}, bf16[128,512]{1,0:T(8,128)(2,1)S(1)}, u32[]{:S(2)}, u32[]{:S(2)}) collective-permute-start(bf16[128,512]{1,0:T(8,128)(2,1)S(1)} %get-tuple-element.17.refs_0_.refs_1_), channel_id=1, source_target_pairs={{0,6},{1,7},{2,0},{3,1},{4,2},{5,3},{6,4},{7,5},{8,14},{9,15},{10,... | collective-permute-start | bytes 393224 | tf_op jit(solution)/shard_map/ppermute | solution.py:32
  42.9 11.8 %collective-permute-start.14 = (bf16[128,512]{1,0:T(8,128)(2,1)S(1)}, bf16[128,512]{1,0:T(8,128)(2,1)S(1)}, u32[]{:S(2)}, u32[]{:S(2)}) collective-permute-start(bf16[128,512]{1,0:T(8,128)(2,1)S(1)} %get-tuple-element.17.refs_0_.refs_1_), channel_id=1, source_target_pairs={{0,8},{8,16},{16,24},{1,9},{9,17},{17,25},{2,10},{10,18},{18,26},{... | collective-permute-start | bytes 393224 | tf_op jit(solution)/shard_map/ppermute | solution.py:19
  48.6 10.6 %collective-permute-start.8 = (bf16[128,512]{1,0:T(8,128)(2,1)S(1)}, bf16[128,512]{1,0:T(8,128)(2,1)S(1)}, u32[]{:S(2)}, u32[]{:S(2)}) collective-permute-start(bf16[128,512]{1,0:T(8,128)(2,1)S(1)} %get-tuple-element.17.refs_0_.refs_1_), channel_id=1, source_target_pairs={{0,4},{1,5},{2,6},{3,7},{4,0},{5,1},{6,2},{7,3},{8,12},{9,13},{10,... | collective-permute-start | bytes 393224 | tf_op jit(solution)/shard_map/ppermute | solution.py:32
  48.7 10.7 %collective-permute-start.7 = (bf16[128,512]{1,0:T(8,128)(2,1)S(1)}, bf16[128,512]{1,0:T(8,128)(2,1)S(1)}, u32[]{:S(2)}, u32[]{:S(2)}) collective-permute-start(bf16[128,512]{1,0:T(8,128)(2,1)S(1)} %get-tuple-element.17.refs_0_.refs_1_), channel_id=1, source_target_pairs={{0,2},{1,3},{2,4},{3,5},{4,6},{5,7},{6,0},{7,1},{8,10},{9,11},{10,... | collective-permute-start | bytes 393224 | tf_op jit(solution)/shard_map/ppermute | solution.py:32
  50.5 10.2 %collective-permute-start.18 = (bf16[128,512]{1,0:T(8,128)(2,1)S(1)}, bf16[128,512]{1,0:T(8,128)(2,1)S(1)}, u32[]{:S(2)}, u32[]{:S(2)}) collective-permute-start(bf16[128,512]{1,0:T(8,128)(2,1)S(1)} %collective-permute-done.10.refs_4_.refs_5_), channel_id=1, source_target_pairs={{0,8},{8,16},{16,24},{1,9},{9,17},{17,25},{2,10},{10,18},{18,26},{... | collective-permute-start | bytes 393224 | tf_op jit(solution)/shard_map/ppermute | solution.py:19
  52.7 9.9 %collective-permute-start.17 = (bf16[128,512]{1,0:T(8,128)(2,1)S(1)}, bf16[128,512]{1,0:T(8,128)(2,1)S(1)}, u32[]{:S(2)}, u32[]{:S(2)}) collective-permute-start(bf16[128,512]{1,0:T(8,128)(2,1)S(1)} %collective-permute-done.9.refs_3_.refs_4_), channel_id=1, source_target_pairs={{0,8},{8,16},{16,24},{1,9},{9,17},{17,25},{2,10},{10,18},{18,26},{... | collective-permute-start | bytes 393224 | tf_op jit(solution)/shard_map/ppermute | solution.py:19
  54.6 9.9 %collective-permute-start.13 = (bf16[128,512]{1,0:T(8,128)(2,1)S(1)}, bf16[128,512]{1,0:T(8,128)(2,1)S(1)}, u32[]{:S(2)}, u32[]{:S(2)}) collective-permute-start(bf16[128,512]{1,0:T(8,128)(2,1)S(1)} %collective-permute-done.9.refs_3_.refs_4_), channel_id=1, source_target_pairs={{0,1},{1,0},{2,3},{3,2},{4,5},{5,4},{6,7},{7,6},{8,9},{9,8},{10,11... | collective-permute-start | bytes 393224 | tf_op jit(solution)/shard_map/ppermute | solution.py:37
  59.2 7.3 %collective-permute-start.12 = (bf16[128,512]{1,0:T(8,128)(2,1)S(1)}, bf16[128,512]{1,0:T(8,128)(2,1)S(1)}, u32[]{:S(2)}, u32[]{:S(2)}) collective-permute-start(bf16[128,512]{1,0:T(8,128)(2,1)S(1)} %collective-permute-done.8.refs_2_.refs_3_), channel_id=1, source_target_pairs={{0,1},{1,0},{2,3},{3,2},{4,5},{5,4},{6,7},{7,6},{8,9},{9,8},{10,11... | collective-permute-start | bytes 393224 | tf_op jit(solution)/shard_map/ppermute | solution.py:37
  59.4 9.0 %collective-permute-start.11 = (bf16[128,512]{1,0:T(8,128)(2,1)S(1)}, bf16[128,512]{1,0:T(8,128)(2,1)S(1)}, u32[]{:S(2)}, u32[]{:S(2)}) collective-permute-start(bf16[128,512]{1,0:T(8,128)(2,1)S(1)} %collective-permute-done.7.refs_1_.refs_2_), channel_id=1, source_target_pairs={{0,1},{1,0},{2,3},{3,2},{4,5},{5,4},{6,7},{7,6},{8,9},{9,8},{10,11... | collective-permute-start | bytes 393224 | tf_op jit(solution)/shard_map/ppermute | solution.py:37
  60.7 9.7 %collective-permute-start.16 = (bf16[128,512]{1,0:T(8,128)(2,1)S(1)}, bf16[128,512]{1,0:T(8,128)(2,1)S(1)}, u32[]{:S(2)}, u32[]{:S(2)}) collective-permute-start(bf16[128,512]{1,0:T(8,128)(2,1)S(1)} %collective-permute-done.8.refs_2_.refs_3_), channel_id=1, source_target_pairs={{0,8},{8,16},{16,24},{1,9},{9,17},{17,25},{2,10},{10,18},{18,26},{... | collective-permute-start | bytes 393224 | tf_op jit(solution)/shard_map/ppermute | solution.py:19
  62.6 7.8 %collective-permute-start.15 = (bf16[128,512]{1,0:T(8,128)(2,1)S(1)}, bf16[128,512]{1,0:T(8,128)(2,1)S(1)}, u32[]{:S(2)}, u32[]{:S(2)}) collective-permute-start(bf16[128,512]{1,0:T(8,128)(2,1)S(1)} %collective-permute-done.7.refs_1_.refs_2_), channel_id=1, source_target_pairs={{0,8},{8,16},{16,24},{1,9},{9,17},{17,25},{2,10},{10,18},{18,26},{... | collective-permute-start | bytes 393224 | tf_op jit(solution)/shard_map/ppermute | solution.py:19
  64.5 5.8 %collective-permute-start.21 = (bf16[128,512]{1,0:T(8,128)(2,1)S(1)}, bf16[128,512]{1,0:T(8,128)(2,1)S(1)}, u32[]{:S(2)}, u32[]{:S(2)}) collective-permute-start(bf16[128,512]{1,0:T(8,128)(2,1)S(1)} %collective-permute-done.13.refs_7_.refs_8_), channel_id=1, source_target_pairs={{0,8},{8,16},{16,24},{1,9},{9,17},{17,25},{2,10},{10,18},{18,26},{... | collective-permute-start | bytes 393224 | tf_op jit(solution)/shard_map/ppermute | solution.py:19
  66.5 3.9 %collective-permute-start.20 = (bf16[128,512]{1,0:T(8,128)(2,1)S(1)}, bf16[128,512]{1,0:T(8,128)(2,1)S(1)}, u32[]{:S(2)}, u32[]{:S(2)}) collective-permute-start(bf16[128,512]{1,0:T(8,128)(2,1)S(1)} %collective-permute-done.12.refs_6_.refs_7_), channel_id=1, source_target_pairs={{0,8},{8,16},{16,24},{1,9},{9,17},{17,25},{2,10},{10,18},{18,26},{... | collective-permute-start | bytes 393224 | tf_op jit(solution)/shard_map/ppermute | solution.py:19
  68.4 3.9 %collective-permute-start.19 = (bf16[128,512]{1,0:T(8,128)(2,1)S(1)}, bf16[128,512]{1,0:T(8,128)(2,1)S(1)}, u32[]{:S(2)}, u32[]{:S(2)}) collective-permute-start(bf16[128,512]{1,0:T(8,128)(2,1)S(1)} %collective-permute-done.11.refs_5_.refs_6_), channel_id=1, source_target_pairs={{0,8},{8,16},{16,24},{1,9},{9,17},{17,25},{2,10},{10,18},{18,26},{... | collective-permute-start | bytes 393224 | tf_op jit(solution)/shard_map/ppermute | solution.py:19
  81.1 17.1 %collective-permute-start.22 = (bf16[128,4096]{1,0:T(8,128)(2,1)S(1)}, bf16[128,4096]{1,0:T(8,128)(2,1)S(1)}, u32[]{:S(2)}, u32[]{:S(2)}) collective-permute-start(bf16[128,4096]{1,0:T(8,128)(2,1)S(1)} %get-tuple-element.20), channel_id=1, source_target_pairs={{8,0},{16,8},{24,16},{9,1},{17,9},{25,17},{10,2},{18,10},{26,18},{... | collective-permute-start | bytes 3145736 | tf_op jit(solution)/shard_map/ppermute | solution.py:19
  98.4 6.7 %collective-permute-start.23 = (bf16[128,512]{1,0:T(8,128)(2,1)S(1)}, bf16[128,512]{1,0:T(8,128)(2,1)S(1)}, u32[]{:S(2)}, u32[]{:S(2)}) collective-permute-start(bf16[128,512]{1,0:T(8,128)(2,1)S(1)} %get-tuple-element.22), channel_id=1, source_target_pairs={{0,1},{1,2},{2,3},{3,4},{4,5},{5,6},{6,7},{7,0},{8,9},{9,10},{10,1... | collective-permute-start | bytes 393224 | tf_op jit(solution)/shard_map/ppermute | solution.py:32
  98.5 6.8 %collective-permute-start.24 = (bf16[128,512]{1,0:T(8,128)(2,1)S(1)}, bf16[128,512]{1,0:T(8,128)(2,1)S(1)}, u32[]{:S(2)}, u32[]{:S(2)}) collective-permute-start(bf16[128,512]{1,0:T(8,128)(2,1)S(1)} %get-tuple-element.23), channel_id=1, source_target_pairs={{0,2},{1,3},{2,4},{3,5},{4,6},{5,7},{6,0},{7,1},{8,10},{9,11},{10,... | collective-permute-start | bytes 393224 | tf_op jit(solution)/shard_map/ppermute | solution.py:32
  98.6 17.4 %collective-permute-start.25 = (bf16[128,512]{1,0:T(8,128)(2,1)S(1)}, bf16[128,512]{1,0:T(8,128)(2,1)S(1)}, u32[]{:S(2)}, u32[]{:S(2)}) collective-permute-start(bf16[128,512]{1,0:T(8,128)(2,1)S(1)} %get-tuple-element.24), channel_id=1, source_target_pairs={{0,3},{1,4},{2,5},{3,6},{4,7},{5,0},{6,1},{7,2},{8,11},{9,12},{10,... | collective-permute-start | bytes 393224 | tf_op jit(solution)/shard_map/ppermute | solution.py:32
  99.9 16.0 %collective-permute-start.26 = (bf16[128,512]{1,0:T(8,128)(2,1)S(1)}, bf16[128,512]{1,0:T(8,128)(2,1)S(1)}, u32[]{:S(2)}, u32[]{:S(2)}) collective-permute-start(bf16[128,512]{1,0:T(8,128)(2,1)S(1)} %get-tuple-element.25), channel_id=1, source_target_pairs={{0,4},{1,5},{2,6},{3,7},{4,0},{5,1},{6,2},{7,3},{8,12},{9,13},{10,... | collective-permute-start | bytes 393224 | tf_op jit(solution)/shard_map/ppermute | solution.py:32
  102.9 13.0 %collective-permute-start.27 = (bf16[128,512]{1,0:T(8,128)(2,1)S(1)}, bf16[128,512]{1,0:T(8,128)(2,1)S(1)}, u32[]{:S(2)}, u32[]{:S(2)}) collective-permute-start(bf16[128,512]{1,0:T(8,128)(2,1)S(1)} %get-tuple-element.26), channel_id=1, source_target_pairs={{0,5},{1,6},{2,7},{3,0},{4,1},{5,2},{6,3},{7,4},{8,13},{9,14},{10,... | collective-permute-start | bytes 393224 | tf_op jit(solution)/shard_map/ppermute | solution.py:32
  105.1 10.8 %collective-permute-start.28 = (bf16[128,512]{1,0:T(8,128)(2,1)S(1)}, bf16[128,512]{1,0:T(8,128)(2,1)S(1)}, u32[]{:S(2)}, u32[]{:S(2)}) collective-permute-start(bf16[128,512]{1,0:T(8,128)(2,1)S(1)} %get-tuple-element.27), channel_id=1, source_target_pairs={{0,6},{1,7},{2,0},{3,1},{4,2},{5,3},{6,4},{7,5},{8,14},{9,15},{10,... | collective-permute-start | bytes 393224 | tf_op jit(solution)/shard_map/ppermute | solution.py:32
  105.3 10.6 %collective-permute-start.29 = (bf16[128,512]{1,0:T(8,128)(2,1)S(1)}, bf16[128,512]{1,0:T(8,128)(2,1)S(1)}, u32[]{:S(2)}, u32[]{:S(2)}) collective-permute-start(bf16[128,512]{1,0:T(8,128)(2,1)S(1)} %get-tuple-element.28), channel_id=1, source_target_pairs={{0,7},{1,0},{2,1},{3,2},{4,3},{5,4},{6,5},{7,6},{8,15},{9,8},{10,9... | collective-permute-start | bytes 393224 | tf_op jit(solution)/shard_map/ppermute | solution.py:32

commit v2 on v0

v2 whole, which is shorter than its diff:
```python
import functools

import jax
import jax.numpy as jnp
from jax import lax
from jax.experimental import pallas as pl
from jax.experimental.pallas import tpu as pltpu
from jax.sharding import PartitionSpec as P

LANES = 128
MIB = 1024 * 1024
BF16 = jnp.bfloat16
F32 = jnp.float32

MASKS = (0, 2, 6, 4, 1, 3, 7, 5)
NEAR = (0, 1, 2, 3)
FAR = (6, 7, 4, 5)
BLOCKS = ((0,), (1, 2, 3), (6, 4), (7, 5))


def from_behind(value, axis, steps):
    count = lax.axis_size(axis)
    initial, last = (max(0, -steps), min(count, count - steps))
    return lax.ppermute(value, axis, [(source, source + steps) for source in range(initial, last)])


def transposed(left, right):
    return lax.dot_general(left, right, (((0,), (0,)), ((), ())), preferred_element_type=F32)


def against(left, right):
    return lax.dot_general(left, right, (((1,), (1,)), ((), ())), preferred_element_type=F32)


def exchanged(value, mask):
    count = lax.axis_size("feat")
    return lax.ppermute(value, "feat", [(i, i ^ mask) for i in range(count)])


def owner(mask):
    return jnp.bitwise_xor(lax.axis_index("feat"), mask)


def columns(index, width):
    return pl.ds(pl.multiple_of(index * width, width), width)


def vmem(count):
    return [pl.BlockSpec(memory_space=pltpu.VMEM)] * count


def params(mib):
    return pltpu.CompilerParams(vmem_limit_bytes=mib * MIB)


def flat(groups):
    return [(i, row, mask) for i, masks in enumerate(groups) for row, mask in enumerate(masks)]


def fetch_kernel(_, enc_ref, dec_ref, enc_out, dec_out, sems):
    copies = [
        pltpu.make_async_copy(enc_ref, enc_out, sems.at[0]),
        pltpu.make_async_copy(dec_ref.at[0], dec_out.at[0], sems.at[1]),
        pltpu.make_async_copy(dec_ref.at[1], dec_out.at[1], sems.at[2]),
    ]
    for copy in copies:
        copy.start()
    for copy in copies:
        copy.wait()


def pack_kernel(count, *refs):
    out_ref, start = refs[-1], 0
    for ref in refs[:count]:
        out_ref[start : start + ref.shape[0], :] = ref[...]
        start += ref.shape[0]


def packed(parts, after=()):
    rows = sum(part.shape[0] for part in parts)
    return pl.pallas_call(
        functools.partial(pack_kernel, len(parts)),
        name="pack",
        out_shape=jax.ShapeDtypeStruct((rows, parts[0].shape[1]), parts[0].dtype),
        in_specs=[*vmem(len(parts)), *[pl.BlockSpec(memory_space=pl.ANY) for _ in after]],
        out_specs=vmem(1)[0],
        compiler_params=params(1),
        cost_estimate=pl.CostEstimate(
            flops=0, bytes_accessed=4 * rows * parts[0].shape[1], transcendentals=0
        ),
    )(*parts, *after)


def pre_kernel(*refs):
    parts, (w_ref, b_ref, codes_ref, active_ref) = refs[: len(MASKS)], refs[len(MASKS) :]
    width = parts[0].shape[1]
    total = None
    for mask, part in zip(MASKS, parts):
        term = against(part[...], w_ref[:, columns(owner(mask), width)])
        total = term if total is None else total + term
    active = jnp.maximum(total + b_ref[...], 0.0)
    active_ref[...] = active
    codes_ref[...] = (active * active).astype(BF16)


def decoded(w_ref, slot, here, parts, groups, tok, total):
    width = parts[0].shape[1]
    for i, row, mask in flat(groups):
        part = parts[i][row * tok : (row + 1) * tok, :]
        term = against(w_ref[slot, here, columns(owner(mask), width)], part)
        total = term if total is None else total + term
    return total


def tiles(size):
    tile = 256 if size % 256 == 0 else LANES
    return size // tile, tile


def own_recon_kernel(*refs):
    parts, (w_ref, total_ref) = refs[: len(BLOCKS)], refs[len(BLOCKS) :]
    tok = total_ref.shape[1]
    steps, tile = tiles(w_ref.shape[1])

    @pl.loop(0, steps)
    def _(j):
        here = pl.ds(pl.multiple_of(j * tile, tile), tile)
        total_ref[here, :] = decoded(w_ref, 0, here, parts, BLOCKS, tok, None)


def product(error_ref, w_ref, slot, out_ref, first):
    wide = out_ref.shape[1]
    steps, tile = (wide // 512, 512) if wide % 512 == 0 else (wide // LANES, LANES)

    @pl.loop(0, steps)
    def _(j):
        source = pl.ds(pl.multiple_of(first * wide + j * tile, tile), tile)
        here = pl.ds(pl.multiple_of(j * tile, tile), tile)
        out_ref[:, here] = jnp.dot(
            error_ref[...], w_ref[slot, :, source], preferred_element_type=F32
        ).astype(out_ref.dtype)


def halves():
    near = lax.axis_index("feat") // (len(MASKS) // 2)
    return near, 1 - near


def recon_kernel(scale, *refs):
    parts, (total_ref, w_ref, b_ref, target_ref, error_ref, far_ref) = refs[: len(BLOCKS)], refs[len(BLOCKS) :]
    tok = total_ref.shape[1]
    steps, tile = tiles(w_ref.shape[1])

    @pl.loop(0, steps)
    def _(j):
        here = pl.ds(pl.multiple_of(j * tile, tile), tile)
        total = decoded(w_ref, 1, here, parts, BLOCKS, tok, total_ref[here, :])
        error = total.T + b_ref[:, here] - target_ref[:, here].astype(F32)
        error_ref[:, here] = (error * scale).astype(BF16)

    product(error_ref, w_ref, 1, far_ref, halves()[1])


def near_kernel(error_ref, w_ref, near_ref):
    product(error_ref, w_ref, 1, near_ref, halves()[0])


def own_grad_kernel(error_ref, w_ref, near_ref, far_ref):
    near, far = halves()
    product(error_ref, w_ref, 0, far_ref, far)
    product(error_ref, w_ref, 0, near_ref, near)


def dec_grad_kernel(groups, *refs):
    error_ref, parts, out_ref = refs[0], refs[1 : 1 + len(groups)], refs[-1]
    width = parts[0].shape[1]
    tok = error_ref.shape[0]
    for i, row, mask in flat(groups):
        part = parts[i][row * tok : (row + 1) * tok, :]
        out_ref[0, 0, :, columns(owner(mask), width)] = transposed(error_ref[...], part).astype(BF16)


def sum_kernel(masks, own_ref, arrived_ref, _, *outs):
    width = outs[0].shape[1]
    for mask, out_ref in zip(masks, outs):
        here = columns(lax.rem(owner(mask), len(MASKS) // 2), width)
        total = own_ref[:, here] + arrived_ref[:, here].astype(F32)
        out_ref[...] = total.astype(out_ref.dtype)


def enc_grad_kernel(*refs):
    count = len(MASKS)
    grads, parts = refs[:count], refs[count : 2 * count]
    active_ref, out_ref = refs[2 * count :]
    width = parts[0].shape[1]
    total = grads[0][...]
    for grad in grads[1:]:
        total = total + grad[...].astype(F32)
    pre_grad = (total * 2.0 * active_ref[...]).astype(BF16)
    for mask, part in zip(MASKS, parts):
        out_ref[0, :, columns(owner(mask), width)] = transposed(pre_grad, part[...]).astype(BF16)


def cost(flops, moved):
    return pl.CostEstimate(flops=flops, bytes_accessed=moved, transcendentals=0)


def on_device(inputs, targets, enc_w, enc_b, dec_w, dec_b):
    count = len(MASKS)
    tok, width = inputs.shape[1:]
    own_features, model = enc_w.shape[1:]
    features = dec_w.shape[3]
    scale = tok ** (-0.5)
    matmul = 2 * tok * width * features
    half = (tok, features // 2)
    struct = jax.ShapeDtypeStruct

    blocks = {0: inputs[0]}
    blocks[2] = exchanged(blocks[0], 2)
    blocks[6] = exchanged(blocks[0], 6)
    blocks[1] = exchanged(blocks[0], 1)
    blocks[3] = exchanged(blocks[0], 3)
    blocks[4] = exchanged(blocks[2], 6)
    for mask in (6, 4):
        blocks[mask ^ 1] = exchanged(blocks[mask], 1)
    inputs_of = [blocks[mask] for mask in MASKS]

    enc_weights, weights = pl.pallas_call(
        fetch_kernel,
        name="fetch",
        out_shape=(pltpu.VMEM(enc_w.shape[1:], BF16), pltpu.VMEM(dec_w.shape[1:], BF16)),
        in_specs=[pl.BlockSpec(memory_space=pl.ANY), *[pl.BlockSpec(memory_space=pltpu.HBM)] * 2],
        out_specs=tuple(vmem(2)),
        scratch_shapes=[pltpu.SemaphoreType.DMA((3,))],
        compiler_params=params(1),
        cost_estimate=cost(0, 2 * (own_features * model + 2 * width * features)),
    )(blocks[6], *[pltpu.with_memory_space_constraint(w[0], pltpu.HBM) for w in (enc_w, dec_w)])

    codes, active = pl.pallas_call(
        pre_kernel,
        name="pre",
        out_shape=(struct((tok, own_features), BF16), struct((tok, own_features), F32)),
        in_specs=vmem(count + 2),
        out_specs=tuple(vmem(2)),
        compiler_params=params(16),
        cost_estimate=cost(matmul, 4 * MIB),
    )(*inputs_of, enc_weights, enc_b)

    near_line = exchanged(codes, 2)
    across = exchanged(codes, 1)
    far_line = exchanged(codes, 6)
    farther_line = exchanged(codes, 4)
    near_across = exchanged(codes, 3)
    near_three = packed((across, near_line, near_across))
    previous_codes = from_behind(codes, "section", 1)
    previous_near = from_behind(near_three, "section", 1)
    far_pair = packed((far_line, farther_line), (previous_codes, near_three))
    far_across = exchanged(far_pair, 1)
    own = [codes, near_three, far_pair, far_across]
    previous = [
        previous_codes,
        previous_near,
        from_behind(far_pair, "section", 1),
        from_behind(far_across, "section", 1),
    ]

    total = pl.pallas_call(
        own_recon_kernel,
        name="own_recon",
        out_shape=struct((width, tok), F32),
        in_specs=vmem(len(own) + 1),
        out_specs=vmem(1)[0],
        compiler_params=params(8),
        cost_estimate=cost(matmul, 4 * MIB),
    )(*own, weights)

    error, sent_far = pl.pallas_call(
        functools.partial(recon_kernel, scale),
        name="recon",
        out_shape=(struct((tok, width), BF16), struct(half, BF16)),
        in_specs=vmem(len(previous) + 4),
        out_specs=tuple(vmem(2)),
        compiler_params=params(8),
        cost_estimate=cost(2 * matmul, 4 * MIB),
    )(*previous, total, weights, dec_b, targets[0])
    arrived_far = from_behind(sent_far, "section", -1)

    sent_near = pl.pallas_call(
        near_kernel,
        name="near",
        out_shape=struct(half, BF16),
        in_specs=vmem(2),
        out_specs=vmem(1)[0],
        compiler_params=params(8),
        cost_estimate=cost(matmul // 2, 2 * MIB),
    )(error, weights)
    arrived_near = from_behind(sent_near, "section", -1)

    own_near, own_far = pl.pallas_call(
        own_grad_kernel,
        name="own_grad",
        out_shape=(struct(half, F32), struct(half, F32)),
        in_specs=vmem(2),
        out_specs=tuple(vmem(2)),
        compiler_params=params(8),
        cost_estimate=cost(matmul, 4 * MIB),
    )(error, weights)

    rows = 256 if width % 256 == 0 else LANES

    def dec_grad_slot(slot, groups, parts, *held):
        return pl.pallas_call(
            functools.partial(dec_grad_kernel, groups),
            name="dec_grad",
            grid=(width // rows,),
            out_shape=struct(dec_w.shape, BF16),
            in_specs=[
                pl.BlockSpec((tok, rows), lambda j: (0, j)),
                *[pl.BlockSpec(part.shape, lambda j: (0, 0)) for part in parts],
                *[pl.BlockSpec(memory_space=pl.ANY) for _ in held],
            ],
            out_specs=pl.BlockSpec((1, 1, rows, features), lambda j: (0, slot, j, 0)),
            input_output_aliases={1 + len(parts): 0} if held else {},
            compiler_params=params(12),
            cost_estimate=cost(matmul, 2 * width * features),
        )(error, *parts, *held)

    dec_grad = dec_grad_slot(0, BLOCKS, own)

    def pieces_of(masks, own_half, arrived):
        return pl.pallas_call(
            functools.partial(sum_kernel, masks),
            name="sum",
            out_shape=tuple(struct((tok, own_features), F32 if mask == 0 else BF16) for mask in masks),
            in_specs=[*vmem(2), pl.BlockSpec(memory_space=pl.ANY)],
            out_specs=tuple(vmem(len(masks))),
            compiler_params=params(2),
            cost_estimate=cost(tok * features, 2 * MIB),
        )(own_half, arrived, dec_grad)

    grads = {}
    for masks, own_half, arrived in ((FAR, own_far, arrived_far), (NEAR, own_near, arrived_near)):
        for mask, piece in zip(masks, pieces_of(masks, own_half, arrived)):
            grads[mask] = exchanged(piece, mask) if mask else piece
    dec_grad = dec_grad_slot(1, BLOCKS, previous, dec_grad)

    block = 128 if own_features % 128 == 0 else own_features
    enc_grad = pl.pallas_call(
        enc_grad_kernel,
        name="enc_grad",
        grid=(own_features // block,),
        out_shape=struct(enc_w.shape, BF16),
        in_specs=[
            *[pl.BlockSpec((tok, block), lambda j: (0, j))] * count,
            *[pl.BlockSpec((tok, width), lambda j: (0, 0))] * count,
            pl.BlockSpec((tok, block), lambda j: (0, j)),
        ],
        out_specs=pl.BlockSpec((1, block, model), lambda j: (0, j, 0)),
        compiler_params=params(16),
        cost_estimate=cost(matmul, 2 * own_features * model),
    )(*[grads[mask] for mask in MASKS], *inputs_of, active)
    return enc_grad, dec_grad


def plain(inputs, targets, enc_w, enc_b, dec_w, dec_b):
    scale = inputs.shape[1] ** (-0.5)
    gathered = lax.all_gather(inputs[0], "feat", axis=1, tiled=True)
    active = jnp.maximum(against(gathered, enc_w[0]) + enc_b[0], 0.0)
    codes = (active * active).astype(BF16)
    own = lax.all_gather(codes, "feat", axis=1, tiled=True)
    previous = from_behind(own, "section", 1)
    weights = dec_w[0]
    total = dec_b[0] + against(own, weights[0]) + against(previous, weights[1])
    error = ((total - targets[0].astype(F32)) * scale).astype(BF16)
    sent = jnp.dot(error, weights[1], preferred_element_type=F32)
    code_grad = jnp.dot(error, weights[0], preferred_element_type=F32) + from_behind(sent, "section", -1)
    mine = lax.psum_scatter(code_grad, "feat", scatter_dimension=1, tiled=True)
    pre_grad = (mine * 2.0 * active).astype(BF16)
    enc_grad = transposed(pre_grad, gathered).astype(BF16)[None]
    dec_grad = jnp.stack([transposed(error, source).astype(BF16) for source in (own, previous)])[None]
    return enc_grad, dec_grad


def chosen(inputs, targets, enc_w, enc_b, dec_w, dec_b):
    aligned = all(size % LANES == 0 for size in (*inputs.shape[1:], enc_w.shape[1]))
    fits = lax.axis_size("feat") == len(MASKS) and dec_w.shape[1] == 2
    body = on_device if aligned and fits else plain
    return body(inputs, targets, enc_w, enc_b, dec_w, dec_b)


def solution(mesh):
    return jax.shard_map(
        chosen,
        mesh=mesh,
        in_specs=(
            P("section", None, "feat"),
            P("section", None, "feat"),
            P("section", "feat", None),
            P("section", "feat"),
            P("section", None, "feat", None),
            P("section", "feat"),
        ),
        out_specs=(P("section", "feat", None), P("section", None, "feat", None)),
        check_vma=False,
    )
```

time: 225 us -> 130 us (0.58)
  the two profiles are of different devices: /device:TPU:1 before, /device:TPU:2 now
where the time goes in v2:
time: 130 us
  starting transfers between devices  51.1 us (39%)
  Pallas kernels  37.8 us (29%)
  waiting for transfers between devices  34.7 us (27%)
  local copies, waits for them, and re-layouts  5.79 us (4%)
    ppermute x20, starting transfers between devices, exchanged(): return lax.ppermute(value, 'feat', [(i, i ^ mask) for i in range(count)])  39.6 us
    ppermute x20, waiting for transfers between devices, exchanged(): return lax.ppermute(value, 'feat', [(i, i ^ mask) for i in range(count)])  29.3 us
    ppermute x6, starting transfers between devices, from_behind(): lax.ppermute(value, axis, [(source, source + steps) for source in range(i...  11.5 us
    pallas_call x2, Pallas kernels, dec_grad_slot(): pl.pallas_call(functools.partial(dec_grad_kernel, groups), name='dec_grad...  9.85 us
    pallas_call x1, Pallas kernels, on_device(): pl.pallas_call(fetch_kernel, name='fetch', out_shape=(pltpu.VMEM(enc_w.sh...  8.18 us
    unnamed x10, local copies, waits for them, and re-layouts  5.79 us
    ppermute x6, waiting for transfers between devices, from_behind(): lax.ppermute(value, axis, [(source, source + steps) for source in range(i...  5.39 us
    pallas_call x1, Pallas kernels, on_device(): pl.pallas_call(enc_grad_kernel, name='enc_grad', grid=(own_features // bl...  5.27 us
  transfers between devices with their start and end apart: 26, of which 11 were waited for; matrix products, arithmetic and copies ran while one was open for 0% of the time, Pallas kernels for 19%

profile of v2, /device:TPU:2, one launch (start us, length us, event | category | flops | bytes accessed | tf_op | source)
XLA Modules:
  0.0 130.2 jit_solution(15137283703285045893)
XLA Ops:
  0.7 1.6 %collective-permute-start = (bf16[128,1024]{1,0:T(8,128)(2,1)}, bf16[128,1024]{1,0:T(8,128)(2,1)S(1)}, u32[]{:S(2)}, u32[]{:S(2)}) collective-permute-start(bf16[128,1024]{1,0:T(8,128)(2,1)} %bitcast.4), channel_id=1, source_target_pairs={{0,2},{1,3},{2,0},{3,1},{4,6},{5,7},{6,4},{7,5},{8,10},{9,11},{10,... | collective-permute-start | bytes 786440 | tf_op jit(solution)/shard_map/ppermute | solution.py:37
  2.3 2.5 %collective-permute-start.1 = (bf16[128,1024]{1,0:T(8,128)(2,1)}, bf16[128,1024]{1,0:T(8,128)(2,1)S(1)}, u32[]{:S(2)}, u32[]{:S(2)}) collective-permute-start(bf16[128,1024]{1,0:T(8,128)(2,1)} %bitcast.5), channel_id=1, source_target_pairs={{0,6},{1,7},{2,4},{3,5},{4,2},{5,3},{6,0},{7,1},{8,14},{9,15},{10,... | collective-permute-start | bytes 786440 | tf_op jit(solution)/shard_map/ppermute | solution.py:37
  4.8 4.6 %collective-permute-done.refs_1_.refs_9_ = bf16[128,1024]{1,0:T(8,128)(2,1)S(1)} collective-permute-done((bf16[128,1024]{1,0:T(8,128)(2,1)}, bf16[128,1024]{1,0:T(8,128)(2,1)S(1)}, u32[]{:S(2)}, u32[]{:S(2)}) %collective-permute-start) | collective-permute-done | bytes 262176 | tf_op jit(solution)/shard_map/ppermute | solution.py:37
  9.3 11.7 %collective-permute-start.2 = (bf16[128,1024]{1,0:T(8,128)(2,1)S(1)}, bf16[128,1024]{1,0:T(8,128)(2,1)S(1)}, u32[]{:S(2)}, u32[]{:S(2)}) collective-permute-start(bf16[128,1024]{1,0:T(8,128)(2,1)S(1)} %collective-permute-done.refs_1_.refs_9_), channel_id=1, source_target_pairs={{0,6},{1,7},{2,4},{3,5},{4,2},{5,3},{6,0},{7,1},{8,14},{9,15},{10,... | collective-permute-start | bytes 786440 | tf_op jit(solution)/shard_map/ppermute | solution.py:37
  21.0 1.5 %collective-permute-start.3 = (bf16[128,1024]{1,0:T(8,128)(2,1)}, bf16[128,1024]{1,0:T(8,128)(2,1)S(1)}, u32[]{:S(2)}, u32[]{:S(2)}) collective-permute-start(bf16[128,1024]{1,0:T(8,128)(2,1)} %bitcast.7), channel_id=1, source_target_pairs={{0,1},{1,0},{2,3},{3,2},{4,5},{5,4},{6,7},{7,6},{8,9},{9,8},{10,11... | collective-permute-start | bytes 786440 | tf_op jit(solution)/shard_map/ppermute | solution.py:37
  22.5 0.5 collective-permute-start.5
  23.0 2.4 %collective-permute-done.2.refs_3_.refs_11_ = bf16[128,1024]{1,0:T(8,128)(2,1)S(1)} collective-permute-done((bf16[128,1024]{1,0:T(8,128)(2,1)S(1)}, bf16[128,1024]{1,0:T(8,128)(2,1)S(1)}, u32[]{:S(2)}, u32[]{:S(2)}) %collective-permute-start.2) | collective-permute-done | bytes 262176 | tf_op jit(solution)/shard_map/ppermute | solution.py:37
  25.5 1.6 %collective-permute-start.6 = (bf16[128,1024]{1,0:T(8,128)(2,1)S(1)}, bf16[128,1024]{1,0:T(8,128)(2,1)S(1)}, u32[]{:S(2)}, u32[]{:S(2)}) collective-permute-start(bf16[128,1024]{1,0:T(8,128)(2,1)S(1)} %collective-permute-done.2.refs_3_.refs_11_), channel_id=1, source_target_pairs={{0,1},{1,0},{2,3},{3,2},{4,5},{5,4},{6,7},{7,6},{8,9},{9,8},{10,11... | collective-permute-start | bytes 786440 | tf_op jit(solution)/shard_map/ppermute | solution.py:37
  27.1 8.2 %fetch.1 = (bf16[512,8192]{1,0:T(8,128)(2,1)S(1)}, bf16[2,1024,4096]{2,1,0:T(8,128)(2,1)S(1)}) custom-call(bf16[128,1024]{1,0:T(8,128)(2,1)S(1)} %collective-permute-done.1._.refs_2_.refs_10_, bf16[512,8192]{1,0:T(8,128)(2,1)} %bitcast.12, bf16[2,1024,4096]{2,1,0:T(8,128)(2,1)} %bitcast.11), custom_call_target="tpu_custom_call" | custom-call | bytes 25165824 | tf_op jit(solution)/shard_map/fetch/pallas_call | solution.py:228
  35.3 0.0 copy-start.3
  35.3 2.5 %collective-permute-done.6.refs_7_.refs_15_ = bf16[128,1024]{1,0:T(8,128)(2,1)S(1)} collective-permute-done((bf16[128,1024]{1,0:T(8,128)(2,1)S(1)}, bf16[128,1024]{1,0:T(8,128)(2,1)S(1)}, u32[]{:S(2)}, u32[]{:S(2)}) %collective-permute-start.6) | collective-permute-done | bytes 262176 | tf_op jit(solution)/shard_map/ppermute | solution.py:37
  37.8 2.9 %pre.1 = (bf16[128,512]{1,0:T(8,128)(2,1)S(1)}, f32[128,512]{1,0:T(8,128)S(1)}) custom-call(bf16[128,1024]{1,0:T(8,128)(2,1)S(1)} %bitcast.8, bf16[128,1024]{1,0:T(8,128)(2,1)S(1)} %collective-permute-done.refs_1_.refs_9_, bf16[128,1024]{1,0:T(8,128)(2,1)S(1)} %collective-permute-done.1._.refs_2_.refs_10_, ...), custom_call_target="tpu_custom_call" | custom-call | flops 1073741824 | bytes 4194304 | tf_op jit(solution)/shard_map/pre/pallas_call | solution.py:239
  40.7 4.0 %collective-permute-start.10 = (bf16[128,512]{1,0:T(8,128)(2,1)S(1)}, bf16[128,512]{1,0:T(8,128)(2,1)S(1)}, u32[]{:S(2)}, u32[]{:S(2)}) collective-permute-start(bf16[128,512]{1,0:T(8,128)(2,1)S(1)} %get-tuple-element.19.refs_0_.refs_1_), channel_id=1, source_target_pairs={{0,3},{1,2},{2,1},{3,0},{4,7},{5,6},{6,5},{7,4},{8,11},{9,10},{10,... | collective-permute-start | bytes 393224 | tf_op jit(solution)/shard_map/ppermute | solution.py:37
  44.8 0.1 collective-permute-start.9
  44.9 1.4 %collective-permute-start.8 = (bf16[128,512]{1,0:T(8,128)(2,1)S(1)}, bf16[128,512]{1,0:T(8,128)(2,1)S(1)}, u32[]{:S(2)}, u32[]{:S(2)}) collective-permute-start(bf16[128,512]{1,0:T(8,128)(2,1)S(1)} %get-tuple-element.19.refs_0_.refs_1_), channel_id=1, source_target_pairs={{0,1},{1,0},{2,3},{3,2},{4,5},{5,4},{6,7},{7,6},{8,9},{9,8},{10,11... | collective-permute-start | bytes 393224 | tf_op jit(solution)/shard_map/ppermute | solution.py:37
  46.3 0.6 collective-permute-start.13
  46.9 3.8 %collective-permute-start.12 = (bf16[128,512]{1,0:T(8,128)(2,1)S(1)}, bf16[128,512]{1,0:T(8,128)(2,1)S(1)}, u32[]{:S(2)}, u32[]{:S(2)}) collective-permute-start(bf16[128,512]{1,0:T(8,128)(2,1)S(1)} %get-tuple-element.19.refs_0_.refs_1_), channel_id=1, source_target_pairs={{0,6},{1,7},{2,4},{3,5},{4,2},{5,3},{6,0},{7,1},{8,14},{9,15},{10,... | collective-permute-start | bytes 393224 | tf_op jit(solution)/shard_map/ppermute | solution.py:37
  50.7 1.9 %collective-permute-start.7 = (bf16[128,512]{1,0:T(8,128)(2,1)S(1)}, bf16[128,512]{1,0:T(8,128)(2,1)S(1)}, u32[]{:S(2)}, u32[]{:S(2)}) collective-permute-start(bf16[128,512]{1,0:T(8,128)(2,1)S(1)} %get-tuple-element.19.refs_0_.refs_1_), channel_id=1, source_target_pairs={{0,8},{8,16},{16,24},{1,9},{9,17},{17,25},{2,10},{10,18},{18,26},{... | collective-permute-start | bytes 393224 | tf_op jit(solution)/shard_map/ppermute | solution.py:24
  52.7 2.9 %collective-permute-done.13.refs_1_ = bf16[128,512]{1,0:T(8,128)(2,1)S(1)} collective-permute-done((bf16[128,512]{1,0:T(8,128)(2,1)S(1)}, bf16[128,512]{1,0:T(8,128)(2,1)S(1)}, u32[]{:S(2)}, u32[]{:S(2)}) %collective-permute-start.13) | collective-permute-done | bytes 131104 | tf_op jit(solution)/shard_map/ppermute | solution.py:37
  55.6 1.4 %collective-permute-done.7.refs_2_.refs_0_.refs_1_ = bf16[128,512]{1,0:T(8,128)(2,1)S(1)} collective-permute-done((bf16[128,512]{1,0:T(8,128)(2,1)S(1)}, bf16[128,512]{1,0:T(8,128)(2,1)S(1)}, u32[]{:S(2)}, u32[]{:S(2)}) %collective-permute-start.7) | collective-permute-done | bytes 131104 | tf_op jit(solution)/shard_map/ppermute | solution.py:24
  57.0 0.6 collective-permute-start.15
  57.6 1.9 %collective-permute-start.11 = (bf16[384,512]{1,0:T(8,128)(2,1)S(1)}, bf16[384,512]{1,0:T(8,128)(2,1)S(1)}, u32[]{:S(2)}, u32[]{:S(2)}) collective-permute-start(bf16[384,512]{1,0:T(8,128)(2,1)S(1)} %pack.2.refs_3_.refs_1_.refs_2_), channel_id=1, source_target_pairs={{0,8},{8,16},{16,24},{1,9},{9,17},{17,25},{2,10},{10,18},{18,26},{... | collective-permute-start | bytes 1179656 | tf_op jit(solution)/shard_map/ppermute | solution.py:24
  59.5 1.9 %collective-permute-start.14 = (bf16[256,512]{1,0:T(8,128)(2,1)S(1)}, bf16[256,512]{1,0:T(8,128)(2,1)S(1)}, u32[]{:S(2)}, u32[]{:S(2)}) collective-permute-start(bf16[256,512]{1,0:T(8,128)(2,1)S(1)} %pack.3.refs_2_.refs_3_), channel_id=1, source_target_pairs={{0,8},{8,16},{16,24},{1,9},{9,17},{17,25},{2,10},{10,18},{18,26},{... | collective-permute-start | bytes 786440 | tf_op jit(solution)/shard_map/ppermute | solution.py:24
  61.4 2.0 %collective-permute-done.15.refs_3_.refs_4_ = bf16[256,512]{1,0:T(8,128)(2,1)S(1)} collective-permute-done((bf16[256,512]{1,0:T(8,128)(2,1)S(1)}, bf16[256,512]{1,0:T(8,128)(2,1)S(1)}, u32[]{:S(2)}, u32[]{:S(2)}) %collective-permute-start.15) | collective-permute-done | bytes 262176 | tf_op jit(solution)/shard_map/ppermute | solution.py:37
  63.4 1.9 %collective-permute-start.16 = (bf16[256,512]{1,0:T(8,128)(2,1)S(1)}, bf16[256,512]{1,0:T(8,128)(2,1)S(1)}, u32[]{:S(2)}, u32[]{:S(2)}) collective-permute-start(bf16[256,512]{1,0:T(8,128)(2,1)S(1)} %collective-permute-done.15.refs_3_.refs_4_), channel_id=1, source_target_pairs={{0,8},{8,16},{16,24},{1,9},{9,17},{17,25},{2,10},{10,18},{18,26},{... | collective-permute-start | bytes 786440 | tf_op jit(solution)/shard_map/ppermute | solution.py:24
  65.3 2.9 %own_recon.1.refs_4_ = f32[1024,128]{1,0:T(8,128)S(1)} custom-call(bf16[128,512]{1,0:T(8,128)(2,1)S(1)} %get-tuple-element.19.refs_0_.refs_1_, bf16[384,512]{1,0:T(8,128)(2,1)S(1)} %pack.2.refs_3_.refs_1_.refs_2_, bf16[256,512]{1,0:T(8,128)(2,1)S(1)} %pack.3.refs_2_.refs_3_, bf16[256,512]{1,0:T(8,128)(2,1)S(1)} %collective-permute-done.15.refs_3_.refs_4_, ...), custom_call_target="tpu_custom_call" | custom-call | flops 1073741824 | bytes 4194304 | tf_op jit(solution)/shard_map/own_recon/pallas_call | solution.py:267
  68.2 1.2 collective-permute-done.14.refs_2_.refs_3_
  69.5 2.8 %collective-permute-done.16.refs_3_.refs_4_ = bf16[256,512]{1,0:T(8,128)(2,1)S(1)} collective-permute-done((bf16[256,512]{1,0:T(8,128)(2,1)S(1)}, bf16[256,512]{1,0:T(8,128)(2,1)S(1)}, u32[]{:S(2)}, u32[]{:S(2)}) %collective-permute-start.16) | collective-permute-done | bytes 262176 | tf_op jit(solution)/shard_map/ppermute | solution.py:24
  72.3 4.5 %recon.1 = (bf16[128,1024]{1,0:T(8,128)(2,1)S(1)}, bf16[128,2048]{1,0:T(8,128)(2,1)S(1)}) custom-call(bf16[128,512]{1,0:T(8,128)(2,1)S(1)} %collective-permute-done.7.refs_2_.refs_0_.refs_1_, bf16[384,512]{1,0:T(8,128)(2,1)S(1)} %collective-permute-done.11.refs_1_.refs_2_, bf16[256,512]{1,0:T(8,128)(2,1)S(1)} %collective-permute-done.14.refs_2_.refs_3_, ...), custom_call_target="tpu_custom_call" | custom-call | flops 2147483648 | bytes 4194304 | tf_op jit(solution)/shard_map/recon/pallas_call | solution.py:277
  76.8 1.9 %collective-permute-start.19 = (bf16[128,2048]{1,0:T(8,128)(2,1)S(1)}, bf16[128,2048]{1,0:T(8,128)(2,1)S(1)}, u32[]{:S(2)}, u32[]{:S(2)}) collective-permute-start(bf16[128,2048]{1,0:T(8,128)(2,1)S(1)} %get-tuple-element.26), channel_id=1, source_target_pairs={{8,0},{16,8},{24,16},{9,1},{17,9},{25,17},{10,2},{18,10},{26,18},{... | collective-permute-start | bytes 1572872 | tf_op jit(solution)/shard_map/ppermute | solution.py:24
  78.7 1.3 near.1
  80.0 1.9 %collective-permute-start.17 = (bf16[128,2048]{1,0:T(8,128)(2,1)S(1)}, bf16[128,2048]{1,0:T(8,128)(2,1)S(1)}, u32[]{:S(2)}, u32[]{:S(2)}) collective-permute-start(bf16[128,2048]{1,0:T(8,128)(2,1)S(1)} %near.1), channel_id=1, source_target_pairs={{8,0},{16,8},{24,16},{9,1},{17,9},{25,17},{10,2},{18,10},{26,18},{... | collective-permute-start | bytes 1572872 | tf_op jit(solution)/shard_map/ppermute | solution.py:24
  81.9 2.6 %own_grad.1 = (f32[128,2048]{1,0:T(8,128)S(1)}, f32[128,2048]{1,0:T(8,128)S(1)}) custom-call(bf16[128,1024]{1,0:T(8,128)(2,1)S(1)} %get-tuple-element.21.error_ref.refs_0_, bf16[2,1024,4096]{2,1,0:T(8,128)(2,1)S(1)} %get-tuple-element.20.refs_4_.refs_5_.w_ref), custom_call_target="tpu_custom_call" | custom-call | flops 1073741824 | bytes 4194304 | tf_op jit(solution)/shard_map/own_grad/pallas_call | solution.py:299
  84.5 4.9 %dec_grad.2._.refs_5_ = bf16[1,2,1024,4096]{3,2,1,0:T(8,128)(2,1)} custom-call(bf16[128,1024]{1,0:T(8,128)(2,1)S(1)} %get-tuple-element.21.error_ref.refs_0_, bf16[128,512]{1,0:T(8,128)(2,1)S(1)} %get-tuple-element.19.refs_0_.refs_1_, bf16[384,512]{1,0:T(8,128)(2,1)S(1)} %pack.2.refs_3_.refs_1_.refs_2_, bf16[256,512]{1,0:T(8,128)(2,1)S(1)} %pack.3.refs_2_.refs_3_, ...), custom_call_target="tpu_custom_call" | custom-call | flops 1073741824 | bytes 8388608 | tf_op jit(solution)/shard_map/dec_grad/pallas_call | solution.py:312
  89.5 5.8 %copy-done = bf16[1,2,1024,4096]{3,2,1,0:T(8,128)(2,1)S(1)} copy-done((bf16[1,2,1024,4096]{3,2,1,0:T(8,128)(2,1)S(1)}, bf16[1,2,1024,4096]{3,2,1,0:T(8,128)(2,1)}, u32[]{:S(2)}) %copy-start) | copy-done | bytes 16777240
  95.2 0.1 sum.3
  95.4 0.7 collective-permute-start.20
  96.0 2.2 %collective-permute-start.21 = (bf16[128,512]{1,0:T(8,128)(2,1)S(1)}, bf16[128,512]{1,0:T(8,128)(2,1)S(1)}, u32[]{:S(2)}, u32[]{:S(2)}) collective-permute-start(bf16[128,512]{1,0:T(8,128)(2,1)S(1)} %get-tuple-element.28), channel_id=1, source_target_pairs={{0,4},{1,5},{2,6},{3,7},{4,0},{5,1},{6,2},{7,3},{8,12},{9,13},{10,... | collective-permute-start | bytes 393224 | tf_op jit(solution)/shard_map/ppermute | solution.py:37
  98.2 2.0 %collective-permute-start.24 = (bf16[128,512]{1,0:T(8,128)(2,1)S(1)}, bf16[128,512]{1,0:T(8,128)(2,1)S(1)}, u32[]{:S(2)}, u32[]{:S(2)}) collective-permute-start(bf16[128,512]{1,0:T(8,128)(2,1)S(1)} %get-tuple-element.31), channel_id=1, source_target_pairs={{0,7},{1,6},{2,5},{3,4},{4,3},{5,2},{6,1},{7,0},{8,15},{9,14},{10,... | collective-permute-start | bytes 393224 | tf_op jit(solution)/shard_map/ppermute | solution.py:37
  100.2 2.0 %collective-permute-start.25 = (bf16[128,512]{1,0:T(8,128)(2,1)S(1)}, bf16[128,512]{1,0:T(8,128)(2,1)S(1)}, u32[]{:S(2)}, u32[]{:S(2)}) collective-permute-start(bf16[128,512]{1,0:T(8,128)(2,1)S(1)} %get-tuple-element.32), channel_id=1, source_target_pairs={{0,5},{1,4},{2,7},{3,6},{4,1},{5,0},{6,3},{7,2},{8,13},{9,12},{10,... | collective-permute-start | bytes 393224 | tf_op jit(solution)/shard_map/ppermute | solution.py:37
  102.2 0.1 sum.2
  102.3 1.4 %collective-permute-start.18 = (bf16[128,512]{1,0:T(8,128)(2,1)S(1)}, bf16[128,512]{1,0:T(8,128)(2,1)S(1)}, u32[]{:S(2)}, u32[]{:S(2)}) collective-permute-start(bf16[128,512]{1,0:T(8,128)(2,1)S(1)} %get-tuple-element.24), channel_id=1, source_target_pairs={{0,2},{1,3},{2,0},{3,1},{4,6},{5,7},{6,4},{7,5},{8,10},{9,11},{10,... | collective-permute-start | bytes 393224 | tf_op jit(solution)/shard_map/ppermute | solution.py:37
  103.7 1.4 %collective-permute-start.22 = (bf16[128,512]{1,0:T(8,128)(2,1)S(1)}, bf16[128,512]{1,0:T(8,128)(2,1)S(1)}, u32[]{:S(2)}, u32[]{:S(2)}) collective-permute-start(bf16[128,512]{1,0:T(8,128)(2,1)S(1)} %get-tuple-element.29), channel_id=1, source_target_pairs={{0,1},{1,0},{2,3},{3,2},{4,5},{5,4},{6,7},{7,6},{8,9},{9,8},{10,11... | collective-permute-start | bytes 393224 | tf_op jit(solution)/shard_map/ppermute | solution.py:37
  105.1 11.4 %collective-permute-done.21.refs_3_ = bf16[128,512]{1,0:T(8,128)(2,1)S(1)} collective-permute-done((bf16[128,512]{1,0:T(8,128)(2,1)S(1)}, bf16[128,512]{1,0:T(8,128)(2,1)S(1)}, u32[]{:S(2)}, u32[]{:S(2)}) %collective-permute-start.21) | collective-permute-done | bytes 131104 | tf_op jit(solution)/shard_map/ppermute | solution.py:37
  116.5 4.9 %dec_grad.3 = bf16[1,2,1024,4096]{3,2,1,0:T(8,128)(2,1)} custom-call(bf16[128,1024]{1,0:T(8,128)(2,1)S(1)} %get-tuple-element.21.error_ref.refs_0_, bf16[128,512]{1,0:T(8,128)(2,1)S(1)} %collective-permute-done.7.refs_2_.refs_0_.refs_1_, bf16[384,512]{1,0:T(8,128)(2,1)S(1)} %collective-permute-done.11.refs_1_.refs_2_, ...), custom_call_target="tpu_custom_call", output_to_operand_aliasing={{}: (5, {})} | custom-call | flops 1073741824 | bytes 8388608 | tf_op jit(solution)/shard_map/dec_grad/pallas_call | solution.py:312
  121.4 0.9 collective-permute-done.25.refs_7_
  122.4 2.5 %collective-permute-done.23.refs_5_ = bf16[128,512]{1,0:T(8,128)(2,1)S(1)} collective-permute-done((bf16[128,512]{1,0:T(8,128)(2,1)S(1)}, bf16[128,512]{1,0:T(8,128)(2,1)S(1)}, u32[]{:S(2)}, u32[]{:S(2)}) %collective-permute-start.23) | collective-permute-done | bytes 131104 | tf_op jit(solution)/shard_map/ppermute | solution.py:37
  124.9 5.3 %enc_grad.1 = bf16[1,512,8192]{2,1,0:T(8,128)(2,1)} custom-call(f32[128,512]{1,0:T(8,128)S(1)} %get-tuple-element.23.refs_0_, bf16[128,512]{1,0:T(8,128)(2,1)S(1)} %collective-permute-done.18.refs_1_, bf16[128,512]{1,0:T(8,128)(2,1)S(1)} %collective-permute-done.20.refs_2_, bf16[128,512]{1,0:T(8,128)(2,1)S(1)} %collective-permute-done.21.refs_3_, ...), custom_call_target="tpu_custom_call" | custom-call | flops 1073741824 | bytes 8388608 | tf_op jit(solution)/shard_map/enc_grad/pallas_call | solution.py:348
  (27 shorter events, 0.1 us)
Async XLA Ops:
  0.6 37.2 %copy-start.1 = (bf16[1,128,1024]{2,1,0:T(8,128)(2,1)S(1)}, bf16[1,128,1024]{2,1,0:T(8,128)(2,1)}, u32[]{:S(2)}) copy-start(bf16[1,128,1024]{2,1,0:T(8,128)(2,1)} %param.6) | copy-start | bytes 786436
  0.6 37.1 %copy-start.4 = (f32[1,512]{1,0:T(1,128)S(1)}, f32[1,512]{1,0:T(1,128)}, u32[]{:S(2)}) copy-start(f32[1,512]{1,0:T(1,128)} %refs_9_.1) | copy-start | bytes 6148
  0.7 8.7 %collective-permute-start = (bf16[128,1024]{1,0:T(8,128)(2,1)}, bf16[128,1024]{1,0:T(8,128)(2,1)S(1)}, u32[]{:S(2)}, u32[]{:S(2)}) collective-permute-start(bf16[128,1024]{1,0:T(8,128)(2,1)} %bitcast.4), channel_id=1, source_target_pairs={{0,2},{1,3},{2,0},{3,1},{4,6},{5,7},{6,4},{7,5},{8,10},{9,11},{10,... | collective-permute-start | bytes 786440 | tf_op jit(solution)/shard_map/ppermute | solution.py:37
  2.3 20.2 %collective-permute-start.1 = (bf16[128,1024]{1,0:T(8,128)(2,1)}, bf16[128,1024]{1,0:T(8,128)(2,1)S(1)}, u32[]{:S(2)}, u32[]{:S(2)}) collective-permute-start(bf16[128,1024]{1,0:T(8,128)(2,1)} %bitcast.5), channel_id=1, source_target_pairs={{0,6},{1,7},{2,4},{3,5},{4,2},{5,3},{6,0},{7,1},{8,14},{9,15},{10,... | collective-permute-start | bytes 786440 | tf_op jit(solution)/shard_map/ppermute | solution.py:37
  9.3 16.1 %collective-permute-start.2 = (bf16[128,1024]{1,0:T(8,128)(2,1)S(1)}, bf16[128,1024]{1,0:T(8,128)(2,1)S(1)}, u32[]{:S(2)}, u32[]{:S(2)}) collective-permute-start(bf16[128,1024]{1,0:T(8,128)(2,1)S(1)} %collective-permute-done.refs_1_.refs_9_), channel_id=1, source_target_pairs={{0,6},{1,7},{2,4},{3,5},{4,2},{5,3},{6,0},{7,1},{8,14},{9,15},{10,... | collective-permute-start | bytes 786440 | tf_op jit(solution)/shard_map/ppermute | solution.py:37
  21.0 14.3 %collective-permute-start.4 = (bf16[128,1024]{1,0:T(8,128)(2,1)}, bf16[128,1024]{1,0:T(8,128)(2,1)S(1)}, u32[]{:S(2)}, u32[]{:S(2)}) collective-permute-start(bf16[128,1024]{1,0:T(8,128)(2,1)} %bitcast.6), channel_id=1, source_target_pairs={{0,3},{1,2},{2,1},{3,0},{4,7},{5,6},{6,5},{7,4},{8,11},{9,10},{10,... | collective-permute-start | bytes 786440 | tf_op jit(solution)/shard_map/ppermute | solution.py:37
  21.0 14.3 %collective-permute-start.3 = (bf16[128,1024]{1,0:T(8,128)(2,1)}, bf16[128,1024]{1,0:T(8,128)(2,1)S(1)}, u32[]{:S(2)}, u32[]{:S(2)}) collective-permute-start(bf16[128,1024]{1,0:T(8,128)(2,1)} %bitcast.7), channel_id=1, source_target_pairs={{0,1},{1,0},{2,3},{3,2},{4,5},{5,4},{6,7},{7,6},{8,9},{9,8},{10,11... | collective-permute-start | bytes 786440 | tf_op jit(solution)/shard_map/ppermute | solution.py:37
  22.5 12.8 %collective-permute-start.5 = (bf16[128,1024]{1,0:T(8,128)(2,1)S(1)}, bf16[128,1024]{1,0:T(8,128)(2,1)S(1)}, u32[]{:S(2)}, u32[]{:S(2)}) collective-permute-start(bf16[128,1024]{1,0:T(8,128)(2,1)S(1)} %collective-permute-done.1._.refs_2_.refs_10_), channel_id=1, source_target_pairs={{0,1},{1,0},{2,3},{3,2},{4,5},{5,4},{6,7},{7,6},{8,9},{9,8},{10,11... | collective-permute-start | bytes 786440 | tf_op jit(solution)/shard_map/ppermute | solution.py:37
  25.5 12.3 %collective-permute-start.6 = (bf16[128,1024]{1,0:T(8,128)(2,1)S(1)}, bf16[128,1024]{1,0:T(8,128)(2,1)S(1)}, u32[]{:S(2)}, u32[]{:S(2)}) collective-permute-start(bf16[128,1024]{1,0:T(8,128)(2,1)S(1)} %collective-permute-done.2.refs_3_.refs_11_), channel_id=1, source_target_pairs={{0,1},{1,0},{2,3},{3,2},{4,5},{5,4},{6,7},{7,6},{8,9},{9,8},{10,11... | collective-permute-start | bytes 786440 | tf_op jit(solution)/shard_map/ppermute | solution.py:37
  35.2 37.0 %copy-start.2 = (bf16[1,128,1024]{2,1,0:T(8,128)(2,1)S(1)}, bf16[1,128,1024]{2,1,0:T(8,128)(2,1)}, u32[]{:S(2)}) copy-start(bf16[1,128,1024]{2,1,0:T(8,128)(2,1)} %param.7) | copy-start | bytes 786436
  35.3 37.0 %copy-start.3 = (f32[1,1024]{1,0:T(1,128)S(1)}, f32[1,1024]{1,0:T(1,128)}, u32[]{:S(2)}) copy-start(f32[1,1024]{1,0:T(1,128)} %refs_6_.1) | copy-start | bytes 12292
  40.7 10.0 %collective-permute-start.10 = (bf16[128,512]{1,0:T(8,128)(2,1)S(1)}, bf16[128,512]{1,0:T(8,128)(2,1)S(1)}, u32[]{:S(2)}, u32[]{:S(2)}) collective-permute-start(bf16[128,512]{1,0:T(8,128)(2,1)S(1)} %get-tuple-element.19.refs_0_.refs_1_), channel_id=1, source_target_pairs={{0,3},{1,2},{2,1},{3,0},{4,7},{5,6},{6,5},{7,4},{8,11},{9,10},{10,... | collective-permute-start | bytes 393224 | tf_op jit(solution)/shard_map/ppermute | solution.py:37
  44.8 7.8 %collective-permute-start.9 = (bf16[128,512]{1,0:T(8,128)(2,1)S(1)}, bf16[128,512]{1,0:T(8,128)(2,1)S(1)}, u32[]{:S(2)}, u32[]{:S(2)}) collective-permute-start(bf16[128,512]{1,0:T(8,128)(2,1)S(1)} %get-tuple-element.19.refs_0_.refs_1_), channel_id=1, source_target_pairs={{0,2},{1,3},{2,0},{3,1},{4,6},{5,7},{6,4},{7,5},{8,10},{9,11},{10,... | collective-permute-start | bytes 393224 | tf_op jit(solution)/shard_map/ppermute | solution.py:37
  44.9 7.7 %collective-permute-start.8 = (bf16[128,512]{1,0:T(8,128)(2,1)S(1)}, bf16[128,512]{1,0:T(8,128)(2,1)S(1)}, u32[]{:S(2)}, u32[]{:S(2)}) collective-permute-start(bf16[128,512]{1,0:T(8,128)(2,1)S(1)} %get-tuple-element.19.refs_0_.refs_1_), channel_id=1, source_target_pairs={{0,1},{1,0},{2,3},{3,2},{4,5},{5,4},{6,7},{7,6},{8,9},{9,8},{10,11... | collective-permute-start | bytes 393224 | tf_op jit(solution)/shard_map/ppermute | solution.py:37
  46.3 9.3 %collective-permute-start.13 = (bf16[128,512]{1,0:T(8,128)(2,1)S(1)}, bf16[128,512]{1,0:T(8,128)(2,1)S(1)}, u32[]{:S(2)}, u32[]{:S(2)}) collective-permute-start(bf16[128,512]{1,0:T(8,128)(2,1)S(1)} %get-tuple-element.19.refs_0_.refs_1_), channel_id=1, source_target_pairs={{0,4},{1,5},{2,6},{3,7},{4,0},{5,1},{6,2},{7,3},{8,12},{9,13},{10,... | collective-permute-start | bytes 393224 | tf_op jit(solution)/shard_map/ppermute | solution.py:37
  46.9 8.7 %collective-permute-start.12 = (bf16[128,512]{1,0:T(8,128)(2,1)S(1)}, bf16[128,512]{1,0:T(8,128)(2,1)S(1)}, u32[]{:S(2)}, u32[]{:S(2)}) collective-permute-start(bf16[128,512]{1,0:T(8,128)(2,1)S(1)} %get-tuple-element.19.refs_0_.refs_1_), channel_id=1, source_target_pairs={{0,6},{1,7},{2,4},{3,5},{4,2},{5,3},{6,0},{7,1},{8,14},{9,15},{10,... | collective-permute-start | bytes 393224 | tf_op jit(solution)/shard_map/ppermute | solution.py:37
  50.7 6.3 %collective-permute-start.7 = (bf16[128,512]{1,0:T(8,128)(2,1)S(1)}, bf16[128,512]{1,0:T(8,128)(2,1)S(1)}, u32[]{:S(2)}, u32[]{:S(2)}) collective-permute-start(bf16[128,512]{1,0:T(8,128)(2,1)S(1)} %get-tuple-element.19.refs_0_.refs_1_), channel_id=1, source_target_pairs={{0,8},{8,16},{16,24},{1,9},{9,17},{17,25},{2,10},{10,18},{18,26},{... | collective-permute-start | bytes 393224 | tf_op jit(solution)/shard_map/ppermute | solution.py:24
  57.0 6.4 %collective-permute-start.15 = (bf16[256,512]{1,0:T(8,128)(2,1)S(1)}, bf16[256,512]{1,0:T(8,128)(2,1)S(1)}, u32[]{:S(2)}, u32[]{:S(2)}) collective-permute-start(bf16[256,512]{1,0:T(8,128)(2,1)S(1)} %pack.3.refs_2_.refs_3_), channel_id=1, source_target_pairs={{0,1},{1,0},{2,3},{3,2},{4,5},{5,4},{6,7},{7,6},{8,9},{9,8},{10,11... | collective-permute-start | bytes 786440 | tf_op jit(solution)/shard_map/ppermute | solution.py:37
  57.6 11.9 %collective-permute-start.11 = (bf16[384,512]{1,0:T(8,128)(2,1)S(1)}, bf16[384,512]{1,0:T(8,128)(2,1)S(1)}, u32[]{:S(2)}, u32[]{:S(2)}) collective-permute-start(bf16[384,512]{1,0:T(8,128)(2,1)S(1)} %pack.2.refs_3_.refs_1_.refs_2_), channel_id=1, source_target_pairs={{0,8},{8,16},{16,24},{1,9},{9,17},{17,25},{2,10},{10,18},{18,26},{... | collective-permute-start | bytes 1179656 | tf_op jit(solution)/shard_map/ppermute | solution.py:24
  59.5 10.0 %collective-permute-start.14 = (bf16[256,512]{1,0:T(8,128)(2,1)S(1)}, bf16[256,512]{1,0:T(8,128)(2,1)S(1)}, u32[]{:S(2)}, u32[]{:S(2)}) collective-permute-start(bf16[256,512]{1,0:T(8,128)(2,1)S(1)} %pack.3.refs_2_.refs_3_), channel_id=1, source_target_pairs={{0,8},{8,16},{16,24},{1,9},{9,17},{17,25},{2,10},{10,18},{18,26},{... | collective-permute-start | bytes 786440 | tf_op jit(solution)/shard_map/ppermute | solution.py:24
  63.4 8.8 %collective-permute-start.16 = (bf16[256,512]{1,0:T(8,128)(2,1)S(1)}, bf16[256,512]{1,0:T(8,128)(2,1)S(1)}, u32[]{:S(2)}, u32[]{:S(2)}) collective-permute-start(bf16[256,512]{1,0:T(8,128)(2,1)S(1)} %collective-permute-done.15.refs_3_.refs_4_), channel_id=1, source_target_pairs={{0,8},{8,16},{16,24},{1,9},{9,17},{17,25},{2,10},{10,18},{18,26},{... | collective-permute-start | bytes 786440 | tf_op jit(solution)/shard_map/ppermute | solution.py:24
  76.8 12.7 %collective-permute-start.19 = (bf16[128,2048]{1,0:T(8,128)(2,1)S(1)}, bf16[128,2048]{1,0:T(8,128)(2,1)S(1)}, u32[]{:S(2)}, u32[]{:S(2)}) collective-permute-start(bf16[128,2048]{1,0:T(8,128)(2,1)S(1)} %get-tuple-element.26), channel_id=1, source_target_pairs={{8,0},{16,8},{24,16},{9,1},{17,9},{25,17},{10,2},{18,10},{26,18},{... | collective-permute-start | bytes 1572872 | tf_op jit(solution)/shard_map/ppermute | solution.py:24
  80.0 22.2 %collective-permute-start.17 = (bf16[128,2048]{1,0:T(8,128)(2,1)S(1)}, bf16[128,2048]{1,0:T(8,128)(2,1)S(1)}, u32[]{:S(2)}, u32[]{:S(2)}) collective-permute-start(bf16[128,2048]{1,0:T(8,128)(2,1)S(1)} %near.1), channel_id=1, source_target_pairs={{8,0},{16,8},{24,16},{9,1},{17,9},{25,17},{10,2},{18,10},{26,18},{... | collective-permute-start | bytes 1572872 | tf_op jit(solution)/shard_map/ppermute | solution.py:24
  89.5 5.8 %copy-start = (bf16[1,2,1024,4096]{3,2,1,0:T(8,128)(2,1)S(1)}, bf16[1,2,1024,4096]{3,2,1,0:T(8,128)(2,1)}, u32[]{:S(2)}) copy-start(bf16[1,2,1024,4096]{3,2,1,0:T(8,128)(2,1)} %dec_grad.2._.refs_5_) | copy-start | bytes 50331652
  95.4 8.3 %collective-permute-start.20 = (bf16[128,512]{1,0:T(8,128)(2,1)S(1)}, bf16[128,512]{1,0:T(8,128)(2,1)S(1)}, u32[]{:S(2)}, u32[]{:S(2)}) collective-permute-start(bf16[128,512]{1,0:T(8,128)(2,1)S(1)} %get-tuple-element.27), channel_id=1, source_target_pairs={{0,6},{1,7},{2,4},{3,5},{4,2},{5,3},{6,0},{7,1},{8,14},{9,15},{10,... | collective-permute-start | bytes 393224 | tf_op jit(solution)/shard_map/ppermute | solution.py:37
  96.0 20.5 %collective-permute-start.21 = (bf16[128,512]{1,0:T(8,128)(2,1)S(1)}, bf16[128,512]{1,0:T(8,128)(2,1)S(1)}, u32[]{:S(2)}, u32[]{:S(2)}) collective-permute-start(bf16[128,512]{1,0:T(8,128)(2,1)S(1)} %get-tuple-element.28), channel_id=1, source_target_pairs={{0,4},{1,5},{2,6},{3,7},{4,0},{5,1},{6,2},{7,3},{8,12},{9,13},{10,... | collective-permute-start | bytes 393224 | tf_op jit(solution)/shard_map/ppermute | solution.py:37
  98.2 23.2 %collective-permute-start.24 = (bf16[128,512]{1,0:T(8,128)(2,1)S(1)}, bf16[128,512]{1,0:T(8,128)(2,1)S(1)}, u32[]{:S(2)}, u32[]{:S(2)}) collective-permute-start(bf16[128,512]{1,0:T(8,128)(2,1)S(1)} %get-tuple-element.31), channel_id=1, source_target_pairs={{0,7},{1,6},{2,5},{3,4},{4,3},{5,2},{6,1},{7,0},{8,15},{9,14},{10,... | collective-permute-start | bytes 393224 | tf_op jit(solution)/shard_map/ppermute | solution.py:37
  100.2 22.2 %collective-permute-start.25 = (bf16[128,512]{1,0:T(8,128)(2,1)S(1)}, bf16[128,512]{1,0:T(8,128)(2,1)S(1)}, u32[]{:S(2)}, u32[]{:S(2)}) collective-permute-start(bf16[128,512]{1,0:T(8,128)(2,1)S(1)} %get-tuple-element.32), channel_id=1, source_target_pairs={{0,5},{1,4},{2,7},{3,6},{4,1},{5,0},{6,3},{7,2},{8,13},{9,12},{10,... | collective-permute-start | bytes 393224 | tf_op jit(solution)/shard_map/ppermute | solution.py:37
  102.3 20.1 %collective-permute-start.18 = (bf16[128,512]{1,0:T(8,128)(2,1)S(1)}, bf16[128,512]{1,0:T(8,128)(2,1)S(1)}, u32[]{:S(2)}, u32[]{:S(2)}) collective-permute-start(bf16[128,512]{1,0:T(8,128)(2,1)S(1)} %get-tuple-element.24), channel_id=1, source_target_pairs={{0,2},{1,3},{2,0},{3,1},{4,6},{5,7},{6,4},{7,5},{8,10},{9,11},{10,... | collective-permute-start | bytes 393224 | tf_op jit(solution)/shard_map/ppermute | solution.py:37
  103.7 18.7 %collective-permute-start.22 = (bf16[128,512]{1,0:T(8,128)(2,1)S(1)}, bf16[128,512]{1,0:T(8,128)(2,1)S(1)}, u32[]{:S(2)}, u32[]{:S(2)}) collective-permute-start(bf16[128,512]{1,0:T(8,128)(2,1)S(1)} %get-tuple-element.29), channel_id=1, source_target_pairs={{0,1},{1,0},{2,3},{3,2},{4,5},{5,4},{6,7},{7,6},{8,9},{9,8},{10,11... | collective-permute-start | bytes 393224 | tf_op jit(solution)/shard_map/ppermute | solution.py:37
  116.5 8.4 %collective-permute-start.23 = (bf16[128,512]{1,0:T(8,128)(2,1)S(1)}, bf16[128,512]{1,0:T(8,128)(2,1)S(1)}, u32[]{:S(2)}, u32[]{:S(2)}) collective-permute-start(bf16[128,512]{1,0:T(8,128)(2,1)S(1)} %get-tuple-element.30), channel_id=1, source_target_pairs={{0,3},{1,2},{2,1},{3,0},{4,7},{5,6},{6,5},{7,4},{8,11},{9,10},{10,... | collective-permute-start | bytes 393224 | tf_op jit(solution)/shard_map/ppermute | solution.py:37

commit v3 on v2

v3 whole, which is shorter than its diff:
```python
import functools

import jax
import jax.numpy as jnp
from jax import lax
from jax.experimental import pallas as pl
from jax.experimental.pallas import tpu as pltpu
from jax.sharding import PartitionSpec as P

LANES = 128
MIB = 1024 * 1024
BF16 = jnp.bfloat16
F32 = jnp.float32

OFFSETS = (0, -1, 1, -2, 2, -3, 3, 4)
COUNT = len(OFFSETS)
BLOCKS = ((0,), (1, 2, 3), (6, 4), (7, 5))


def from_behind(value, axis, steps):
    count = lax.axis_size(axis)
    initial, last = (max(0, -steps), min(count, count - steps))
    return lax.ppermute(value, axis, [(source, source + steps) for source in range(initial, last)])


def transposed(left, right):
    return lax.dot_general(left, right, (((0,), (0,)), ((), ())), preferred_element_type=F32)


def against(left, right):
    return lax.dot_general(left, right, (((1,), (1,)), ((), ())), preferred_element_type=F32)


def exchanged(value, mask):
    count = lax.axis_size("feat")
    return lax.ppermute(value, "feat", [(i, i ^ mask) for i in range(count)])


def ring(count):
    return [*range(0, count, 2), *range(count - 1, 0, -2)]


def passed_on(value, by):
    count = lax.axis_size("feat")
    order = ring(count)
    return lax.ppermute(value, "feat", [(order[p], order[(p + by) % count]) for p in range(count)])


def ring_owner(offset):
    count = COUNT
    me = lax.axis_index("feat")
    half = me // 2
    place = jnp.where(lax.rem(me, 2) == 0, half, count - 1 - half)
    place = lax.rem(place + offset + count, count)
    return jnp.where(place < count // 2, 2 * place, 2 * (count - 1 - place) + 1)


def ring_gather(own):
    count = lax.axis_size("feat")
    middle = own.shape[0] // 2
    found = {0: (own[:middle], own[middle:])}
    first, last = ({0: part} for part in found[0])
    for step in range(1, count // 2):
        for held in (first, last):
            held[-step] = passed_on(held[1 - step], 1)
            held[step] = passed_on(held[step - 1], -1)
    far = count // 2
    first[far] = passed_on(first[1 - far], 1)
    last[far] = passed_on(last[far - 1], -1)
    return first, last


def owner(mask):
    return jnp.bitwise_xor(lax.axis_index("feat"), mask)


def columns(index, width):
    return pl.ds(pl.multiple_of(index * width, width), width)


def vmem(count):
    return [pl.BlockSpec(memory_space=pltpu.VMEM)] * count


def params(mib):
    return pltpu.CompilerParams(vmem_limit_bytes=mib * MIB)


def flat(groups):
    return [(i, row, mask) for i, masks in enumerate(groups) for row, mask in enumerate(masks)]


def pack_kernel(count, *refs):
    out_ref, start = refs[-1], 0
    for ref in refs[:count]:
        out_ref[start : start + ref.shape[0], :] = ref[...]
        start += ref.shape[0]


def packed(parts, after=()):
    rows = sum(part.shape[0] for part in parts)
    return pl.pallas_call(
        functools.partial(pack_kernel, len(parts)),
        name="pack",
        out_shape=jax.ShapeDtypeStruct((rows, parts[0].shape[1]), parts[0].dtype),
        in_specs=[*vmem(len(parts)), *[pl.BlockSpec(memory_space=pl.ANY) for _ in after]],
        out_specs=vmem(1)[0],
        compiler_params=params(1),
        cost_estimate=pl.CostEstimate(
            flops=0, bytes_accessed=4 * rows * parts[0].shape[1], transcendentals=0
        ),
    )(*parts, *after)


def block(parts, k):
    return jnp.concatenate([parts[2 * k][...], parts[2 * k + 1][...]], axis=0)


def pre_kernel(*refs):
    count = len(OFFSETS)
    parts, (w_ref, b_ref, codes_ref, active_ref, held, sems) = refs[: 2 * count], refs[2 * count :]
    width = parts[0].shape[1]
    copies = [
        pltpu.make_async_copy(w_ref.at[:, columns(ring_owner(offset), width)], held.at[k], sems.at[k])
        for k, offset in enumerate(OFFSETS)
    ]
    for copy in copies:
        copy.start()
    total = None
    for k, copy in enumerate(copies):
        copy.wait()
        term = against(block(parts, k), held[k])
        total = term if total is None else total + term
    active = jnp.maximum(total + b_ref[...], 0.0)
    active_ref[...] = active
    codes_ref[...] = (active * active).astype(BF16)


def row_copies(source, slot, target, sems):
    steps, tile = tiles(target.shape[0])
    return [
        pltpu.make_async_copy(
            source.at[slot, j * tile : (j + 1) * tile, :], target.at[j * tile : (j + 1) * tile, :], sems.at[j]
        )
        for j in range(steps)
    ]


def decoded(w_ref, here, parts, groups, tok, total):
    width = parts[0].shape[1]
    for i, row, mask in flat(groups):
        part = parts[i][row * tok : (row + 1) * tok, :]
        term = against(w_ref[here, columns(owner(mask), width)], part)
        total = term if total is None else total + term
    return total


def tiles(size):
    tile = 256 if size % 256 == 0 else LANES
    return size // tile, tile


def own_recon_kernel(*refs):
    parts, (w_ref, total_ref, held_ref, sems) = refs[: len(BLOCKS)], refs[len(BLOCKS) :]
    tok = total_ref.shape[1]
    _, tile = tiles(held_ref.shape[0])
    copies = row_copies(w_ref, 0, held_ref, sems)
    for copy in copies:
        copy.start()
    for j, copy in enumerate(copies):
        copy.wait()
        here = slice(j * tile, (j + 1) * tile)
        total_ref[here, :] = decoded(held_ref, here, parts, BLOCKS, tok, None)


def product(error_ref, w_ref, out_ref, first):
    wide = out_ref.shape[1]
    steps, tile = (wide // 512, 512) if wide % 512 == 0 else (wide // LANES, LANES)

    @pl.loop(0, steps)
    def _(j):
        source = pl.ds(pl.multiple_of(first * wide + j * tile, tile), tile)
        here = pl.ds(pl.multiple_of(j * tile, tile), tile)
        out_ref[:, here] = jnp.dot(
            error_ref[...], w_ref[:, source], preferred_element_type=F32
        ).astype(out_ref.dtype)


def halves():
    near = lax.axis_index("feat") // (COUNT // 2)
    return near, 1 - near


def recon_kernel(scale, *refs):
    parts = refs[: len(BLOCKS)]
    total_ref, w_ref, b_ref, target_ref, error_ref, far_ref, held_ref, sems = refs[len(BLOCKS) :]
    tok = total_ref.shape[1]
    _, tile = tiles(held_ref.shape[0])
    copies = row_copies(w_ref, 1, held_ref, sems)
    for copy in copies:
        copy.start()
    for j, copy in enumerate(copies):
        copy.wait()
        here = slice(j * tile, (j + 1) * tile)
        total = decoded(held_ref, here, parts, BLOCKS, tok, total_ref[here, :])
        error = total.T + b_ref[:, here] - target_ref[:, here].astype(F32)
        error_ref[:, here] = (error * scale).astype(BF16)
    product(error_ref, held_ref, far_ref, halves()[1])


def own_grad_kernel(error_ref, own_ref, next_ref, sent_ref, near_ref, far_ref):
    near, far = halves()
    product(error_ref, next_ref, sent_ref, near)
    product(error_ref, own_ref, far_ref, far)
    product(error_ref, own_ref, near_ref, near)


def dec_grad_kernel(groups, *refs):
    error_ref, parts, out_ref = refs[0], refs[1 : 1 + len(groups)], refs[-1]
    width = parts[0].shape[1]
    tok = error_ref.shape[0]
    for i, row, mask in flat(groups):
        part = parts[i][row * tok : (row + 1) * tok, :]
        out_ref[0, 0, :, columns(owner(mask), width)] = transposed(error_ref[...], part).astype(BF16)


def sum_kernel(groups, own_ref, arrived_ref, *outs):
    width = outs[0].shape[1]
    tok = own_ref.shape[0]
    for i, row, mask in flat(groups):
        here = columns(lax.rem(owner(mask), COUNT // 2), width)
        total = own_ref[:, here] + arrived_ref[:, here].astype(F32)
        outs[i][row * tok : (row + 1) * tok, :] = total.astype(outs[i].dtype)


def add_kernel(kept_ref, arrived_ref, *outs):
    tok = outs[0].shape[0]
    for row, out_ref in enumerate(outs):
        here = slice(row * tok, (row + 1) * tok)
        out_ref[...] = (kept_ref[here, :] + arrived_ref[here, :].astype(F32)).astype(out_ref.dtype)


def enc_grad_kernel(*refs):
    grads, parts = refs[: -2 - 2 * COUNT], refs[-2 - 2 * COUNT : -2]
    active_ref, out_ref = refs[-2:]
    width = parts[0].shape[1]
    total = grads[0][...]
    for grad in grads[1:]:
        total = total + grad[...].astype(F32)
    pre_grad = (total * 2.0 * active_ref[...]).astype(BF16)
    for k, offset in enumerate(OFFSETS):
        out_ref[0, :, columns(ring_owner(offset), width)] = transposed(pre_grad, block(parts, k)).astype(BF16)


def cost(flops, moved):
    return pl.CostEstimate(flops=flops, bytes_accessed=moved, transcendentals=0)


def on_device(inputs, targets, enc_w, enc_b, dec_w, dec_b):
    count = COUNT
    tok, width = inputs.shape[1:]
    own_features, model = enc_w.shape[1:]
    features = dec_w.shape[3]
    scale = tok ** (-0.5)
    matmul = 2 * tok * width * features
    half = (tok, features // 2)
    struct = jax.ShapeDtypeStruct

    first, last = ring_gather(inputs[0])
    inputs_of = [part for offset in OFFSETS for part in (first[offset], last[offset])]
    enc_weights, weights = [pltpu.with_memory_space_constraint(w[0], pltpu.HBM) for w in (enc_w, dec_w)]

    codes, active = pl.pallas_call(
        pre_kernel,
        name="pre",
        out_shape=(struct((tok, own_features), BF16), struct((tok, own_features), F32)),
        in_specs=[*vmem(2 * count), pl.BlockSpec(memory_space=pltpu.HBM), *vmem(1)],
        out_specs=tuple(vmem(2)),
        scratch_shapes=[pltpu.VMEM((count, own_features, width), BF16), pltpu.SemaphoreType.DMA((count,))],
        compiler_params=params(20),
        cost_estimate=cost(2 * tok * own_features * model, 2 * own_features * model),
    )(*inputs_of, enc_weights, enc_b)

    near_line = exchanged(codes, 2)
    across = exchanged(codes, 1)
    far_line = exchanged(codes, 6)
    farther_line = exchanged(codes, 4)
    near_across = exchanged(codes, 3)
    near_three = packed((across, near_line, near_across))
    previous_codes = from_behind(codes, "section", 1)
    previous_near = from_behind(near_three, "section", 1)
    far_pair = packed((far_line, farther_line), (previous_codes, near_three))
    far_across = exchanged(far_pair, 1)
    own = [codes, near_three, far_pair, far_across]
    previous = [
        previous_codes,
        previous_near,
        from_behind(far_pair, "section", 1),
        from_behind(far_across, "section", 1),
    ]

    held = pltpu.VMEM((width, features), BF16)
    sems = [pltpu.SemaphoreType.DMA((tiles(width)[0],))]
    total, own_weights = pl.pallas_call(
        own_recon_kernel,
        name="own_recon",
        out_shape=(struct((width, tok), F32), held),
        in_specs=[*vmem(len(own)), pl.BlockSpec(memory_space=pltpu.HBM)],
        out_specs=tuple(vmem(2)),
        scratch_shapes=sems,
        compiler_params=params(8),
        cost_estimate=cost(matmul, 4 * MIB),
    )(*own, weights)

    error, sent_far, next_weights = pl.pallas_call(
        functools.partial(recon_kernel, scale),
        name="recon",
        out_shape=(struct((tok, width), BF16), struct(half, BF16), held),
        in_specs=[*vmem(len(previous) + 1), pl.BlockSpec(memory_space=pltpu.HBM), *vmem(2)],
        out_specs=tuple(vmem(3)),
        scratch_shapes=sems,
        compiler_params=params(8),
        cost_estimate=cost(2 * matmul, 4 * MIB),
    )(*previous, total, weights, dec_b, targets[0])
    arrived_far = from_behind(sent_far, "section", -1)

    sent_near, own_near, own_far = pl.pallas_call(
        own_grad_kernel,
        name="own_grad",
        out_shape=(struct(half, BF16), struct(half, F32), struct(half, F32)),
        in_specs=vmem(3),
        out_specs=tuple(vmem(3)),
        compiler_params=params(8),
        cost_estimate=cost(3 * matmul // 2, 6 * MIB),
    )(error, own_weights, next_weights)
    arrived_near = from_behind(sent_near, "section", -1)

    rows = 256 if width % 256 == 0 else LANES

    def dec_grad_slot(slot, groups, parts, *held):
        return pl.pallas_call(
            functools.partial(dec_grad_kernel, groups),
            name="dec_grad",
            grid=(width // rows,),
            out_shape=struct(dec_w.shape, BF16),
            in_specs=[
                pl.BlockSpec((tok, rows), lambda j: (0, j)),
                *[pl.BlockSpec(part.shape, lambda j: (0, 0)) for part in parts],
                *[pl.BlockSpec(memory_space=pltpu.HBM) for _ in held],
            ],
            out_specs=pl.BlockSpec((1, 1, rows, features), lambda j: (0, slot, j, 0)),
            input_output_aliases={1 + len(parts): 0} if held else {},
            compiler_params=params(12),
            cost_estimate=cost(matmul, 2 * width * features),
        )(error, *parts, *held)

    dec_grad = dec_grad_slot(0, BLOCKS, own)

    def sums(groups, kinds, own_half, arrived):
        return pl.pallas_call(
            functools.partial(sum_kernel, groups),
            name="sum",
            out_shape=tuple(struct((len(g) * tok, own_features), kind) for g, kind in zip(groups, kinds)),
            in_specs=vmem(2),
            out_specs=tuple(vmem(len(groups))),
            compiler_params=params(2),
            cost_estimate=cost(tok * features, 2 * MIB),
        )(own_half, arrived)

    kept, crossing = sums(((6, 4), (7, 5)), (F32, BF16), own_far, arrived_far)
    lines = pl.pallas_call(
        add_kernel,
        name="add",
        out_shape=(struct((tok, own_features), BF16),) * 2,
        in_specs=vmem(2),
        out_specs=tuple(vmem(2)),
        compiler_params=params(2),
        cost_estimate=cost(tok * own_features, MIB),
    )(kept, exchanged(crossing, 1))
    near_sums = sums(((0,), (1,), (2,), (3,)), (F32, BF16, BF16, BF16), own_near, arrived_near)
    grads = [
        near_sums[0],
        *[exchanged(near_sums[mask], mask) for mask in (1, 2, 3)],
        *[exchanged(line, mask) for mask, line in zip((6, 4), lines)],
    ]
    held_grad = pltpu.with_memory_space_constraint(dec_grad, pltpu.HBM)
    dec_grad = dec_grad_slot(1, BLOCKS, previous, held_grad)

    enc_grad = pl.pallas_call(
        enc_grad_kernel,
        name="enc_grad",
        grid=(own_features // LANES,),
        out_shape=struct(enc_w.shape, BF16),
        in_specs=[
            *[pl.BlockSpec((tok, LANES), lambda j: (0, j))] * len(grads),
            *[pl.BlockSpec((tok // 2, width), lambda j: (0, 0))] * (2 * count),
            pl.BlockSpec((tok, LANES), lambda j: (0, j)),
        ],
        out_specs=pl.BlockSpec((1, LANES, model), lambda j: (0, j, 0)),
        compiler_params=params(16),
        cost_estimate=cost(matmul, 2 * own_features * model),
    )(*grads, *inputs_of, active)
    return enc_grad, dec_grad


def plain(inputs, targets, enc_w, enc_b, dec_w, dec_b):
    scale = inputs.shape[1] ** (-0.5)
    gathered = lax.all_gather(inputs[0], "feat", axis=1, tiled=True)
    active = jnp.maximum(against(gathered, enc_w[0]) + enc_b[0], 0.0)
    codes = (active * active).astype(BF16)
    own = lax.all_gather(codes, "feat", axis=1, tiled=True)
    previous = from_behind(own, "section", 1)
    weights = dec_w[0]
    total = dec_b[0] + against(own, weights[0]) + against(previous, weights[1])
    error = ((total - targets[0].astype(F32)) * scale).astype(BF16)
    sent = jnp.dot(error, weights[1], preferred_element_type=F32)
    code_grad = jnp.dot(error, weights[0], preferred_element_type=F32) + from_behind(sent, "section", -1)
    mine = lax.psum_scatter(code_grad, "feat", scatter_dimension=1, tiled=True)
    pre_grad = (mine * 2.0 * active).astype(BF16)
    enc_grad = transposed(pre_grad, gathered).astype(BF16)[None]
    dec_grad = jnp.stack([transposed(error, source).astype(BF16) for source in (own, previous)])[None]
    return enc_grad, dec_grad


def chosen(inputs, targets, enc_w, enc_b, dec_w, dec_b):
    aligned = all(size % LANES == 0 for size in (*inputs.shape[1:], enc_w.shape[1]))
    fits = lax.axis_size("feat") == COUNT and dec_w.shape[1] == 2
    body = on_device if aligned and fits else plain
    return body(inputs, targets, enc_w, enc_b, dec_w, dec_b)


def solution(mesh):
    return jax.shard_map(
        chosen,
        mesh=mesh,
        in_specs=(
            P("section", None, "feat"),
            P("section", None, "feat"),
            P("section", "feat", None),
            P("section", "feat"),
            P("section", None, "feat", None),
            P("section", "feat"),
        ),
        out_specs=(P("section", "feat", None), P("section", None, "feat", None)),
        check_vma=False,
    )
```

time: 130 us -> 110 us (0.85)
  the two profiles are of different devices: /device:TPU:2 before, /device:TPU:1 now
where the time goes in v3:
time: 110 us
  starting transfers between devices  49.6 us (45%)
  Pallas kernels  38.5 us (35%)
  waiting for transfers between devices  19 us (17%)
  local copies, waits for them, and re-layouts  1.68 us (2%)
    ppermute x6, starting transfers between devices, from_behind(): lax.ppermute(value, axis, [(source, source + steps) for source in range(i...  22.4 us
    ppermute x12, starting transfers between devices, exchanged(): return lax.ppermute(value, 'feat', [(i, i ^ mask) for i in range(count)])  15.7 us
    ppermute x14, starting transfers between devices, passed_on(): lax.ppermute(value, 'feat', [(order[p], order[(p + by) % count]) for p in...  11.5 us
    ppermute x14, waiting for transfers between devices, passed_on(): lax.ppermute(value, 'feat', [(order[p], order[(p + by) % count]) for p in...  10.3 us
    pallas_call x2, Pallas kernels, dec_grad_slot(): pl.pallas_call(functools.partial(dec_grad_kernel, groups), name='dec_grad...  9.83 us
    ppermute x6, waiting for transfers between devices, from_behind(): lax.ppermute(value, axis, [(source, source + steps) for source in range(i...  8.73 us
    pallas_call x1, Pallas kernels, on_device(): pl.pallas_call(functools.partial(recon_kernel, scale), name='recon', out_...  8.11 us
    pallas_call x1, Pallas kernels, on_device(): pl.pallas_call(own_recon_kernel, name='own_recon', out_shape=(struct((wid...  6.57 us
  transfers between devices with their start and end apart: 32, of which 12 were waited for; matrix products, arithmetic and copies ran while one was open for 0% of the time, Pallas kernels for 19%

profile of v3, /device:TPU:1, one launch (start us, length us, event | category | flops | bytes accessed | tf_op | source)
XLA Modules:
  0.0 109.8 jit_solution(6685449688242101416)
XLA Ops:
  0.6 1.0 slice_bitcast_fusion
  1.6 2.1 %collective-permute-start.3 = (bf16[64,1024]{1,0:T(8,128)(2,1)S(1)}, bf16[64,1024]{1,0:T(8,128)(2,1)S(1)}, u32[]{:S(2)}, u32[]{:S(2)}) collective-permute-start(bf16[64,1024]{1,0:T(8,128)(2,1)S(1)} %get-tuple-element.38.refs_1_.refs_7_), channel_id=1, source_target_pairs={{0,1},{2,0},{4,2},{6,4},{7,6},{5,7},{3,5},{1,3},{8,9},{10,8},{12,1... | collective-permute-start | bytes 393224 | tf_op jit(solution)/shard_map/ppermute | solution.py:46
  3.9 1.4 %collective-permute-start.1 = (bf16[64,1024]{1,0:T(8,128)(2,1)S(1)}, bf16[64,1024]{1,0:T(8,128)(2,1)S(1)}, u32[]{:S(2)}, u32[]{:S(2)}) collective-permute-start(bf16[64,1024]{1,0:T(8,128)(2,1)S(1)} %get-tuple-element.38.refs_1_.refs_7_), channel_id=1, source_target_pairs={{0,2},{2,4},{4,6},{6,7},{7,5},{5,3},{3,1},{1,0},{8,10},{10,12},{12... | collective-permute-start | bytes 393224 | tf_op jit(solution)/shard_map/ppermute | solution.py:46
  5.3 1.7 %collective-permute-done.3.refs_5_.refs_11_ = bf16[64,1024]{1,0:T(8,128)(2,1)S(1)} collective-permute-done((bf16[64,1024]{1,0:T(8,128)(2,1)S(1)}, bf16[64,1024]{1,0:T(8,128)(2,1)S(1)}, u32[]{:S(2)}, u32[]{:S(2)}) %collective-permute-start.3) | collective-permute-done | bytes 131104 | tf_op jit(solution)/shard_map/ppermute | solution.py:46
  7.0 1.1 collective-permute-start.7
  8.1 0.4 collective-permute-start.4
  8.5 2.1 %collective-permute-done.1.refs_3_.refs_9_ = bf16[64,1024]{1,0:T(8,128)(2,1)S(1)} collective-permute-done((bf16[64,1024]{1,0:T(8,128)(2,1)S(1)}, bf16[64,1024]{1,0:T(8,128)(2,1)S(1)}, u32[]{:S(2)}, u32[]{:S(2)}) %collective-permute-start.1) | collective-permute-done | bytes 131104 | tf_op jit(solution)/shard_map/ppermute | solution.py:46
  10.6 0.4 collective-permute-start.5
  11.0 1.0 collective-permute-start.6
  12.1 0.3 collective-permute-done.7.refs_9_.refs_15_
  12.3 1.2 %collective-permute-start.11 = (bf16[64,1024]{1,0:T(8,128)(2,1)S(1)}, bf16[64,1024]{1,0:T(8,128)(2,1)S(1)}, u32[]{:S(2)}, u32[]{:S(2)}) collective-permute-start(bf16[64,1024]{1,0:T(8,128)(2,1)S(1)} %collective-permute-done.7.refs_9_.refs_15_), channel_id=1, source_target_pairs={{0,1},{2,0},{4,2},{6,4},{7,6},{5,7},{3,5},{1,3},{8,9},{10,8},{12,1... | collective-permute-start | bytes 393224 | tf_op jit(solution)/shard_map/ppermute | solution.py:46
  13.5 0.3 collective-permute-start.8
  13.8 1.6 %collective-permute-done.5.refs_7_.refs_13_ = bf16[64,1024]{1,0:T(8,128)(2,1)S(1)} collective-permute-done((bf16[64,1024]{1,0:T(8,128)(2,1)S(1)}, bf16[64,1024]{1,0:T(8,128)(2,1)S(1)}, u32[]{:S(2)}, u32[]{:S(2)}) %collective-permute-start.5) | collective-permute-done | bytes 131104 | tf_op jit(solution)/shard_map/ppermute | solution.py:46
  15.4 0.8 collective-permute-start.9
  16.2 0.7 collective-permute-start.10
  16.9 1.3 %collective-permute-start.13 = (bf16[64,1024]{1,0:T(8,128)(2,1)S(1)}, bf16[64,1024]{1,0:T(8,128)(2,1)S(1)}, u32[]{:S(2)}, u32[]{:S(2)}) collective-permute-start(bf16[64,1024]{1,0:T(8,128)(2,1)S(1)} %collective-permute-done.11.refs_13_.refs_19_), channel_id=1, source_target_pairs={{0,1},{2,0},{4,2},{6,4},{7,6},{5,7},{3,5},{1,3},{8,9},{10,8},{12,1... | collective-permute-start | bytes 393224 | tf_op jit(solution)/shard_map/ppermute | solution.py:46
  18.2 0.4 collective-permute-done.8.refs_10_.refs_16_
  18.6 0.6 collective-permute-start.12
  19.2 1.2 %collective-permute-done.9.refs_11_.refs_17_ = bf16[64,1024]{1,0:T(8,128)(2,1)S(1)} collective-permute-done((bf16[64,1024]{1,0:T(8,128)(2,1)S(1)}, bf16[64,1024]{1,0:T(8,128)(2,1)S(1)}, u32[]{:S(2)}, u32[]{:S(2)}) %collective-permute-start.9) | collective-permute-done | bytes 131104 | tf_op jit(solution)/shard_map/ppermute | solution.py:46
  20.5 1.2 %collective-permute-done.10.refs_12_.refs_18_ = bf16[64,1024]{1,0:T(8,128)(2,1)S(1)} collective-permute-done((bf16[64,1024]{1,0:T(8,128)(2,1)S(1)}, bf16[64,1024]{1,0:T(8,128)(2,1)S(1)}, u32[]{:S(2)}, u32[]{:S(2)}) %collective-permute-start.10) | collective-permute-done | bytes 131104 | tf_op jit(solution)/shard_map/ppermute | solution.py:46
  21.7 1.1 %collective-permute-done.13.refs_15_.refs_21_ = bf16[64,1024]{1,0:T(8,128)(2,1)S(1)} collective-permute-done((bf16[64,1024]{1,0:T(8,128)(2,1)S(1)}, bf16[64,1024]{1,0:T(8,128)(2,1)S(1)}, u32[]{:S(2)}, u32[]{:S(2)}) %collective-permute-start.13) | collective-permute-done | bytes 131104 | tf_op jit(solution)/shard_map/ppermute | solution.py:46
  22.8 0.6 collective-permute-done.12.refs_14_.refs_20_
  23.4 0.7 copy-done.2
  24.1 4.7 %pre.1 = (bf16[128,512]{1,0:T(8,128)(2,1)S(1)}, f32[128,512]{1,0:T(8,128)S(1)}) custom-call(bf16[64,1024]{1,0:T(8,128)(2,1)S(1)} %get-tuple-element.39.refs_0_.refs_6_, bf16[64,1024]{1,0:T(8,128)(2,1)S(1)} %get-tuple-element.38.refs_1_.refs_7_, bf16[64,1024]{1,0:T(8,128)(2,1)S(1)} %collective-permute-done.refs_2_.refs_8_, ...), custom_call_target="tpu_custom_call" | custom-call | flops 1073741824 | bytes 8388608 | tf_op jit(solution)/shard_map/pre/pallas_call | solution.py:273
  28.8 2.4 %collective-permute-start.17 = (bf16[128,512]{1,0:T(8,128)(2,1)S(1)}, bf16[128,512]{1,0:T(8,128)(2,1)S(1)}, u32[]{:S(2)}, u32[]{:S(2)}) collective-permute-start(bf16[128,512]{1,0:T(8,128)(2,1)S(1)} %get-tuple-element.20.refs_0_.refs_1_), channel_id=1, source_target_pairs={{0,3},{1,2},{2,1},{3,0},{4,7},{5,6},{6,5},{7,4},{8,11},{9,10},{10,... | collective-permute-start | bytes 393224 | tf_op jit(solution)/shard_map/ppermute | solution.py:36
  31.3 0.2 collective-permute-start.15
  31.5 2.1 %collective-permute-start.20 = (bf16[128,512]{1,0:T(8,128)(2,1)S(1)}, bf16[128,512]{1,0:T(8,128)(2,1)S(1)}, u32[]{:S(2)}, u32[]{:S(2)}) collective-permute-start(bf16[128,512]{1,0:T(8,128)(2,1)S(1)} %get-tuple-element.20.refs_0_.refs_1_), channel_id=1, source_target_pairs={{0,4},{1,5},{2,6},{3,7},{4,0},{5,1},{6,2},{7,3},{8,12},{9,13},{10,... | collective-permute-start | bytes 393224 | tf_op jit(solution)/shard_map/ppermute | solution.py:36
  33.7 1.1 collective-permute-start.19
  34.7 9.5 %collective-permute-start.14 = (bf16[128,512]{1,0:T(8,128)(2,1)S(1)}, bf16[128,512]{1,0:T(8,128)(2,1)S(1)}, u32[]{:S(2)}, u32[]{:S(2)}) collective-permute-start(bf16[128,512]{1,0:T(8,128)(2,1)S(1)} %get-tuple-element.20.refs_0_.refs_1_), channel_id=1, source_target_pairs={{0,8},{8,16},{16,24},{1,9},{9,17},{17,25},{2,10},{10,18},{18,26},{... | collective-permute-start | bytes 393224 | tf_op jit(solution)/shard_map/ppermute | solution.py:23
  44.3 1.8 %collective-permute-done.14.refs_2_.refs_0_.refs_1_ = bf16[128,512]{1,0:T(8,128)(2,1)S(1)} collective-permute-done((bf16[128,512]{1,0:T(8,128)(2,1)S(1)}, bf16[128,512]{1,0:T(8,128)(2,1)S(1)}, u32[]{:S(2)}, u32[]{:S(2)}) %collective-permute-start.14) | collective-permute-done | bytes 131104 | tf_op jit(solution)/shard_map/ppermute | solution.py:23
  46.1 1.8 %collective-permute-start.22 = (bf16[256,512]{1,0:T(8,128)(2,1)S(1)}, bf16[256,512]{1,0:T(8,128)(2,1)S(1)}, u32[]{:S(2)}, u32[]{:S(2)}) collective-permute-start(bf16[256,512]{1,0:T(8,128)(2,1)S(1)} %pack.3.refs_2_.refs_3_), channel_id=1, source_target_pairs={{0,1},{1,0},{2,3},{3,2},{4,5},{5,4},{6,7},{7,6},{8,9},{9,8},{10,11... | collective-permute-start | bytes 786440 | tf_op jit(solution)/shard_map/ppermute | solution.py:36
  48.0 4.6 %collective-permute-start.18 = (bf16[384,512]{1,0:T(8,128)(2,1)S(1)}, bf16[384,512]{1,0:T(8,128)(2,1)S(1)}, u32[]{:S(2)}, u32[]{:S(2)}) collective-permute-start(bf16[384,512]{1,0:T(8,128)(2,1)S(1)} %pack.2.refs_3_.refs_1_.refs_2_), channel_id=1, source_target_pairs={{0,8},{8,16},{16,24},{1,9},{9,17},{17,25},{2,10},{10,18},{18,26},{... | collective-permute-start | bytes 1179656 | tf_op jit(solution)/shard_map/ppermute | solution.py:23
  52.6 1.9 %collective-permute-start.21 = (bf16[256,512]{1,0:T(8,128)(2,1)S(1)}, bf16[256,512]{1,0:T(8,128)(2,1)S(1)}, u32[]{:S(2)}, u32[]{:S(2)}) collective-permute-start(bf16[256,512]{1,0:T(8,128)(2,1)S(1)} %pack.3.refs_2_.refs_3_), channel_id=1, source_target_pairs={{0,8},{8,16},{16,24},{1,9},{9,17},{17,25},{2,10},{10,18},{18,26},{... | collective-permute-start | bytes 786440 | tf_op jit(solution)/shard_map/ppermute | solution.py:23
  54.5 2.4 %collective-permute-start.23 = (bf16[256,512]{1,0:T(8,128)(2,1)S(1)}, bf16[256,512]{1,0:T(8,128)(2,1)S(1)}, u32[]{:S(2)}, u32[]{:S(2)}) collective-permute-start(bf16[256,512]{1,0:T(8,128)(2,1)S(1)} %collective-permute-done.22.refs_3_.refs_4_), channel_id=1, source_target_pairs={{0,8},{8,16},{16,24},{1,9},{9,17},{17,25},{2,10},{10,18},{18,26},{... | collective-permute-start | bytes 786440 | tf_op jit(solution)/shard_map/ppermute | solution.py:23
  57.0 6.6 %own_recon.1 = (f32[1024,128]{1,0:T(8,128)S(1)}, bf16[1024,4096]{1,0:T(8,128)(2,1)S(1)}) custom-call(bf16[128,512]{1,0:T(8,128)(2,1)S(1)} %get-tuple-element.20.refs_0_.refs_1_, bf16[384,512]{1,0:T(8,128)(2,1)S(1)} %pack.2.refs_3_.refs_1_.refs_2_, bf16[256,512]{1,0:T(8,128)(2,1)S(1)} %pack.3.refs_2_.refs_3_, ...), custom_call_target="tpu_custom_call" | custom-call | flops 1073741824 | bytes 4194304 | tf_op jit(solution)/shard_map/own_recon/pallas_call | solution.py:304
  63.6 8.1 %recon.1 = (bf16[128,1024]{1,0:T(8,128)(2,1)S(1)}, bf16[128,2048]{1,0:T(8,128)(2,1)S(1)}, bf16[1024,4096]{1,0:T(8,128)(2,1)S(1)}) custom-call(bf16[128,512]{1,0:T(8,128)(2,1)S(1)} %collective-permute-done.14.refs_2_.refs_0_.refs_1_, bf16[384,512]{1,0:T(8,128)(2,1)S(1)} %collective-permute-done.18.refs_1_.refs_2_, ...), custom_call_target="tpu_custom_call" | custom-call | flops 2147483648 | bytes 4194304 | tf_op jit(solution)/shard_map/recon/pallas_call | solution.py:315
  71.7 1.9 %collective-permute-start.28 = (bf16[128,2048]{1,0:T(8,128)(2,1)S(1)}, bf16[128,2048]{1,0:T(8,128)(2,1)S(1)}, u32[]{:S(2)}, u32[]{:S(2)}) collective-permute-start(bf16[128,2048]{1,0:T(8,128)(2,1)S(1)} %get-tuple-element.32), channel_id=1, source_target_pairs={{8,0},{16,8},{24,16},{9,1},{17,9},{25,17},{10,2},{18,10},{26,18},{... | collective-permute-start | bytes 1572872 | tf_op jit(solution)/shard_map/ppermute | solution.py:23
  73.7 3.8 %own_grad.1 = (bf16[128,2048]{1,0:T(8,128)(2,1)S(1)}, f32[128,2048]{1,0:T(8,128)S(1)}, f32[128,2048]{1,0:T(8,128)S(1)}) custom-call(bf16[128,1024]{1,0:T(8,128)(2,1)S(1)} %get-tuple-element.22.error_ref.refs_0_, bf16[1024,4096]{1,0:T(8,128)(2,1)S(1)} %get-tuple-element.23.own_ref, bf16[1024,4096]{1,0:T(8,128)(2,1)S(1)} %get-tuple-element.24.next_ref), custom_call_target="tpu_custom_call" | custom-call | flops 1610612736 | bytes 6291456 | tf_op jit(solution)/shard_map/own_grad/pallas_call | solution.py:327
  77.5 2.1 %collective-permute-start.24 = (bf16[128,2048]{1,0:T(8,128)(2,1)S(1)}, bf16[128,2048]{1,0:T(8,128)(2,1)S(1)}, u32[]{:S(2)}, u32[]{:S(2)}) collective-permute-start(bf16[128,2048]{1,0:T(8,128)(2,1)S(1)} %get-tuple-element.26), channel_id=1, source_target_pairs={{8,0},{16,8},{24,16},{9,1},{17,9},{25,17},{10,2},{18,10},{26,18},{... | collective-permute-start | bytes 1572872 | tf_op jit(solution)/shard_map/ppermute | solution.py:23
  79.6 2.9 %collective-permute-done.28.arrived_ref = bf16[128,2048]{1,0:T(8,128)(2,1)S(1)} collective-permute-done((bf16[128,2048]{1,0:T(8,128)(2,1)S(1)}, bf16[128,2048]{1,0:T(8,128)(2,1)S(1)}, u32[]{:S(2)}, u32[]{:S(2)}) %collective-permute-start.28) | collective-permute-done | bytes 524320 | tf_op jit(solution)/shard_map/ppermute | solution.py:23
  82.7 1.7 %collective-permute-start.29 = (bf16[256,512]{1,0:T(8,128)(2,1)S(1)}, bf16[256,512]{1,0:T(8,128)(2,1)S(1)}, u32[]{:S(2)}, u32[]{:S(2)}) collective-permute-start(bf16[256,512]{1,0:T(8,128)(2,1)S(1)} %get-tuple-element.34), channel_id=1, source_target_pairs={{0,1},{1,0},{2,3},{3,2},{4,5},{5,4},{6,7},{7,6},{8,9},{9,8},{10,11... | collective-permute-start | bytes 786440 | tf_op jit(solution)/shard_map/ppermute | solution.py:36
  84.4 3.9 %collective-permute-done.24.arrived_ref = bf16[128,2048]{1,0:T(8,128)(2,1)S(1)} collective-permute-done((bf16[128,2048]{1,0:T(8,128)(2,1)S(1)}, bf16[128,2048]{1,0:T(8,128)(2,1)S(1)}, u32[]{:S(2)}, u32[]{:S(2)}) %collective-permute-start.24) | collective-permute-done | bytes 524320 | tf_op jit(solution)/shard_map/ppermute | solution.py:23
  88.5 1.8 %collective-permute-start.25 = (bf16[128,512]{1,0:T(8,128)(2,1)S(1)}, bf16[128,512]{1,0:T(8,128)(2,1)S(1)}, u32[]{:S(2)}, u32[]{:S(2)}) collective-permute-start(bf16[128,512]{1,0:T(8,128)(2,1)S(1)} %get-tuple-element.28), channel_id=1, source_target_pairs={{0,1},{1,0},{2,3},{3,2},{4,5},{5,4},{6,7},{7,6},{8,9},{9,8},{10,11... | collective-permute-start | bytes 393224 | tf_op jit(solution)/shard_map/ppermute | solution.py:36
  90.4 1.1 %collective-permute-start.27 = (bf16[128,512]{1,0:T(8,128)(2,1)S(1)}, bf16[128,512]{1,0:T(8,128)(2,1)S(1)}, u32[]{:S(2)}, u32[]{:S(2)}) collective-permute-start(bf16[128,512]{1,0:T(8,128)(2,1)S(1)} %get-tuple-element.30), channel_id=1, source_target_pairs={{0,3},{1,2},{2,1},{3,0},{4,7},{5,6},{6,5},{7,4},{8,11},{9,10},{10,... | collective-permute-start | bytes 393224 | tf_op jit(solution)/shard_map/ppermute | solution.py:36
  91.5 3.2 %collective-permute-start.30 = (bf16[128,512]{1,0:T(8,128)(2,1)S(1)}, bf16[128,512]{1,0:T(8,128)(2,1)S(1)}, u32[]{:S(2)}, u32[]{:S(2)}) collective-permute-start(bf16[128,512]{1,0:T(8,128)(2,1)S(1)} %get-tuple-element.35), channel_id=1, source_target_pairs={{0,6},{1,7},{2,4},{3,5},{4,2},{5,3},{6,0},{7,1},{8,14},{9,15},{10,... | collective-permute-start | bytes 393224 | tf_op jit(solution)/shard_map/ppermute | solution.py:36
  94.7 4.9 %dec_grad.2.refs_5_ = bf16[1,2,1024,4096]{3,2,1,0:T(8,128)(2,1)} custom-call(bf16[128,1024]{1,0:T(8,128)(2,1)S(1)} %get-tuple-element.22.error_ref.refs_0_, bf16[128,512]{1,0:T(8,128)(2,1)S(1)} %get-tuple-element.20.refs_0_.refs_1_, bf16[384,512]{1,0:T(8,128)(2,1)S(1)} %pack.2.refs_3_.refs_1_.refs_2_, bf16[256,512]{1,0:T(8,128)(2,1)S(1)} %pack.3.refs_2_.refs_3_, ...), custom_call_target="tpu_custom_call" | custom-call | flops 1073741824 | bytes 8388608 | tf_op jit(solution)/shard_map/dec_grad/pallas_call | solution.py:341
  99.6 4.9 %dec_grad.3 = bf16[1,2,1024,4096]{3,2,1,0:T(8,128)(2,1)} custom-call(bf16[128,1024]{1,0:T(8,128)(2,1)S(1)} %get-tuple-element.22.error_ref.refs_0_, bf16[128,512]{1,0:T(8,128)(2,1)S(1)} %collective-permute-done.14.refs_2_.refs_0_.refs_1_, bf16[384,512]{1,0:T(8,128)(2,1)S(1)} %collective-permute-done.18.refs_1_.refs_2_, ...), custom_call_target="tpu_custom_call", output_to_operand_aliasing={{}: (5, {})} | custom-call | flops 1073741824 | bytes 8388608 | tf_op jit(solution)/shard_map/dec_grad/pallas_call | solution.py:341
  104.6 5.2 %enc_grad.1 = bf16[1,512,8192]{2,1,0:T(8,128)(2,1)} custom-call(f32[128,512]{1,0:T(8,128)S(1)} %get-tuple-element.27.refs_0_, bf16[128,512]{1,0:T(8,128)(2,1)S(1)} %collective-permute-done.25.refs_1_, bf16[128,512]{1,0:T(8,128)(2,1)S(1)} %collective-permute-done.26.refs_2_, bf16[128,512]{1,0:T(8,128)(2,1)S(1)} %collective-permute-done.27.refs_3_, ...), custom_call_target="tpu_custom_call" | custom-call | flops 1073741824 | bytes 8388608 | tf_op jit(solution)/shard_map/enc_grad/pallas_call | solution.py:389
  (35 shorter events, 0.9 us)
Async XLA Ops:
  1.6 5.4 %collective-permute-start.3 = (bf16[64,1024]{1,0:T(8,128)(2,1)S(1)}, bf16[64,1024]{1,0:T(8,128)(2,1)S(1)}, u32[]{:S(2)}, u32[]{:S(2)}) collective-permute-start(bf16[64,1024]{1,0:T(8,128)(2,1)S(1)} %get-tuple-element.38.refs_1_.refs_7_), channel_id=1, source_target_pairs={{0,1},{2,0},{4,2},{6,4},{7,6},{5,7},{3,5},{1,3},{8,9},{10,8},{12,1... | collective-permute-start | bytes 393224 | tf_op jit(solution)/shard_map/ppermute | solution.py:46
  3.7 4.4 %collective-permute-start = (bf16[64,1024]{1,0:T(8,128)(2,1)S(1)}, bf16[64,1024]{1,0:T(8,128)(2,1)S(1)}, u32[]{:S(2)}, u32[]{:S(2)}) collective-permute-start(bf16[64,1024]{1,0:T(8,128)(2,1)S(1)} %get-tuple-element.39.refs_0_.refs_6_), channel_id=1, source_target_pairs={{0,2},{2,4},{4,6},{6,7},{7,5},{5,3},{3,1},{1,0},{8,10},{10,12},{12... | collective-permute-start | bytes 393224 | tf_op jit(solution)/shard_map/ppermute | solution.py:46
  3.9 6.7 %collective-permute-start.1 = (bf16[64,1024]{1,0:T(8,128)(2,1)S(1)}, bf16[64,1024]{1,0:T(8,128)(2,1)S(1)}, u32[]{:S(2)}, u32[]{:S(2)}) collective-permute-start(bf16[64,1024]{1,0:T(8,128)(2,1)S(1)} %get-tuple-element.38.refs_1_.refs_7_), channel_id=1, source_target_pairs={{0,2},{2,4},{4,6},{6,7},{7,5},{5,3},{3,1},{1,0},{8,10},{10,12},{12... | collective-permute-start | bytes 393224 | tf_op jit(solution)/shard_map/ppermute | solution.py:46
  5.3 5.8 %collective-permute-start.2 = (bf16[64,1024]{1,0:T(8,128)(2,1)S(1)}, bf16[64,1024]{1,0:T(8,128)(2,1)S(1)}, u32[]{:S(2)}, u32[]{:S(2)}) collective-permute-start(bf16[64,1024]{1,0:T(8,128)(2,1)S(1)} %get-tuple-element.39.refs_0_.refs_6_), channel_id=1, source_target_pairs={{0,1},{2,0},{4,2},{6,4},{7,6},{5,7},{3,5},{1,3},{8,9},{10,8},{12,1... | collective-permute-start | bytes 393224 | tf_op jit(solution)/shard_map/ppermute | solution.py:46
  7.0 5.3 %collective-permute-start.7 = (bf16[64,1024]{1,0:T(8,128)(2,1)S(1)}, bf16[64,1024]{1,0:T(8,128)(2,1)S(1)}, u32[]{:S(2)}, u32[]{:S(2)}) collective-permute-start(bf16[64,1024]{1,0:T(8,128)(2,1)S(1)} %collective-permute-done.3.refs_5_.refs_11_), channel_id=1, source_target_pairs={{0,1},{2,0},{4,2},{6,4},{7,6},{5,7},{3,5},{1,3},{8,9},{10,8},{12,1... | collective-permute-start | bytes 393224 | tf_op jit(solution)/shard_map/ppermute | solution.py:46
  8.1 5.4 %collective-permute-start.4 = (bf16[64,1024]{1,0:T(8,128)(2,1)S(1)}, bf16[64,1024]{1,0:T(8,128)(2,1)S(1)}, u32[]{:S(2)}, u32[]{:S(2)}) collective-permute-start(bf16[64,1024]{1,0:T(8,128)(2,1)S(1)} %collective-permute-done.refs_2_.refs_8_), channel_id=1, source_target_pairs={{0,2},{2,4},{4,6},{6,7},{7,5},{5,3},{3,1},{1,0},{8,10},{10,12},{12... | collective-permute-start | bytes 393224 | tf_op jit(solution)/shard_map/ppermute | solution.py:46
  10.6 4.8 %collective-permute-start.5 = (bf16[64,1024]{1,0:T(8,128)(2,1)S(1)}, bf16[64,1024]{1,0:T(8,128)(2,1)S(1)}, u32[]{:S(2)}, u32[]{:S(2)}) collective-permute-start(bf16[64,1024]{1,0:T(8,128)(2,1)S(1)} %collective-permute-done.1.refs_3_.refs_9_), channel_id=1, source_target_pairs={{0,2},{2,4},{4,6},{6,7},{7,5},{5,3},{3,1},{1,0},{8,10},{10,12},{12... | collective-permute-start | bytes 393224 | tf_op jit(solution)/shard_map/ppermute | solution.py:46
  11.0 5.2 %collective-permute-start.6 = (bf16[64,1024]{1,0:T(8,128)(2,1)S(1)}, bf16[64,1024]{1,0:T(8,128)(2,1)S(1)}, u32[]{:S(2)}, u32[]{:S(2)}) collective-permute-start(bf16[64,1024]{1,0:T(8,128)(2,1)S(1)} %collective-permute-done.2.refs_4_.refs_10_), channel_id=1, source_target_pairs={{0,1},{2,0},{4,2},{6,4},{7,6},{5,7},{3,5},{1,3},{8,9},{10,8},{12,1... | collective-permute-start | bytes 393224 | tf_op jit(solution)/shard_map/ppermute | solution.py:46
  12.3 4.6 %collective-permute-start.11 = (bf16[64,1024]{1,0:T(8,128)(2,1)S(1)}, bf16[64,1024]{1,0:T(8,128)(2,1)S(1)}, u32[]{:S(2)}, u32[]{:S(2)}) collective-permute-start(bf16[64,1024]{1,0:T(8,128)(2,1)S(1)} %collective-permute-done.7.refs_9_.refs_15_), channel_id=1, source_target_pairs={{0,1},{2,0},{4,2},{6,4},{7,6},{5,7},{3,5},{1,3},{8,9},{10,8},{12,1... | collective-permute-start | bytes 393224 | tf_op jit(solution)/shard_map/ppermute | solution.py:46
  13.5 5.1 %collective-permute-start.8 = (bf16[64,1024]{1,0:T(8,128)(2,1)S(1)}, bf16[64,1024]{1,0:T(8,128)(2,1)S(1)}, u32[]{:S(2)}, u32[]{:S(2)}) collective-permute-start(bf16[64,1024]{1,0:T(8,128)(2,1)S(1)} %collective-permute-done.4.refs_6_.refs_12_), channel_id=1, source_target_pairs={{0,2},{2,4},{4,6},{6,7},{7,5},{5,3},{3,1},{1,0},{8,10},{10,12},{12... | collective-permute-start | bytes 393224 | tf_op jit(solution)/shard_map/ppermute | solution.py:46
  15.4 5.1 %collective-permute-start.9 = (bf16[64,1024]{1,0:T(8,128)(2,1)S(1)}, bf16[64,1024]{1,0:T(8,128)(2,1)S(1)}, u32[]{:S(2)}, u32[]{:S(2)}) collective-permute-start(bf16[64,1024]{1,0:T(8,128)(2,1)S(1)} %collective-permute-done.5.refs_7_.refs_13_), channel_id=1, source_target_pairs={{0,2},{2,4},{4,6},{6,7},{7,5},{5,3},{3,1},{1,0},{8,10},{10,12},{12... | collective-permute-start | bytes 393224 | tf_op jit(solution)/shard_map/ppermute | solution.py:46
  16.2 5.4 %collective-permute-start.10 = (bf16[64,1024]{1,0:T(8,128)(2,1)S(1)}, bf16[64,1024]{1,0:T(8,128)(2,1)S(1)}, u32[]{:S(2)}, u32[]{:S(2)}) collective-permute-start(bf16[64,1024]{1,0:T(8,128)(2,1)S(1)} %collective-permute-done.6.refs_8_.refs_14_), channel_id=1, source_target_pairs={{0,1},{2,0},{4,2},{6,4},{7,6},{5,7},{3,5},{1,3},{8,9},{10,8},{12,1... | collective-permute-start | bytes 393224 | tf_op jit(solution)/shard_map/ppermute | solution.py:46
  16.9 5.9 %collective-permute-start.13 = (bf16[64,1024]{1,0:T(8,128)(2,1)S(1)}, bf16[64,1024]{1,0:T(8,128)(2,1)S(1)}, u32[]{:S(2)}, u32[]{:S(2)}) collective-permute-start(bf16[64,1024]{1,0:T(8,128)(2,1)S(1)} %collective-permute-done.11.refs_13_.refs_19_), channel_id=1, source_target_pairs={{0,1},{2,0},{4,2},{6,4},{7,6},{5,7},{3,5},{1,3},{8,9},{10,8},{12,1... | collective-permute-start | bytes 393224 | tf_op jit(solution)/shard_map/ppermute | solution.py:46
  18.6 4.8 %collective-permute-start.12 = (bf16[64,1024]{1,0:T(8,128)(2,1)S(1)}, bf16[64,1024]{1,0:T(8,128)(2,1)S(1)}, u32[]{:S(2)}, u32[]{:S(2)}) collective-permute-start(bf16[64,1024]{1,0:T(8,128)(2,1)S(1)} %collective-permute-done.8.refs_10_.refs_16_), channel_id=1, source_target_pairs={{0,2},{2,4},{4,6},{6,7},{7,5},{5,3},{3,1},{1,0},{8,10},{10,12},{12... | collective-permute-start | bytes 393224 | tf_op jit(solution)/shard_map/ppermute | solution.py:46
  23.4 0.7 copy-start.2
  28.8 5.9 %collective-permute-start.17 = (bf16[128,512]{1,0:T(8,128)(2,1)S(1)}, bf16[128,512]{1,0:T(8,128)(2,1)S(1)}, u32[]{:S(2)}, u32[]{:S(2)}) collective-permute-start(bf16[128,512]{1,0:T(8,128)(2,1)S(1)} %get-tuple-element.20.refs_0_.refs_1_), channel_id=1, source_target_pairs={{0,3},{1,2},{2,1},{3,0},{4,7},{5,6},{6,5},{7,4},{8,11},{9,10},{10,... | collective-permute-start | bytes 393224 | tf_op jit(solution)/shard_map/ppermute | solution.py:36
  31.2 13.0 %collective-permute-start.16 = (bf16[128,512]{1,0:T(8,128)(2,1)S(1)}, bf16[128,512]{1,0:T(8,128)(2,1)S(1)}, u32[]{:S(2)}, u32[]{:S(2)}) collective-permute-start(bf16[128,512]{1,0:T(8,128)(2,1)S(1)} %get-tuple-element.20.refs_0_.refs_1_), channel_id=1, source_target_pairs={{0,2},{1,3},{2,0},{3,1},{4,6},{5,7},{6,4},{7,5},{8,10},{9,11},{10,... | collective-permute-start | bytes 393224 | tf_op jit(solution)/shard_map/ppermute | solution.py:36
  31.3 12.9 %collective-permute-start.15 = (bf16[128,512]{1,0:T(8,128)(2,1)S(1)}, bf16[128,512]{1,0:T(8,128)(2,1)S(1)}, u32[]{:S(2)}, u32[]{:S(2)}) collective-permute-start(bf16[128,512]{1,0:T(8,128)(2,1)S(1)} %get-tuple-element.20.refs_0_.refs_1_), channel_id=1, source_target_pairs={{0,1},{1,0},{2,3},{3,2},{4,5},{5,4},{6,7},{7,6},{8,9},{9,8},{10,11... | collective-permute-start | bytes 393224 | tf_op jit(solution)/shard_map/ppermute | solution.py:36
  31.5 12.7 %collective-permute-start.20 = (bf16[128,512]{1,0:T(8,128)(2,1)S(1)}, bf16[128,512]{1,0:T(8,128)(2,1)S(1)}, u32[]{:S(2)}, u32[]{:S(2)}) collective-permute-start(bf16[128,512]{1,0:T(8,128)(2,1)S(1)} %get-tuple-element.20.refs_0_.refs_1_), channel_id=1, source_target_pairs={{0,4},{1,5},{2,6},{3,7},{4,0},{5,1},{6,2},{7,3},{8,12},{9,13},{10,... | collective-permute-start | bytes 393224 | tf_op jit(solution)/shard_map/ppermute | solution.py:36
  33.7 10.6 %collective-permute-start.19 = (bf16[128,512]{1,0:T(8,128)(2,1)S(1)}, bf16[128,512]{1,0:T(8,128)(2,1)S(1)}, u32[]{:S(2)}, u32[]{:S(2)}) collective-permute-start(bf16[128,512]{1,0:T(8,128)(2,1)S(1)} %get-tuple-element.20.refs_0_.refs_1_), channel_id=1, source_target_pairs={{0,6},{1,7},{2,4},{3,5},{4,2},{5,3},{6,0},{7,1},{8,14},{9,15},{10,... | collective-permute-start | bytes 393224 | tf_op jit(solution)/shard_map/ppermute | solution.py:36
  34.7 11.4 %collective-permute-start.14 = (bf16[128,512]{1,0:T(8,128)(2,1)S(1)}, bf16[128,512]{1,0:T(8,128)(2,1)S(1)}, u32[]{:S(2)}, u32[]{:S(2)}) collective-permute-start(bf16[128,512]{1,0:T(8,128)(2,1)S(1)} %get-tuple-element.20.refs_0_.refs_1_), channel_id=1, source_target_pairs={{0,8},{8,16},{16,24},{1,9},{9,17},{17,25},{2,10},{10,18},{18,26},{... | collective-permute-start | bytes 393224 | tf_op jit(solution)/shard_map/ppermute | solution.py:23
  46.1 8.4 %collective-permute-start.22 = (bf16[256,512]{1,0:T(8,128)(2,1)S(1)}, bf16[256,512]{1,0:T(8,128)(2,1)S(1)}, u32[]{:S(2)}, u32[]{:S(2)}) collective-permute-start(bf16[256,512]{1,0:T(8,128)(2,1)S(1)} %pack.3.refs_2_.refs_3_), channel_id=1, source_target_pairs={{0,1},{1,0},{2,3},{3,2},{4,5},{5,4},{6,7},{7,6},{8,9},{9,8},{10,11... | collective-permute-start | bytes 786440 | tf_op jit(solution)/shard_map/ppermute | solution.py:36
  48.0 15.6 %collective-permute-start.18 = (bf16[384,512]{1,0:T(8,128)(2,1)S(1)}, bf16[384,512]{1,0:T(8,128)(2,1)S(1)}, u32[]{:S(2)}, u32[]{:S(2)}) collective-permute-start(bf16[384,512]{1,0:T(8,128)(2,1)S(1)} %pack.2.refs_3_.refs_1_.refs_2_), channel_id=1, source_target_pairs={{0,8},{8,16},{16,24},{1,9},{9,17},{17,25},{2,10},{10,18},{18,26},{... | collective-permute-start | bytes 1179656 | tf_op jit(solution)/shard_map/ppermute | solution.py:23
  52.6 11.0 %collective-permute-start.21 = (bf16[256,512]{1,0:T(8,128)(2,1)S(1)}, bf16[256,512]{1,0:T(8,128)(2,1)S(1)}, u32[]{:S(2)}, u32[]{:S(2)}) collective-permute-start(bf16[256,512]{1,0:T(8,128)(2,1)S(1)} %pack.3.refs_2_.refs_3_), channel_id=1, source_target_pairs={{0,8},{8,16},{16,24},{1,9},{9,17},{17,25},{2,10},{10,18},{18,26},{... | collective-permute-start | bytes 786440 | tf_op jit(solution)/shard_map/ppermute | solution.py:23
  54.5 9.0 %collective-permute-start.23 = (bf16[256,512]{1,0:T(8,128)(2,1)S(1)}, bf16[256,512]{1,0:T(8,128)(2,1)S(1)}, u32[]{:S(2)}, u32[]{:S(2)}) collective-permute-start(bf16[256,512]{1,0:T(8,128)(2,1)S(1)} %collective-permute-done.22.refs_3_.refs_4_), channel_id=1, source_target_pairs={{0,8},{8,16},{16,24},{1,9},{9,17},{17,25},{2,10},{10,18},{18,26},{... | collective-permute-start | bytes 786440 | tf_op jit(solution)/shard_map/ppermute | solution.py:23
  56.9 6.6 %copy-start = (bf16[1,128,1024]{2,1,0:T(8,128)(2,1)S(1)}, bf16[1,128,1024]{2,1,0:T(8,128)(2,1)}, u32[]{:S(2)}) copy-start(bf16[1,128,1024]{2,1,0:T(8,128)(2,1)} %param.7) | copy-start | bytes 786436
  56.9 6.6 %copy-start.1 = (f32[1,1024]{1,0:T(1,128)S(1)}, f32[1,1024]{1,0:T(1,128)}, u32[]{:S(2)}) copy-start(f32[1,1024]{1,0:T(1,128)} %refs_6_.1) | copy-start | bytes 12292
  71.7 10.9 %collective-permute-start.28 = (bf16[128,2048]{1,0:T(8,128)(2,1)S(1)}, bf16[128,2048]{1,0:T(8,128)(2,1)S(1)}, u32[]{:S(2)}, u32[]{:S(2)}) collective-permute-start(bf16[128,2048]{1,0:T(8,128)(2,1)S(1)} %get-tuple-element.32), channel_id=1, source_target_pairs={{8,0},{16,8},{24,16},{9,1},{17,9},{25,17},{10,2},{18,10},{26,18},{... | collective-permute-start | bytes 1572872 | tf_op jit(solution)/shard_map/ppermute | solution.py:23
  77.5 10.8 %collective-permute-start.24 = (bf16[128,2048]{1,0:T(8,128)(2,1)S(1)}, bf16[128,2048]{1,0:T(8,128)(2,1)S(1)}, u32[]{:S(2)}, u32[]{:S(2)}) collective-permute-start(bf16[128,2048]{1,0:T(8,128)(2,1)S(1)} %get-tuple-element.26), channel_id=1, source_target_pairs={{8,0},{16,8},{24,16},{9,1},{17,9},{25,17},{10,2},{18,10},{26,18},{... | collective-permute-start | bytes 1572872 | tf_op jit(solution)/shard_map/ppermute | solution.py:23
  82.7 8.8 %collective-permute-start.29 = (bf16[256,512]{1,0:T(8,128)(2,1)S(1)}, bf16[256,512]{1,0:T(8,128)(2,1)S(1)}, u32[]{:S(2)}, u32[]{:S(2)}) collective-permute-start(bf16[256,512]{1,0:T(8,128)(2,1)S(1)} %get-tuple-element.34), channel_id=1, source_target_pairs={{0,1},{1,0},{2,3},{3,2},{4,5},{5,4},{6,7},{7,6},{8,9},{9,8},{10,11... | collective-permute-start | bytes 786440 | tf_op jit(solution)/shard_map/ppermute | solution.py:36
  88.5 16.1 %collective-permute-start.25 = (bf16[128,512]{1,0:T(8,128)(2,1)S(1)}, bf16[128,512]{1,0:T(8,128)(2,1)S(1)}, u32[]{:S(2)}, u32[]{:S(2)}) collective-permute-start(bf16[128,512]{1,0:T(8,128)(2,1)S(1)} %get-tuple-element.28), channel_id=1, source_target_pairs={{0,1},{1,0},{2,3},{3,2},{4,5},{5,4},{6,7},{7,6},{8,9},{9,8},{10,11... | collective-permute-start | bytes 393224 | tf_op jit(solution)/shard_map/ppermute | solution.py:36
  90.2 14.3 %collective-permute-start.26 = (bf16[128,512]{1,0:T(8,128)(2,1)S(1)}, bf16[128,512]{1,0:T(8,128)(2,1)S(1)}, u32[]{:S(2)}, u32[]{:S(2)}) collective-permute-start(bf16[128,512]{1,0:T(8,128)(2,1)S(1)} %get-tuple-element.29), channel_id=1, source_target_pairs={{0,2},{1,3},{2,0},{3,1},{4,6},{5,7},{6,4},{7,5},{8,10},{9,11},{10,... | collective-permute-start | bytes 393224 | tf_op jit(solution)/shard_map/ppermute | solution.py:36
  90.4 14.2 %collective-permute-start.27 = (bf16[128,512]{1,0:T(8,128)(2,1)S(1)}, bf16[128,512]{1,0:T(8,128)(2,1)S(1)}, u32[]{:S(2)}, u32[]{:S(2)}) collective-permute-start(bf16[128,512]{1,0:T(8,128)(2,1)S(1)} %get-tuple-element.30), channel_id=1, source_target_pairs={{0,3},{1,2},{2,1},{3,0},{4,7},{5,6},{6,5},{7,4},{8,11},{9,10},{10,... | collective-permute-start | bytes 393224 | tf_op jit(solution)/shard_map/ppermute | solution.py:36
  91.5 13.0 %collective-permute-start.30 = (bf16[128,512]{1,0:T(8,128)(2,1)S(1)}, bf16[128,512]{1,0:T(8,128)(2,1)S(1)}, u32[]{:S(2)}, u32[]{:S(2)}) collective-permute-start(bf16[128,512]{1,0:T(8,128)(2,1)S(1)} %get-tuple-element.35), channel_id=1, source_target_pairs={{0,6},{1,7},{2,4},{3,5},{4,2},{5,3},{6,0},{7,1},{8,14},{9,15},{10,... | collective-permute-start | bytes 393224 | tf_op jit(solution)/shard_map/ppermute | solution.py:36
  94.7 9.9 %collective-permute-start.31 = (bf16[128,512]{1,0:T(8,128)(2,1)S(1)}, bf16[128,512]{1,0:T(8,128)(2,1)S(1)}, u32[]{:S(2)}, u32[]{:S(2)}) collective-permute-start(bf16[128,512]{1,0:T(8,128)(2,1)S(1)} %get-tuple-element.36), channel_id=1, source_target_pairs={{0,4},{1,5},{2,6},{3,7},{4,0},{5,1},{6,2},{7,3},{8,12},{9,13},{10,... | collective-permute-start | bytes 393224 | tf_op jit(solution)/shard_map/ppermute | solution.py:36

commit v4 on v3

--- a/solution.py
+++ b/solution.py
@@ -14,7 +14,10 @@
 
 OFFSETS = (0, -1, 1, -2, 2, -3, 3, 4)
 COUNT = len(OFFSETS)
-BLOCKS = ((0,), (1, 2, 3), (6, 4), (7, 5))
+NEAR = (0, 1, 2, 3)
+FAR = (6, 4)
+CROSSING = (7, 5)
+BLOCKS = ((0, 1, 2, 3), (6, 4), (7, 5))
 
 
 def from_behind(value, axis, steps):
@@ -90,48 +93,58 @@
     return [(i, row, mask) for i, masks in enumerate(groups) for row, mask in enumerate(masks)]
 
 
-def pack_kernel(count, *refs):
+def pack_kernel(*refs):
     out_ref, start = refs[-1], 0
-    for ref in refs[:count]:
+    for ref in refs[:-1]:
         out_ref[start : start + ref.shape[0], :] = ref[...]
         start += ref.shape[0]
 
 
-def packed(parts, after=()):
+def packed(*parts):
     rows = sum(part.shape[0] for part in parts)
     return pl.pallas_call(
-        functools.partial(pack_kernel, len(parts)),
+        pack_kernel,
         name="pack",
         out_shape=jax.ShapeDtypeStruct((rows, parts[0].shape[1]), parts[0].dtype),
-        in_specs=[*vmem(len(parts)), *[pl.BlockSpec(memory_space=pl.ANY) for _ in after]],
+        in_specs=vmem(len(parts)),
         out_specs=vmem(1)[0],
         compiler_params=params(1),
         cost_estimate=pl.CostEstimate(
             flops=0, bytes_accessed=4 * rows * parts[0].shape[1], transcendentals=0
         ),
-    )(*parts, *after)
+    )(*parts)
 
 
 def block(parts, k):
     return jnp.concatenate([parts[2 * k][...], parts[2 * k + 1][...]], axis=0)
 
 
+def in_turn(copies, ahead):
+    for copy in copies[:ahead]:
+        copy.start()
+    for k, copy in enumerate(copies):
+        copy.wait()
+        for later in copies[k + ahead : k + ahead + 1]:
+            later.start()
+        yield k
+
+
 def pre_kernel(*refs):
     count = len(OFFSETS)
-    parts, (w_ref, b_ref, codes_ref, active_ref, held, sems) = refs[: 2 * count], refs[2 * count :]
+    parts, (w_ref, b_ref, codes_ref, active_ref, held, bias, sems) = refs[: 2 * count], refs[2 * count :]
     width = parts[0].shape[1]
     copies = [
         pltpu.make_async_copy(w_ref.at[:, columns(ring_owner(offset), width)], held.at[k], sems.at[k])
         for k, offset in enumerate(OFFSETS)
     ]
-    for copy in copies:
-        copy.start()
+    bias_copy = pltpu.make_async_copy(b_ref, bias, sems.at[count])
+    bias_copy.start()
     total = None
-    for k, copy in enumerate(copies):
-        copy.wait()
+    for k in in_turn(copies, 3):
         term = against(block(parts, k), held[k])
         total = term if total is None else total + term
-    active = jnp.maximum(total + b_ref[...], 0.0)
+    bias_copy.wait()
+    active = jnp.maximum(total + bias[...], 0.0)
     active_ref[...] = active
     codes_ref[...] = (active * active).astype(BF16)
 
@@ -165,30 +178,18 @@
     tok = total_ref.shape[1]
     _, tile = tiles(held_ref.shape[0])
     copies = row_copies(w_ref, 0, held_ref, sems)
-    for copy in copies:
-        copy.start()
-    for j, copy in enumerate(copies):
-        copy.wait()
+    for j in in_turn(copies, 2):
         here = slice(j * tile, (j + 1) * tile)
         total_ref[here, :] = decoded(held_ref, here, parts, BLOCKS, tok, None)
 
 
-def product(error_ref, w_ref, out_ref, first):
-    wide = out_ref.shape[1]
-    steps, tile = (wide // 512, 512) if wide % 512 == 0 else (wide // LANES, LANES)
-
-    @pl.loop(0, steps)
-    def _(j):
-        source = pl.ds(pl.multiple_of(first * wide + j * tile, tile), tile)
-        here = pl.ds(pl.multiple_of(j * tile, tile), tile)
-        out_ref[:, here] = jnp.dot(
-            error_ref[...], w_ref[:, source], preferred_element_type=F32
-        ).astype(out_ref.dtype)
-
-
-def halves():
-    near = lax.axis_index("feat") // (COUNT // 2)
-    return near, 1 - near
+def products(error_ref, w_ref, masks, out_ref):
+    tok = error_ref.shape[0]
+    for row, mask in enumerate(masks):
+        term = jnp.dot(
+            error_ref[...], w_ref[:, columns(owner(mask), out_ref.shape[1])], preferred_element_type=F32
+        )
+        out_ref[row * tok : (row + 1) * tok, :] = term.astype(out_ref.dtype)
 
 
 def recon_kernel(scale, *refs):
@@ -197,22 +198,18 @@
     tok = total_ref.shape[1]
     _, tile = tiles(held_ref.shape[0])
     copies = row_copies(w_ref, 1, held_ref, sems)
-    for copy in copies:
-        copy.start()
-    for j, copy in enumerate(copies):
-        copy.wait()
+    for j in in_turn(copies, 2):
         here = slice(j * tile, (j + 1) * tile)
         total = decoded(held_ref, here, parts, BLOCKS, tok, total_ref[here, :])
         error = total.T + b_ref[:, here] - target_ref[:, here].astype(F32)
         error_ref[:, here] = (error * scale).astype(BF16)
-    product(error_ref, held_ref, far_ref, halves()[1])
+    products(error_ref, held_ref, FAR + CROSSING, far_ref)
 
 
 def own_grad_kernel(error_ref, own_ref, next_ref, sent_ref, near_ref, far_ref):
-    near, far = halves()
-    product(error_ref, next_ref, sent_ref, near)
-    product(error_ref, own_ref, far_ref, far)
-    product(error_ref, own_ref, near_ref, near)
+    products(error_ref, next_ref, NEAR, sent_ref)
+    products(error_ref, own_ref, FAR + CROSSING, far_ref)
+    products(error_ref, own_ref, NEAR, near_ref)
 
 
 def dec_grad_kernel(groups, *refs):
@@ -224,20 +221,12 @@
         out_ref[0, 0, :, columns(owner(mask), width)] = transposed(error_ref[...], part).astype(BF16)
 
 
-def sum_kernel(groups, own_ref, arrived_ref, *outs):
-    width = outs[0].shape[1]
-    tok = own_ref.shape[0]
-    for i, row, mask in flat(groups):
-        here = columns(lax.rem(owner(mask), COUNT // 2), width)
-        total = own_ref[:, here] + arrived_ref[:, here].astype(F32)
-        outs[i][row * tok : (row + 1) * tok, :] = total.astype(outs[i].dtype)
-
-
-def add_kernel(kept_ref, arrived_ref, *outs):
-    tok = outs[0].shape[0]
-    for row, out_ref in enumerate(outs):
-        here = slice(row * tok, (row + 1) * tok)
-        out_ref[...] = (kept_ref[here, :] + arrived_ref[here, :].astype(F32)).astype(out_ref.dtype)
+def add_kernel(own_ref, arrived_ref, *outs):
+    first = 0
+    for out_ref in outs:
+        here = slice(first, first + out_ref.shape[0])
+        out_ref[...] = (own_ref[here, :] + arrived_ref[here, :].astype(F32)).astype(out_ref.dtype)
+        first += out_ref.shape[0]
 
 
 def enc_grad_kernel(*refs):
@@ -263,8 +252,11 @@
     features = dec_w.shape[3]
     scale = tok ** (-0.5)
     matmul = 2 * tok * width * features
-    half = (tok, features // 2)
     struct = jax.ShapeDtypeStruct
+
+    def stack(masks, kind):
+        return struct((len(masks) * tok, own_features), kind)
+
 
     first, last = ring_gather(inputs[0])
     inputs_of = [part for offset in OFFSETS for part in (first[offset], last[offset])]
@@ -274,30 +266,21 @@
         pre_kernel,
         name="pre",
         out_shape=(struct((tok, own_features), BF16), struct((tok, own_features), F32)),
-        in_specs=[*vmem(2 * count), pl.BlockSpec(memory_space=pltpu.HBM), *vmem(1)],
+        in_specs=[*vmem(2 * count), *[pl.BlockSpec(memory_space=pltpu.HBM)] * 2],
         out_specs=tuple(vmem(2)),
-        scratch_shapes=[pltpu.VMEM((count, own_features, width), BF16), pltpu.SemaphoreType.DMA((count,))],
+        scratch_shapes=[
+            pltpu.VMEM((count, own_features, width), BF16),
+            pltpu.VMEM(enc_b.shape, F32),
+            pltpu.SemaphoreType.DMA((count + 1,)),
+        ],
         compiler_params=params(20),
         cost_estimate=cost(2 * tok * own_features * model, 2 * own_features * model),
-    )(*inputs_of, enc_weights, enc_b)
-
-    near_line = exchanged(codes, 2)
-    across = exchanged(codes, 1)
-    far_line = exchanged(codes, 6)
-    farther_line = exchanged(codes, 4)
-    near_across = exchanged(codes, 3)
-    near_three = packed((across, near_line, near_across))
-    previous_codes = from_behind(codes, "section", 1)
-    previous_near = from_behind(near_three, "section", 1)
-    far_pair = packed((far_line, farther_line), (previous_codes, near_three))
+    )(*inputs_of, enc_weights, pltpu.with_memory_space_constraint(enc_b, pltpu.HBM))
+
+    far_pair = packed(exchanged(codes, 6), exchanged(codes, 4))
     far_across = exchanged(far_pair, 1)
-    own = [codes, near_three, far_pair, far_across]
-    previous = [
-        previous_codes,
-        previous_near,
-        from_behind(far_pair, "section", 1),
-        from_behind(far_across, "section", 1),
-    ]
+    own = [packed(codes, *[exchanged(codes, mask) for mask in (1, 2, 3)]), far_pair, far_across]
+    previous = [from_behind(part, "section", 1) for part in own]
 
     held = pltpu.VMEM((width, features), BF16)
     sems = [pltpu.SemaphoreType.DMA((tiles(width)[0],))]
@@ -315,7 +298,7 @@
     error, sent_far, next_weights = pl.pallas_call(
         functools.partial(recon_kernel, scale),
         name="recon",
-        out_shape=(struct((tok, width), BF16), struct(half, BF16), held),
+        out_shape=(struct((tok, width), BF16), stack(FAR + CROSSING, BF16), held),
         in_specs=[*vmem(len(previous) + 1), pl.BlockSpec(memory_space=pltpu.HBM), *vmem(2)],
         out_specs=tuple(vmem(3)),
         scratch_shapes=sems,
@@ -327,7 +310,7 @@
     sent_near, own_near, own_far = pl.pallas_call(
         own_grad_kernel,
         name="own_grad",
-        out_shape=(struct(half, BF16), struct(half, F32), struct(half, F32)),
+        out_shape=(stack(NEAR, BF16), stack(NEAR, F32), stack(FAR + CROSSING, F32)),
         in_specs=vmem(3),
         out_specs=tuple(vmem(3)),
         compiler_params=params(8),
@@ -356,32 +339,24 @@
 
     dec_grad = dec_grad_slot(0, BLOCKS, own)
 
-    def sums(groups, kinds, own_half, arrived):
+    def sums(outs, own_part, arrived):
         return pl.pallas_call(
-            functools.partial(sum_kernel, groups),
+            add_kernel,
             name="sum",
-            out_shape=tuple(struct((len(g) * tok, own_features), kind) for g, kind in zip(groups, kinds)),
+            out_shape=tuple(stack(masks, kind) for masks, kind in outs),
             in_specs=vmem(2),
-            out_specs=tuple(vmem(len(groups))),
+            out_specs=tuple(vmem(len(outs))),
             compiler_params=params(2),
             cost_estimate=cost(tok * features, 2 * MIB),
-        )(own_half, arrived)
-
-    kept, crossing = sums(((6, 4), (7, 5)), (F32, BF16), own_far, arrived_far)
-    lines = pl.pallas_call(
-        add_kernel,
-        name="add",
-        out_shape=(struct((tok, own_features), BF16),) * 2,
-        in_specs=vmem(2),
-        out_specs=tuple(vmem(2)),
-        compiler_params=params(2),
-        cost_estimate=cost(tok * own_features, MIB),
-    )(kept, exchanged(crossing, 1))
-    near_sums = sums(((0,), (1,), (2,), (3,)), (F32, BF16, BF16, BF16), own_near, arrived_near)
+        )(own_part, arrived)
+
+    kept, crossing = sums(((FAR, F32), (CROSSING, BF16)), own_far, arrived_far)
+    lines = sums([((mask,), BF16) for mask in FAR], kept, exchanged(crossing, 1))
+    near = sums([((mask,), BF16 if mask else F32) for mask in NEAR], own_near, arrived_near)
     grads = [
-        near_sums[0],
-        *[exchanged(near_sums[mask], mask) for mask in (1, 2, 3)],
-        *[exchanged(line, mask) for mask, line in zip((6, 4), lines)],
+        near[0],
+        *[exchanged(near[mask], mask) for mask in NEAR[1:]],
+        *[exchanged(line, mask) for mask, line in zip(FAR, lines)],
     ]
     held_grad = pltpu.with_memory_space_constraint(dec_grad, pltpu.HBM)
     dec_grad = dec_grad_slot(1, BLOCKS, previous, held_grad)

time: 110 us -> 106 us (0.964)
  starting transfers between devices: 49.6 us -> 42.1 us
  waiting for transfers between devices: 19 us -> 26.1 us
  Pallas kernels: 38.5 us -> 36.1 us
    ppermute x6 -> x5, starting transfers between devices: 22.4 us -> 16.2 us  [from_behind(): lax.ppermute(value, axis, [(source, source + steps) for source in range(i...]
    ppermute x12, waiting for transfers between devices: 0.03 us -> 4.3 us  [exchanged(): return lax.ppermute(value, 'feat', [(i, i ^ mask) for i in range(count)])]
    ppermute x6 -> x5, waiting for transfers between devices: 8.73 us -> 11.5 us  [from_behind(): lax.ppermute(value, axis, [(source, source + steps) for source in range(i...]
    pallas_call x6, Pallas kernels: 4.15 us -> 2.12 us  [the longest x1 1.85 us: on_device(): pl.pallas_call(own_grad_kernel, name='own_grad', out_shape=(stack(NEAR, B...]
    ppermute x12, starting transfers between devices: 15.7 us -> 14.4 us  [exchanged(): return lax.ppermute(value, 'feat', [(i, i ^ mask) for i in range(count)])]
  transfers between devices with their start and end apart: 32 -> 31, of which waited for: 12 -> 16; matrix products, arithmetic and copies ran while one was open for 0% -> 0% of each run, Pallas kernels for 19% -> 17%
where the time goes in v4:
time: 106 us
  starting transfers between devices  42.1 us (40%)
  Pallas kernels  36.1 us (34%)
  waiting for transfers between devices  26.1 us (25%)
    ppermute x5, starting transfers between devices, from_behind(): lax.ppermute(value, axis, [(source, source + steps) for source in range(i...  16.2 us
    ppermute x12, starting transfers between devices, exchanged(): return lax.ppermute(value, 'feat', [(i, i ^ mask) for i in range(count)])  14.4 us
    ppermute x14, starting transfers between devices, passed_on(): lax.ppermute(value, 'feat', [(order[p], order[(p + by) % count]) for p in...  11.5 us
    ppermute x5, waiting for transfers between devices, from_behind(): lax.ppermute(value, axis, [(source, source + steps) for source in range(i...  11.5 us
    ppermute x14, waiting for transfers between devices, passed_on(): lax.ppermute(value, 'feat', [(order[p], order[(p + by) % count]) for p in...  10.3 us
    pallas_call x2, Pallas kernels, dec_grad_slot(): pl.pallas_call(functools.partial(dec_grad_kernel, groups), name='dec_grad...  9.81 us
    pallas_call x1, Pallas kernels, on_device(): pl.pallas_call(functools.partial(recon_kernel, scale), name='recon', out_...  7.4 us
    pallas_call x1, Pallas kernels, on_device(): pl.pallas_call(own_recon_kernel, name='own_recon', out_shape=(struct((wid...  6.57 us
  transfers between devices with their start and end apart: 31, of which 16 were waited for; matrix products, arithmetic and copies ran while one was open for 0% of the time, Pallas kernels for 17%

profile of v4, /device:TPU:1, one launch (start us, length us, event | category | flops | bytes accessed | tf_op | source)
XLA Modules:
  0.0 106.1 jit_solution(13849104459234393479)
XLA Ops:
  0.6 1.0 slice_bitcast_fusion
  1.6 2.1 %collective-permute-start.3 = (bf16[64,1024]{1,0:T(8,128)(2,1)S(1)}, bf16[64,1024]{1,0:T(8,128)(2,1)S(1)}, u32[]{:S(2)}, u32[]{:S(2)}) collective-permute-start(bf16[64,1024]{1,0:T(8,128)(2,1)S(1)} %get-tuple-element.38.refs_1_.refs_7_), channel_id=1, source_target_pairs={{0,1},{2,0},{4,2},{6,4},{7,6},{5,7},{3,5},{1,3},{8,9},{10,8},{12,1... | collective-permute-start | bytes 393224 | tf_op jit(solution)/shard_map/ppermute | solution.py:49
  3.9 1.4 %collective-permute-start.1 = (bf16[64,1024]{1,0:T(8,128)(2,1)S(1)}, bf16[64,1024]{1,0:T(8,128)(2,1)S(1)}, u32[]{:S(2)}, u32[]{:S(2)}) collective-permute-start(bf16[64,1024]{1,0:T(8,128)(2,1)S(1)} %get-tuple-element.38.refs_1_.refs_7_), channel_id=1, source_target_pairs={{0,2},{2,4},{4,6},{6,7},{7,5},{5,3},{3,1},{1,0},{8,10},{10,12},{12... | collective-permute-start | bytes 393224 | tf_op jit(solution)/shard_map/ppermute | solution.py:49
  5.3 1.7 %collective-permute-done.3.refs_5_.refs_11_ = bf16[64,1024]{1,0:T(8,128)(2,1)S(1)} collective-permute-done((bf16[64,1024]{1,0:T(8,128)(2,1)S(1)}, bf16[64,1024]{1,0:T(8,128)(2,1)S(1)}, u32[]{:S(2)}, u32[]{:S(2)}) %collective-permute-start.3) | collective-permute-done | bytes 131104 | tf_op jit(solution)/shard_map/ppermute | solution.py:49
  7.0 1.1 %collective-permute-start.7 = (bf16[64,1024]{1,0:T(8,128)(2,1)S(1)}, bf16[64,1024]{1,0:T(8,128)(2,1)S(1)}, u32[]{:S(2)}, u32[]{:S(2)}) collective-permute-start(bf16[64,1024]{1,0:T(8,128)(2,1)S(1)} %collective-permute-done.3.refs_5_.refs_11_), channel_id=1, source_target_pairs={{0,1},{2,0},{4,2},{6,4},{7,6},{5,7},{3,5},{1,3},{8,9},{10,8},{12,1... | collective-permute-start | bytes 393224 | tf_op jit(solution)/shard_map/ppermute | solution.py:49
  8.1 0.4 collective-permute-start.4
  8.5 2.1 %collective-permute-done.1.refs_3_.refs_9_ = bf16[64,1024]{1,0:T(8,128)(2,1)S(1)} collective-permute-done((bf16[64,1024]{1,0:T(8,128)(2,1)S(1)}, bf16[64,1024]{1,0:T(8,128)(2,1)S(1)}, u32[]{:S(2)}, u32[]{:S(2)}) %collective-permute-start.1) | collective-permute-done | bytes 131104 | tf_op jit(solution)/shard_map/ppermute | solution.py:49
  10.6 0.4 collective-permute-start.5
  11.0 1.0 collective-permute-start.6
  12.3 1.2 %collective-permute-start.11 = (bf16[64,1024]{1,0:T(8,128)(2,1)S(1)}, bf16[64,1024]{1,0:T(8,128)(2,1)S(1)}, u32[]{:S(2)}, u32[]{:S(2)}) collective-permute-start(bf16[64,1024]{1,0:T(8,128)(2,1)S(1)} %collective-permute-done.7.refs_9_.refs_15_), channel_id=1, source_target_pairs={{0,1},{2,0},{4,2},{6,4},{7,6},{5,7},{3,5},{1,3},{8,9},{10,8},{12,1... | collective-permute-start | bytes 393224 | tf_op jit(solution)/shard_map/ppermute | solution.py:49
  13.8 1.6 %collective-permute-done.5.refs_7_.refs_13_ = bf16[64,1024]{1,0:T(8,128)(2,1)S(1)} collective-permute-done((bf16[64,1024]{1,0:T(8,128)(2,1)S(1)}, bf16[64,1024]{1,0:T(8,128)(2,1)S(1)}, u32[]{:S(2)}, u32[]{:S(2)}) %collective-permute-start.5) | collective-permute-done | bytes 131104 | tf_op jit(solution)/shard_map/ppermute | solution.py:49
  15.4 0.8 collective-permute-start.9
  16.2 0.7 collective-permute-start.10
  16.9 1.3 %collective-permute-start.13 = (bf16[64,1024]{1,0:T(8,128)(2,1)S(1)}, bf16[64,1024]{1,0:T(8,128)(2,1)S(1)}, u32[]{:S(2)}, u32[]{:S(2)}) collective-permute-start(bf16[64,1024]{1,0:T(8,128)(2,1)S(1)} %collective-permute-done.11.refs_13_.refs_19_), channel_id=1, source_target_pairs={{0,1},{2,0},{4,2},{6,4},{7,6},{5,7},{3,5},{1,3},{8,9},{10,8},{12,1... | collective-permute-start | bytes 393224 | tf_op jit(solution)/shard_map/ppermute | solution.py:49
  18.2 0.4 collective-permute-done.8.refs_10_.refs_16_
  18.6 0.6 collective-permute-start.12
  19.2 1.2 %collective-permute-done.9.refs_11_.refs_17_ = bf16[64,1024]{1,0:T(8,128)(2,1)S(1)} collective-permute-done((bf16[64,1024]{1,0:T(8,128)(2,1)S(1)}, bf16[64,1024]{1,0:T(8,128)(2,1)S(1)}, u32[]{:S(2)}, u32[]{:S(2)}) %collective-permute-start.9) | collective-permute-done | bytes 131104 | tf_op jit(solution)/shard_map/ppermute | solution.py:49
  20.5 1.2 %collective-permute-done.10.refs_12_.refs_18_ = bf16[64,1024]{1,0:T(8,128)(2,1)S(1)} collective-permute-done((bf16[64,1024]{1,0:T(8,128)(2,1)S(1)}, bf16[64,1024]{1,0:T(8,128)(2,1)S(1)}, u32[]{:S(2)}, u32[]{:S(2)}) %collective-permute-start.10) | collective-permute-done | bytes 131104 | tf_op jit(solution)/shard_map/ppermute | solution.py:49
  21.7 1.1 %collective-permute-done.13.refs_15_.refs_21_ = bf16[64,1024]{1,0:T(8,128)(2,1)S(1)} collective-permute-done((bf16[64,1024]{1,0:T(8,128)(2,1)S(1)}, bf16[64,1024]{1,0:T(8,128)(2,1)S(1)}, u32[]{:S(2)}, u32[]{:S(2)}) %collective-permute-start.13) | collective-permute-done | bytes 131104 | tf_op jit(solution)/shard_map/ppermute | solution.py:49
  22.8 0.6 collective-permute-done.12.refs_14_.refs_20_
  23.4 5.0 %pre.1 = (bf16[128,512]{1,0:T(8,128)(2,1)S(1)}, f32[128,512]{1,0:T(8,128)S(1)}) custom-call(bf16[64,1024]{1,0:T(8,128)(2,1)S(1)} %get-tuple-element.39.refs_0_.refs_6_, bf16[64,1024]{1,0:T(8,128)(2,1)S(1)} %get-tuple-element.38.refs_1_.refs_7_, bf16[64,1024]{1,0:T(8,128)(2,1)S(1)} %collective-permute-done.refs_2_.refs_8_, ...), custom_call_target="tpu_custom_call" | custom-call | flops 1073741824 | bytes 8388608 | tf_op jit(solution)/shard_map/pre/pallas_call | solution.py:265
  28.4 1.9 %collective-permute-start.19 = (bf16[128,512]{1,0:T(8,128)(2,1)S(1)}, bf16[128,512]{1,0:T(8,128)(2,1)S(1)}, u32[]{:S(2)}, u32[]{:S(2)}) collective-permute-start(bf16[128,512]{1,0:T(8,128)(2,1)S(1)} %get-tuple-element.20.refs_0_), channel_id=1, source_target_pairs={{0,4},{1,5},{2,6},{3,7},{4,0},{5,1},{6,2},{7,3},{8,12},{9,13},{10,... | collective-permute-start | bytes 393224 | tf_op jit(solution)/shard_map/ppermute | solution.py:39
  30.3 1.1 %collective-permute-start.18 = (bf16[128,512]{1,0:T(8,128)(2,1)S(1)}, bf16[128,512]{1,0:T(8,128)(2,1)S(1)}, u32[]{:S(2)}, u32[]{:S(2)}) collective-permute-start(bf16[128,512]{1,0:T(8,128)(2,1)S(1)} %get-tuple-element.20.refs_0_), channel_id=1, source_target_pairs={{0,6},{1,7},{2,4},{3,5},{4,2},{5,3},{6,0},{7,1},{8,14},{9,15},{10,... | collective-permute-start | bytes 393224 | tf_op jit(solution)/shard_map/ppermute | solution.py:39
  31.4 1.2 %collective-permute-start.16 = (bf16[128,512]{1,0:T(8,128)(2,1)S(1)}, bf16[128,512]{1,0:T(8,128)(2,1)S(1)}, u32[]{:S(2)}, u32[]{:S(2)}) collective-permute-start(bf16[128,512]{1,0:T(8,128)(2,1)S(1)} %get-tuple-element.20.refs_0_), channel_id=1, source_target_pairs={{0,3},{1,2},{2,1},{3,0},{4,7},{5,6},{6,5},{7,4},{8,11},{9,10},{10,... | collective-permute-start | bytes 393224 | tf_op jit(solution)/shard_map/ppermute | solution.py:39
  32.6 1.8 %collective-permute-start.15 = (bf16[128,512]{1,0:T(8,128)(2,1)S(1)}, bf16[128,512]{1,0:T(8,128)(2,1)S(1)}, u32[]{:S(2)}, u32[]{:S(2)}) collective-permute-start(bf16[128,512]{1,0:T(8,128)(2,1)S(1)} %get-tuple-element.20.refs_0_), channel_id=1, source_target_pairs={{0,2},{1,3},{2,0},{3,1},{4,6},{5,7},{6,4},{7,5},{8,10},{9,11},{10,... | collective-permute-start | bytes 393224 | tf_op jit(solution)/shard_map/ppermute | solution.py:39
  34.6 1.5 %collective-permute-done.18.refs_0_ = bf16[128,512]{1,0:T(8,128)(2,1)S(1)} collective-permute-done((bf16[128,512]{1,0:T(8,128)(2,1)S(1)}, bf16[128,512]{1,0:T(8,128)(2,1)S(1)}, u32[]{:S(2)}, u32[]{:S(2)}) %collective-permute-start.18) | collective-permute-done | bytes 131104 | tf_op jit(solution)/shard_map/ppermute | solution.py:39
  36.1 1.8 %collective-permute-start.21 = (bf16[256,512]{1,0:T(8,128)(2,1)S(1)}, bf16[256,512]{1,0:T(8,128)(2,1)S(1)}, u32[]{:S(2)}, u32[]{:S(2)}) collective-permute-start(bf16[256,512]{1,0:T(8,128)(2,1)S(1)} %pack.3.refs_1_.refs_2_), channel_id=1, source_target_pairs={{0,1},{1,0},{2,3},{3,2},{4,5},{5,4},{6,7},{7,6},{8,9},{9,8},{10,11... | collective-permute-start | bytes 786440 | tf_op jit(solution)/shard_map/ppermute | solution.py:39
  38.1 2.3 %collective-permute-done.15.refs_2_ = bf16[128,512]{1,0:T(8,128)(2,1)S(1)} collective-permute-done((bf16[128,512]{1,0:T(8,128)(2,1)S(1)}, bf16[128,512]{1,0:T(8,128)(2,1)S(1)}, u32[]{:S(2)}, u32[]{:S(2)}) %collective-permute-start.15) | collective-permute-done | bytes 131104 | tf_op jit(solution)/shard_map/ppermute | solution.py:39
  40.5 8.4 %collective-permute-start.17 = (bf16[512,512]{1,0:T(8,128)(2,1)S(1)}, bf16[512,512]{1,0:T(8,128)(2,1)S(1)}, u32[]{:S(2)}, u32[]{:S(2)}) collective-permute-start(bf16[512,512]{1,0:T(8,128)(2,1)S(1)} %pack.2.refs_0_.refs_1_), channel_id=1, source_target_pairs={{0,8},{8,16},{16,24},{1,9},{9,17},{17,25},{2,10},{10,18},{18,26},{... | collective-permute-start | bytes 1572872 | tf_op jit(solution)/shard_map/ppermute | solution.py:26
  48.8 1.9 %collective-permute-start.20 = (bf16[256,512]{1,0:T(8,128)(2,1)S(1)}, bf16[256,512]{1,0:T(8,128)(2,1)S(1)}, u32[]{:S(2)}, u32[]{:S(2)}) collective-permute-start(bf16[256,512]{1,0:T(8,128)(2,1)S(1)} %pack.3.refs_1_.refs_2_), channel_id=1, source_target_pairs={{0,8},{8,16},{16,24},{1,9},{9,17},{17,25},{2,10},{10,18},{18,26},{... | collective-permute-start | bytes 786440 | tf_op jit(solution)/shard_map/ppermute | solution.py:26
  50.8 1.9 %collective-permute-start.22 = (bf16[256,512]{1,0:T(8,128)(2,1)S(1)}, bf16[256,512]{1,0:T(8,128)(2,1)S(1)}, u32[]{:S(2)}, u32[]{:S(2)}) collective-permute-start(bf16[256,512]{1,0:T(8,128)(2,1)S(1)} %collective-permute-done.21.refs_2_.refs_3_), channel_id=1, source_target_pairs={{0,8},{8,16},{16,24},{1,9},{9,17},{17,25},{2,10},{10,18},{18,26},{... | collective-permute-start | bytes 786440 | tf_op jit(solution)/shard_map/ppermute | solution.py:26
  52.7 6.6 %own_recon.1 = (f32[1024,128]{1,0:T(8,128)S(1)}, bf16[1024,4096]{1,0:T(8,128)(2,1)S(1)}) custom-call(bf16[512,512]{1,0:T(8,128)(2,1)S(1)} %pack.2.refs_0_.refs_1_, bf16[256,512]{1,0:T(8,128)(2,1)S(1)} %pack.3.refs_1_.refs_2_, bf16[256,512]{1,0:T(8,128)(2,1)S(1)} %collective-permute-done.21.refs_2_.refs_3_, bf16[2,1024,4096]{2,1,0:T(8,128)(2,1)} %bitcast.8), custom_call_target="tpu_custom_call" | custom-call | flops 1073741824 | bytes 4194304 | tf_op jit(solution)/shard_map/own_recon/pallas_call | solution.py:287
  59.3 1.2 %collective-permute-done.22.refs_2_.refs_3_ = bf16[256,512]{1,0:T(8,128)(2,1)S(1)} collective-permute-done((bf16[256,512]{1,0:T(8,128)(2,1)S(1)}, bf16[256,512]{1,0:T(8,128)(2,1)S(1)}, u32[]{:S(2)}, u32[]{:S(2)}) %collective-permute-start.22) | collective-permute-done | bytes 262176 | tf_op jit(solution)/shard_map/ppermute | solution.py:26
  60.6 7.4 %recon.1 = (bf16[128,1024]{1,0:T(8,128)(2,1)S(1)}, bf16[512,512]{1,0:T(8,128)(2,1)S(1)}, bf16[1024,4096]{1,0:T(8,128)(2,1)S(1)}) custom-call(bf16[512,512]{1,0:T(8,128)(2,1)S(1)} %collective-permute-done.17.refs_0_.refs_1_, bf16[256,512]{1,0:T(8,128)(2,1)S(1)} %collective-permute-done.20.refs_1_.refs_2_, ...), custom_call_target="tpu_custom_call" | custom-call | flops 2147483648 | bytes 4194304 | tf_op jit(solution)/shard_map/recon/pallas_call | solution.py:298
  68.0 1.9 %collective-permute-start.27 = (bf16[512,512]{1,0:T(8,128)(2,1)S(1)}, bf16[512,512]{1,0:T(8,128)(2,1)S(1)}, u32[]{:S(2)}, u32[]{:S(2)}) collective-permute-start(bf16[512,512]{1,0:T(8,128)(2,1)S(1)} %get-tuple-element.32), channel_id=1, source_target_pairs={{8,0},{16,8},{24,16},{9,1},{17,9},{25,17},{10,2},{18,10},{26,18},{... | collective-permute-start | bytes 1572872 | tf_op jit(solution)/shard_map/ppermute | solution.py:26
  69.9 1.8 %own_grad.1 = (bf16[512,512]{1,0:T(8,128)(2,1)S(1)}, f32[512,512]{1,0:T(8,128)S(1)}, f32[512,512]{1,0:T(8,128)S(1)}) custom-call(bf16[128,1024]{1,0:T(8,128)(2,1)S(1)} %get-tuple-element.22.error_ref.refs_0_, bf16[1024,4096]{1,0:T(8,128)(2,1)S(1)} %get-tuple-element.23.own_ref, bf16[1024,4096]{1,0:T(8,128)(2,1)S(1)} %get-tuple-element.24.next_ref), custom_call_target="tpu_custom_call" | custom-call | flops 1610612736 | bytes 6291456 | tf_op jit(solution)/shard_map/own_grad/pallas_call | solution.py:310
  71.8 2.1 %collective-permute-start.23 = (bf16[512,512]{1,0:T(8,128)(2,1)S(1)}, bf16[512,512]{1,0:T(8,128)(2,1)S(1)}, u32[]{:S(2)}, u32[]{:S(2)}) collective-permute-start(bf16[512,512]{1,0:T(8,128)(2,1)S(1)} %get-tuple-element.26), channel_id=1, source_target_pairs={{8,0},{16,8},{24,16},{9,1},{17,9},{25,17},{10,2},{18,10},{26,18},{... | collective-permute-start | bytes 1572872 | tf_op jit(solution)/shard_map/ppermute | solution.py:26
  73.9 5.6 %collective-permute-done.27.arrived_ref = bf16[512,512]{1,0:T(8,128)(2,1)S(1)} collective-permute-done((bf16[512,512]{1,0:T(8,128)(2,1)S(1)}, bf16[512,512]{1,0:T(8,128)(2,1)S(1)}, u32[]{:S(2)}, u32[]{:S(2)}) %collective-permute-start.27) | collective-permute-done | bytes 524320 | tf_op jit(solution)/shard_map/ppermute | solution.py:26
  79.6 0.9 collective-permute-start.28
  80.5 4.6 %collective-permute-done.23.arrived_ref = bf16[512,512]{1,0:T(8,128)(2,1)S(1)} collective-permute-done((bf16[512,512]{1,0:T(8,128)(2,1)S(1)}, bf16[512,512]{1,0:T(8,128)(2,1)S(1)}, u32[]{:S(2)}, u32[]{:S(2)}) %collective-permute-start.23) | collective-permute-done | bytes 524320 | tf_op jit(solution)/shard_map/ppermute | solution.py:26
  85.2 0.6 collective-permute-start.24
  85.8 0.9 collective-permute-start.25
  86.7 1.2 %collective-permute-start.26 = (bf16[128,512]{1,0:T(8,128)(2,1)S(1)}, bf16[128,512]{1,0:T(8,128)(2,1)S(1)}, u32[]{:S(2)}, u32[]{:S(2)}) collective-permute-start(bf16[128,512]{1,0:T(8,128)(2,1)S(1)} %get-tuple-element.30), channel_id=1, source_target_pairs={{0,3},{1,2},{2,1},{3,0},{4,7},{5,6},{6,5},{7,4},{8,11},{9,10},{10,... | collective-permute-start | bytes 393224 | tf_op jit(solution)/shard_map/ppermute | solution.py:39
  88.0 2.7 %collective-permute-start.29 = (bf16[128,512]{1,0:T(8,128)(2,1)S(1)}, bf16[128,512]{1,0:T(8,128)(2,1)S(1)}, u32[]{:S(2)}, u32[]{:S(2)}) collective-permute-start(bf16[128,512]{1,0:T(8,128)(2,1)S(1)} %get-tuple-element.35), channel_id=1, source_target_pairs={{0,6},{1,7},{2,4},{3,5},{4,2},{5,3},{6,0},{7,1},{8,14},{9,15},{10,... | collective-permute-start | bytes 393224 | tf_op jit(solution)/shard_map/ppermute | solution.py:39
  90.7 0.4 collective-permute-start.30
  91.0 4.9 %dec_grad.2.refs_4_ = bf16[1,2,1024,4096]{3,2,1,0:T(8,128)(2,1)} custom-call(bf16[128,1024]{1,0:T(8,128)(2,1)S(1)} %get-tuple-element.22.error_ref.refs_0_, bf16[512,512]{1,0:T(8,128)(2,1)S(1)} %pack.2.refs_0_.refs_1_, bf16[256,512]{1,0:T(8,128)(2,1)S(1)} %pack.3.refs_1_.refs_2_, bf16[256,512]{1,0:T(8,128)(2,1)S(1)} %collective-permute-done.21.refs_2_.refs_3_), custom_call_target="tpu_custom_call" | custom-call | flops 1073741824 | bytes 8388608 | tf_op jit(solution)/shard_map/dec_grad/pallas_call | solution.py:324
  95.9 4.9 %dec_grad.3 = bf16[1,2,1024,4096]{3,2,1,0:T(8,128)(2,1)} custom-call(bf16[128,1024]{1,0:T(8,128)(2,1)S(1)} %get-tuple-element.22.error_ref.refs_0_, bf16[512,512]{1,0:T(8,128)(2,1)S(1)} %collective-permute-done.17.refs_0_.refs_1_, bf16[256,512]{1,0:T(8,128)(2,1)S(1)} %collective-permute-done.20.refs_1_.refs_2_, ...), custom_call_target="tpu_custom_call", output_to_operand_aliasing={{}: (4, {})} | custom-call | flops 1073741824 | bytes 8388608 | tf_op jit(solution)/shard_map/dec_grad/pallas_call | solution.py:324
  100.9 5.2 %enc_grad.1 = bf16[1,512,8192]{2,1,0:T(8,128)(2,1)} custom-call(f32[128,512]{1,0:T(8,128)S(1)} %get-tuple-element.27.refs_0_, bf16[128,512]{1,0:T(8,128)(2,1)S(1)} %collective-permute-done.24.refs_1_, bf16[128,512]{1,0:T(8,128)(2,1)S(1)} %collective-permute-done.25.refs_2_, bf16[128,512]{1,0:T(8,128)(2,1)S(1)} %collective-permute-done.26.refs_3_, ...), custom_call_target="tpu_custom_call" | custom-call | flops 1073741824 | bytes 8388608 | tf_op jit(solution)/shard_map/enc_grad/pallas_call | solution.py:364
  (31 shorter events, 1.6 us)
Async XLA Ops:
  1.6 5.4 %collective-permute-start.3 = (bf16[64,1024]{1,0:T(8,128)(2,1)S(1)}, bf16[64,1024]{1,0:T(8,128)(2,1)S(1)}, u32[]{:S(2)}, u32[]{:S(2)}) collective-permute-start(bf16[64,1024]{1,0:T(8,128)(2,1)S(1)} %get-tuple-element.38.refs_1_.refs_7_), channel_id=1, source_target_pairs={{0,1},{2,0},{4,2},{6,4},{7,6},{5,7},{3,5},{1,3},{8,9},{10,8},{12,1... | collective-permute-start | bytes 393224 | tf_op jit(solution)/shard_map/ppermute | solution.py:49
  3.7 4.4 %collective-permute-start = (bf16[64,1024]{1,0:T(8,128)(2,1)S(1)}, bf16[64,1024]{1,0:T(8,128)(2,1)S(1)}, u32[]{:S(2)}, u32[]{:S(2)}) collective-permute-start(bf16[64,1024]{1,0:T(8,128)(2,1)S(1)} %get-tuple-element.39.refs_0_.refs_6_), channel_id=1, source_target_pairs={{0,2},{2,4},{4,6},{6,7},{7,5},{5,3},{3,1},{1,0},{8,10},{10,12},{12... | collective-permute-start | bytes 393224 | tf_op jit(solution)/shard_map/ppermute | solution.py:49
  3.9 6.7 %collective-permute-start.1 = (bf16[64,1024]{1,0:T(8,128)(2,1)S(1)}, bf16[64,1024]{1,0:T(8,128)(2,1)S(1)}, u32[]{:S(2)}, u32[]{:S(2)}) collective-permute-start(bf16[64,1024]{1,0:T(8,128)(2,1)S(1)} %get-tuple-element.38.refs_1_.refs_7_), channel_id=1, source_target_pairs={{0,2},{2,4},{4,6},{6,7},{7,5},{5,3},{3,1},{1,0},{8,10},{10,12},{12... | collective-permute-start | bytes 393224 | tf_op jit(solution)/shard_map/ppermute | solution.py:49
  5.3 5.8 %collective-permute-start.2 = (bf16[64,1024]{1,0:T(8,128)(2,1)S(1)}, bf16[64,1024]{1,0:T(8,128)(2,1)S(1)}, u32[]{:S(2)}, u32[]{:S(2)}) collective-permute-start(bf16[64,1024]{1,0:T(8,128)(2,1)S(1)} %get-tuple-element.39.refs_0_.refs_6_), channel_id=1, source_target_pairs={{0,1},{2,0},{4,2},{6,4},{7,6},{5,7},{3,5},{1,3},{8,9},{10,8},{12,1... | collective-permute-start | bytes 393224 | tf_op jit(solution)/shard_map/ppermute | solution.py:49
  7.0 5.3 %collective-permute-start.7 = (bf16[64,1024]{1,0:T(8,128)(2,1)S(1)}, bf16[64,1024]{1,0:T(8,128)(2,1)S(1)}, u32[]{:S(2)}, u32[]{:S(2)}) collective-permute-start(bf16[64,1024]{1,0:T(8,128)(2,1)S(1)} %collective-permute-done.3.refs_5_.refs_11_), channel_id=1, source_target_pairs={{0,1},{2,0},{4,2},{6,4},{7,6},{5,7},{3,5},{1,3},{8,9},{10,8},{12,1... | collective-permute-start | bytes 393224 | tf_op jit(solution)/shard_map/ppermute | solution.py:49
  8.1 5.4 %collective-permute-start.4 = (bf16[64,1024]{1,0:T(8,128)(2,1)S(1)}, bf16[64,1024]{1,0:T(8,128)(2,1)S(1)}, u32[]{:S(2)}, u32[]{:S(2)}) collective-permute-start(bf16[64,1024]{1,0:T(8,128)(2,1)S(1)} %collective-permute-done.refs_2_.refs_8_), channel_id=1, source_target_pairs={{0,2},{2,4},{4,6},{6,7},{7,5},{5,3},{3,1},{1,0},{8,10},{10,12},{12... | collective-permute-start | bytes 393224 | tf_op jit(solution)/shard_map/ppermute | solution.py:49
  10.6 4.8 %collective-permute-start.5 = (bf16[64,1024]{1,0:T(8,128)(2,1)S(1)}, bf16[64,1024]{1,0:T(8,128)(2,1)S(1)}, u32[]{:S(2)}, u32[]{:S(2)}) collective-permute-start(bf16[64,1024]{1,0:T(8,128)(2,1)S(1)} %collective-permute-done.1.refs_3_.refs_9_), channel_id=1, source_target_pairs={{0,2},{2,4},{4,6},{6,7},{7,5},{5,3},{3,1},{1,0},{8,10},{10,12},{12... | collective-permute-start | bytes 393224 | tf_op jit(solution)/shard_map/ppermute | solution.py:49
  11.0 5.2 %collective-permute-start.6 = (bf16[64,1024]{1,0:T(8,128)(2,1)S(1)}, bf16[64,1024]{1,0:T(8,128)(2,1)S(1)}, u32[]{:S(2)}, u32[]{:S(2)}) collective-permute-start(bf16[64,1024]{1,0:T(8,128)(2,1)S(1)} %collective-permute-done.2.refs_4_.refs_10_), channel_id=1, source_target_pairs={{0,1},{2,0},{4,2},{6,4},{7,6},{5,7},{3,5},{1,3},{8,9},{10,8},{12,1... | collective-permute-start | bytes 393224 | tf_op jit(solution)/shard_map/ppermute | solution.py:49
  12.3 4.6 %collective-permute-start.11 = (bf16[64,1024]{1,0:T(8,128)(2,1)S(1)}, bf16[64,1024]{1,0:T(8,128)(2,1)S(1)}, u32[]{:S(2)}, u32[]{:S(2)}) collective-permute-start(bf16[64,1024]{1,0:T(8,128)(2,1)S(1)} %collective-permute-done.7.refs_9_.refs_15_), channel_id=1, source_target_pairs={{0,1},{2,0},{4,2},{6,4},{7,6},{5,7},{3,5},{1,3},{8,9},{10,8},{12,1... | collective-permute-start | bytes 393224 | tf_op jit(solution)/shard_map/ppermute | solution.py:49
  13.5 5.1 %collective-permute-start.8 = (bf16[64,1024]{1,0:T(8,128)(2,1)S(1)}, bf16[64,1024]{1,0:T(8,128)(2,1)S(1)}, u32[]{:S(2)}, u32[]{:S(2)}) collective-permute-start(bf16[64,1024]{1,0:T(8,128)(2,1)S(1)} %collective-permute-done.4.refs_6_.refs_12_), channel_id=1, source_target_pairs={{0,2},{2,4},{4,6},{6,7},{7,5},{5,3},{3,1},{1,0},{8,10},{10,12},{12... | collective-permute-start | bytes 393224 | tf_op jit(solution)/shard_map/ppermute | solution.py:49
  15.4 5.1 %collective-permute-start.9 = (bf16[64,1024]{1,0:T(8,128)(2,1)S(1)}, bf16[64,1024]{1,0:T(8,128)(2,1)S(1)}, u32[]{:S(2)}, u32[]{:S(2)}) collective-permute-start(bf16[64,1024]{1,0:T(8,128)(2,1)S(1)} %collective-permute-done.5.refs_7_.refs_13_), channel_id=1, source_target_pairs={{0,2},{2,4},{4,6},{6,7},{7,5},{5,3},{3,1},{1,0},{8,10},{10,12},{12... | collective-permute-start | bytes 393224 | tf_op jit(solution)/shard_map/ppermute | solution.py:49
  16.2 5.4 %collective-permute-start.10 = (bf16[64,1024]{1,0:T(8,128)(2,1)S(1)}, bf16[64,1024]{1,0:T(8,128)(2,1)S(1)}, u32[]{:S(2)}, u32[]{:S(2)}) collective-permute-start(bf16[64,1024]{1,0:T(8,128)(2,1)S(1)} %collective-permute-done.6.refs_8_.refs_14_), channel_id=1, source_target_pairs={{0,1},{2,0},{4,2},{6,4},{7,6},{5,7},{3,5},{1,3},{8,9},{10,8},{12,1... | collective-permute-start | bytes 393224 | tf_op jit(solution)/shard_map/ppermute | solution.py:49
  16.9 5.9 %collective-permute-start.13 = (bf16[64,1024]{1,0:T(8,128)(2,1)S(1)}, bf16[64,1024]{1,0:T(8,128)(2,1)S(1)}, u32[]{:S(2)}, u32[]{:S(2)}) collective-permute-start(bf16[64,1024]{1,0:T(8,128)(2,1)S(1)} %collective-permute-done.11.refs_13_.refs_19_), channel_id=1, source_target_pairs={{0,1},{2,0},{4,2},{6,4},{7,6},{5,7},{3,5},{1,3},{8,9},{10,8},{12,1... | collective-permute-start | bytes 393224 | tf_op jit(solution)/shard_map/ppermute | solution.py:49
  18.6 4.8 %collective-permute-start.12 = (bf16[64,1024]{1,0:T(8,128)(2,1)S(1)}, bf16[64,1024]{1,0:T(8,128)(2,1)S(1)}, u32[]{:S(2)}, u32[]{:S(2)}) collective-permute-start(bf16[64,1024]{1,0:T(8,128)(2,1)S(1)} %collective-permute-done.8.refs_10_.refs_16_), channel_id=1, source_target_pairs={{0,2},{2,4},{4,6},{6,7},{7,5},{5,3},{3,1},{1,0},{8,10},{10,12},{12... | collective-permute-start | bytes 393224 | tf_op jit(solution)/shard_map/ppermute | solution.py:49
  28.4 6.2 %collective-permute-start.19 = (bf16[128,512]{1,0:T(8,128)(2,1)S(1)}, bf16[128,512]{1,0:T(8,128)(2,1)S(1)}, u32[]{:S(2)}, u32[]{:S(2)}) collective-permute-start(bf16[128,512]{1,0:T(8,128)(2,1)S(1)} %get-tuple-element.20.refs_0_), channel_id=1, source_target_pairs={{0,4},{1,5},{2,6},{3,7},{4,0},{5,1},{6,2},{7,3},{8,12},{9,13},{10,... | collective-permute-start | bytes 393224 | tf_op jit(solution)/shard_map/ppermute | solution.py:39
  30.3 5.8 %collective-permute-start.18 = (bf16[128,512]{1,0:T(8,128)(2,1)S(1)}, bf16[128,512]{1,0:T(8,128)(2,1)S(1)}, u32[]{:S(2)}, u32[]{:S(2)}) collective-permute-start(bf16[128,512]{1,0:T(8,128)(2,1)S(1)} %get-tuple-element.20.refs_0_), channel_id=1, source_target_pairs={{0,6},{1,7},{2,4},{3,5},{4,2},{5,3},{6,0},{7,1},{8,14},{9,15},{10,... | collective-permute-start | bytes 393224 | tf_op jit(solution)/shard_map/ppermute | solution.py:39
  31.4 6.7 %collective-permute-start.16 = (bf16[128,512]{1,0:T(8,128)(2,1)S(1)}, bf16[128,512]{1,0:T(8,128)(2,1)S(1)}, u32[]{:S(2)}, u32[]{:S(2)}) collective-permute-start(bf16[128,512]{1,0:T(8,128)(2,1)S(1)} %get-tuple-element.20.refs_0_), channel_id=1, source_target_pairs={{0,3},{1,2},{2,1},{3,0},{4,7},{5,6},{6,5},{7,4},{8,11},{9,10},{10,... | collective-permute-start | bytes 393224 | tf_op jit(solution)/shard_map/ppermute | solution.py:39
  32.6 7.9 %collective-permute-start.15 = (bf16[128,512]{1,0:T(8,128)(2,1)S(1)}, bf16[128,512]{1,0:T(8,128)(2,1)S(1)}, u32[]{:S(2)}, u32[]{:S(2)}) collective-permute-start(bf16[128,512]{1,0:T(8,128)(2,1)S(1)} %get-tuple-element.20.refs_0_), channel_id=1, source_target_pairs={{0,2},{1,3},{2,0},{3,1},{4,6},{5,7},{6,4},{7,5},{8,10},{9,11},{10,... | collective-permute-start | bytes 393224 | tf_op jit(solution)/shard_map/ppermute | solution.py:39
  34.4 6.1 %collective-permute-start.14 = (bf16[128,512]{1,0:T(8,128)(2,1)S(1)}, bf16[128,512]{1,0:T(8,128)(2,1)S(1)}, u32[]{:S(2)}, u32[]{:S(2)}) collective-permute-start(bf16[128,512]{1,0:T(8,128)(2,1)S(1)} %get-tuple-element.20.refs_0_), channel_id=1, source_target_pairs={{0,1},{1,0},{2,3},{3,2},{4,5},{5,4},{6,7},{7,6},{8,9},{9,8},{10,11... | collective-permute-start | bytes 393224 | tf_op jit(solution)/shard_map/ppermute | solution.py:39
  36.1 14.6 %collective-permute-start.21 = (bf16[256,512]{1,0:T(8,128)(2,1)S(1)}, bf16[256,512]{1,0:T(8,128)(2,1)S(1)}, u32[]{:S(2)}, u32[]{:S(2)}) collective-permute-start(bf16[256,512]{1,0:T(8,128)(2,1)S(1)} %pack.3.refs_1_.refs_2_), channel_id=1, source_target_pairs={{0,1},{1,0},{2,3},{3,2},{4,5},{5,4},{6,7},{7,6},{8,9},{9,8},{10,11... | collective-permute-start | bytes 786440 | tf_op jit(solution)/shard_map/ppermute | solution.py:39
  40.5 18.9 %collective-permute-start.17 = (bf16[512,512]{1,0:T(8,128)(2,1)S(1)}, bf16[512,512]{1,0:T(8,128)(2,1)S(1)}, u32[]{:S(2)}, u32[]{:S(2)}) collective-permute-start(bf16[512,512]{1,0:T(8,128)(2,1)S(1)} %pack.2.refs_0_.refs_1_), channel_id=1, source_target_pairs={{0,8},{8,16},{16,24},{1,9},{9,17},{17,25},{2,10},{10,18},{18,26},{... | collective-permute-start | bytes 1572872 | tf_op jit(solution)/shard_map/ppermute | solution.py:26
  48.8 10.5 %collective-permute-start.20 = (bf16[256,512]{1,0:T(8,128)(2,1)S(1)}, bf16[256,512]{1,0:T(8,128)(2,1)S(1)}, u32[]{:S(2)}, u32[]{:S(2)}) collective-permute-start(bf16[256,512]{1,0:T(8,128)(2,1)S(1)} %pack.3.refs_1_.refs_2_), channel_id=1, source_target_pairs={{0,8},{8,16},{16,24},{1,9},{9,17},{17,25},{2,10},{10,18},{18,26},{... | collective-permute-start | bytes 786440 | tf_op jit(solution)/shard_map/ppermute | solution.py:26
  50.8 9.8 %collective-permute-start.22 = (bf16[256,512]{1,0:T(8,128)(2,1)S(1)}, bf16[256,512]{1,0:T(8,128)(2,1)S(1)}, u32[]{:S(2)}, u32[]{:S(2)}) collective-permute-start(bf16[256,512]{1,0:T(8,128)(2,1)S(1)} %collective-permute-done.21.refs_2_.refs_3_), channel_id=1, source_target_pairs={{0,8},{8,16},{16,24},{1,9},{9,17},{17,25},{2,10},{10,18},{18,26},{... | collective-permute-start | bytes 786440 | tf_op jit(solution)/shard_map/ppermute | solution.py:26
  52.7 7.9 %copy-start = (bf16[1,128,1024]{2,1,0:T(8,128)(2,1)S(1)}, bf16[1,128,1024]{2,1,0:T(8,128)(2,1)}, u32[]{:S(2)}) copy-start(bf16[1,128,1024]{2,1,0:T(8,128)(2,1)} %param.7) | copy-start | bytes 786436
  52.7 7.8 %copy-start.1 = (f32[1,1024]{1,0:T(1,128)S(1)}, f32[1,1024]{1,0:T(1,128)}, u32[]{:S(2)}) copy-start(f32[1,1024]{1,0:T(1,128)} %refs_5_.1) | copy-start | bytes 12292
  68.0 11.5 %collective-permute-start.27 = (bf16[512,512]{1,0:T(8,128)(2,1)S(1)}, bf16[512,512]{1,0:T(8,128)(2,1)S(1)}, u32[]{:S(2)}, u32[]{:S(2)}) collective-permute-start(bf16[512,512]{1,0:T(8,128)(2,1)S(1)} %get-tuple-element.32), channel_id=1, source_target_pairs={{8,0},{16,8},{24,16},{9,1},{17,9},{25,17},{10,2},{18,10},{26,18},{... | collective-permute-start | bytes 1572872 | tf_op jit(solution)/shard_map/ppermute | solution.py:26
  71.8 13.4 %collective-permute-start.23 = (bf16[512,512]{1,0:T(8,128)(2,1)S(1)}, bf16[512,512]{1,0:T(8,128)(2,1)S(1)}, u32[]{:S(2)}, u32[]{:S(2)}) collective-permute-start(bf16[512,512]{1,0:T(8,128)(2,1)S(1)} %get-tuple-element.26), channel_id=1, source_target_pairs={{8,0},{16,8},{24,16},{9,1},{17,9},{25,17},{10,2},{18,10},{26,18},{... | collective-permute-start | bytes 1572872 | tf_op jit(solution)/shard_map/ppermute | solution.py:26
  79.6 8.3 %collective-permute-start.28 = (bf16[256,512]{1,0:T(8,128)(2,1)S(1)}, bf16[256,512]{1,0:T(8,128)(2,1)S(1)}, u32[]{:S(2)}, u32[]{:S(2)}) collective-permute-start(bf16[256,512]{1,0:T(8,128)(2,1)S(1)} %get-tuple-element.34), channel_id=1, source_target_pairs={{0,1},{1,0},{2,3},{3,2},{4,5},{5,4},{6,7},{7,6},{8,9},{9,8},{10,11... | collective-permute-start | bytes 786440 | tf_op jit(solution)/shard_map/ppermute | solution.py:39
  85.2 15.6 %collective-permute-start.24 = (bf16[128,512]{1,0:T(8,128)(2,1)S(1)}, bf16[128,512]{1,0:T(8,128)(2,1)S(1)}, u32[]{:S(2)}, u32[]{:S(2)}) collective-permute-start(bf16[128,512]{1,0:T(8,128)(2,1)S(1)} %get-tuple-element.28), channel_id=1, source_target_pairs={{0,1},{1,0},{2,3},{3,2},{4,5},{5,4},{6,7},{7,6},{8,9},{9,8},{10,11... | collective-permute-start | bytes 393224 | tf_op jit(solution)/shard_map/ppermute | solution.py:39
  85.8 15.0 %collective-permute-start.25 = (bf16[128,512]{1,0:T(8,128)(2,1)S(1)}, bf16[128,512]{1,0:T(8,128)(2,1)S(1)}, u32[]{:S(2)}, u32[]{:S(2)}) collective-permute-start(bf16[128,512]{1,0:T(8,128)(2,1)S(1)} %get-tuple-element.29), channel_id=1, source_target_pairs={{0,2},{1,3},{2,0},{3,1},{4,6},{5,7},{6,4},{7,5},{8,10},{9,11},{10,... | collective-permute-start | bytes 393224 | tf_op jit(solution)/shard_map/ppermute | solution.py:39
  86.7 14.1 %collective-permute-start.26 = (bf16[128,512]{1,0:T(8,128)(2,1)S(1)}, bf16[128,512]{1,0:T(8,128)(2,1)S(1)}, u32[]{:S(2)}, u32[]{:S(2)}) collective-permute-start(bf16[128,512]{1,0:T(8,128)(2,1)S(1)} %get-tuple-element.30), channel_id=1, source_target_pairs={{0,3},{1,2},{2,1},{3,0},{4,7},{5,6},{6,5},{7,4},{8,11},{9,10},{10,... | collective-permute-start | bytes 393224 | tf_op jit(solution)/shard_map/ppermute | solution.py:39
  88.0 12.9 %collective-permute-start.29 = (bf16[128,512]{1,0:T(8,128)(2,1)S(1)}, bf16[128,512]{1,0:T(8,128)(2,1)S(1)}, u32[]{:S(2)}, u32[]{:S(2)}) collective-permute-start(bf16[128,512]{1,0:T(8,128)(2,1)S(1)} %get-tuple-element.35), channel_id=1, source_target_pairs={{0,6},{1,7},{2,4},{3,5},{4,2},{5,3},{6,0},{7,1},{8,14},{9,15},{10,... | collective-permute-start | bytes 393224 | tf_op jit(solution)/shard_map/ppermute | solution.py:39
  90.7 10.2 %collective-permute-start.30 = (bf16[128,512]{1,0:T(8,128)(2,1)S(1)}, bf16[128,512]{1,0:T(8,128)(2,1)S(1)}, u32[]{:S(2)}, u32[]{:S(2)}) collective-permute-start(bf16[128,512]{1,0:T(8,128)(2,1)S(1)} %get-tuple-element.36), channel_id=1, source_target_pairs={{0,4},{1,5},{2,6},{3,7},{4,0},{5,1},{6,2},{7,3},{8,12},{9,13},{10,... | collective-permute-start | bytes 393224 | tf_op jit(solution)/shard_map/ppermute | solution.py:39

commit v5 on v4

--- a/solution.py
+++ b/solution.py
@@ -11,6 +11,8 @@
 MIB = 1024 * 1024
 BF16 = jnp.bfloat16
 F32 = jnp.float32
+
+SPLIT_FLOPS = 10**10
 
 OFFSETS = (0, -1, 1, -2, 2, -3, 3, 4)
 COUNT = len(OFFSETS)
@@ -58,11 +60,27 @@
     return jnp.where(place < count // 2, 2 * place, 2 * (count - 1 - place) + 1)
 
 
+def split_kernel(in_ref, first_ref, last_ref):
+    middle = first_ref.shape[0]
+    first_ref[...] = in_ref[:middle, :]
+    last_ref[...] = in_ref[middle:, :]
+
+
 def ring_gather(own):
     count = lax.axis_size("feat")
-    middle = own.shape[0] // 2
-    found = {0: (own[:middle], own[middle:])}
-    first, last = ({0: part} for part in found[0])
+    part = jax.ShapeDtypeStruct((own.shape[0] // 2, own.shape[1]), own.dtype)
+    first, last = (
+        {0: part}
+        for part in pl.pallas_call(
+            split_kernel,
+            name="split",
+            out_shape=(part, part),
+            in_specs=vmem(1),
+            out_specs=tuple(vmem(2)),
+            compiler_params=params(2),
+            cost_estimate=cost(SPLIT_FLOPS, 0),
+        )(own)
+    )
     for step in range(1, count // 2):
         for held in (first, last):
             held[-step] = passed_on(held[1 - step], 1)
@@ -119,51 +137,27 @@
     return jnp.concatenate([parts[2 * k][...], parts[2 * k + 1][...]], axis=0)
 
 
-def in_turn(copies, ahead):
-    for copy in copies[:ahead]:
-        copy.start()
-    for k, copy in enumerate(copies):
-        copy.wait()
-        for later in copies[k + ahead : k + ahead + 1]:
-            later.start()
-        yield k
-
-
 def pre_kernel(*refs):
     count = len(OFFSETS)
-    parts, (w_ref, b_ref, codes_ref, active_ref, held, bias, sems) = refs[: 2 * count], refs[2 * count :]
+    parts, (w_ref, b_ref, codes_ref, active_ref) = refs[: 2 * count], refs[2 * count :]
     width = parts[0].shape[1]
-    copies = [
-        pltpu.make_async_copy(w_ref.at[:, columns(ring_owner(offset), width)], held.at[k], sems.at[k])
-        for k, offset in enumerate(OFFSETS)
-    ]
-    bias_copy = pltpu.make_async_copy(b_ref, bias, sems.at[count])
-    bias_copy.start()
-    total = None
-    for k in in_turn(copies, 3):
-        term = against(block(parts, k), held[k])
-        total = term if total is None else total + term
-    bias_copy.wait()
-    active = jnp.maximum(total + bias[...], 0.0)
-    active_ref[...] = active
-    codes_ref[...] = (active * active).astype(BF16)
-
-
-def row_copies(source, slot, target, sems):
-    steps, tile = tiles(target.shape[0])
-    return [
-        pltpu.make_async_copy(
-            source.at[slot, j * tile : (j + 1) * tile, :], target.at[j * tile : (j + 1) * tile, :], sems.at[j]
-        )
-        for j in range(steps)
-    ]
-
-
-def decoded(w_ref, here, parts, groups, tok, total):
+    steps, tile = tiles(w_ref.shape[0])
+    for j in range(steps):
+        here = slice(j * tile, (j + 1) * tile)
+        total = None
+        for k, offset in enumerate(OFFSETS):
+            term = against(w_ref[here, columns(ring_owner(offset), width)], block(parts, k))
+            total = term if total is None else total + term
+        active = jnp.maximum(total.T + b_ref[:, here], 0.0)
+        active_ref[:, here] = active
+        codes_ref[:, here] = (active * active).astype(BF16)
+
+
+def decoded(w_ref, slot, here, parts, groups, tok, total):
     width = parts[0].shape[1]
     for i, row, mask in flat(groups):
         part = parts[i][row * tok : (row + 1) * tok, :]
-        term = against(w_ref[here, columns(owner(mask), width)], part)
+        term = against(w_ref[slot, here, columns(owner(mask), width)], part)
         total = term if total is None else total + term
     return total
 
@@ -174,42 +168,42 @@
 
 
 def own_recon_kernel(*refs):
-    parts, (w_ref, total_ref, held_ref, sems) = refs[: len(BLOCKS)], refs[len(BLOCKS) :]
+    parts, (w_ref, total_ref) = refs[: len(BLOCKS)], refs[len(BLOCKS) :]
     tok = total_ref.shape[1]
-    _, tile = tiles(held_ref.shape[0])
-    copies = row_copies(w_ref, 0, held_ref, sems)
-    for j in in_turn(copies, 2):
+    steps, tile = tiles(w_ref.shape[1])
+
+    for j in range(steps):
         here = slice(j * tile, (j + 1) * tile)
-        total_ref[here, :] = decoded(held_ref, here, parts, BLOCKS, tok, None)
-
-
-def products(error_ref, w_ref, masks, out_ref):
+        total_ref[here, :] = decoded(w_ref, 0, here, parts, BLOCKS, tok, None)
+
+
+def products(error_ref, w_ref, slot, masks, out_ref):
     tok = error_ref.shape[0]
     for row, mask in enumerate(masks):
         term = jnp.dot(
-            error_ref[...], w_ref[:, columns(owner(mask), out_ref.shape[1])], preferred_element_type=F32
+            error_ref[...], w_ref[slot, :, columns(owner(mask), out_ref.shape[1])], preferred_element_type=F32
         )
         out_ref[row * tok : (row + 1) * tok, :] = term.astype(out_ref.dtype)
 
 
 def recon_kernel(scale, *refs):
-    parts = refs[: len(BLOCKS)]
-    total_ref, w_ref, b_ref, target_ref, error_ref, far_ref, held_ref, sems = refs[len(BLOCKS) :]
+    parts, (total_ref, w_ref, b_ref, target_ref, error_ref, far_ref) = refs[: len(BLOCKS)], refs[len(BLOCKS) :]
     tok = total_ref.shape[1]
-    _, tile = tiles(held_ref.shape[0])
-    copies = row_copies(w_ref, 1, held_ref, sems)
-    for j in in_turn(copies, 2):
+    steps, tile = tiles(w_ref.shape[1])
+
+    for j in range(steps):
         here = slice(j * tile, (j + 1) * tile)
-        total = decoded(held_ref, here, parts, BLOCKS, tok, total_ref[here, :])
+        total = decoded(w_ref, 1, here, parts, BLOCKS, tok, total_ref[here, :])
         error = total.T + b_ref[:, here] - target_ref[:, here].astype(F32)
         error_ref[:, here] = (error * scale).astype(BF16)
-    products(error_ref, held_ref, FAR + CROSSING, far_ref)
-
-
-def own_grad_kernel(error_ref, own_ref, next_ref, sent_ref, near_ref, far_ref):
-    products(error_ref, next_ref, NEAR, sent_ref)
-    products(error_ref, own_ref, FAR + CROSSING, far_ref)
-    products(error_ref, own_ref, NEAR, near_ref)
+
+    products(error_ref, w_ref, 1, FAR + CROSSING, far_ref)
+
+
+def own_grad_kernel(error_ref, w_ref, sent_ref, near_ref, far_ref):
+    products(error_ref, w_ref, 1, NEAR, sent_ref)
+    products(error_ref, w_ref, 0, FAR + CROSSING, far_ref)
+    products(error_ref, w_ref, 0, NEAR, near_ref)
 
 
 def dec_grad_kernel(groups, *refs):
@@ -260,48 +254,39 @@
 
     first, last = ring_gather(inputs[0])
     inputs_of = [part for offset in OFFSETS for part in (first[offset], last[offset])]
-    enc_weights, weights = [pltpu.with_memory_space_constraint(w[0], pltpu.HBM) for w in (enc_w, dec_w)]
+    enc_weights, weights = [pltpu.with_memory_space_constraint(w[0], pltpu.VMEM) for w in (enc_w, dec_w)]
 
     codes, active = pl.pallas_call(
         pre_kernel,
         name="pre",
         out_shape=(struct((tok, own_features), BF16), struct((tok, own_features), F32)),
-        in_specs=[*vmem(2 * count), *[pl.BlockSpec(memory_space=pltpu.HBM)] * 2],
+        in_specs=vmem(2 * count + 2),
         out_specs=tuple(vmem(2)),
-        scratch_shapes=[
-            pltpu.VMEM((count, own_features, width), BF16),
-            pltpu.VMEM(enc_b.shape, F32),
-            pltpu.SemaphoreType.DMA((count + 1,)),
-        ],
-        compiler_params=params(20),
-        cost_estimate=cost(2 * tok * own_features * model, 2 * own_features * model),
-    )(*inputs_of, enc_weights, pltpu.with_memory_space_constraint(enc_b, pltpu.HBM))
+        compiler_params=params(16),
+        cost_estimate=cost(2 * tok * own_features * model, 0),
+    )(*inputs_of, enc_weights, enc_b)
 
     far_pair = packed(exchanged(codes, 6), exchanged(codes, 4))
     far_across = exchanged(far_pair, 1)
     own = [packed(codes, *[exchanged(codes, mask) for mask in (1, 2, 3)]), far_pair, far_across]
     previous = [from_behind(part, "section", 1) for part in own]
 
-    held = pltpu.VMEM((width, features), BF16)
-    sems = [pltpu.SemaphoreType.DMA((tiles(width)[0],))]
-    total, own_weights = pl.pallas_call(
+    total = pl.pallas_call(
         own_recon_kernel,
         name="own_recon",
-        out_shape=(struct((width, tok), F32), held),
-        in_specs=[*vmem(len(own)), pl.BlockSpec(memory_space=pltpu.HBM)],
-        out_specs=tuple(vmem(2)),
-        scratch_shapes=sems,
+        out_shape=struct((width, tok), F32),
+        in_specs=vmem(len(own) + 1),
+        out_specs=vmem(1)[0],
         compiler_params=params(8),
-        cost_estimate=cost(matmul, 4 * MIB),
+        cost_estimate=cost(matmul, 0),
     )(*own, weights)
 
-    error, sent_far, next_weights = pl.pallas_call(
+    error, sent_far = pl.pallas_call(
         functools.partial(recon_kernel, scale),
         name="recon",
-        out_shape=(struct((tok, width), BF16), stack(FAR + CROSSING, BF16), held),
-        in_specs=[*vmem(len(previous) + 1), pl.BlockSpec(memory_space=pltpu.HBM), *vmem(2)],
-        out_specs=tuple(vmem(3)),
-        scratch_shapes=sems,
+        out_shape=(struct((tok, width), BF16), stack(FAR + CROSSING, BF16)),
+        in_specs=vmem(len(previous) + 4),
+        out_specs=tuple(vmem(2)),
         compiler_params=params(8),
         cost_estimate=cost(2 * matmul, 4 * MIB),
     )(*previous, total, weights, dec_b, targets[0])
@@ -311,11 +296,11 @@
         own_grad_kernel,
         name="own_grad",
         out_shape=(stack(NEAR, BF16), stack(NEAR, F32), stack(FAR + CROSSING, F32)),
-        in_specs=vmem(3),
+        in_specs=vmem(2),
         out_specs=tuple(vmem(3)),
         compiler_params=params(8),
         cost_estimate=cost(3 * matmul // 2, 6 * MIB),
-    )(error, own_weights, next_weights)
+    )(error, weights)
     arrived_near = from_behind(sent_near, "section", -1)
 
     rows = 256 if width % 256 == 0 else LANES

time: 106 us -> 99 us (0.934)
  Pallas kernels: 36.1 us -> 24.9 us
  waiting for transfers between devices: 26.1 us -> 30.5 us
    pallas_call x1, Pallas kernels: 7.4 us -> 3 us  [on_device(): pl.pallas_call(functools.partial(recon_kernel, scale), name='recon', out_...]
    pallas_call x1 -> x2, Pallas kernels: 6.57 us -> 2.33 us  [the longest x1 2.31 us: on_device(): pl.pallas_call(own_recon_kernel, name='own_recon', out_shape=struct((widt...]
    ppermute x5, waiting for transfers between devices: 11.5 us -> 14.8 us  [from_behind(): lax.ppermute(value, axis, [(source, source + steps) for source in range(i...]
    pallas_call x1, Pallas kernels: 5 us -> 2.42 us  [on_device(): pl.pallas_call(pre_kernel, name='pre', out_shape=(struct((tok, own_featur...]
    ppermute x12, starting transfers between devices: 14.4 us -> 13 us  [exchanged(): return lax.ppermute(value, 'feat', [(i, i ^ mask) for i in range(count)])]
    unnamed x4 -> x18, local copies, waits for them, and re-layouts: 0.01 us -> 1.13 us
  transfers between devices with their start and end apart: 31 -> 31, of which waited for: 16 -> 15; matrix products, arithmetic and copies ran while one was open for 0% -> 0% of each run, Pallas kernels for 17% -> 14%
where the time goes in v5:
time: 99 us; the launch traced here: 98.7 us
  starting transfers between devices  41.4 us (42%)
  waiting for transfers between devices  30.5 us (31%)
  Pallas kernels  24.9 us (25%)
  local copies, waits for them, and re-layouts  1.13 us (1%)
    ppermute x5, starting transfers between devices, from_behind(): lax.ppermute(value, axis, [(source, source + steps) for source in range(i...  17 us
    ppermute x5, waiting for transfers between devices, from_behind(): lax.ppermute(value, axis, [(source, source + steps) for source in range(i...  14.8 us
    ppermute x12, starting transfers between devices, exchanged(): return lax.ppermute(value, 'feat', [(i, i ^ mask) for i in range(count)])  13 us
    ppermute x14, starting transfers between devices, passed_on(): lax.ppermute(value, 'feat', [(order[p], order[(p + by) % count]) for p in...  11.4 us
    ppermute x14, waiting for transfers between devices, passed_on(): lax.ppermute(value, 'feat', [(order[p], order[(p + by) % count]) for p in...  10.5 us
    pallas_call x2, Pallas kernels, dec_grad_slot(): pl.pallas_call(functools.partial(dec_grad_kernel, groups), name='dec_grad...  9.81 us
    ppermute x12, waiting for transfers between devices, exchanged(): return lax.ppermute(value, 'feat', [(i, i ^ mask) for i in range(count)])  5.21 us
    pallas_call x1, Pallas kernels, on_device(): pl.pallas_call(enc_grad_kernel, name='enc_grad', grid=(own_features // LA...  5.2 us
  transfers between devices with their start and end apart: 31, of which 15 were waited for; matrix products, arithmetic and copies ran while one was open for 0% of the time, Pallas kernels for 14%

profile of v5, /device:TPU:1, one launch (start us, length us, event | category | flops | bytes accessed | tf_op | source)
XLA Modules:
  0.0 98.7 jit_solution(14774972017704670856)
XLA Ops:
  0.7 1.1 %copy-done.4 = bf16[1,128,1024]{2,1,0:T(8,128)(2,1)S(1)} copy-done((bf16[1,128,1024]{2,1,0:T(8,128)(2,1)S(1)}, bf16[1,128,1024]{2,1,0:T(8,128)(2,1)}, u32[]{:S(2)}) %copy-start.4) | copy-done | bytes 262168
  1.8 2.2 %collective-permute-start = (bf16[64,1024]{1,0:T(8,128)(2,1)S(1)}, bf16[64,1024]{1,0:T(8,128)(2,1)S(1)}, u32[]{:S(2)}, u32[]{:S(2)}) collective-permute-start(bf16[64,1024]{1,0:T(8,128)(2,1)S(1)} %get-tuple-element.19.refs_0_.refs_6_), channel_id=1, source_target_pairs={{0,2},{2,4},{4,6},{6,7},{7,5},{5,3},{3,1},{1,0},{8,10},{10,12},{12... | collective-permute-start | bytes 393224 | tf_op jit(solution)/shard_map/ppermute | solution.py:51
  4.0 1.4 %collective-permute-start.2 = (bf16[64,1024]{1,0:T(8,128)(2,1)S(1)}, bf16[64,1024]{1,0:T(8,128)(2,1)S(1)}, u32[]{:S(2)}, u32[]{:S(2)}) collective-permute-start(bf16[64,1024]{1,0:T(8,128)(2,1)S(1)} %get-tuple-element.19.refs_0_.refs_6_), channel_id=1, source_target_pairs={{0,1},{2,0},{4,2},{6,4},{7,6},{5,7},{3,5},{1,3},{8,9},{10,8},{12,1... | collective-permute-start | bytes 393224 | tf_op jit(solution)/shard_map/ppermute | solution.py:51
  5.5 1.7 %collective-permute-done.refs_2_.refs_8_ = bf16[64,1024]{1,0:T(8,128)(2,1)S(1)} collective-permute-done((bf16[64,1024]{1,0:T(8,128)(2,1)S(1)}, bf16[64,1024]{1,0:T(8,128)(2,1)S(1)}, u32[]{:S(2)}, u32[]{:S(2)}) %collective-permute-start) | collective-permute-done | bytes 131104 | tf_op jit(solution)/shard_map/ppermute | solution.py:51
  7.2 1.2 %collective-permute-start.4 = (bf16[64,1024]{1,0:T(8,128)(2,1)S(1)}, bf16[64,1024]{1,0:T(8,128)(2,1)S(1)}, u32[]{:S(2)}, u32[]{:S(2)}) collective-permute-start(bf16[64,1024]{1,0:T(8,128)(2,1)S(1)} %collective-permute-done.refs_2_.refs_8_), channel_id=1, source_target_pairs={{0,2},{2,4},{4,6},{6,7},{7,5},{5,3},{3,1},{1,0},{8,10},{10,12},{12... | collective-permute-start | bytes 393224 | tf_op jit(solution)/shard_map/ppermute | solution.py:51
  8.4 0.3 collective-permute-start.7
  8.6 2.2 %collective-permute-done.2.refs_4_.refs_10_ = bf16[64,1024]{1,0:T(8,128)(2,1)S(1)} collective-permute-done((bf16[64,1024]{1,0:T(8,128)(2,1)S(1)}, bf16[64,1024]{1,0:T(8,128)(2,1)S(1)}, u32[]{:S(2)}, u32[]{:S(2)}) %collective-permute-start.2) | collective-permute-done | bytes 131104 | tf_op jit(solution)/shard_map/ppermute | solution.py:51
  10.9 0.3 collective-permute-start.6
  11.2 1.1 %collective-permute-start.5 = (bf16[64,1024]{1,0:T(8,128)(2,1)S(1)}, bf16[64,1024]{1,0:T(8,128)(2,1)S(1)}, u32[]{:S(2)}, u32[]{:S(2)}) collective-permute-start(bf16[64,1024]{1,0:T(8,128)(2,1)S(1)} %collective-permute-done.1.refs_3_.refs_9_), channel_id=1, source_target_pairs={{0,2},{2,4},{4,6},{6,7},{7,5},{5,3},{3,1},{1,0},{8,10},{10,12},{12... | collective-permute-start | bytes 393224 | tf_op jit(solution)/shard_map/ppermute | solution.py:51
  12.5 1.3 %collective-permute-start.8 = (bf16[64,1024]{1,0:T(8,128)(2,1)S(1)}, bf16[64,1024]{1,0:T(8,128)(2,1)S(1)}, u32[]{:S(2)}, u32[]{:S(2)}) collective-permute-start(bf16[64,1024]{1,0:T(8,128)(2,1)S(1)} %collective-permute-done.4.refs_6_.refs_12_), channel_id=1, source_target_pairs={{0,2},{2,4},{4,6},{6,7},{7,5},{5,3},{3,1},{1,0},{8,10},{10,12},{12... | collective-permute-start | bytes 393224 | tf_op jit(solution)/shard_map/ppermute | solution.py:51
  13.7 0.2 collective-permute-start.11
  13.9 1.8 %collective-permute-done.6.refs_8_.refs_14_ = bf16[64,1024]{1,0:T(8,128)(2,1)S(1)} collective-permute-done((bf16[64,1024]{1,0:T(8,128)(2,1)S(1)}, bf16[64,1024]{1,0:T(8,128)(2,1)S(1)}, u32[]{:S(2)}, u32[]{:S(2)}) %collective-permute-start.6) | collective-permute-done | bytes 131104 | tf_op jit(solution)/shard_map/ppermute | solution.py:51
  15.7 0.7 collective-permute-start.10
  16.4 0.8 collective-permute-start.9
  17.2 1.3 %collective-permute-start.12 = (bf16[64,1024]{1,0:T(8,128)(2,1)S(1)}, bf16[64,1024]{1,0:T(8,128)(2,1)S(1)}, u32[]{:S(2)}, u32[]{:S(2)}) collective-permute-start(bf16[64,1024]{1,0:T(8,128)(2,1)S(1)} %collective-permute-done.8.refs_10_.refs_16_), channel_id=1, source_target_pairs={{0,2},{2,4},{4,6},{6,7},{7,5},{5,3},{3,1},{1,0},{8,10},{10,12},{12... | collective-permute-start | bytes 393224 | tf_op jit(solution)/shard_map/ppermute | solution.py:51
  18.5 0.4 collective-permute-done.11.refs_13_.refs_19_
  18.9 0.5 collective-permute-start.13
  19.4 1.4 %collective-permute-done.10.refs_12_.refs_18_ = bf16[64,1024]{1,0:T(8,128)(2,1)S(1)} collective-permute-done((bf16[64,1024]{1,0:T(8,128)(2,1)S(1)}, bf16[64,1024]{1,0:T(8,128)(2,1)S(1)}, u32[]{:S(2)}, u32[]{:S(2)}) %collective-permute-start.10) | collective-permute-done | bytes 131104 | tf_op jit(solution)/shard_map/ppermute | solution.py:51
  20.7 1.1 %collective-permute-done.9.refs_11_.refs_17_ = bf16[64,1024]{1,0:T(8,128)(2,1)S(1)} collective-permute-done((bf16[64,1024]{1,0:T(8,128)(2,1)S(1)}, bf16[64,1024]{1,0:T(8,128)(2,1)S(1)}, u32[]{:S(2)}, u32[]{:S(2)}) %collective-permute-start.9) | collective-permute-done | bytes 131104 | tf_op jit(solution)/shard_map/ppermute | solution.py:51
  21.8 1.1 %collective-permute-done.12.refs_14_.refs_20_ = bf16[64,1024]{1,0:T(8,128)(2,1)S(1)} collective-permute-done((bf16[64,1024]{1,0:T(8,128)(2,1)S(1)}, bf16[64,1024]{1,0:T(8,128)(2,1)S(1)}, u32[]{:S(2)}, u32[]{:S(2)}) %collective-permute-start.12) | collective-permute-done | bytes 131104 | tf_op jit(solution)/shard_map/ppermute | solution.py:51
  23.0 0.7 collective-permute-done.13.refs_15_.refs_21_
  23.7 2.4 %pre.1 = (bf16[128,512]{1,0:T(8,128)(2,1)S(1)}, f32[128,512]{1,0:T(8,128)S(1)}) custom-call(bf16[64,1024]{1,0:T(8,128)(2,1)S(1)} %get-tuple-element.19.refs_0_.refs_6_, bf16[64,1024]{1,0:T(8,128)(2,1)S(1)} %get-tuple-element.20.refs_1_.refs_7_, bf16[64,1024]{1,0:T(8,128)(2,1)S(1)} %collective-permute-done.refs_2_.refs_8_, ...), custom_call_target="tpu_custom_call" | custom-call | flops 1073741824 | tf_op jit(solution)/shard_map/pre/pallas_call | solution.py:259
  26.1 3.3 %collective-permute-start.18 = (bf16[128,512]{1,0:T(8,128)(2,1)S(1)}, bf16[128,512]{1,0:T(8,128)(2,1)S(1)}, u32[]{:S(2)}, u32[]{:S(2)}) collective-permute-start(bf16[128,512]{1,0:T(8,128)(2,1)S(1)} %get-tuple-element.21.refs_0_), channel_id=1, source_target_pairs={{0,6},{1,7},{2,4},{3,5},{4,2},{5,3},{6,0},{7,1},{8,14},{9,15},{10,... | collective-permute-start | bytes 393224 | tf_op jit(solution)/shard_map/ppermute | solution.py:41
  29.4 0.8 collective-permute-start.14
  30.2 0.4 collective-permute-start.15
  30.6 1.5 %collective-permute-start.16 = (bf16[128,512]{1,0:T(8,128)(2,1)S(1)}, bf16[128,512]{1,0:T(8,128)(2,1)S(1)}, u32[]{:S(2)}, u32[]{:S(2)}) collective-permute-start(bf16[128,512]{1,0:T(8,128)(2,1)S(1)} %get-tuple-element.21.refs_0_), channel_id=1, source_target_pairs={{0,3},{1,2},{2,1},{3,0},{4,7},{5,6},{6,5},{7,4},{8,11},{9,10},{10,... | collective-permute-start | bytes 393224 | tf_op jit(solution)/shard_map/ppermute | solution.py:41
  32.1 3.2 %collective-permute-done.19.refs_1_ = bf16[128,512]{1,0:T(8,128)(2,1)S(1)} collective-permute-done((bf16[128,512]{1,0:T(8,128)(2,1)S(1)}, bf16[128,512]{1,0:T(8,128)(2,1)S(1)}, u32[]{:S(2)}, u32[]{:S(2)}) %collective-permute-start.19) | collective-permute-done | bytes 131104 | tf_op jit(solution)/shard_map/ppermute | solution.py:41
  35.3 1.6 %collective-permute-start.21 = (bf16[256,512]{1,0:T(8,128)(2,1)S(1)}, bf16[256,512]{1,0:T(8,128)(2,1)S(1)}, u32[]{:S(2)}, u32[]{:S(2)}) collective-permute-start(bf16[256,512]{1,0:T(8,128)(2,1)S(1)} %pack.3.refs_1_.refs_2_), channel_id=1, source_target_pairs={{0,1},{1,0},{2,3},{3,2},{4,5},{5,4},{6,7},{7,6},{8,9},{9,8},{10,11... | collective-permute-start | bytes 786440 | tf_op jit(solution)/shard_map/ppermute | solution.py:41
  36.9 1.9 %collective-permute-done.16.refs_3_ = bf16[128,512]{1,0:T(8,128)(2,1)S(1)} collective-permute-done((bf16[128,512]{1,0:T(8,128)(2,1)S(1)}, bf16[128,512]{1,0:T(8,128)(2,1)S(1)}, u32[]{:S(2)}, u32[]{:S(2)}) %collective-permute-start.16) | collective-permute-done | bytes 131104 | tf_op jit(solution)/shard_map/ppermute | solution.py:41
  38.9 8.2 %collective-permute-start.17 = (bf16[512,512]{1,0:T(8,128)(2,1)S(1)}, bf16[512,512]{1,0:T(8,128)(2,1)S(1)}, u32[]{:S(2)}, u32[]{:S(2)}) collective-permute-start(bf16[512,512]{1,0:T(8,128)(2,1)S(1)} %pack.2.refs_0_.refs_1_), channel_id=1, source_target_pairs={{0,8},{8,16},{16,24},{1,9},{9,17},{17,25},{2,10},{10,18},{18,26},{... | collective-permute-start | bytes 1572872 | tf_op jit(solution)/shard_map/ppermute | solution.py:28
  47.1 1.9 %collective-permute-start.20 = (bf16[256,512]{1,0:T(8,128)(2,1)S(1)}, bf16[256,512]{1,0:T(8,128)(2,1)S(1)}, u32[]{:S(2)}, u32[]{:S(2)}) collective-permute-start(bf16[256,512]{1,0:T(8,128)(2,1)S(1)} %pack.3.refs_1_.refs_2_), channel_id=1, source_target_pairs={{0,8},{8,16},{16,24},{1,9},{9,17},{17,25},{2,10},{10,18},{18,26},{... | collective-permute-start | bytes 786440 | tf_op jit(solution)/shard_map/ppermute | solution.py:28
  49.0 2.9 %collective-permute-start.22 = (bf16[256,512]{1,0:T(8,128)(2,1)S(1)}, bf16[256,512]{1,0:T(8,128)(2,1)S(1)}, u32[]{:S(2)}, u32[]{:S(2)}) collective-permute-start(bf16[256,512]{1,0:T(8,128)(2,1)S(1)} %collective-permute-done.21.refs_2_.refs_3_), channel_id=1, source_target_pairs={{0,8},{8,16},{16,24},{1,9},{9,17},{17,25},{2,10},{10,18},{18,26},{... | collective-permute-start | bytes 786440 | tf_op jit(solution)/shard_map/ppermute | solution.py:28
  52.0 2.3 %own_recon.1.refs_3_ = f32[1024,128]{1,0:T(8,128)S(1)} custom-call(bf16[512,512]{1,0:T(8,128)(2,1)S(1)} %pack.2.refs_0_.refs_1_, bf16[256,512]{1,0:T(8,128)(2,1)S(1)} %pack.3.refs_1_.refs_2_, bf16[256,512]{1,0:T(8,128)(2,1)S(1)} %collective-permute-done.21.refs_2_.refs_3_, bf16[2,1024,4096]{2,1,0:T(8,128)(2,1)S(1)} %bitcast.6), custom_call_target="tpu_custom_call" | custom-call | flops 1073741824 | tf_op jit(solution)/shard_map/own_recon/pallas_call | solution.py:274
  54.3 1.7 %collective-permute-done.20.refs_1_.refs_2_ = bf16[256,512]{1,0:T(8,128)(2,1)S(1)} collective-permute-done((bf16[256,512]{1,0:T(8,128)(2,1)S(1)}, bf16[256,512]{1,0:T(8,128)(2,1)S(1)}, u32[]{:S(2)}, u32[]{:S(2)}) %collective-permute-start.20) | collective-permute-done | bytes 262176 | tf_op jit(solution)/shard_map/ppermute | solution.py:28
  56.0 2.8 %collective-permute-done.22.refs_2_.refs_3_ = bf16[256,512]{1,0:T(8,128)(2,1)S(1)} collective-permute-done((bf16[256,512]{1,0:T(8,128)(2,1)S(1)}, bf16[256,512]{1,0:T(8,128)(2,1)S(1)}, u32[]{:S(2)}, u32[]{:S(2)}) %collective-permute-start.22) | collective-permute-done | bytes 262176 | tf_op jit(solution)/shard_map/ppermute | solution.py:28
  58.8 3.0 %recon.1 = (bf16[128,1024]{1,0:T(8,128)(2,1)S(1)}, bf16[512,512]{1,0:T(8,128)(2,1)S(1)}) custom-call(bf16[512,512]{1,0:T(8,128)(2,1)S(1)} %collective-permute-done.17.refs_0_.refs_1_, bf16[256,512]{1,0:T(8,128)(2,1)S(1)} %collective-permute-done.20.refs_1_.refs_2_, bf16[256,512]{1,0:T(8,128)(2,1)S(1)} %collective-permute-done.22.refs_2_.refs_3_, ...), custom_call_target="tpu_custom_call" | custom-call | flops 2147483648 | bytes 4194304 | tf_op jit(solution)/shard_map/recon/pallas_call | solution.py:284
  61.8 1.9 %collective-permute-start.27 = (bf16[512,512]{1,0:T(8,128)(2,1)S(1)}, bf16[512,512]{1,0:T(8,128)(2,1)S(1)}, u32[]{:S(2)}, u32[]{:S(2)}) collective-permute-start(bf16[512,512]{1,0:T(8,128)(2,1)S(1)} %get-tuple-element.30), channel_id=1, source_target_pairs={{8,0},{16,8},{24,16},{9,1},{17,9},{25,17},{10,2},{18,10},{26,18},{... | collective-permute-start | bytes 1572872 | tf_op jit(solution)/shard_map/ppermute | solution.py:28
  63.8 1.8 %own_grad.1 = (bf16[512,512]{1,0:T(8,128)(2,1)S(1)}, f32[512,512]{1,0:T(8,128)S(1)}, f32[512,512]{1,0:T(8,128)S(1)}) custom-call(bf16[128,1024]{1,0:T(8,128)(2,1)S(1)} %get-tuple-element.22.error_ref.refs_0_, bf16[2,1024,4096]{2,1,0:T(8,128)(2,1)S(1)} %bitcast.8), custom_call_target="tpu_custom_call" | custom-call | flops 1610612736 | bytes 6291456 | tf_op jit(solution)/shard_map/own_grad/pallas_call | solution.py:295
  65.6 2.1 %collective-permute-start.23 = (bf16[512,512]{1,0:T(8,128)(2,1)S(1)}, bf16[512,512]{1,0:T(8,128)(2,1)S(1)}, u32[]{:S(2)}, u32[]{:S(2)}) collective-permute-start(bf16[512,512]{1,0:T(8,128)(2,1)S(1)} %get-tuple-element.24), channel_id=1, source_target_pairs={{8,0},{16,8},{24,16},{9,1},{17,9},{25,17},{10,2},{18,10},{26,18},{... | collective-permute-start | bytes 1572872 | tf_op jit(solution)/shard_map/ppermute | solution.py:28
  67.7 5.6 %collective-permute-done.27.arrived_ref = bf16[512,512]{1,0:T(8,128)(2,1)S(1)} collective-permute-done((bf16[512,512]{1,0:T(8,128)(2,1)S(1)}, bf16[512,512]{1,0:T(8,128)(2,1)S(1)}, u32[]{:S(2)}, u32[]{:S(2)}) %collective-permute-start.27) | collective-permute-done | bytes 524320 | tf_op jit(solution)/shard_map/ppermute | solution.py:28
  73.5 0.9 collective-permute-start.28
  74.3 4.7 %collective-permute-done.23.arrived_ref = bf16[512,512]{1,0:T(8,128)(2,1)S(1)} collective-permute-done((bf16[512,512]{1,0:T(8,128)(2,1)S(1)}, bf16[512,512]{1,0:T(8,128)(2,1)S(1)}, u32[]{:S(2)}, u32[]{:S(2)}) %collective-permute-start.23) | collective-permute-done | bytes 524320 | tf_op jit(solution)/shard_map/ppermute | solution.py:28
  79.1 0.9 collective-permute-start.24
  80.0 1.8 %collective-permute-start.26 = (bf16[128,512]{1,0:T(8,128)(2,1)S(1)}, bf16[128,512]{1,0:T(8,128)(2,1)S(1)}, u32[]{:S(2)}, u32[]{:S(2)}) collective-permute-start(bf16[128,512]{1,0:T(8,128)(2,1)S(1)} %get-tuple-element.28), channel_id=1, source_target_pairs={{0,3},{1,2},{2,1},{3,0},{4,7},{5,6},{6,5},{7,4},{8,11},{9,10},{10,... | collective-permute-start | bytes 393224 | tf_op jit(solution)/shard_map/ppermute | solution.py:41
  81.8 1.8 %collective-permute-start.29 = (bf16[128,512]{1,0:T(8,128)(2,1)S(1)}, bf16[128,512]{1,0:T(8,128)(2,1)S(1)}, u32[]{:S(2)}, u32[]{:S(2)}) collective-permute-start(bf16[128,512]{1,0:T(8,128)(2,1)S(1)} %get-tuple-element.33), channel_id=1, source_target_pairs={{0,6},{1,7},{2,4},{3,5},{4,2},{5,3},{6,0},{7,1},{8,14},{9,15},{10,... | collective-permute-start | bytes 393224 | tf_op jit(solution)/shard_map/ppermute | solution.py:41
  83.7 4.9 %dec_grad.2.refs_4_ = bf16[1,2,1024,4096]{3,2,1,0:T(8,128)(2,1)} custom-call(bf16[128,1024]{1,0:T(8,128)(2,1)S(1)} %get-tuple-element.22.error_ref.refs_0_, bf16[512,512]{1,0:T(8,128)(2,1)S(1)} %pack.2.refs_0_.refs_1_, bf16[256,512]{1,0:T(8,128)(2,1)S(1)} %pack.3.refs_1_.refs_2_, bf16[256,512]{1,0:T(8,128)(2,1)S(1)} %collective-permute-done.21.refs_2_.refs_3_), custom_call_target="tpu_custom_call" | custom-call | flops 1073741824 | bytes 8388608 | tf_op jit(solution)/shard_map/dec_grad/pallas_call | solution.py:309
  88.6 4.9 %dec_grad.3 = bf16[1,2,1024,4096]{3,2,1,0:T(8,128)(2,1)} custom-call(bf16[128,1024]{1,0:T(8,128)(2,1)S(1)} %get-tuple-element.22.error_ref.refs_0_, bf16[512,512]{1,0:T(8,128)(2,1)S(1)} %collective-permute-done.17.refs_0_.refs_1_, bf16[256,512]{1,0:T(8,128)(2,1)S(1)} %collective-permute-done.20.refs_1_.refs_2_, ...), custom_call_target="tpu_custom_call", output_to_operand_aliasing={{}: (4, {})} | custom-call | flops 1073741824 | bytes 8388608 | tf_op jit(solution)/shard_map/dec_grad/pallas_call | solution.py:309
  93.5 5.2 %enc_grad.1 = bf16[1,512,8192]{2,1,0:T(8,128)(2,1)} custom-call(f32[128,512]{1,0:T(8,128)S(1)} %get-tuple-element.25.refs_0_, bf16[128,512]{1,0:T(8,128)(2,1)S(1)} %collective-permute-done.24.refs_1_, bf16[128,512]{1,0:T(8,128)(2,1)S(1)} %collective-permute-done.25.refs_2_, bf16[128,512]{1,0:T(8,128)(2,1)S(1)} %collective-permute-done.26.refs_3_, ...), custom_call_target="tpu_custom_call" | custom-call | flops 1073741824 | bytes 8388608 | tf_op jit(solution)/shard_map/enc_grad/pallas_call | solution.py:349
  (46 shorter events, 0.7 us)
Async XLA Ops:
  0.6 51.4 %slice-start = ((s8[16777216]{0:T(1024)(128)(4,1)}), s8[4194304]{0:T(1024)(128)(4,1)S(1)}, s32[]{:S(2)}) async-start(s8[16777216]{0:T(1024)(128)(4,1)} %bitcast.4), calls=%async_computation | async-start | bytes 8388608
  0.6 1.1 %copy-start.4 = (bf16[1,128,1024]{2,1,0:T(8,128)(2,1)S(1)}, bf16[1,128,1024]{2,1,0:T(8,128)(2,1)}, u32[]{:S(2)}) copy-start(bf16[1,128,1024]{2,1,0:T(8,128)(2,1)} %param.6) | copy-start | bytes 786436
  1.7 21.9 %copy-start = (bf16[1,512,8192]{2,1,0:T(8,128)(2,1)S(1)}, bf16[1,512,8192]{2,1,0:T(8,128)(2,1)}, u32[]{:S(2)}) copy-start(bf16[1,512,8192]{2,1,0:T(8,128)(2,1)} %param.8) | copy-start | bytes 25165828
  1.7 21.9 %copy-start.3 = (f32[1,512]{1,0:T(1,128)S(1)}, f32[1,512]{1,0:T(1,128)}, u32[]{:S(2)}) copy-start(f32[1,512]{1,0:T(1,128)} %refs_17_.1) | copy-start | bytes 6148
  1.7 50.2 %slice-start.1 = ((s8[16777216]{0:T(1024)(128)(4,1)}), s8[4194304]{0:T(1024)(128)(4,1)S(1)}, s32[]{:S(2)}) async-start(s8[16777216]{0:T(1024)(128)(4,1)} %bitcast.4), calls=%async_computation.1 | async-start | bytes 8388608
  1.7 50.3 %slice-start.2 = ((s8[16777216]{0:T(1024)(128)(4,1)}), s8[4194304]{0:T(1024)(128)(4,1)S(1)}, s32[]{:S(2)}) async-start(s8[16777216]{0:T(1024)(128)(4,1)} %bitcast.4), calls=%async_computation.2 | async-start | bytes 8388608
  1.8 50.3 %slice-start.3 = ((s8[16777216]{0:T(1024)(128)(4,1)}), s8[4194304]{0:T(1024)(128)(4,1)S(1)}, s32[]{:S(2)}) async-start(s8[16777216]{0:T(1024)(128)(4,1)} %bitcast.4), calls=%async_computation.3 | async-start | bytes 8388608
  1.8 57.0 %copy-start.1 = (bf16[1,128,1024]{2,1,0:T(8,128)(2,1)S(1)}, bf16[1,128,1024]{2,1,0:T(8,128)(2,1)}, u32[]{:S(2)}) copy-start(bf16[1,128,1024]{2,1,0:T(8,128)(2,1)} %param.7) | copy-start | bytes 786436
  1.8 57.0 %copy-start.2 = (f32[1,1024]{1,0:T(1,128)S(1)}, f32[1,1024]{1,0:T(1,128)}, u32[]{:S(2)}) copy-start(f32[1,1024]{1,0:T(1,128)} %refs_5_.1) | copy-start | bytes 12292
  1.8 5.3 %collective-permute-start = (bf16[64,1024]{1,0:T(8,128)(2,1)S(1)}, bf16[64,1024]{1,0:T(8,128)(2,1)S(1)}, u32[]{:S(2)}, u32[]{:S(2)}) collective-permute-start(bf16[64,1024]{1,0:T(8,128)(2,1)S(1)} %get-tuple-element.19.refs_0_.refs_6_), channel_id=1, source_target_pairs={{0,2},{2,4},{4,6},{6,7},{7,5},{5,3},{3,1},{1,0},{8,10},{10,12},{12... | collective-permute-start | bytes 393224 | tf_op jit(solution)/shard_map/ppermute | solution.py:51
  4.0 4.4 %collective-permute-start.3 = (bf16[64,1024]{1,0:T(8,128)(2,1)S(1)}, bf16[64,1024]{1,0:T(8,128)(2,1)S(1)}, u32[]{:S(2)}, u32[]{:S(2)}) collective-permute-start(bf16[64,1024]{1,0:T(8,128)(2,1)S(1)} %get-tuple-element.20.refs_1_.refs_7_), channel_id=1, source_target_pairs={{0,1},{2,0},{4,2},{6,4},{7,6},{5,7},{3,5},{1,3},{8,9},{10,8},{12,1... | collective-permute-start | bytes 393224 | tf_op jit(solution)/shard_map/ppermute | solution.py:51
  4.0 6.8 %collective-permute-start.2 = (bf16[64,1024]{1,0:T(8,128)(2,1)S(1)}, bf16[64,1024]{1,0:T(8,128)(2,1)S(1)}, u32[]{:S(2)}, u32[]{:S(2)}) collective-permute-start(bf16[64,1024]{1,0:T(8,128)(2,1)S(1)} %get-tuple-element.19.refs_0_.refs_6_), channel_id=1, source_target_pairs={{0,1},{2,0},{4,2},{6,4},{7,6},{5,7},{3,5},{1,3},{8,9},{10,8},{12,1... | collective-permute-start | bytes 393224 | tf_op jit(solution)/shard_map/ppermute | solution.py:51
  5.4 5.8 %collective-permute-start.1 = (bf16[64,1024]{1,0:T(8,128)(2,1)S(1)}, bf16[64,1024]{1,0:T(8,128)(2,1)S(1)}, u32[]{:S(2)}, u32[]{:S(2)}) collective-permute-start(bf16[64,1024]{1,0:T(8,128)(2,1)S(1)} %get-tuple-element.20.refs_1_.refs_7_), channel_id=1, source_target_pairs={{0,2},{2,4},{4,6},{6,7},{7,5},{5,3},{3,1},{1,0},{8,10},{10,12},{12... | collective-permute-start | bytes 393224 | tf_op jit(solution)/shard_map/ppermute | solution.py:51
  7.2 5.3 %collective-permute-start.4 = (bf16[64,1024]{1,0:T(8,128)(2,1)S(1)}, bf16[64,1024]{1,0:T(8,128)(2,1)S(1)}, u32[]{:S(2)}, u32[]{:S(2)}) collective-permute-start(bf16[64,1024]{1,0:T(8,128)(2,1)S(1)} %collective-permute-done.refs_2_.refs_8_), channel_id=1, source_target_pairs={{0,2},{2,4},{4,6},{6,7},{7,5},{5,3},{3,1},{1,0},{8,10},{10,12},{12... | collective-permute-start | bytes 393224 | tf_op jit(solution)/shard_map/ppermute | solution.py:51
  8.4 5.4 %collective-permute-start.7 = (bf16[64,1024]{1,0:T(8,128)(2,1)S(1)}, bf16[64,1024]{1,0:T(8,128)(2,1)S(1)}, u32[]{:S(2)}, u32[]{:S(2)}) collective-permute-start(bf16[64,1024]{1,0:T(8,128)(2,1)S(1)} %collective-permute-done.3.refs_5_.refs_11_), channel_id=1, source_target_pairs={{0,1},{2,0},{4,2},{6,4},{7,6},{5,7},{3,5},{1,3},{8,9},{10,8},{12,1... | collective-permute-start | bytes 393224 | tf_op jit(solution)/shard_map/ppermute | solution.py:51
  10.9 4.8 %collective-permute-start.6 = (bf16[64,1024]{1,0:T(8,128)(2,1)S(1)}, bf16[64,1024]{1,0:T(8,128)(2,1)S(1)}, u32[]{:S(2)}, u32[]{:S(2)}) collective-permute-start(bf16[64,1024]{1,0:T(8,128)(2,1)S(1)} %collective-permute-done.2.refs_4_.refs_10_), channel_id=1, source_target_pairs={{0,1},{2,0},{4,2},{6,4},{7,6},{5,7},{3,5},{1,3},{8,9},{10,8},{12,1... | collective-permute-start | bytes 393224 | tf_op jit(solution)/shard_map/ppermute | solution.py:51
  11.2 5.2 %collective-permute-start.5 = (bf16[64,1024]{1,0:T(8,128)(2,1)S(1)}, bf16[64,1024]{1,0:T(8,128)(2,1)S(1)}, u32[]{:S(2)}, u32[]{:S(2)}) collective-permute-start(bf16[64,1024]{1,0:T(8,128)(2,1)S(1)} %collective-permute-done.1.refs_3_.refs_9_), channel_id=1, source_target_pairs={{0,2},{2,4},{4,6},{6,7},{7,5},{5,3},{3,1},{1,0},{8,10},{10,12},{12... | collective-permute-start | bytes 393224 | tf_op jit(solution)/shard_map/ppermute | solution.py:51
  12.5 4.7 %collective-permute-start.8 = (bf16[64,1024]{1,0:T(8,128)(2,1)S(1)}, bf16[64,1024]{1,0:T(8,128)(2,1)S(1)}, u32[]{:S(2)}, u32[]{:S(2)}) collective-permute-start(bf16[64,1024]{1,0:T(8,128)(2,1)S(1)} %collective-permute-done.4.refs_6_.refs_12_), channel_id=1, source_target_pairs={{0,2},{2,4},{4,6},{6,7},{7,5},{5,3},{3,1},{1,0},{8,10},{10,12},{12... | collective-permute-start | bytes 393224 | tf_op jit(solution)/shard_map/ppermute | solution.py:51
  13.7 5.1 %collective-permute-start.11 = (bf16[64,1024]{1,0:T(8,128)(2,1)S(1)}, bf16[64,1024]{1,0:T(8,128)(2,1)S(1)}, u32[]{:S(2)}, u32[]{:S(2)}) collective-permute-start(bf16[64,1024]{1,0:T(8,128)(2,1)S(1)} %collective-permute-done.7.refs_9_.refs_15_), channel_id=1, source_target_pairs={{0,1},{2,0},{4,2},{6,4},{7,6},{5,7},{3,5},{1,3},{8,9},{10,8},{12,1... | collective-permute-start | bytes 393224 | tf_op jit(solution)/shard_map/ppermute | solution.py:51
  15.7 5.1 %collective-permute-start.10 = (bf16[64,1024]{1,0:T(8,128)(2,1)S(1)}, bf16[64,1024]{1,0:T(8,128)(2,1)S(1)}, u32[]{:S(2)}, u32[]{:S(2)}) collective-permute-start(bf16[64,1024]{1,0:T(8,128)(2,1)S(1)} %collective-permute-done.6.refs_8_.refs_14_), channel_id=1, source_target_pairs={{0,1},{2,0},{4,2},{6,4},{7,6},{5,7},{3,5},{1,3},{8,9},{10,8},{12,1... | collective-permute-start | bytes 393224 | tf_op jit(solution)/shard_map/ppermute | solution.py:51
  16.4 5.5 %collective-permute-start.9 = (bf16[64,1024]{1,0:T(8,128)(2,1)S(1)}, bf16[64,1024]{1,0:T(8,128)(2,1)S(1)}, u32[]{:S(2)}, u32[]{:S(2)}) collective-permute-start(bf16[64,1024]{1,0:T(8,128)(2,1)S(1)} %collective-permute-done.5.refs_7_.refs_13_), channel_id=1, source_target_pairs={{0,2},{2,4},{4,6},{6,7},{7,5},{5,3},{3,1},{1,0},{8,10},{10,12},{12... | collective-permute-start | bytes 393224 | tf_op jit(solution)/shard_map/ppermute | solution.py:51
  17.2 5.8 %collective-permute-start.12 = (bf16[64,1024]{1,0:T(8,128)(2,1)S(1)}, bf16[64,1024]{1,0:T(8,128)(2,1)S(1)}, u32[]{:S(2)}, u32[]{:S(2)}) collective-permute-start(bf16[64,1024]{1,0:T(8,128)(2,1)S(1)} %collective-permute-done.8.refs_10_.refs_16_), channel_id=1, source_target_pairs={{0,2},{2,4},{4,6},{6,7},{7,5},{5,3},{3,1},{1,0},{8,10},{10,12},{12... | collective-permute-start | bytes 393224 | tf_op jit(solution)/shard_map/ppermute | solution.py:51
  18.9 4.8 %collective-permute-start.13 = (bf16[64,1024]{1,0:T(8,128)(2,1)S(1)}, bf16[64,1024]{1,0:T(8,128)(2,1)S(1)}, u32[]{:S(2)}, u32[]{:S(2)}) collective-permute-start(bf16[64,1024]{1,0:T(8,128)(2,1)S(1)} %collective-permute-done.11.refs_13_.refs_19_), channel_id=1, source_target_pairs={{0,1},{2,0},{4,2},{6,4},{7,6},{5,7},{3,5},{1,3},{8,9},{10,8},{12,1... | collective-permute-start | bytes 393224 | tf_op jit(solution)/shard_map/ppermute | solution.py:51
  26.1 6.0 %collective-permute-start.18 = (bf16[128,512]{1,0:T(8,128)(2,1)S(1)}, bf16[128,512]{1,0:T(8,128)(2,1)S(1)}, u32[]{:S(2)}, u32[]{:S(2)}) collective-permute-start(bf16[128,512]{1,0:T(8,128)(2,1)S(1)} %get-tuple-element.21.refs_0_), channel_id=1, source_target_pairs={{0,6},{1,7},{2,4},{3,5},{4,2},{5,3},{6,0},{7,1},{8,14},{9,15},{10,... | collective-permute-start | bytes 393224 | tf_op jit(solution)/shard_map/ppermute | solution.py:41
  29.4 5.9 %collective-permute-start.19 = (bf16[128,512]{1,0:T(8,128)(2,1)S(1)}, bf16[128,512]{1,0:T(8,128)(2,1)S(1)}, u32[]{:S(2)}, u32[]{:S(2)}) collective-permute-start(bf16[128,512]{1,0:T(8,128)(2,1)S(1)} %get-tuple-element.21.refs_0_), channel_id=1, source_target_pairs={{0,4},{1,5},{2,6},{3,7},{4,0},{5,1},{6,2},{7,3},{8,12},{9,13},{10,... | collective-permute-start | bytes 393224 | tf_op jit(solution)/shard_map/ppermute | solution.py:41
  29.4 7.5 %collective-permute-start.14 = (bf16[128,512]{1,0:T(8,128)(2,1)S(1)}, bf16[128,512]{1,0:T(8,128)(2,1)S(1)}, u32[]{:S(2)}, u32[]{:S(2)}) collective-permute-start(bf16[128,512]{1,0:T(8,128)(2,1)S(1)} %get-tuple-element.21.refs_0_), channel_id=1, source_target_pairs={{0,1},{1,0},{2,3},{3,2},{4,5},{5,4},{6,7},{7,6},{8,9},{9,8},{10,11... | collective-permute-start | bytes 393224 | tf_op jit(solution)/shard_map/ppermute | solution.py:41
  30.2 6.7 %collective-permute-start.15 = (bf16[128,512]{1,0:T(8,128)(2,1)S(1)}, bf16[128,512]{1,0:T(8,128)(2,1)S(1)}, u32[]{:S(2)}, u32[]{:S(2)}) collective-permute-start(bf16[128,512]{1,0:T(8,128)(2,1)S(1)} %get-tuple-element.21.refs_0_), channel_id=1, source_target_pairs={{0,2},{1,3},{2,0},{3,1},{4,6},{5,7},{6,4},{7,5},{8,10},{9,11},{10,... | collective-permute-start | bytes 393224 | tf_op jit(solution)/shard_map/ppermute | solution.py:41
  30.6 8.3 %collective-permute-start.16 = (bf16[128,512]{1,0:T(8,128)(2,1)S(1)}, bf16[128,512]{1,0:T(8,128)(2,1)S(1)}, u32[]{:S(2)}, u32[]{:S(2)}) collective-permute-start(bf16[128,512]{1,0:T(8,128)(2,1)S(1)} %get-tuple-element.21.refs_0_), channel_id=1, source_target_pairs={{0,3},{1,2},{2,1},{3,0},{4,7},{5,6},{6,5},{7,4},{8,11},{9,10},{10,... | collective-permute-start | bytes 393224 | tf_op jit(solution)/shard_map/ppermute | solution.py:41
  35.3 13.7 %collective-permute-start.21 = (bf16[256,512]{1,0:T(8,128)(2,1)S(1)}, bf16[256,512]{1,0:T(8,128)(2,1)S(1)}, u32[]{:S(2)}, u32[]{:S(2)}) collective-permute-start(bf16[256,512]{1,0:T(8,128)(2,1)S(1)} %pack.3.refs_1_.refs_2_), channel_id=1, source_target_pairs={{0,1},{1,0},{2,3},{3,2},{4,5},{5,4},{6,7},{7,6},{8,9},{9,8},{10,11... | collective-permute-start | bytes 786440 | tf_op jit(solution)/shard_map/ppermute | solution.py:41
  38.9 17.1 %collective-permute-start.17 = (bf16[512,512]{1,0:T(8,128)(2,1)S(1)}, bf16[512,512]{1,0:T(8,128)(2,1)S(1)}, u32[]{:S(2)}, u32[]{:S(2)}) collective-permute-start(bf16[512,512]{1,0:T(8,128)(2,1)S(1)} %pack.2.refs_0_.refs_1_), channel_id=1, source_target_pairs={{0,8},{8,16},{16,24},{1,9},{9,17},{17,25},{2,10},{10,18},{18,26},{... | collective-permute-start | bytes 1572872 | tf_op jit(solution)/shard_map/ppermute | solution.py:28
  47.1 8.9 %collective-permute-start.20 = (bf16[256,512]{1,0:T(8,128)(2,1)S(1)}, bf16[256,512]{1,0:T(8,128)(2,1)S(1)}, u32[]{:S(2)}, u32[]{:S(2)}) collective-permute-start(bf16[256,512]{1,0:T(8,128)(2,1)S(1)} %pack.3.refs_1_.refs_2_), channel_id=1, source_target_pairs={{0,8},{8,16},{16,24},{1,9},{9,17},{17,25},{2,10},{10,18},{18,26},{... | collective-permute-start | bytes 786440 | tf_op jit(solution)/shard_map/ppermute | solution.py:28
  49.0 9.8 %collective-permute-start.22 = (bf16[256,512]{1,0:T(8,128)(2,1)S(1)}, bf16[256,512]{1,0:T(8,128)(2,1)S(1)}, u32[]{:S(2)}, u32[]{:S(2)}) collective-permute-start(bf16[256,512]{1,0:T(8,128)(2,1)S(1)} %collective-permute-done.21.refs_2_.refs_3_), channel_id=1, source_target_pairs={{0,8},{8,16},{16,24},{1,9},{9,17},{17,25},{2,10},{10,18},{18,26},{... | collective-permute-start | bytes 786440 | tf_op jit(solution)/shard_map/ppermute | solution.py:28
  61.8 11.5 %collective-permute-start.27 = (bf16[512,512]{1,0:T(8,128)(2,1)S(1)}, bf16[512,512]{1,0:T(8,128)(2,1)S(1)}, u32[]{:S(2)}, u32[]{:S(2)}) collective-permute-start(bf16[512,512]{1,0:T(8,128)(2,1)S(1)} %get-tuple-element.30), channel_id=1, source_target_pairs={{8,0},{16,8},{24,16},{9,1},{17,9},{25,17},{10,2},{18,10},{26,18},{... | collective-permute-start | bytes 1572872 | tf_op jit(solution)/shard_map/ppermute | solution.py:28
  65.6 13.4 %collective-permute-start.23 = (bf16[512,512]{1,0:T(8,128)(2,1)S(1)}, bf16[512,512]{1,0:T(8,128)(2,1)S(1)}, u32[]{:S(2)}, u32[]{:S(2)}) collective-permute-start(bf16[512,512]{1,0:T(8,128)(2,1)S(1)} %get-tuple-element.24), channel_id=1, source_target_pairs={{8,0},{16,8},{24,16},{9,1},{17,9},{25,17},{10,2},{18,10},{26,18},{... | collective-permute-start | bytes 1572872 | tf_op jit(solution)/shard_map/ppermute | solution.py:28
  73.5 8.3 %collective-permute-start.28 = (bf16[256,512]{1,0:T(8,128)(2,1)S(1)}, bf16[256,512]{1,0:T(8,128)(2,1)S(1)}, u32[]{:S(2)}, u32[]{:S(2)}) collective-permute-start(bf16[256,512]{1,0:T(8,128)(2,1)S(1)} %get-tuple-element.32), channel_id=1, source_target_pairs={{0,1},{1,0},{2,3},{3,2},{4,5},{5,4},{6,7},{7,6},{8,9},{9,8},{10,11... | collective-permute-start | bytes 786440 | tf_op jit(solution)/shard_map/ppermute | solution.py:41
  79.1 14.4 %collective-permute-start.24 = (bf16[128,512]{1,0:T(8,128)(2,1)S(1)}, bf16[128,512]{1,0:T(8,128)(2,1)S(1)}, u32[]{:S(2)}, u32[]{:S(2)}) collective-permute-start(bf16[128,512]{1,0:T(8,128)(2,1)S(1)} %get-tuple-element.26), channel_id=1, source_target_pairs={{0,1},{1,0},{2,3},{3,2},{4,5},{5,4},{6,7},{7,6},{8,9},{9,8},{10,11... | collective-permute-start | bytes 393224 | tf_op jit(solution)/shard_map/ppermute | solution.py:41
  79.9 13.6 %collective-permute-start.25 = (bf16[128,512]{1,0:T(8,128)(2,1)S(1)}, bf16[128,512]{1,0:T(8,128)(2,1)S(1)}, u32[]{:S(2)}, u32[]{:S(2)}) collective-permute-start(bf16[128,512]{1,0:T(8,128)(2,1)S(1)} %get-tuple-element.27), channel_id=1, source_target_pairs={{0,2},{1,3},{2,0},{3,1},{4,6},{5,7},{6,4},{7,5},{8,10},{9,11},{10,... | collective-permute-start | bytes 393224 | tf_op jit(solution)/shard_map/ppermute | solution.py:41
  80.0 13.5 %collective-permute-start.26 = (bf16[128,512]{1,0:T(8,128)(2,1)S(1)}, bf16[128,512]{1,0:T(8,128)(2,1)S(1)}, u32[]{:S(2)}, u32[]{:S(2)}) collective-permute-start(bf16[128,512]{1,0:T(8,128)(2,1)S(1)} %get-tuple-element.28), channel_id=1, source_target_pairs={{0,3},{1,2},{2,1},{3,0},{4,7},{5,6},{6,5},{7,4},{8,11},{9,10},{10,... | collective-permute-start | bytes 393224 | tf_op jit(solution)/shard_map/ppermute | solution.py:41
  81.8 11.7 %collective-permute-start.29 = (bf16[128,512]{1,0:T(8,128)(2,1)S(1)}, bf16[128,512]{1,0:T(8,128)(2,1)S(1)}, u32[]{:S(2)}, u32[]{:S(2)}) collective-permute-start(bf16[128,512]{1,0:T(8,128)(2,1)S(1)} %get-tuple-element.33), channel_id=1, source_target_pairs={{0,6},{1,7},{2,4},{3,5},{4,2},{5,3},{6,0},{7,1},{8,14},{9,15},{10,... | collective-permute-start | bytes 393224 | tf_op jit(solution)/shard_map/ppermute | solution.py:41
  83.7 9.8 %collective-permute-start.30 = (bf16[128,512]{1,0:T(8,128)(2,1)S(1)}, bf16[128,512]{1,0:T(8,128)(2,1)S(1)}, u32[]{:S(2)}, u32[]{:S(2)}) collective-permute-start(bf16[128,512]{1,0:T(8,128)(2,1)S(1)} %get-tuple-element.34), channel_id=1, source_target_pairs={{0,4},{1,5},{2,6},{3,7},{4,0},{5,1},{6,2},{7,3},{8,12},{9,13},{10,... | collective-permute-start | bytes 393224 | tf_op jit(solution)/shard_map/ppermute | solution.py:41

commit v6 on v5

--- a/solution.py
+++ b/solution.py
@@ -177,6 +177,14 @@
         total_ref[here, :] = decoded(w_ref, 0, here, parts, BLOCKS, tok, None)
 
 
+def near_recon_kernel(part_ref, before_ref, w_ref, total_ref):
+    tok = total_ref.shape[1]
+    steps, tile = tiles(w_ref.shape[1])
+    for j in range(steps):
+        here = slice(j * tile, (j + 1) * tile)
+        total_ref[here, :] = decoded(w_ref, 1, here, [part_ref], BLOCKS[:1], tok, before_ref[here, :])
+
+
 def products(error_ref, w_ref, slot, masks, out_ref):
     tok = error_ref.shape[0]
     for row, mask in enumerate(masks):
@@ -187,13 +195,14 @@
 
 
 def recon_kernel(scale, *refs):
-    parts, (total_ref, w_ref, b_ref, target_ref, error_ref, far_ref) = refs[: len(BLOCKS)], refs[len(BLOCKS) :]
+    rest = BLOCKS[1:]
+    parts, (total_ref, w_ref, b_ref, target_ref, error_ref, far_ref) = refs[: len(rest)], refs[len(rest) :]
     tok = total_ref.shape[1]
     steps, tile = tiles(w_ref.shape[1])
 
     for j in range(steps):
         here = slice(j * tile, (j + 1) * tile)
-        total = decoded(w_ref, 1, here, parts, BLOCKS, tok, total_ref[here, :])
+        total = decoded(w_ref, 1, here, parts, rest, tok, total_ref[here, :])
         error = total.T + b_ref[:, here] - target_ref[:, here].astype(F32)
         error_ref[:, here] = (error * scale).astype(BF16)
 
@@ -206,13 +215,29 @@
     products(error_ref, w_ref, 0, NEAR, near_ref)
 
 
-def dec_grad_kernel(groups, *refs):
-    error_ref, parts, out_ref = refs[0], refs[1 : 1 + len(groups)], refs[-1]
-    width = parts[0].shape[1]
-    tok = error_ref.shape[0]
-    for i, row, mask in flat(groups):
-        part = parts[i][row * tok : (row + 1) * tok, :]
-        out_ref[0, 0, :, columns(owner(mask), width)] = transposed(error_ref[...], part).astype(BF16)
+def written(blocks, left_ref, width, target, held, sems):
+    steps, tile = tiles(left_ref.shape[0])
+    copies = []
+    for k, (value, index) in enumerate(blocks):
+        buffer = held.at[k % 2]
+        if k >= 2:
+            copies[k - 2].wait()
+        for j in range(steps):
+            here = slice(j * tile, (j + 1) * tile)
+            buffer[here, :] = jnp.dot(left_ref[here, :], value, preferred_element_type=F32).astype(BF16)
+        copies.append(pltpu.make_async_copy(buffer, target(columns(index, width)), sems.at[k % 2]))
+        copies[k].start()
+    for copy in copies[-2:]:
+        copy.wait()
+
+
+def dec_grad_kernel(slot, held_count, *refs):
+    error_ref, parts = refs[0], refs[1 : 1 + len(BLOCKS)]
+    out_ref, left_ref, held, sems = refs[1 + len(BLOCKS) + held_count :]
+    tok, width = error_ref.shape[0], parts[0].shape[1]
+    left_ref[...] = error_ref[...].T
+    blocks = [(parts[i][row * tok : (row + 1) * tok, :], owner(mask)) for i, row, mask in flat(BLOCKS)]
+    written(blocks, left_ref, width, lambda here: out_ref.at[0, slot, :, here], held, sems)
 
 
 def add_kernel(own_ref, arrived_ref, *outs):
@@ -224,15 +249,14 @@
 
 
 def enc_grad_kernel(*refs):
-    grads, parts = refs[: -2 - 2 * COUNT], refs[-2 - 2 * COUNT : -2]
-    active_ref, out_ref = refs[-2:]
-    width = parts[0].shape[1]
+    grads, parts = refs[: -5 - 2 * COUNT], refs[-5 - 2 * COUNT : -5]
+    active_ref, out_ref, left_ref, held, sems = refs[-5:]
     total = grads[0][...]
     for grad in grads[1:]:
         total = total + grad[...].astype(F32)
-    pre_grad = (total * 2.0 * active_ref[...]).astype(BF16)
-    for k, offset in enumerate(OFFSETS):
-        out_ref[0, :, columns(ring_owner(offset), width)] = transposed(pre_grad, block(parts, k)).astype(BF16)
+    left_ref[...] = (total * 2.0 * active_ref[...]).astype(BF16).T
+    blocks = [(block(parts, k), ring_owner(offset)) for k, offset in enumerate(OFFSETS)]
+    written(blocks, left_ref, parts[0].shape[1], lambda here: out_ref.at[0, :, here], held, sems)
 
 
 def cost(flops, moved):
@@ -281,15 +305,25 @@
         cost_estimate=cost(matmul, 0),
     )(*own, weights)
 
+    total = pl.pallas_call(
+        near_recon_kernel,
+        name="near_recon",
+        out_shape=struct((width, tok), F32),
+        in_specs=vmem(3),
+        out_specs=vmem(1)[0],
+        compiler_params=params(8),
+        cost_estimate=cost(matmul // 2, 0),
+    )(previous[0], total, weights)
+
     error, sent_far = pl.pallas_call(
         functools.partial(recon_kernel, scale),
         name="recon",
         out_shape=(struct((tok, width), BF16), stack(FAR + CROSSING, BF16)),
-        in_specs=vmem(len(previous) + 4),
+        in_specs=vmem(len(previous) + 3),
         out_specs=tuple(vmem(2)),
         compiler_params=params(8),
         cost_estimate=cost(2 * matmul, 4 * MIB),
-    )(*previous, total, weights, dec_b, targets[0])
+    )(*previous[1:], total, weights, dec_b, targets[0])
     arrived_far = from_behind(sent_far, "section", -1)
 
     sent_near, own_near, own_far = pl.pallas_call(
@@ -303,26 +337,29 @@
     )(error, weights)
     arrived_near = from_behind(sent_near, "section", -1)
 
-    rows = 256 if width % 256 == 0 else LANES
-
-    def dec_grad_slot(slot, groups, parts, *held):
+    def buffers(rows, block_width):
+        return [
+            pltpu.VMEM((rows, tok), BF16),
+            pltpu.VMEM((2, rows, block_width), BF16),
+            pltpu.SemaphoreType.DMA((2,)),
+        ]
+
+    in_hbm = pl.BlockSpec(memory_space=pltpu.HBM)
+
+    def dec_grad_slot(slot, parts, *held):
         return pl.pallas_call(
-            functools.partial(dec_grad_kernel, groups),
+            functools.partial(dec_grad_kernel, slot, len(held)),
             name="dec_grad",
-            grid=(width // rows,),
             out_shape=struct(dec_w.shape, BF16),
-            in_specs=[
-                pl.BlockSpec((tok, rows), lambda j: (0, j)),
-                *[pl.BlockSpec(part.shape, lambda j: (0, 0)) for part in parts],
-                *[pl.BlockSpec(memory_space=pltpu.HBM) for _ in held],
-            ],
-            out_specs=pl.BlockSpec((1, 1, rows, features), lambda j: (0, slot, j, 0)),
+            in_specs=[*vmem(1 + len(parts)), *[in_hbm for _ in held]],
+            out_specs=in_hbm,
+            scratch_shapes=buffers(width, own_features),
             input_output_aliases={1 + len(parts): 0} if held else {},
-            compiler_params=params(12),
+            compiler_params=params(8),
             cost_estimate=cost(matmul, 2 * width * features),
         )(error, *parts, *held)
 
-    dec_grad = dec_grad_slot(0, BLOCKS, own)
+    dec_grad = dec_grad_slot(0, own)
 
     def sums(outs, own_part, arrived):
         return pl.pallas_call(
@@ -344,20 +381,16 @@
         *[exchanged(line, mask) for mask, line in zip(FAR, lines)],
     ]
     held_grad = pltpu.with_memory_space_constraint(dec_grad, pltpu.HBM)
-    dec_grad = dec_grad_slot(1, BLOCKS, previous, held_grad)
+    dec_grad = dec_grad_slot(1, previous, held_grad)
 
     enc_grad = pl.pallas_call(
         enc_grad_kernel,
         name="enc_grad",
-        grid=(own_features // LANES,),
         out_shape=struct(enc_w.shape, BF16),
-        in_specs=[
-            *[pl.BlockSpec((tok, LANES), lambda j: (0, j))] * len(grads),
-            *[pl.BlockSpec((tok // 2, width), lambda j: (0, 0))] * (2 * count),
-            pl.BlockSpec((tok, LANES), lambda j: (0, j)),
-        ],
-        out_specs=pl.BlockSpec((1, LANES, model), lambda j: (0, j, 0)),
-        compiler_params=params(16),
+        in_specs=vmem(len(grads) + 2 * count + 1),
+        out_specs=in_hbm,
+        scratch_shapes=buffers(own_features, width),
+        compiler_params=params(8),
         cost_estimate=cost(matmul, 2 * own_features * model),
     )(*grads, *inputs_of, active)
     return enc_grad, dec_grad

time: 99 us -> 102 us (1.030)
  waiting for transfers between devices: 30.5 us -> 23.1 us
  starting transfers between devices: 41.4 us -> 48 us
  Pallas kernels: 24.9 us -> 28.3 us
    ppermute x5, starting transfers between devices: 17 us -> 23.8 us  [from_behind(): lax.ppermute(value, axis, [(source, source + steps) for source in range(i...]
    ppermute x5, waiting for transfers between devices: 14.8 us -> 10.2 us  [from_behind(): lax.ppermute(value, axis, [(source, source + steps) for source in range(i...]
    pallas_call x3 -> x4, Pallas kernels: 15 us -> 19.5 us  [the longest x2 12.1 us: dec_grad_slot(): pl.pallas_call(functools.partial(dec_grad_kernel, slot, len(held)), name=...]
    ppermute x12, waiting for transfers between devices: 5.21 us -> 2.43 us  [exchanged(): return lax.ppermute(value, 'feat', [(i, i ^ mask) for i in range(count)])]
    pallas_call x1, Pallas kernels: 3 us -> 1.94 us  [on_device(): pl.pallas_call(functools.partial(recon_kernel, scale), name='recon', out_...]
  transfers between devices with their start and end apart: 31 -> 31, of which waited for: 15 -> 13; matrix products, arithmetic and copies ran while one was open for 0% -> 0% of each run, Pallas kernels for 14% -> 17%
where the time goes in v6:
time: 102 us
  starting transfers between devices  48 us (47%)
  Pallas kernels  28.3 us (28%)
  waiting for transfers between devices  23.1 us (23%)
  local copies, waits for them, and re-layouts  1.13 us (1%)
  between operations  1.12 us (1%)
    ppermute x5, starting transfers between devices, from_behind(): lax.ppermute(value, axis, [(source, source + steps) for source in range(i...  23.8 us
    ppermute x12, starting transfers between devices, exchanged(): return lax.ppermute(value, 'feat', [(i, i ^ mask) for i in range(count)])  12.8 us
    pallas_call x2, Pallas kernels, dec_grad_slot(): pl.pallas_call(functools.partial(dec_grad_kernel, slot, len(held)), name=...  12.1 us
    ppermute x14, starting transfers between devices, passed_on(): lax.ppermute(value, 'feat', [(order[p], order[(p + by) % count]) for p in...  11.4 us
    ppermute x14, waiting for transfers between devices, passed_on(): lax.ppermute(value, 'feat', [(order[p], order[(p + by) % count]) for p in...  10.5 us
    ppermute x5, waiting for transfers between devices, from_behind(): lax.ppermute(value, axis, [(source, source + steps) for source in range(i...  10.2 us
    pallas_call x1, Pallas kernels, on_device(): pl.pallas_call(enc_grad_kernel, name='enc_grad', out_shape=struct(enc_w.s...  6.19 us
    ppermute x12, waiting for transfers between devices, exchanged(): return lax.ppermute(value, 'feat', [(i, i ^ mask) for i in range(count)])  2.43 us
  transfers between devices with their start and end apart: 31, of which 13 were waited for; matrix products, arithmetic and copies ran while one was open for 0% of the time, Pallas kernels for 17%

profile of v6, /device:TPU:1, one launch (start us, length us, event | category | flops | bytes accessed | tf_op | source)
XLA Modules:
  0.0 101.7 jit_solution(4321563708511137256)
XLA Ops:
  0.7 1.1 %copy-done.4 = bf16[1,128,1024]{2,1,0:T(8,128)(2,1)S(1)} copy-done((bf16[1,128,1024]{2,1,0:T(8,128)(2,1)S(1)}, bf16[1,128,1024]{2,1,0:T(8,128)(2,1)}, u32[]{:S(2)}) %copy-start.4) | copy-done | bytes 262168
  1.8 2.2 %collective-permute-start = (bf16[64,1024]{1,0:T(8,128)(2,1)S(1)}, bf16[64,1024]{1,0:T(8,128)(2,1)S(1)}, u32[]{:S(2)}, u32[]{:S(2)}) collective-permute-start(bf16[64,1024]{1,0:T(8,128)(2,1)S(1)} %get-tuple-element.19.refs_0_.refs_6_), channel_id=1, source_target_pairs={{0,2},{2,4},{4,6},{6,7},{7,5},{5,3},{3,1},{1,0},{8,10},{10,12},{12... | collective-permute-start | bytes 393224 | tf_op jit(solution)/shard_map/ppermute | solution.py:51
  4.0 1.4 %collective-permute-start.2 = (bf16[64,1024]{1,0:T(8,128)(2,1)S(1)}, bf16[64,1024]{1,0:T(8,128)(2,1)S(1)}, u32[]{:S(2)}, u32[]{:S(2)}) collective-permute-start(bf16[64,1024]{1,0:T(8,128)(2,1)S(1)} %get-tuple-element.19.refs_0_.refs_6_), channel_id=1, source_target_pairs={{0,1},{2,0},{4,2},{6,4},{7,6},{5,7},{3,5},{1,3},{8,9},{10,8},{12,1... | collective-permute-start | bytes 393224 | tf_op jit(solution)/shard_map/ppermute | solution.py:51
  5.5 1.7 %collective-permute-done.refs_2_.refs_8_ = bf16[64,1024]{1,0:T(8,128)(2,1)S(1)} collective-permute-done((bf16[64,1024]{1,0:T(8,128)(2,1)S(1)}, bf16[64,1024]{1,0:T(8,128)(2,1)S(1)}, u32[]{:S(2)}, u32[]{:S(2)}) %collective-permute-start) | collective-permute-done | bytes 131104 | tf_op jit(solution)/shard_map/ppermute | solution.py:51
  7.1 1.2 %collective-permute-start.4 = (bf16[64,1024]{1,0:T(8,128)(2,1)S(1)}, bf16[64,1024]{1,0:T(8,128)(2,1)S(1)}, u32[]{:S(2)}, u32[]{:S(2)}) collective-permute-start(bf16[64,1024]{1,0:T(8,128)(2,1)S(1)} %collective-permute-done.refs_2_.refs_8_), channel_id=1, source_target_pairs={{0,2},{2,4},{4,6},{6,7},{7,5},{5,3},{3,1},{1,0},{8,10},{10,12},{12... | collective-permute-start | bytes 393224 | tf_op jit(solution)/shard_map/ppermute | solution.py:51
  8.3 0.3 collective-permute-start.7
  8.6 2.2 %collective-permute-done.2.refs_4_.refs_10_ = bf16[64,1024]{1,0:T(8,128)(2,1)S(1)} collective-permute-done((bf16[64,1024]{1,0:T(8,128)(2,1)S(1)}, bf16[64,1024]{1,0:T(8,128)(2,1)S(1)}, u32[]{:S(2)}, u32[]{:S(2)}) %collective-permute-start.2) | collective-permute-done | bytes 131104 | tf_op jit(solution)/shard_map/ppermute | solution.py:51
  10.8 0.3 collective-permute-start.6
  11.2 1.1 %collective-permute-start.5 = (bf16[64,1024]{1,0:T(8,128)(2,1)S(1)}, bf16[64,1024]{1,0:T(8,128)(2,1)S(1)}, u32[]{:S(2)}, u32[]{:S(2)}) collective-permute-start(bf16[64,1024]{1,0:T(8,128)(2,1)S(1)} %collective-permute-done.1.refs_3_.refs_9_), channel_id=1, source_target_pairs={{0,2},{2,4},{4,6},{6,7},{7,5},{5,3},{3,1},{1,0},{8,10},{10,12},{12... | collective-permute-start | bytes 393224 | tf_op jit(solution)/shard_map/ppermute | solution.py:51
  12.3 0.1 collective-permute-done.4.refs_6_.refs_12_
  12.4 1.3 %collective-permute-start.8 = (bf16[64,1024]{1,0:T(8,128)(2,1)S(1)}, bf16[64,1024]{1,0:T(8,128)(2,1)S(1)}, u32[]{:S(2)}, u32[]{:S(2)}) collective-permute-start(bf16[64,1024]{1,0:T(8,128)(2,1)S(1)} %collective-permute-done.4.refs_6_.refs_12_), channel_id=1, source_target_pairs={{0,2},{2,4},{4,6},{6,7},{7,5},{5,3},{3,1},{1,0},{8,10},{10,12},{12... | collective-permute-start | bytes 393224 | tf_op jit(solution)/shard_map/ppermute | solution.py:51
  13.7 0.2 collective-permute-start.11
  13.9 1.8 %collective-permute-done.6.refs_8_.refs_14_ = bf16[64,1024]{1,0:T(8,128)(2,1)S(1)} collective-permute-done((bf16[64,1024]{1,0:T(8,128)(2,1)S(1)}, bf16[64,1024]{1,0:T(8,128)(2,1)S(1)}, u32[]{:S(2)}, u32[]{:S(2)}) %collective-permute-start.6) | collective-permute-done | bytes 131104 | tf_op jit(solution)/shard_map/ppermute | solution.py:51
  15.7 0.7 collective-permute-start.10
  16.3 0.8 collective-permute-start.9
  17.1 1.3 %collective-permute-start.12 = (bf16[64,1024]{1,0:T(8,128)(2,1)S(1)}, bf16[64,1024]{1,0:T(8,128)(2,1)S(1)}, u32[]{:S(2)}, u32[]{:S(2)}) collective-permute-start(bf16[64,1024]{1,0:T(8,128)(2,1)S(1)} %collective-permute-done.8.refs_10_.refs_16_), channel_id=1, source_target_pairs={{0,2},{2,4},{4,6},{6,7},{7,5},{5,3},{3,1},{1,0},{8,10},{10,12},{12... | collective-permute-start | bytes 393224 | tf_op jit(solution)/shard_map/ppermute | solution.py:51
  18.4 0.4 collective-permute-done.11.refs_13_.refs_19_
  18.8 0.5 collective-permute-start.13
  19.4 1.4 %collective-permute-done.10.refs_12_.refs_18_ = bf16[64,1024]{1,0:T(8,128)(2,1)S(1)} collective-permute-done((bf16[64,1024]{1,0:T(8,128)(2,1)S(1)}, bf16[64,1024]{1,0:T(8,128)(2,1)S(1)}, u32[]{:S(2)}, u32[]{:S(2)}) %collective-permute-start.10) | collective-permute-done | bytes 131104 | tf_op jit(solution)/shard_map/ppermute | solution.py:51
  20.7 1.1 %collective-permute-done.9.refs_11_.refs_17_ = bf16[64,1024]{1,0:T(8,128)(2,1)S(1)} collective-permute-done((bf16[64,1024]{1,0:T(8,128)(2,1)S(1)}, bf16[64,1024]{1,0:T(8,128)(2,1)S(1)}, u32[]{:S(2)}, u32[]{:S(2)}) %collective-permute-start.9) | collective-permute-done | bytes 131104 | tf_op jit(solution)/shard_map/ppermute | solution.py:51
  21.8 1.1 %collective-permute-done.12.refs_14_.refs_20_ = bf16[64,1024]{1,0:T(8,128)(2,1)S(1)} collective-permute-done((bf16[64,1024]{1,0:T(8,128)(2,1)S(1)}, bf16[64,1024]{1,0:T(8,128)(2,1)S(1)}, u32[]{:S(2)}, u32[]{:S(2)}) %collective-permute-start.12) | collective-permute-done | bytes 131104 | tf_op jit(solution)/shard_map/ppermute | solution.py:51
  23.0 0.7 collective-permute-done.13.refs_15_.refs_21_
  23.6 2.4 %pre.1 = (bf16[128,512]{1,0:T(8,128)(2,1)S(1)}, f32[128,512]{1,0:T(8,128)S(1)}) custom-call(bf16[64,1024]{1,0:T(8,128)(2,1)S(1)} %get-tuple-element.19.refs_0_.refs_6_, bf16[64,1024]{1,0:T(8,128)(2,1)S(1)} %get-tuple-element.20.refs_1_.refs_7_, bf16[64,1024]{1,0:T(8,128)(2,1)S(1)} %collective-permute-done.refs_2_.refs_8_, ...), custom_call_target="tpu_custom_call" | custom-call | flops 1073741824 | tf_op jit(solution)/shard_map/pre/pallas_call | solution.py:283
  26.1 0.8 collective-permute-start.19
  26.9 1.3 %collective-permute-start.20 = (bf16[128,512]{1,0:T(8,128)(2,1)S(1)}, bf16[128,512]{1,0:T(8,128)(2,1)S(1)}, u32[]{:S(2)}, u32[]{:S(2)}) collective-permute-start(bf16[128,512]{1,0:T(8,128)(2,1)S(1)} %get-tuple-element.21.refs_0_), channel_id=1, source_target_pairs={{0,2},{1,3},{2,0},{3,1},{4,6},{5,7},{6,4},{7,5},{8,10},{9,11},{10,... | collective-permute-start | bytes 393224 | tf_op jit(solution)/shard_map/ppermute | solution.py:41
  28.2 0.6 collective-permute-start.21
  28.8 3.3 %collective-permute-start.14 = (bf16[128,512]{1,0:T(8,128)(2,1)S(1)}, bf16[128,512]{1,0:T(8,128)(2,1)S(1)}, u32[]{:S(2)}, u32[]{:S(2)}) collective-permute-start(bf16[128,512]{1,0:T(8,128)(2,1)S(1)} %get-tuple-element.21.refs_0_), channel_id=1, source_target_pairs={{0,6},{1,7},{2,4},{3,5},{4,2},{5,3},{6,0},{7,1},{8,14},{9,15},{10,... | collective-permute-start | bytes 393224 | tf_op jit(solution)/shard_map/ppermute | solution.py:41
  32.1 0.8 collective-permute-done.21.refs_3_
  32.9 11.3 %collective-permute-start.22 = (bf16[512,512]{1,0:T(8,128)(2,1)S(1)}, bf16[512,512]{1,0:T(8,128)(2,1)S(1)}, u32[]{:S(2)}, u32[]{:S(2)}) collective-permute-start(bf16[512,512]{1,0:T(8,128)(2,1)S(1)} %pack.3.refs_0_.refs_1_), channel_id=1, source_target_pairs={{0,8},{8,16},{16,24},{1,9},{9,17},{17,25},{2,10},{10,18},{18,26},{... | collective-permute-start | bytes 1572872 | tf_op jit(solution)/shard_map/ppermute | solution.py:28
  44.3 0.8 collective-permute-start.17
  45.1 4.1 %collective-permute-start.16 = (bf16[256,512]{1,0:T(8,128)(2,1)S(1)}, bf16[256,512]{1,0:T(8,128)(2,1)S(1)}, u32[]{:S(2)}, u32[]{:S(2)}) collective-permute-start(bf16[256,512]{1,0:T(8,128)(2,1)S(1)} %pack.2.refs_1_.refs_2_), channel_id=1, source_target_pairs={{0,8},{8,16},{16,24},{1,9},{9,17},{17,25},{2,10},{10,18},{18,26},{... | collective-permute-start | bytes 786440 | tf_op jit(solution)/shard_map/ppermute | solution.py:28
  49.2 1.6 %collective-permute-done.17.refs_2_.refs_3_ = bf16[256,512]{1,0:T(8,128)(2,1)S(1)} collective-permute-done((bf16[256,512]{1,0:T(8,128)(2,1)S(1)}, bf16[256,512]{1,0:T(8,128)(2,1)S(1)}, u32[]{:S(2)}, u32[]{:S(2)}) %collective-permute-start.17) | collective-permute-done | bytes 262176 | tf_op jit(solution)/shard_map/ppermute | solution.py:41
  50.8 4.3 %collective-permute-start.18 = (bf16[256,512]{1,0:T(8,128)(2,1)S(1)}, bf16[256,512]{1,0:T(8,128)(2,1)S(1)}, u32[]{:S(2)}, u32[]{:S(2)}) collective-permute-start(bf16[256,512]{1,0:T(8,128)(2,1)S(1)} %collective-permute-done.17.refs_2_.refs_3_), channel_id=1, source_target_pairs={{0,8},{8,16},{16,24},{1,9},{9,17},{17,25},{2,10},{10,18},{18,26},{... | collective-permute-start | bytes 786440 | tf_op jit(solution)/shard_map/ppermute | solution.py:28
  55.2 2.3 %own_recon.1.before_ref = f32[1024,128]{1,0:T(8,128)S(1)} custom-call(bf16[512,512]{1,0:T(8,128)(2,1)S(1)} %pack.3.refs_0_.refs_1_, bf16[256,512]{1,0:T(8,128)(2,1)S(1)} %pack.2.refs_1_.refs_2_, bf16[256,512]{1,0:T(8,128)(2,1)S(1)} %collective-permute-done.17.refs_2_.refs_3_, bf16[2,1024,4096]{2,1,0:T(8,128)(2,1)S(1)} %bitcast.6), custom_call_target="tpu_custom_call" | custom-call | flops 1073741824 | tf_op jit(solution)/shard_map/own_recon/pallas_call | solution.py:298
  57.5 1.2 %near_recon.1.refs_2_ = f32[1024,128]{1,0:T(8,128)S(1)} custom-call(bf16[512,512]{1,0:T(8,128)(2,1)S(1)} %collective-permute-done.22.part_ref.refs_1_, f32[1024,128]{1,0:T(8,128)S(1)} %own_recon.1.before_ref, bf16[2,1024,4096]{2,1,0:T(8,128)(2,1)S(1)} %bitcast.7), custom_call_target="tpu_custom_call" | custom-call | flops 536870912 | tf_op jit(solution)/shard_map/near_recon/pallas_call | solution.py:308
  58.8 1.9 %recon.1 = (bf16[128,1024]{1,0:T(8,128)(2,1)S(1)}, bf16[512,512]{1,0:T(8,128)(2,1)S(1)}) custom-call(bf16[256,512]{1,0:T(8,128)(2,1)S(1)} %collective-permute-done.16.refs_0_.refs_2_, bf16[256,512]{1,0:T(8,128)(2,1)S(1)} %collective-permute-done.18.refs_1_.refs_3_, f32[1024,128]{1,0:T(8,128)S(1)} %near_recon.1.refs_2_, bf16[2,1024,4096]{2,1,0:T(8,128)(2,1)S(1)} %bitcast.8, ...), custom_call_target="tpu_custom_call" | custom-call | flops 2147483648 | bytes 4194304 | tf_op jit(solution)/shard_map/recon/pallas_call | solution.py:318
  60.7 1.9 %collective-permute-start.27 = (bf16[512,512]{1,0:T(8,128)(2,1)S(1)}, bf16[512,512]{1,0:T(8,128)(2,1)S(1)}, u32[]{:S(2)}, u32[]{:S(2)}) collective-permute-start(bf16[512,512]{1,0:T(8,128)(2,1)S(1)} %get-tuple-element.30), channel_id=1, source_target_pairs={{8,0},{16,8},{24,16},{9,1},{17,9},{25,17},{10,2},{18,10},{26,18},{... | collective-permute-start | bytes 1572872 | tf_op jit(solution)/shard_map/ppermute | solution.py:28
  62.7 1.8 %own_grad.1 = (bf16[512,512]{1,0:T(8,128)(2,1)S(1)}, f32[512,512]{1,0:T(8,128)S(1)}, f32[512,512]{1,0:T(8,128)S(1)}) custom-call(bf16[128,1024]{1,0:T(8,128)(2,1)S(1)} %get-tuple-element.22.error_ref.refs_0_, bf16[2,1024,4096]{2,1,0:T(8,128)(2,1)S(1)} %bitcast.9), custom_call_target="tpu_custom_call" | custom-call | flops 1610612736 | bytes 6291456 | tf_op jit(solution)/shard_map/own_grad/pallas_call | solution.py:329
  64.5 2.1 %collective-permute-start.23 = (bf16[512,512]{1,0:T(8,128)(2,1)S(1)}, bf16[512,512]{1,0:T(8,128)(2,1)S(1)}, u32[]{:S(2)}, u32[]{:S(2)}) collective-permute-start(bf16[512,512]{1,0:T(8,128)(2,1)S(1)} %get-tuple-element.24), channel_id=1, source_target_pairs={{8,0},{16,8},{24,16},{9,1},{17,9},{25,17},{10,2},{18,10},{26,18},{... | collective-permute-start | bytes 1572872 | tf_op jit(solution)/shard_map/ppermute | solution.py:28
  66.6 5.3 %collective-permute-done.27.arrived_ref = bf16[512,512]{1,0:T(8,128)(2,1)S(1)} collective-permute-done((bf16[512,512]{1,0:T(8,128)(2,1)S(1)}, bf16[512,512]{1,0:T(8,128)(2,1)S(1)}, u32[]{:S(2)}, u32[]{:S(2)}) %collective-permute-start.27) | collective-permute-done | bytes 524320 | tf_op jit(solution)/shard_map/ppermute | solution.py:28
  72.0 0.3 collective-permute-start.28
  72.2 5.0 %collective-permute-done.23.arrived_ref = bf16[512,512]{1,0:T(8,128)(2,1)S(1)} collective-permute-done((bf16[512,512]{1,0:T(8,128)(2,1)S(1)}, bf16[512,512]{1,0:T(8,128)(2,1)S(1)}, u32[]{:S(2)}, u32[]{:S(2)}) %collective-permute-start.23) | collective-permute-done | bytes 524320 | tf_op jit(solution)/shard_map/ppermute | solution.py:28
  77.3 0.3 collective-permute-start.24
  77.7 2.4 %collective-permute-start.26 = (bf16[128,512]{1,0:T(8,128)(2,1)S(1)}, bf16[128,512]{1,0:T(8,128)(2,1)S(1)}, u32[]{:S(2)}, u32[]{:S(2)}) collective-permute-start(bf16[128,512]{1,0:T(8,128)(2,1)S(1)} %get-tuple-element.28), channel_id=1, source_target_pairs={{0,3},{1,2},{2,1},{3,0},{4,7},{5,6},{6,5},{7,4},{8,11},{9,10},{10,... | collective-permute-start | bytes 393224 | tf_op jit(solution)/shard_map/ppermute | solution.py:41
  80.1 3.1 %collective-permute-start.29 = (bf16[128,512]{1,0:T(8,128)(2,1)S(1)}, bf16[128,512]{1,0:T(8,128)(2,1)S(1)}, u32[]{:S(2)}, u32[]{:S(2)}) collective-permute-start(bf16[128,512]{1,0:T(8,128)(2,1)S(1)} %get-tuple-element.33), channel_id=1, source_target_pairs={{0,6},{1,7},{2,4},{3,5},{4,2},{5,3},{6,0},{7,1},{8,14},{9,15},{10,... | collective-permute-start | bytes 393224 | tf_op jit(solution)/shard_map/ppermute | solution.py:41
  83.2 6.0 %dec_grad.2.refs_4_ = bf16[1,2,1024,4096]{3,2,1,0:T(8,128)(2,1)} custom-call(bf16[128,1024]{1,0:T(8,128)(2,1)S(1)} %get-tuple-element.22.error_ref.refs_0_, bf16[512,512]{1,0:T(8,128)(2,1)S(1)} %pack.3.refs_0_.refs_1_, bf16[256,512]{1,0:T(8,128)(2,1)S(1)} %pack.2.refs_1_.refs_2_, bf16[256,512]{1,0:T(8,128)(2,1)S(1)} %collective-permute-done.17.refs_2_.refs_3_), custom_call_target="tpu_custom_call" | custom-call | flops 1073741824 | bytes 8388608 | tf_op jit(solution)/shard_map/dec_grad/pallas_call | solution.py:350
  89.2 6.0 %dec_grad.3 = bf16[1,2,1024,4096]{3,2,1,0:T(8,128)(2,1)} custom-call(bf16[128,1024]{1,0:T(8,128)(2,1)S(1)} %get-tuple-element.22.error_ref.refs_0_, bf16[512,512]{1,0:T(8,128)(2,1)S(1)} %collective-permute-done.22.part_ref.refs_1_, bf16[256,512]{1,0:T(8,128)(2,1)S(1)} %collective-permute-done.16.refs_0_.refs_2_, ...), custom_call_target="tpu_custom_call", output_to_operand_aliasing={{}: (4, {})} | custom-call | flops 1073741824 | bytes 8388608 | tf_op jit(solution)/shard_map/dec_grad/pallas_call | solution.py:350
  95.3 6.2 %enc_grad.1 = bf16[1,512,8192]{2,1,0:T(8,128)(2,1)} custom-call(f32[128,512]{1,0:T(8,128)S(1)} %get-tuple-element.25.refs_0_, bf16[128,512]{1,0:T(8,128)(2,1)S(1)} %collective-permute-done.24.refs_1_, bf16[128,512]{1,0:T(8,128)(2,1)S(1)} %collective-permute-done.25.refs_2_, bf16[128,512]{1,0:T(8,128)(2,1)S(1)} %collective-permute-done.26.refs_3_, ...), custom_call_target="tpu_custom_call" | custom-call | flops 1073741824 | bytes 8388608 | tf_op jit(solution)/shard_map/enc_grad/pallas_call | solution.py:386
  (47 shorter events, 0.6 us)
Async XLA Ops:
  0.6 54.5 %slice-start = ((s8[16777216]{0:T(1024)(128)(4,1)}), s8[4194304]{0:T(1024)(128)(4,1)S(1)}, s32[]{:S(2)}) async-start(s8[16777216]{0:T(1024)(128)(4,1)} %bitcast.4), calls=%async_computation | async-start | bytes 8388608
  0.6 1.1 %copy-start.4 = (bf16[1,128,1024]{2,1,0:T(8,128)(2,1)S(1)}, bf16[1,128,1024]{2,1,0:T(8,128)(2,1)}, u32[]{:S(2)}) copy-start(bf16[1,128,1024]{2,1,0:T(8,128)(2,1)} %param.6) | copy-start | bytes 786436
  1.7 21.9 %copy-start = (bf16[1,512,8192]{2,1,0:T(8,128)(2,1)S(1)}, bf16[1,512,8192]{2,1,0:T(8,128)(2,1)}, u32[]{:S(2)}) copy-start(bf16[1,512,8192]{2,1,0:T(8,128)(2,1)} %param.8) | copy-start | bytes 25165828
  1.7 21.9 %copy-start.3 = (f32[1,512]{1,0:T(1,128)S(1)}, f32[1,512]{1,0:T(1,128)}, u32[]{:S(2)}) copy-start(f32[1,512]{1,0:T(1,128)} %refs_17_.1) | copy-start | bytes 6148
  1.7 53.4 %slice-start.1 = ((s8[16777216]{0:T(1024)(128)(4,1)}), s8[4194304]{0:T(1024)(128)(4,1)S(1)}, s32[]{:S(2)}) async-start(s8[16777216]{0:T(1024)(128)(4,1)} %bitcast.4), calls=%async_computation.1 | async-start | bytes 8388608
  1.7 53.4 %slice-start.2 = ((s8[16777216]{0:T(1024)(128)(4,1)}), s8[4194304]{0:T(1024)(128)(4,1)S(1)}, s32[]{:S(2)}) async-start(s8[16777216]{0:T(1024)(128)(4,1)} %bitcast.4), calls=%async_computation.2 | async-start | bytes 8388608
  1.8 53.4 %slice-start.3 = ((s8[16777216]{0:T(1024)(128)(4,1)}), s8[4194304]{0:T(1024)(128)(4,1)S(1)}, s32[]{:S(2)}) async-start(s8[16777216]{0:T(1024)(128)(4,1)} %bitcast.4), calls=%async_computation.3 | async-start | bytes 8388608
  1.8 5.3 %collective-permute-start = (bf16[64,1024]{1,0:T(8,128)(2,1)S(1)}, bf16[64,1024]{1,0:T(8,128)(2,1)S(1)}, u32[]{:S(2)}, u32[]{:S(2)}) collective-permute-start(bf16[64,1024]{1,0:T(8,128)(2,1)S(1)} %get-tuple-element.19.refs_0_.refs_6_), channel_id=1, source_target_pairs={{0,2},{2,4},{4,6},{6,7},{7,5},{5,3},{3,1},{1,0},{8,10},{10,12},{12... | collective-permute-start | bytes 393224 | tf_op jit(solution)/shard_map/ppermute | solution.py:51
  4.0 4.4 %collective-permute-start.3 = (bf16[64,1024]{1,0:T(8,128)(2,1)S(1)}, bf16[64,1024]{1,0:T(8,128)(2,1)S(1)}, u32[]{:S(2)}, u32[]{:S(2)}) collective-permute-start(bf16[64,1024]{1,0:T(8,128)(2,1)S(1)} %get-tuple-element.20.refs_1_.refs_7_), channel_id=1, source_target_pairs={{0,1},{2,0},{4,2},{6,4},{7,6},{5,7},{3,5},{1,3},{8,9},{10,8},{12,1... | collective-permute-start | bytes 393224 | tf_op jit(solution)/shard_map/ppermute | solution.py:51
  4.0 6.8 %collective-permute-start.2 = (bf16[64,1024]{1,0:T(8,128)(2,1)S(1)}, bf16[64,1024]{1,0:T(8,128)(2,1)S(1)}, u32[]{:S(2)}, u32[]{:S(2)}) collective-permute-start(bf16[64,1024]{1,0:T(8,128)(2,1)S(1)} %get-tuple-element.19.refs_0_.refs_6_), channel_id=1, source_target_pairs={{0,1},{2,0},{4,2},{6,4},{7,6},{5,7},{3,5},{1,3},{8,9},{10,8},{12,1... | collective-permute-start | bytes 393224 | tf_op jit(solution)/shard_map/ppermute | solution.py:51
  5.4 5.8 %collective-permute-start.1 = (bf16[64,1024]{1,0:T(8,128)(2,1)S(1)}, bf16[64,1024]{1,0:T(8,128)(2,1)S(1)}, u32[]{:S(2)}, u32[]{:S(2)}) collective-permute-start(bf16[64,1024]{1,0:T(8,128)(2,1)S(1)} %get-tuple-element.20.refs_1_.refs_7_), channel_id=1, source_target_pairs={{0,2},{2,4},{4,6},{6,7},{7,5},{5,3},{3,1},{1,0},{8,10},{10,12},{12... | collective-permute-start | bytes 393224 | tf_op jit(solution)/shard_map/ppermute | solution.py:51
  7.1 5.3 %collective-permute-start.4 = (bf16[64,1024]{1,0:T(8,128)(2,1)S(1)}, bf16[64,1024]{1,0:T(8,128)(2,1)S(1)}, u32[]{:S(2)}, u32[]{:S(2)}) collective-permute-start(bf16[64,1024]{1,0:T(8,128)(2,1)S(1)} %collective-permute-done.refs_2_.refs_8_), channel_id=1, source_target_pairs={{0,2},{2,4},{4,6},{6,7},{7,5},{5,3},{3,1},{1,0},{8,10},{10,12},{12... | collective-permute-start | bytes 393224 | tf_op jit(solution)/shard_map/ppermute | solution.py:51
  8.3 5.4 %collective-permute-start.7 = (bf16[64,1024]{1,0:T(8,128)(2,1)S(1)}, bf16[64,1024]{1,0:T(8,128)(2,1)S(1)}, u32[]{:S(2)}, u32[]{:S(2)}) collective-permute-start(bf16[64,1024]{1,0:T(8,128)(2,1)S(1)} %collective-permute-done.3.refs_5_.refs_11_), channel_id=1, source_target_pairs={{0,1},{2,0},{4,2},{6,4},{7,6},{5,7},{3,5},{1,3},{8,9},{10,8},{12,1... | collective-permute-start | bytes 393224 | tf_op jit(solution)/shard_map/ppermute | solution.py:51
  10.8 4.8 %collective-permute-start.6 = (bf16[64,1024]{1,0:T(8,128)(2,1)S(1)}, bf16[64,1024]{1,0:T(8,128)(2,1)S(1)}, u32[]{:S(2)}, u32[]{:S(2)}) collective-permute-start(bf16[64,1024]{1,0:T(8,128)(2,1)S(1)} %collective-permute-done.2.refs_4_.refs_10_), channel_id=1, source_target_pairs={{0,1},{2,0},{4,2},{6,4},{7,6},{5,7},{3,5},{1,3},{8,9},{10,8},{12,1... | collective-permute-start | bytes 393224 | tf_op jit(solution)/shard_map/ppermute | solution.py:51
  11.2 5.2 %collective-permute-start.5 = (bf16[64,1024]{1,0:T(8,128)(2,1)S(1)}, bf16[64,1024]{1,0:T(8,128)(2,1)S(1)}, u32[]{:S(2)}, u32[]{:S(2)}) collective-permute-start(bf16[64,1024]{1,0:T(8,128)(2,1)S(1)} %collective-permute-done.1.refs_3_.refs_9_), channel_id=1, source_target_pairs={{0,2},{2,4},{4,6},{6,7},{7,5},{5,3},{3,1},{1,0},{8,10},{10,12},{12... | collective-permute-start | bytes 393224 | tf_op jit(solution)/shard_map/ppermute | solution.py:51
  12.4 4.7 %collective-permute-start.8 = (bf16[64,1024]{1,0:T(8,128)(2,1)S(1)}, bf16[64,1024]{1,0:T(8,128)(2,1)S(1)}, u32[]{:S(2)}, u32[]{:S(2)}) collective-permute-start(bf16[64,1024]{1,0:T(8,128)(2,1)S(1)} %collective-permute-done.4.refs_6_.refs_12_), channel_id=1, source_target_pairs={{0,2},{2,4},{4,6},{6,7},{7,5},{5,3},{3,1},{1,0},{8,10},{10,12},{12... | collective-permute-start | bytes 393224 | tf_op jit(solution)/shard_map/ppermute | solution.py:51
  13.7 5.1 %collective-permute-start.11 = (bf16[64,1024]{1,0:T(8,128)(2,1)S(1)}, bf16[64,1024]{1,0:T(8,128)(2,1)S(1)}, u32[]{:S(2)}, u32[]{:S(2)}) collective-permute-start(bf16[64,1024]{1,0:T(8,128)(2,1)S(1)} %collective-permute-done.7.refs_9_.refs_15_), channel_id=1, source_target_pairs={{0,1},{2,0},{4,2},{6,4},{7,6},{5,7},{3,5},{1,3},{8,9},{10,8},{12,1... | collective-permute-start | bytes 393224 | tf_op jit(solution)/shard_map/ppermute | solution.py:51
  15.7 5.1 %collective-permute-start.10 = (bf16[64,1024]{1,0:T(8,128)(2,1)S(1)}, bf16[64,1024]{1,0:T(8,128)(2,1)S(1)}, u32[]{:S(2)}, u32[]{:S(2)}) collective-permute-start(bf16[64,1024]{1,0:T(8,128)(2,1)S(1)} %collective-permute-done.6.refs_8_.refs_14_), channel_id=1, source_target_pairs={{0,1},{2,0},{4,2},{6,4},{7,6},{5,7},{3,5},{1,3},{8,9},{10,8},{12,1... | collective-permute-start | bytes 393224 | tf_op jit(solution)/shard_map/ppermute | solution.py:51
  16.3 5.5 %collective-permute-start.9 = (bf16[64,1024]{1,0:T(8,128)(2,1)S(1)}, bf16[64,1024]{1,0:T(8,128)(2,1)S(1)}, u32[]{:S(2)}, u32[]{:S(2)}) collective-permute-start(bf16[64,1024]{1,0:T(8,128)(2,1)S(1)} %collective-permute-done.5.refs_7_.refs_13_), channel_id=1, source_target_pairs={{0,2},{2,4},{4,6},{6,7},{7,5},{5,3},{3,1},{1,0},{8,10},{10,12},{12... | collective-permute-start | bytes 393224 | tf_op jit(solution)/shard_map/ppermute | solution.py:51
  17.1 5.8 %collective-permute-start.12 = (bf16[64,1024]{1,0:T(8,128)(2,1)S(1)}, bf16[64,1024]{1,0:T(8,128)(2,1)S(1)}, u32[]{:S(2)}, u32[]{:S(2)}) collective-permute-start(bf16[64,1024]{1,0:T(8,128)(2,1)S(1)} %collective-permute-done.8.refs_10_.refs_16_), channel_id=1, source_target_pairs={{0,2},{2,4},{4,6},{6,7},{7,5},{5,3},{3,1},{1,0},{8,10},{10,12},{12... | collective-permute-start | bytes 393224 | tf_op jit(solution)/shard_map/ppermute | solution.py:51
  18.8 4.8 %collective-permute-start.13 = (bf16[64,1024]{1,0:T(8,128)(2,1)S(1)}, bf16[64,1024]{1,0:T(8,128)(2,1)S(1)}, u32[]{:S(2)}, u32[]{:S(2)}) collective-permute-start(bf16[64,1024]{1,0:T(8,128)(2,1)S(1)} %collective-permute-done.11.refs_13_.refs_19_), channel_id=1, source_target_pairs={{0,1},{2,0},{4,2},{6,4},{7,6},{5,7},{3,5},{1,3},{8,9},{10,8},{12,1... | collective-permute-start | bytes 393224 | tf_op jit(solution)/shard_map/ppermute | solution.py:51
  26.1 6.0 %collective-permute-start.19 = (bf16[128,512]{1,0:T(8,128)(2,1)S(1)}, bf16[128,512]{1,0:T(8,128)(2,1)S(1)}, u32[]{:S(2)}, u32[]{:S(2)}) collective-permute-start(bf16[128,512]{1,0:T(8,128)(2,1)S(1)} %get-tuple-element.21.refs_0_), channel_id=1, source_target_pairs={{0,1},{1,0},{2,3},{3,2},{4,5},{5,4},{6,7},{7,6},{8,9},{9,8},{10,11... | collective-permute-start | bytes 393224 | tf_op jit(solution)/shard_map/ppermute | solution.py:41
  26.9 5.2 %collective-permute-start.20 = (bf16[128,512]{1,0:T(8,128)(2,1)S(1)}, bf16[128,512]{1,0:T(8,128)(2,1)S(1)}, u32[]{:S(2)}, u32[]{:S(2)}) collective-permute-start(bf16[128,512]{1,0:T(8,128)(2,1)S(1)} %get-tuple-element.21.refs_0_), channel_id=1, source_target_pairs={{0,2},{1,3},{2,0},{3,1},{4,6},{5,7},{6,4},{7,5},{8,10},{9,11},{10,... | collective-permute-start | bytes 393224 | tf_op jit(solution)/shard_map/ppermute | solution.py:41
  28.2 4.7 %collective-permute-start.21 = (bf16[128,512]{1,0:T(8,128)(2,1)S(1)}, bf16[128,512]{1,0:T(8,128)(2,1)S(1)}, u32[]{:S(2)}, u32[]{:S(2)}) collective-permute-start(bf16[128,512]{1,0:T(8,128)(2,1)S(1)} %get-tuple-element.21.refs_0_), channel_id=1, source_target_pairs={{0,3},{1,2},{2,1},{3,0},{4,7},{5,6},{6,5},{7,4},{8,11},{9,10},{10,... | collective-permute-start | bytes 393224 | tf_op jit(solution)/shard_map/ppermute | solution.py:41
  28.8 15.5 %collective-permute-start.14 = (bf16[128,512]{1,0:T(8,128)(2,1)S(1)}, bf16[128,512]{1,0:T(8,128)(2,1)S(1)}, u32[]{:S(2)}, u32[]{:S(2)}) collective-permute-start(bf16[128,512]{1,0:T(8,128)(2,1)S(1)} %get-tuple-element.21.refs_0_), channel_id=1, source_target_pairs={{0,6},{1,7},{2,4},{3,5},{4,2},{5,3},{6,0},{7,1},{8,14},{9,15},{10,... | collective-permute-start | bytes 393224 | tf_op jit(solution)/shard_map/ppermute | solution.py:41
  32.0 12.2 %collective-permute-start.15 = (bf16[128,512]{1,0:T(8,128)(2,1)S(1)}, bf16[128,512]{1,0:T(8,128)(2,1)S(1)}, u32[]{:S(2)}, u32[]{:S(2)}) collective-permute-start(bf16[128,512]{1,0:T(8,128)(2,1)S(1)} %get-tuple-element.21.refs_0_), channel_id=1, source_target_pairs={{0,4},{1,5},{2,6},{3,7},{4,0},{5,1},{6,2},{7,3},{8,12},{9,13},{10,... | collective-permute-start | bytes 393224 | tf_op jit(solution)/shard_map/ppermute | solution.py:41
  32.9 24.6 %collective-permute-start.22 = (bf16[512,512]{1,0:T(8,128)(2,1)S(1)}, bf16[512,512]{1,0:T(8,128)(2,1)S(1)}, u32[]{:S(2)}, u32[]{:S(2)}) collective-permute-start(bf16[512,512]{1,0:T(8,128)(2,1)S(1)} %pack.3.refs_0_.refs_1_), channel_id=1, source_target_pairs={{0,8},{8,16},{16,24},{1,9},{9,17},{17,25},{2,10},{10,18},{18,26},{... | collective-permute-start | bytes 1572872 | tf_op jit(solution)/shard_map/ppermute | solution.py:28
  44.3 6.5 %collective-permute-start.17 = (bf16[256,512]{1,0:T(8,128)(2,1)S(1)}, bf16[256,512]{1,0:T(8,128)(2,1)S(1)}, u32[]{:S(2)}, u32[]{:S(2)}) collective-permute-start(bf16[256,512]{1,0:T(8,128)(2,1)S(1)} %pack.2.refs_1_.refs_2_), channel_id=1, source_target_pairs={{0,1},{1,0},{2,3},{3,2},{4,5},{5,4},{6,7},{7,6},{8,9},{9,8},{10,11... | collective-permute-start | bytes 786440 | tf_op jit(solution)/shard_map/ppermute | solution.py:41
  45.1 13.7 %collective-permute-start.16 = (bf16[256,512]{1,0:T(8,128)(2,1)S(1)}, bf16[256,512]{1,0:T(8,128)(2,1)S(1)}, u32[]{:S(2)}, u32[]{:S(2)}) collective-permute-start(bf16[256,512]{1,0:T(8,128)(2,1)S(1)} %pack.2.refs_1_.refs_2_), channel_id=1, source_target_pairs={{0,8},{8,16},{16,24},{1,9},{9,17},{17,25},{2,10},{10,18},{18,26},{... | collective-permute-start | bytes 786440 | tf_op jit(solution)/shard_map/ppermute | solution.py:28
  50.8 8.0 %collective-permute-start.18 = (bf16[256,512]{1,0:T(8,128)(2,1)S(1)}, bf16[256,512]{1,0:T(8,128)(2,1)S(1)}, u32[]{:S(2)}, u32[]{:S(2)}) collective-permute-start(bf16[256,512]{1,0:T(8,128)(2,1)S(1)} %collective-permute-done.17.refs_2_.refs_3_), channel_id=1, source_target_pairs={{0,8},{8,16},{16,24},{1,9},{9,17},{17,25},{2,10},{10,18},{18,26},{... | collective-permute-start | bytes 786440 | tf_op jit(solution)/shard_map/ppermute | solution.py:28
  55.2 3.6 %copy-start.1 = (bf16[1,128,1024]{2,1,0:T(8,128)(2,1)S(1)}, bf16[1,128,1024]{2,1,0:T(8,128)(2,1)}, u32[]{:S(2)}) copy-start(bf16[1,128,1024]{2,1,0:T(8,128)(2,1)} %param.7) | copy-start | bytes 786436
  55.2 3.6 %copy-start.2 = (f32[1,1024]{1,0:T(1,128)S(1)}, f32[1,1024]{1,0:T(1,128)}, u32[]{:S(2)}) copy-start(f32[1,1024]{1,0:T(1,128)} %refs_4_.1) | copy-start | bytes 12292
  60.7 11.1 %collective-permute-start.27 = (bf16[512,512]{1,0:T(8,128)(2,1)S(1)}, bf16[512,512]{1,0:T(8,128)(2,1)S(1)}, u32[]{:S(2)}, u32[]{:S(2)}) collective-permute-start(bf16[512,512]{1,0:T(8,128)(2,1)S(1)} %get-tuple-element.30), channel_id=1, source_target_pairs={{8,0},{16,8},{24,16},{9,1},{17,9},{25,17},{10,2},{18,10},{26,18},{... | collective-permute-start | bytes 1572872 | tf_op jit(solution)/shard_map/ppermute | solution.py:28
  64.5 12.7 %collective-permute-start.23 = (bf16[512,512]{1,0:T(8,128)(2,1)S(1)}, bf16[512,512]{1,0:T(8,128)(2,1)S(1)}, u32[]{:S(2)}, u32[]{:S(2)}) collective-permute-start(bf16[512,512]{1,0:T(8,128)(2,1)S(1)} %get-tuple-element.24), channel_id=1, source_target_pairs={{8,0},{16,8},{24,16},{9,1},{17,9},{25,17},{10,2},{18,10},{26,18},{... | collective-permute-start | bytes 1572872 | tf_op jit(solution)/shard_map/ppermute | solution.py:28
  72.0 8.0 %collective-permute-start.28 = (bf16[256,512]{1,0:T(8,128)(2,1)S(1)}, bf16[256,512]{1,0:T(8,128)(2,1)S(1)}, u32[]{:S(2)}, u32[]{:S(2)}) collective-permute-start(bf16[256,512]{1,0:T(8,128)(2,1)S(1)} %get-tuple-element.32), channel_id=1, source_target_pairs={{0,1},{1,0},{2,3},{3,2},{4,5},{5,4},{6,7},{7,6},{8,9},{9,8},{10,11... | collective-permute-start | bytes 786440 | tf_op jit(solution)/shard_map/ppermute | solution.py:41
  77.3 18.0 %collective-permute-start.24 = (bf16[128,512]{1,0:T(8,128)(2,1)S(1)}, bf16[128,512]{1,0:T(8,128)(2,1)S(1)}, u32[]{:S(2)}, u32[]{:S(2)}) collective-permute-start(bf16[128,512]{1,0:T(8,128)(2,1)S(1)} %get-tuple-element.26), channel_id=1, source_target_pairs={{0,1},{1,0},{2,3},{3,2},{4,5},{5,4},{6,7},{7,6},{8,9},{9,8},{10,11... | collective-permute-start | bytes 393224 | tf_op jit(solution)/shard_map/ppermute | solution.py:41
  77.6 17.7 %collective-permute-start.25 = (bf16[128,512]{1,0:T(8,128)(2,1)S(1)}, bf16[128,512]{1,0:T(8,128)(2,1)S(1)}, u32[]{:S(2)}, u32[]{:S(2)}) collective-permute-start(bf16[128,512]{1,0:T(8,128)(2,1)S(1)} %get-tuple-element.27), channel_id=1, source_target_pairs={{0,2},{1,3},{2,0},{3,1},{4,6},{5,7},{6,4},{7,5},{8,10},{9,11},{10,... | collective-permute-start | bytes 393224 | tf_op jit(solution)/shard_map/ppermute | solution.py:41
  77.7 17.7 %collective-permute-start.26 = (bf16[128,512]{1,0:T(8,128)(2,1)S(1)}, bf16[128,512]{1,0:T(8,128)(2,1)S(1)}, u32[]{:S(2)}, u32[]{:S(2)}) collective-permute-start(bf16[128,512]{1,0:T(8,128)(2,1)S(1)} %get-tuple-element.28), channel_id=1, source_target_pairs={{0,3},{1,2},{2,1},{3,0},{4,7},{5,6},{6,5},{7,4},{8,11},{9,10},{10,... | collective-permute-start | bytes 393224 | tf_op jit(solution)/shard_map/ppermute | solution.py:41
  80.1 15.3 %collective-permute-start.29 = (bf16[128,512]{1,0:T(8,128)(2,1)S(1)}, bf16[128,512]{1,0:T(8,128)(2,1)S(1)}, u32[]{:S(2)}, u32[]{:S(2)}) collective-permute-start(bf16[128,512]{1,0:T(8,128)(2,1)S(1)} %get-tuple-element.33), channel_id=1, source_target_pairs={{0,6},{1,7},{2,4},{3,5},{4,2},{5,3},{6,0},{7,1},{8,14},{9,15},{10,... | collective-permute-start | bytes 393224 | tf_op jit(solution)/shard_map/ppermute | solution.py:41
  83.2 12.1 %collective-permute-start.30 = (bf16[128,512]{1,0:T(8,128)(2,1)S(1)}, bf16[128,512]{1,0:T(8,128)(2,1)S(1)}, u32[]{:S(2)}, u32[]{:S(2)}) collective-permute-start(bf16[128,512]{1,0:T(8,128)(2,1)S(1)} %get-tuple-element.34), channel_id=1, source_target_pairs={{0,4},{1,5},{2,6},{3,7},{4,0},{5,1},{6,2},{7,3},{8,12},{9,13},{10,... | collective-permute-start | bytes 393224 | tf_op jit(solution)/shard_map/ppermute | solution.py:41

commit v7 on v5

--- a/solution.py
+++ b/solution.py
@@ -20,12 +20,21 @@
 FAR = (6, 4)
 CROSSING = (7, 5)
 BLOCKS = ((0, 1, 2, 3), (6, 4), (7, 5))
+EARLY = BLOCKS[:1]
 
 
 def from_behind(value, axis, steps):
     count = lax.axis_size(axis)
     initial, last = (max(0, -steps), min(count, count - steps))
     return lax.ppermute(value, axis, [(source, source + steps) for source in range(initial, last)])
+
+
+def diagonal(value):
+    sections, count = lax.axis_size("section"), lax.axis_size("feat")
+    pairs = [
+        (s * count + i, (s + 1) * count + (i ^ 1)) for s in range(sections - 1) for i in range(count)
+    ]
+    return lax.ppermute(value, ("section", "feat"), pairs)
 
 
 def transposed(left, right):
@@ -177,6 +186,15 @@
         total_ref[here, :] = decoded(w_ref, 0, here, parts, BLOCKS, tok, None)
 
 
+def near_recon_kernel(*refs):
+    parts, (before_ref, w_ref, total_ref) = refs[: len(EARLY)], refs[len(EARLY) :]
+    tok = total_ref.shape[1]
+    steps, tile = tiles(w_ref.shape[1])
+    for j in range(steps):
+        here = slice(j * tile, (j + 1) * tile)
+        total_ref[here, :] = decoded(w_ref, 1, here, parts, EARLY, tok, before_ref[here, :])
+
+
 def products(error_ref, w_ref, slot, masks, out_ref):
     tok = error_ref.shape[0]
     for row, mask in enumerate(masks):
@@ -187,13 +205,14 @@
 
 
 def recon_kernel(scale, *refs):
-    parts, (total_ref, w_ref, b_ref, target_ref, error_ref, far_ref) = refs[: len(BLOCKS)], refs[len(BLOCKS) :]
+    rest = BLOCKS[len(EARLY) :]
+    parts, (total_ref, w_ref, b_ref, target_ref, error_ref, far_ref) = refs[: len(rest)], refs[len(rest) :]
     tok = total_ref.shape[1]
     steps, tile = tiles(w_ref.shape[1])
 
     for j in range(steps):
         here = slice(j * tile, (j + 1) * tile)
-        total = decoded(w_ref, 1, here, parts, BLOCKS, tok, total_ref[here, :])
+        total = decoded(w_ref, 1, here, parts, rest, tok, total_ref[here, :])
         error = total.T + b_ref[:, here] - target_ref[:, here].astype(F32)
         error_ref[:, here] = (error * scale).astype(BF16)
 
@@ -267,9 +286,9 @@
     )(*inputs_of, enc_weights, enc_b)
 
     far_pair = packed(exchanged(codes, 6), exchanged(codes, 4))
-    far_across = exchanged(far_pair, 1)
-    own = [packed(codes, *[exchanged(codes, mask) for mask in (1, 2, 3)]), far_pair, far_across]
-    previous = [from_behind(part, "section", 1) for part in own]
+    own = [packed(codes, *[exchanged(codes, mask) for mask in (1, 2, 3)]), far_pair, exchanged(far_pair, 1)]
+    previous = [from_behind(part, "section", 1) for part in own[:2]]
+    previous.append(diagonal(far_pair))
 
     total = pl.pallas_call(
         own_recon_kernel,
@@ -281,15 +300,25 @@
         cost_estimate=cost(matmul, 0),
     )(*own, weights)
 
+    total = pl.pallas_call(
+        near_recon_kernel,
+        name="near_recon",
+        out_shape=struct((width, tok), F32),
+        in_specs=vmem(len(EARLY) + 2),
+        out_specs=vmem(1)[0],
+        compiler_params=params(8),
+        cost_estimate=cost(matmul // 2, 0),
+    )(*previous[: len(EARLY)], total, weights)
+
     error, sent_far = pl.pallas_call(
         functools.partial(recon_kernel, scale),
         name="recon",
         out_shape=(struct((tok, width), BF16), stack(FAR + CROSSING, BF16)),
-        in_specs=vmem(len(previous) + 4),
+        in_specs=vmem(len(previous) - len(EARLY) + 4),
         out_specs=tuple(vmem(2)),
         compiler_params=params(8),
         cost_estimate=cost(2 * matmul, 4 * MIB),
-    )(*previous, total, weights, dec_b, targets[0])
+    )(*previous[len(EARLY) :], total, weights, dec_b, targets[0])
     arrived_far = from_behind(sent_far, "section", -1)
 
     sent_near, own_near, own_far = pl.pallas_call(
@@ -303,7 +332,7 @@
     )(error, weights)
     arrived_near = from_behind(sent_near, "section", -1)
 
-    rows = 256 if width % 256 == 0 else LANES
+    rows = LANES
 
     def dec_grad_slot(slot, groups, parts, *held):
         return pl.pallas_call(

time: 99 us -> 109 us (1.10)
  waiting for transfers between devices: 30.5 us -> 35.9 us
  Pallas kernels: 24.9 us -> 27.7 us
  starting transfers between devices: 41.4 us -> 43 us
    ppermute x12, waiting for transfers between devices: 5.21 us -> 16.1 us  [exchanged(): return lax.ppermute(value, 'feat', [(i, i ^ mask) for i in range(count)])]
    ppermute x5 -> x4, waiting for transfers between devices: 14.8 us -> 9.23 us  [from_behind(): lax.ppermute(value, axis, [(source, source + steps) for source in range(i...]
    pallas_call x2, Pallas kernels: 9.81 us -> 12.5 us  [dec_grad_slot(): pl.pallas_call(functools.partial(dec_grad_kernel, groups), name='dec_grad...]
    ppermute x0 -> x1, starting transfers between devices: none -> 1.92 us  [diagonal(): return lax.ppermute(value, ('section', 'feat'), pairs)]
    ppermute x5 -> x4, starting transfers between devices: 17 us -> 15.6 us  [from_behind(): lax.ppermute(value, axis, [(source, source + steps) for source in range(i...]
    pallas_call x0 -> x1, Pallas kernels: none -> 1.24 us  [on_device(): pl.pallas_call(near_recon_kernel, name='near_recon', out_shape=struct((wi...]
    ppermute x12, starting transfers between devices: 13 us -> 14.2 us  [exchanged(): return lax.ppermute(value, 'feat', [(i, i ^ mask) for i in range(count)])]
  transfers between devices with their start and end apart: 31 -> 31, of which waited for: 15 -> 17; matrix products, arithmetic and copies ran while one was open for 0% -> 0% of each run, Pallas kernels for 14% -> 17%
where the time goes in v7:
time: 109 us
  starting transfers between devices  43 us (39%)
  waiting for transfers between devices  35.9 us (33%)
  Pallas kernels  27.7 us (25%)
  local copies, waits for them, and re-layouts  1.13 us (1%)
    ppermute x12, waiting for transfers between devices, exchanged(): return lax.ppermute(value, 'feat', [(i, i ^ mask) for i in range(count)])  16.1 us
    ppermute x4, starting transfers between devices, from_behind(): lax.ppermute(value, axis, [(source, source + steps) for source in range(i...  15.6 us
    ppermute x12, starting transfers between devices, exchanged(): return lax.ppermute(value, 'feat', [(i, i ^ mask) for i in range(count)])  14.2 us
    pallas_call x2, Pallas kernels, dec_grad_slot(): pl.pallas_call(functools.partial(dec_grad_kernel, groups), name='dec_grad...  12.5 us
    ppermute x14, starting transfers between devices, passed_on(): lax.ppermute(value, 'feat', [(order[p], order[(p + by) % count]) for p in...  11.4 us
    ppermute x14, waiting for transfers between devices, passed_on(): lax.ppermute(value, 'feat', [(order[p], order[(p + by) % count]) for p in...  10.5 us
    ppermute x4, waiting for transfers between devices, from_behind(): lax.ppermute(value, axis, [(source, source + steps) for source in range(i...  9.23 us
    pallas_call x1, Pallas kernels, on_device(): pl.pallas_call(enc_grad_kernel, name='enc_grad', grid=(own_features // LA...  5.2 us
  transfers between devices with their start and end apart: 31, of which 17 were waited for; matrix products, arithmetic and copies ran while one was open for 0% of the time, Pallas kernels for 17%

profile of v7, /device:TPU:1, one launch (start us, length us, event | category | flops | bytes accessed | tf_op | source)
XLA Modules:
  0.0 108.7 jit_solution(6455652562561161113)
XLA Ops:
  0.7 1.1 %copy-done.4 = bf16[1,128,1024]{2,1,0:T(8,128)(2,1)S(1)} copy-done((bf16[1,128,1024]{2,1,0:T(8,128)(2,1)S(1)}, bf16[1,128,1024]{2,1,0:T(8,128)(2,1)}, u32[]{:S(2)}) %copy-start.4) | copy-done | bytes 262168
  1.8 2.2 %collective-permute-start = (bf16[64,1024]{1,0:T(8,128)(2,1)S(1)}, bf16[64,1024]{1,0:T(8,128)(2,1)S(1)}, u32[]{:S(2)}, u32[]{:S(2)}) collective-permute-start(bf16[64,1024]{1,0:T(8,128)(2,1)S(1)} %get-tuple-element.19.refs_0_.refs_6_), channel_id=1, source_target_pairs={{0,2},{2,4},{4,6},{6,7},{7,5},{5,3},{3,1},{1,0},{8,10},{10,12},{12... | collective-permute-start | bytes 393224 | tf_op jit(solution)/shard_map/ppermute | solution.py:60
  4.0 1.4 %collective-permute-start.2 = (bf16[64,1024]{1,0:T(8,128)(2,1)S(1)}, bf16[64,1024]{1,0:T(8,128)(2,1)S(1)}, u32[]{:S(2)}, u32[]{:S(2)}) collective-permute-start(bf16[64,1024]{1,0:T(8,128)(2,1)S(1)} %get-tuple-element.19.refs_0_.refs_6_), channel_id=1, source_target_pairs={{0,1},{2,0},{4,2},{6,4},{7,6},{5,7},{3,5},{1,3},{8,9},{10,8},{12,1... | collective-permute-start | bytes 393224 | tf_op jit(solution)/shard_map/ppermute | solution.py:60
  5.5 1.7 %collective-permute-done.refs_2_.refs_8_ = bf16[64,1024]{1,0:T(8,128)(2,1)S(1)} collective-permute-done((bf16[64,1024]{1,0:T(8,128)(2,1)S(1)}, bf16[64,1024]{1,0:T(8,128)(2,1)S(1)}, u32[]{:S(2)}, u32[]{:S(2)}) %collective-permute-start) | collective-permute-done | bytes 131104 | tf_op jit(solution)/shard_map/ppermute | solution.py:60
  7.1 1.2 %collective-permute-start.4 = (bf16[64,1024]{1,0:T(8,128)(2,1)S(1)}, bf16[64,1024]{1,0:T(8,128)(2,1)S(1)}, u32[]{:S(2)}, u32[]{:S(2)}) collective-permute-start(bf16[64,1024]{1,0:T(8,128)(2,1)S(1)} %collective-permute-done.refs_2_.refs_8_), channel_id=1, source_target_pairs={{0,2},{2,4},{4,6},{6,7},{7,5},{5,3},{3,1},{1,0},{8,10},{10,12},{12... | collective-permute-start | bytes 393224 | tf_op jit(solution)/shard_map/ppermute | solution.py:60
  8.6 2.2 %collective-permute-done.2.refs_4_.refs_10_ = bf16[64,1024]{1,0:T(8,128)(2,1)S(1)} collective-permute-done((bf16[64,1024]{1,0:T(8,128)(2,1)S(1)}, bf16[64,1024]{1,0:T(8,128)(2,1)S(1)}, u32[]{:S(2)}, u32[]{:S(2)}) %collective-permute-start.2) | collective-permute-done | bytes 131104 | tf_op jit(solution)/shard_map/ppermute | solution.py:60
  11.2 1.1 %collective-permute-start.5 = (bf16[64,1024]{1,0:T(8,128)(2,1)S(1)}, bf16[64,1024]{1,0:T(8,128)(2,1)S(1)}, u32[]{:S(2)}, u32[]{:S(2)}) collective-permute-start(bf16[64,1024]{1,0:T(8,128)(2,1)S(1)} %collective-permute-done.1.refs_3_.refs_9_), channel_id=1, source_target_pairs={{0,2},{2,4},{4,6},{6,7},{7,5},{5,3},{3,1},{1,0},{8,10},{10,12},{12... | collective-permute-start | bytes 393224 | tf_op jit(solution)/shard_map/ppermute | solution.py:60
  12.4 1.3 %collective-permute-start.8 = (bf16[64,1024]{1,0:T(8,128)(2,1)S(1)}, bf16[64,1024]{1,0:T(8,128)(2,1)S(1)}, u32[]{:S(2)}, u32[]{:S(2)}) collective-permute-start(bf16[64,1024]{1,0:T(8,128)(2,1)S(1)} %collective-permute-done.4.refs_6_.refs_12_), channel_id=1, source_target_pairs={{0,2},{2,4},{4,6},{6,7},{7,5},{5,3},{3,1},{1,0},{8,10},{10,12},{12... | collective-permute-start | bytes 393224 | tf_op jit(solution)/shard_map/ppermute | solution.py:60
  13.9 1.8 %collective-permute-done.6.refs_8_.refs_14_ = bf16[64,1024]{1,0:T(8,128)(2,1)S(1)} collective-permute-done((bf16[64,1024]{1,0:T(8,128)(2,1)S(1)}, bf16[64,1024]{1,0:T(8,128)(2,1)S(1)}, u32[]{:S(2)}, u32[]{:S(2)}) %collective-permute-start.6) | collective-permute-done | bytes 131104 | tf_op jit(solution)/shard_map/ppermute | solution.py:60
  15.7 0.7 collective-permute-start.10
  16.3 0.8 collective-permute-start.9
  17.1 1.3 %collective-permute-start.12 = (bf16[64,1024]{1,0:T(8,128)(2,1)S(1)}, bf16[64,1024]{1,0:T(8,128)(2,1)S(1)}, u32[]{:S(2)}, u32[]{:S(2)}) collective-permute-start(bf16[64,1024]{1,0:T(8,128)(2,1)S(1)} %collective-permute-done.8.refs_10_.refs_16_), channel_id=1, source_target_pairs={{0,2},{2,4},{4,6},{6,7},{7,5},{5,3},{3,1},{1,0},{8,10},{10,12},{12... | collective-permute-start | bytes 393224 | tf_op jit(solution)/shard_map/ppermute | solution.py:60
  18.4 0.4 collective-permute-done.11.refs_13_.refs_19_
  18.8 0.5 collective-permute-start.13
  19.4 1.4 %collective-permute-done.10.refs_12_.refs_18_ = bf16[64,1024]{1,0:T(8,128)(2,1)S(1)} collective-permute-done((bf16[64,1024]{1,0:T(8,128)(2,1)S(1)}, bf16[64,1024]{1,0:T(8,128)(2,1)S(1)}, u32[]{:S(2)}, u32[]{:S(2)}) %collective-permute-start.10) | collective-permute-done | bytes 131104 | tf_op jit(solution)/shard_map/ppermute | solution.py:60
  20.7 1.1 collective-permute-done.9.refs_11_.refs_17_
  21.8 1.1 %collective-permute-done.12.refs_14_.refs_20_ = bf16[64,1024]{1,0:T(8,128)(2,1)S(1)} collective-permute-done((bf16[64,1024]{1,0:T(8,128)(2,1)S(1)}, bf16[64,1024]{1,0:T(8,128)(2,1)S(1)}, u32[]{:S(2)}, u32[]{:S(2)}) %collective-permute-start.12) | collective-permute-done | bytes 131104 | tf_op jit(solution)/shard_map/ppermute | solution.py:60
  23.0 0.7 collective-permute-done.13.refs_15_.refs_21_
  23.6 2.4 %pre.1 = (bf16[128,512]{1,0:T(8,128)(2,1)S(1)}, f32[128,512]{1,0:T(8,128)S(1)}) custom-call(bf16[64,1024]{1,0:T(8,128)(2,1)S(1)} %get-tuple-element.19.refs_0_.refs_6_, bf16[64,1024]{1,0:T(8,128)(2,1)S(1)} %get-tuple-element.20.refs_1_.refs_7_, bf16[64,1024]{1,0:T(8,128)(2,1)S(1)} %collective-permute-done.refs_2_.refs_8_, ...), custom_call_target="tpu_custom_call" | custom-call | flops 1073741824 | tf_op jit(solution)/shard_map/pre/pallas_call | solution.py:278
  26.1 0.8 collective-permute-start.18
  26.9 1.3 %collective-permute-start.19 = (bf16[128,512]{1,0:T(8,128)(2,1)S(1)}, bf16[128,512]{1,0:T(8,128)(2,1)S(1)}, u32[]{:S(2)}, u32[]{:S(2)}) collective-permute-start(bf16[128,512]{1,0:T(8,128)(2,1)S(1)} %get-tuple-element.21.refs_0_), channel_id=1, source_target_pairs={{0,2},{1,3},{2,0},{3,1},{4,6},{5,7},{6,4},{7,5},{8,10},{9,11},{10,... | collective-permute-start | bytes 393224 | tf_op jit(solution)/shard_map/ppermute | solution.py:50
  28.2 0.6 collective-permute-start.20
  28.8 1.2 %collective-permute-done.18.refs_1_ = bf16[128,512]{1,0:T(8,128)(2,1)S(1)} collective-permute-done((bf16[128,512]{1,0:T(8,128)(2,1)S(1)}, bf16[128,512]{1,0:T(8,128)(2,1)S(1)}, u32[]{:S(2)}, u32[]{:S(2)}) %collective-permute-start.18) | collective-permute-done | bytes 131104 | tf_op jit(solution)/shard_map/ppermute | solution.py:50
  30.0 0.7 collective-permute-done.19.refs_2_
  30.7 2.2 %collective-permute-done.20.refs_3_ = bf16[128,512]{1,0:T(8,128)(2,1)S(1)} collective-permute-done((bf16[128,512]{1,0:T(8,128)(2,1)S(1)}, bf16[128,512]{1,0:T(8,128)(2,1)S(1)}, u32[]{:S(2)}, u32[]{:S(2)}) %collective-permute-start.20) | collective-permute-done | bytes 131104 | tf_op jit(solution)/shard_map/ppermute | solution.py:50
  32.9 9.4 %collective-permute-start.21 = (bf16[512,512]{1,0:T(8,128)(2,1)S(1)}, bf16[512,512]{1,0:T(8,128)(2,1)S(1)}, u32[]{:S(2)}, u32[]{:S(2)}) collective-permute-start(bf16[512,512]{1,0:T(8,128)(2,1)S(1)} %pack.3.refs_0_.refs_1_), channel_id=1, source_target_pairs={{0,8},{8,16},{16,24},{1,9},{9,17},{17,25},{2,10},{10,18},{18,26},{... | collective-permute-start | bytes 1572872 | tf_op jit(solution)/shard_map/ppermute | solution.py:29
  42.4 5.0 %collective-permute-start.14 = (bf16[128,512]{1,0:T(8,128)(2,1)S(1)}, bf16[128,512]{1,0:T(8,128)(2,1)S(1)}, u32[]{:S(2)}, u32[]{:S(2)}) collective-permute-start(bf16[128,512]{1,0:T(8,128)(2,1)S(1)} %get-tuple-element.21.refs_0_), channel_id=1, source_target_pairs={{0,6},{1,7},{2,4},{3,5},{4,2},{5,3},{6,0},{7,1},{8,14},{9,15},{10,... | collective-permute-start | bytes 393224 | tf_op jit(solution)/shard_map/ppermute | solution.py:50
  47.4 2.6 %collective-permute-done.14.refs_0_ = bf16[128,512]{1,0:T(8,128)(2,1)S(1)} collective-permute-done((bf16[128,512]{1,0:T(8,128)(2,1)S(1)}, bf16[128,512]{1,0:T(8,128)(2,1)S(1)}, u32[]{:S(2)}, u32[]{:S(2)}) %collective-permute-start.14) | collective-permute-done | bytes 131104 | tf_op jit(solution)/shard_map/ppermute | solution.py:50
  50.0 5.9 %collective-permute-done.15.refs_1_ = bf16[128,512]{1,0:T(8,128)(2,1)S(1)} collective-permute-done((bf16[128,512]{1,0:T(8,128)(2,1)S(1)}, bf16[128,512]{1,0:T(8,128)(2,1)S(1)}, u32[]{:S(2)}, u32[]{:S(2)}) %collective-permute-start.15) | collective-permute-done | bytes 131104 | tf_op jit(solution)/shard_map/ppermute | solution.py:50
  55.9 1.0 collective-permute-start.22
  56.9 1.9 %collective-permute-start.16 = (bf16[256,512]{1,0:T(8,128)(2,1)S(1)}, bf16[256,512]{1,0:T(8,128)(2,1)S(1)}, u32[]{:S(2)}, u32[]{:S(2)}) collective-permute-start(bf16[256,512]{1,0:T(8,128)(2,1)S(1)} %pack.2.refs_1_.refs_2_), channel_id=1, source_target_pairs={{0,8},{8,16},{16,24},{1,9},{9,17},{17,25},{2,10},{10,18},{18,26},{... | collective-permute-start | bytes 786440 | tf_op jit(solution)/shard_map/ppermute | solution.py:29
  58.8 1.9 %collective-permute-start.17 = (bf16[256,512]{1,0:T(8,128)(2,1)S(1)}, bf16[256,512]{1,0:T(8,128)(2,1)S(1)}, u32[]{:S(2)}, u32[]{:S(2)}) collective-permute-start(bf16[256,512]{1,0:T(8,128)(2,1)S(1)} %pack.2.refs_1_.refs_2_), channel_id=1, source_target_pairs={{0,9},{1,8},{2,11},{3,10},{4,13},{5,12},{6,15},{7,14},{8,17},{9,16... | collective-permute-start | bytes 786440 | tf_op jit(solution)/shard_map/ppermute | solution.py:37
  60.7 3.6 %collective-permute-done.22.refs_2_.refs_3_ = bf16[256,512]{1,0:T(8,128)(2,1)S(1)} collective-permute-done((bf16[256,512]{1,0:T(8,128)(2,1)S(1)}, bf16[256,512]{1,0:T(8,128)(2,1)S(1)}, u32[]{:S(2)}, u32[]{:S(2)}) %collective-permute-start.22) | collective-permute-done | bytes 262176 | tf_op jit(solution)/shard_map/ppermute | solution.py:50
  64.3 2.3 %own_recon.1.refs_1_ = f32[1024,128]{1,0:T(8,128)S(1)} custom-call(bf16[512,512]{1,0:T(8,128)(2,1)S(1)} %pack.3.refs_0_.refs_1_, bf16[256,512]{1,0:T(8,128)(2,1)S(1)} %pack.2.refs_1_.refs_2_, bf16[256,512]{1,0:T(8,128)(2,1)S(1)} %collective-permute-done.22.refs_2_.refs_3_, bf16[2,1024,4096]{2,1,0:T(8,128)(2,1)S(1)} %bitcast.6), custom_call_target="tpu_custom_call" | custom-call | flops 1073741824 | tf_op jit(solution)/shard_map/own_recon/pallas_call | solution.py:293
  66.6 1.2 %near_recon.1.refs_2_ = f32[1024,128]{1,0:T(8,128)S(1)} custom-call(bf16[512,512]{1,0:T(8,128)(2,1)S(1)} %collective-permute-done.21.refs_0_.refs_1_, f32[1024,128]{1,0:T(8,128)S(1)} %own_recon.1.refs_1_, bf16[2,1024,4096]{2,1,0:T(8,128)(2,1)S(1)} %bitcast.7), custom_call_target="tpu_custom_call" | custom-call | flops 536870912 | tf_op jit(solution)/shard_map/near_recon/pallas_call | solution.py:303
  67.9 1.9 %recon.1 = (bf16[128,1024]{1,0:T(8,128)(2,1)S(1)}, bf16[512,512]{1,0:T(8,128)(2,1)S(1)}) custom-call(bf16[256,512]{1,0:T(8,128)(2,1)S(1)} %collective-permute-done.16.refs_0_.refs_2_, bf16[256,512]{1,0:T(8,128)(2,1)S(1)} %collective-permute-done.17.refs_1_.refs_3_, f32[1024,128]{1,0:T(8,128)S(1)} %near_recon.1.refs_2_, bf16[2,1024,4096]{2,1,0:T(8,128)(2,1)S(1)} %bitcast.8, ...), custom_call_target="tpu_custom_call" | custom-call | flops 2147483648 | bytes 4194304 | tf_op jit(solution)/shard_map/recon/pallas_call | solution.py:313
  69.9 2.3 %collective-permute-start.27 = (bf16[512,512]{1,0:T(8,128)(2,1)S(1)}, bf16[512,512]{1,0:T(8,128)(2,1)S(1)}, u32[]{:S(2)}, u32[]{:S(2)}) collective-permute-start(bf16[512,512]{1,0:T(8,128)(2,1)S(1)} %get-tuple-element.30), channel_id=1, source_target_pairs={{8,0},{16,8},{24,16},{9,1},{17,9},{25,17},{10,2},{18,10},{26,18},{... | collective-permute-start | bytes 1572872 | tf_op jit(solution)/shard_map/ppermute | solution.py:29
  72.2 1.8 %own_grad.1 = (bf16[512,512]{1,0:T(8,128)(2,1)S(1)}, f32[512,512]{1,0:T(8,128)S(1)}, f32[512,512]{1,0:T(8,128)S(1)}) custom-call(bf16[128,1024]{1,0:T(8,128)(2,1)S(1)} %get-tuple-element.22.error_ref.refs_0_, bf16[2,1024,4096]{2,1,0:T(8,128)(2,1)S(1)} %bitcast.9), custom_call_target="tpu_custom_call" | custom-call | flops 1610612736 | bytes 6291456 | tf_op jit(solution)/shard_map/own_grad/pallas_call | solution.py:324
  74.0 1.9 %collective-permute-start.23 = (bf16[512,512]{1,0:T(8,128)(2,1)S(1)}, bf16[512,512]{1,0:T(8,128)(2,1)S(1)}, u32[]{:S(2)}, u32[]{:S(2)}) collective-permute-start(bf16[512,512]{1,0:T(8,128)(2,1)S(1)} %get-tuple-element.24), channel_id=1, source_target_pairs={{8,0},{16,8},{24,16},{9,1},{17,9},{25,17},{10,2},{18,10},{26,18},{... | collective-permute-start | bytes 1572872 | tf_op jit(solution)/shard_map/ppermute | solution.py:29
  76.0 4.7 %collective-permute-done.27.arrived_ref = bf16[512,512]{1,0:T(8,128)(2,1)S(1)} collective-permute-done((bf16[512,512]{1,0:T(8,128)(2,1)S(1)}, bf16[512,512]{1,0:T(8,128)(2,1)S(1)}, u32[]{:S(2)}, u32[]{:S(2)}) %collective-permute-start.27) | collective-permute-done | bytes 524320 | tf_op jit(solution)/shard_map/ppermute | solution.py:29
  80.7 0.7 collective-permute-start.28
  81.4 4.5 %collective-permute-done.23.arrived_ref = bf16[512,512]{1,0:T(8,128)(2,1)S(1)} collective-permute-done((bf16[512,512]{1,0:T(8,128)(2,1)S(1)}, bf16[512,512]{1,0:T(8,128)(2,1)S(1)}, u32[]{:S(2)}, u32[]{:S(2)}) %collective-permute-start.23) | collective-permute-done | bytes 524320 | tf_op jit(solution)/shard_map/ppermute | solution.py:29
  86.1 0.7 collective-permute-start.24
  87.1 1.7 %collective-permute-start.26 = (bf16[128,512]{1,0:T(8,128)(2,1)S(1)}, bf16[128,512]{1,0:T(8,128)(2,1)S(1)}, u32[]{:S(2)}, u32[]{:S(2)}) collective-permute-start(bf16[128,512]{1,0:T(8,128)(2,1)S(1)} %get-tuple-element.28), channel_id=1, source_target_pairs={{0,3},{1,2},{2,1},{3,0},{4,7},{5,6},{6,5},{7,4},{8,11},{9,10},{10,... | collective-permute-start | bytes 393224 | tf_op jit(solution)/shard_map/ppermute | solution.py:50
  88.8 2.1 %collective-permute-start.29 = (bf16[128,512]{1,0:T(8,128)(2,1)S(1)}, bf16[128,512]{1,0:T(8,128)(2,1)S(1)}, u32[]{:S(2)}, u32[]{:S(2)}) collective-permute-start(bf16[128,512]{1,0:T(8,128)(2,1)S(1)} %get-tuple-element.33), channel_id=1, source_target_pairs={{0,6},{1,7},{2,4},{3,5},{4,2},{5,3},{6,0},{7,1},{8,14},{9,15},{10,... | collective-permute-start | bytes 393224 | tf_op jit(solution)/shard_map/ppermute | solution.py:50
  90.9 6.3 %dec_grad.2.refs_4_ = bf16[1,2,1024,4096]{3,2,1,0:T(8,128)(2,1)} custom-call(bf16[128,1024]{1,0:T(8,128)(2,1)S(1)} %get-tuple-element.22.error_ref.refs_0_, bf16[512,512]{1,0:T(8,128)(2,1)S(1)} %pack.3.refs_0_.refs_1_, bf16[256,512]{1,0:T(8,128)(2,1)S(1)} %pack.2.refs_1_.refs_2_, bf16[256,512]{1,0:T(8,128)(2,1)S(1)} %collective-permute-done.22.refs_2_.refs_3_), custom_call_target="tpu_custom_call" | custom-call | flops 1073741824 | bytes 8388608 | tf_op jit(solution)/shard_map/dec_grad/pallas_call | solution.py:338
  97.2 6.3 %dec_grad.3 = bf16[1,2,1024,4096]{3,2,1,0:T(8,128)(2,1)} custom-call(bf16[128,1024]{1,0:T(8,128)(2,1)S(1)} %get-tuple-element.22.error_ref.refs_0_, bf16[512,512]{1,0:T(8,128)(2,1)S(1)} %collective-permute-done.21.refs_0_.refs_1_, bf16[256,512]{1,0:T(8,128)(2,1)S(1)} %collective-permute-done.16.refs_0_.refs_2_, ...), custom_call_target="tpu_custom_call", output_to_operand_aliasing={{}: (4, {})} | custom-call | flops 1073741824 | bytes 8388608 | tf_op jit(solution)/shard_map/dec_grad/pallas_call | solution.py:338
  103.5 5.2 %enc_grad.1 = bf16[1,512,8192]{2,1,0:T(8,128)(2,1)} custom-call(f32[128,512]{1,0:T(8,128)S(1)} %get-tuple-element.25.refs_0_, bf16[128,512]{1,0:T(8,128)(2,1)S(1)} %collective-permute-done.24.refs_1_, bf16[128,512]{1,0:T(8,128)(2,1)S(1)} %collective-permute-done.25.refs_2_, bf16[128,512]{1,0:T(8,128)(2,1)S(1)} %collective-permute-done.26.refs_3_, ...), custom_call_target="tpu_custom_call" | custom-call | flops 1073741824 | bytes 8388608 | tf_op jit(solution)/shard_map/enc_grad/pallas_call | solution.py:378
  (47 shorter events, 1.8 us)
Async XLA Ops:
  0.6 63.6 %slice-start = ((s8[16777216]{0:T(1024)(128)(4,1)}), s8[4194304]{0:T(1024)(128)(4,1)S(1)}, s32[]{:S(2)}) async-start(s8[16777216]{0:T(1024)(128)(4,1)} %bitcast.4), calls=%async_computation | async-start | bytes 8388608
  0.6 1.1 %copy-start.4 = (bf16[1,128,1024]{2,1,0:T(8,128)(2,1)S(1)}, bf16[1,128,1024]{2,1,0:T(8,128)(2,1)}, u32[]{:S(2)}) copy-start(bf16[1,128,1024]{2,1,0:T(8,128)(2,1)} %param.6) | copy-start | bytes 786436
  1.7 21.9 %copy-start = (bf16[1,512,8192]{2,1,0:T(8,128)(2,1)S(1)}, bf16[1,512,8192]{2,1,0:T(8,128)(2,1)}, u32[]{:S(2)}) copy-start(bf16[1,512,8192]{2,1,0:T(8,128)(2,1)} %param.8) | copy-start | bytes 25165828
  1.7 21.9 %copy-start.3 = (f32[1,512]{1,0:T(1,128)S(1)}, f32[1,512]{1,0:T(1,128)}, u32[]{:S(2)}) copy-start(f32[1,512]{1,0:T(1,128)} %refs_17_.1) | copy-start | bytes 6148
  1.7 62.5 %slice-start.1 = ((s8[16777216]{0:T(1024)(128)(4,1)}), s8[4194304]{0:T(1024)(128)(4,1)S(1)}, s32[]{:S(2)}) async-start(s8[16777216]{0:T(1024)(128)(4,1)} %bitcast.4), calls=%async_computation.1 | async-start | bytes 8388608
  1.7 62.5 %slice-start.2 = ((s8[16777216]{0:T(1024)(128)(4,1)}), s8[4194304]{0:T(1024)(128)(4,1)S(1)}, s32[]{:S(2)}) async-start(s8[16777216]{0:T(1024)(128)(4,1)} %bitcast.4), calls=%async_computation.2 | async-start | bytes 8388608
  1.8 62.5 %slice-start.3 = ((s8[16777216]{0:T(1024)(128)(4,1)}), s8[4194304]{0:T(1024)(128)(4,1)S(1)}, s32[]{:S(2)}) async-start(s8[16777216]{0:T(1024)(128)(4,1)} %bitcast.4), calls=%async_computation.3 | async-start | bytes 8388608
  1.8 5.3 %collective-permute-start = (bf16[64,1024]{1,0:T(8,128)(2,1)S(1)}, bf16[64,1024]{1,0:T(8,128)(2,1)S(1)}, u32[]{:S(2)}, u32[]{:S(2)}) collective-permute-start(bf16[64,1024]{1,0:T(8,128)(2,1)S(1)} %get-tuple-element.19.refs_0_.refs_6_), channel_id=1, source_target_pairs={{0,2},{2,4},{4,6},{6,7},{7,5},{5,3},{3,1},{1,0},{8,10},{10,12},{12... | collective-permute-start | bytes 393224 | tf_op jit(solution)/shard_map/ppermute | solution.py:60
  4.0 4.4 %collective-permute-start.3 = (bf16[64,1024]{1,0:T(8,128)(2,1)S(1)}, bf16[64,1024]{1,0:T(8,128)(2,1)S(1)}, u32[]{:S(2)}, u32[]{:S(2)}) collective-permute-start(bf16[64,1024]{1,0:T(8,128)(2,1)S(1)} %get-tuple-element.20.refs_1_.refs_7_), channel_id=1, source_target_pairs={{0,1},{2,0},{4,2},{6,4},{7,6},{5,7},{3,5},{1,3},{8,9},{10,8},{12,1... | collective-permute-start | bytes 393224 | tf_op jit(solution)/shard_map/ppermute | solution.py:60
  4.0 6.8 %collective-permute-start.2 = (bf16[64,1024]{1,0:T(8,128)(2,1)S(1)}, bf16[64,1024]{1,0:T(8,128)(2,1)S(1)}, u32[]{:S(2)}, u32[]{:S(2)}) collective-permute-start(bf16[64,1024]{1,0:T(8,128)(2,1)S(1)} %get-tuple-element.19.refs_0_.refs_6_), channel_id=1, source_target_pairs={{0,1},{2,0},{4,2},{6,4},{7,6},{5,7},{3,5},{1,3},{8,9},{10,8},{12,1... | collective-permute-start | bytes 393224 | tf_op jit(solution)/shard_map/ppermute | solution.py:60
  5.4 5.8 %collective-permute-start.1 = (bf16[64,1024]{1,0:T(8,128)(2,1)S(1)}, bf16[64,1024]{1,0:T(8,128)(2,1)S(1)}, u32[]{:S(2)}, u32[]{:S(2)}) collective-permute-start(bf16[64,1024]{1,0:T(8,128)(2,1)S(1)} %get-tuple-element.20.refs_1_.refs_7_), channel_id=1, source_target_pairs={{0,2},{2,4},{4,6},{6,7},{7,5},{5,3},{3,1},{1,0},{8,10},{10,12},{12... | collective-permute-start | bytes 393224 | tf_op jit(solution)/shard_map/ppermute | solution.py:60
  7.1 5.3 %collective-permute-start.4 = (bf16[64,1024]{1,0:T(8,128)(2,1)S(1)}, bf16[64,1024]{1,0:T(8,128)(2,1)S(1)}, u32[]{:S(2)}, u32[]{:S(2)}) collective-permute-start(bf16[64,1024]{1,0:T(8,128)(2,1)S(1)} %collective-permute-done.refs_2_.refs_8_), channel_id=1, source_target_pairs={{0,2},{2,4},{4,6},{6,7},{7,5},{5,3},{3,1},{1,0},{8,10},{10,12},{12... | collective-permute-start | bytes 393224 | tf_op jit(solution)/shard_map/ppermute | solution.py:60
  8.3 5.4 %collective-permute-start.7 = (bf16[64,1024]{1,0:T(8,128)(2,1)S(1)}, bf16[64,1024]{1,0:T(8,128)(2,1)S(1)}, u32[]{:S(2)}, u32[]{:S(2)}) collective-permute-start(bf16[64,1024]{1,0:T(8,128)(2,1)S(1)} %collective-permute-done.3.refs_5_.refs_11_), channel_id=1, source_target_pairs={{0,1},{2,0},{4,2},{6,4},{7,6},{5,7},{3,5},{1,3},{8,9},{10,8},{12,1... | collective-permute-start | bytes 393224 | tf_op jit(solution)/shard_map/ppermute | solution.py:60
  10.8 4.8 %collective-permute-start.6 = (bf16[64,1024]{1,0:T(8,128)(2,1)S(1)}, bf16[64,1024]{1,0:T(8,128)(2,1)S(1)}, u32[]{:S(2)}, u32[]{:S(2)}) collective-permute-start(bf16[64,1024]{1,0:T(8,128)(2,1)S(1)} %collective-permute-done.2.refs_4_.refs_10_), channel_id=1, source_target_pairs={{0,1},{2,0},{4,2},{6,4},{7,6},{5,7},{3,5},{1,3},{8,9},{10,8},{12,1... | collective-permute-start | bytes 393224 | tf_op jit(solution)/shard_map/ppermute | solution.py:60
  11.2 5.2 %collective-permute-start.5 = (bf16[64,1024]{1,0:T(8,128)(2,1)S(1)}, bf16[64,1024]{1,0:T(8,128)(2,1)S(1)}, u32[]{:S(2)}, u32[]{:S(2)}) collective-permute-start(bf16[64,1024]{1,0:T(8,128)(2,1)S(1)} %collective-permute-done.1.refs_3_.refs_9_), channel_id=1, source_target_pairs={{0,2},{2,4},{4,6},{6,7},{7,5},{5,3},{3,1},{1,0},{8,10},{10,12},{12... | collective-permute-start | bytes 393224 | tf_op jit(solution)/shard_map/ppermute | solution.py:60
  12.4 4.7 %collective-permute-start.8 = (bf16[64,1024]{1,0:T(8,128)(2,1)S(1)}, bf16[64,1024]{1,0:T(8,128)(2,1)S(1)}, u32[]{:S(2)}, u32[]{:S(2)}) collective-permute-start(bf16[64,1024]{1,0:T(8,128)(2,1)S(1)} %collective-permute-done.4.refs_6_.refs_12_), channel_id=1, source_target_pairs={{0,2},{2,4},{4,6},{6,7},{7,5},{5,3},{3,1},{1,0},{8,10},{10,12},{12... | collective-permute-start | bytes 393224 | tf_op jit(solution)/shard_map/ppermute | solution.py:60
  13.7 5.1 %collective-permute-start.11 = (bf16[64,1024]{1,0:T(8,128)(2,1)S(1)}, bf16[64,1024]{1,0:T(8,128)(2,1)S(1)}, u32[]{:S(2)}, u32[]{:S(2)}) collective-permute-start(bf16[64,1024]{1,0:T(8,128)(2,1)S(1)} %collective-permute-done.7.refs_9_.refs_15_), channel_id=1, source_target_pairs={{0,1},{2,0},{4,2},{6,4},{7,6},{5,7},{3,5},{1,3},{8,9},{10,8},{12,1... | collective-permute-start | bytes 393224 | tf_op jit(solution)/shard_map/ppermute | solution.py:60
  15.7 5.1 %collective-permute-start.10 = (bf16[64,1024]{1,0:T(8,128)(2,1)S(1)}, bf16[64,1024]{1,0:T(8,128)(2,1)S(1)}, u32[]{:S(2)}, u32[]{:S(2)}) collective-permute-start(bf16[64,1024]{1,0:T(8,128)(2,1)S(1)} %collective-permute-done.6.refs_8_.refs_14_), channel_id=1, source_target_pairs={{0,1},{2,0},{4,2},{6,4},{7,6},{5,7},{3,5},{1,3},{8,9},{10,8},{12,1... | collective-permute-start | bytes 393224 | tf_op jit(solution)/shard_map/ppermute | solution.py:60
  16.3 5.5 %collective-permute-start.9 = (bf16[64,1024]{1,0:T(8,128)(2,1)S(1)}, bf16[64,1024]{1,0:T(8,128)(2,1)S(1)}, u32[]{:S(2)}, u32[]{:S(2)}) collective-permute-start(bf16[64,1024]{1,0:T(8,128)(2,1)S(1)} %collective-permute-done.5.refs_7_.refs_13_), channel_id=1, source_target_pairs={{0,2},{2,4},{4,6},{6,7},{7,5},{5,3},{3,1},{1,0},{8,10},{10,12},{12... | collective-permute-start | bytes 393224 | tf_op jit(solution)/shard_map/ppermute | solution.py:60
  17.1 5.8 %collective-permute-start.12 = (bf16[64,1024]{1,0:T(8,128)(2,1)S(1)}, bf16[64,1024]{1,0:T(8,128)(2,1)S(1)}, u32[]{:S(2)}, u32[]{:S(2)}) collective-permute-start(bf16[64,1024]{1,0:T(8,128)(2,1)S(1)} %collective-permute-done.8.refs_10_.refs_16_), channel_id=1, source_target_pairs={{0,2},{2,4},{4,6},{6,7},{7,5},{5,3},{3,1},{1,0},{8,10},{10,12},{12... | collective-permute-start | bytes 393224 | tf_op jit(solution)/shard_map/ppermute | solution.py:60
  18.8 4.8 %collective-permute-start.13 = (bf16[64,1024]{1,0:T(8,128)(2,1)S(1)}, bf16[64,1024]{1,0:T(8,128)(2,1)S(1)}, u32[]{:S(2)}, u32[]{:S(2)}) collective-permute-start(bf16[64,1024]{1,0:T(8,128)(2,1)S(1)} %collective-permute-done.11.refs_13_.refs_19_), channel_id=1, source_target_pairs={{0,1},{2,0},{4,2},{6,4},{7,6},{5,7},{3,5},{1,3},{8,9},{10,8},{12,1... | collective-permute-start | bytes 393224 | tf_op jit(solution)/shard_map/ppermute | solution.py:60
  26.1 3.9 %collective-permute-start.18 = (bf16[128,512]{1,0:T(8,128)(2,1)S(1)}, bf16[128,512]{1,0:T(8,128)(2,1)S(1)}, u32[]{:S(2)}, u32[]{:S(2)}) collective-permute-start(bf16[128,512]{1,0:T(8,128)(2,1)S(1)} %get-tuple-element.21.refs_0_), channel_id=1, source_target_pairs={{0,1},{1,0},{2,3},{3,2},{4,5},{5,4},{6,7},{7,6},{8,9},{9,8},{10,11... | collective-permute-start | bytes 393224 | tf_op jit(solution)/shard_map/ppermute | solution.py:50
  26.9 3.8 %collective-permute-start.19 = (bf16[128,512]{1,0:T(8,128)(2,1)S(1)}, bf16[128,512]{1,0:T(8,128)(2,1)S(1)}, u32[]{:S(2)}, u32[]{:S(2)}) collective-permute-start(bf16[128,512]{1,0:T(8,128)(2,1)S(1)} %get-tuple-element.21.refs_0_), channel_id=1, source_target_pairs={{0,2},{1,3},{2,0},{3,1},{4,6},{5,7},{6,4},{7,5},{8,10},{9,11},{10,... | collective-permute-start | bytes 393224 | tf_op jit(solution)/shard_map/ppermute | solution.py:50
  28.2 4.7 %collective-permute-start.20 = (bf16[128,512]{1,0:T(8,128)(2,1)S(1)}, bf16[128,512]{1,0:T(8,128)(2,1)S(1)}, u32[]{:S(2)}, u32[]{:S(2)}) collective-permute-start(bf16[128,512]{1,0:T(8,128)(2,1)S(1)} %get-tuple-element.21.refs_0_), channel_id=1, source_target_pairs={{0,3},{1,2},{2,1},{3,0},{4,7},{5,6},{6,5},{7,4},{8,11},{9,10},{10,... | collective-permute-start | bytes 393224 | tf_op jit(solution)/shard_map/ppermute | solution.py:50
  32.9 33.7 %collective-permute-start.21 = (bf16[512,512]{1,0:T(8,128)(2,1)S(1)}, bf16[512,512]{1,0:T(8,128)(2,1)S(1)}, u32[]{:S(2)}, u32[]{:S(2)}) collective-permute-start(bf16[512,512]{1,0:T(8,128)(2,1)S(1)} %pack.3.refs_0_.refs_1_), channel_id=1, source_target_pairs={{0,8},{8,16},{16,24},{1,9},{9,17},{17,25},{2,10},{10,18},{18,26},{... | collective-permute-start | bytes 1572872 | tf_op jit(solution)/shard_map/ppermute | solution.py:29
  42.4 7.6 %collective-permute-start.14 = (bf16[128,512]{1,0:T(8,128)(2,1)S(1)}, bf16[128,512]{1,0:T(8,128)(2,1)S(1)}, u32[]{:S(2)}, u32[]{:S(2)}) collective-permute-start(bf16[128,512]{1,0:T(8,128)(2,1)S(1)} %get-tuple-element.21.refs_0_), channel_id=1, source_target_pairs={{0,6},{1,7},{2,4},{3,5},{4,2},{5,3},{6,0},{7,1},{8,14},{9,15},{10,... | collective-permute-start | bytes 393224 | tf_op jit(solution)/shard_map/ppermute | solution.py:50
  47.4 8.5 %collective-permute-start.15 = (bf16[128,512]{1,0:T(8,128)(2,1)S(1)}, bf16[128,512]{1,0:T(8,128)(2,1)S(1)}, u32[]{:S(2)}, u32[]{:S(2)}) collective-permute-start(bf16[128,512]{1,0:T(8,128)(2,1)S(1)} %get-tuple-element.21.refs_0_), channel_id=1, source_target_pairs={{0,4},{1,5},{2,6},{3,7},{4,0},{5,1},{6,2},{7,3},{8,12},{9,13},{10,... | collective-permute-start | bytes 393224 | tf_op jit(solution)/shard_map/ppermute | solution.py:50
  55.9 8.4 %collective-permute-start.22 = (bf16[256,512]{1,0:T(8,128)(2,1)S(1)}, bf16[256,512]{1,0:T(8,128)(2,1)S(1)}, u32[]{:S(2)}, u32[]{:S(2)}) collective-permute-start(bf16[256,512]{1,0:T(8,128)(2,1)S(1)} %pack.2.refs_1_.refs_2_), channel_id=1, source_target_pairs={{0,1},{1,0},{2,3},{3,2},{4,5},{5,4},{6,7},{7,6},{8,9},{9,8},{10,11... | collective-permute-start | bytes 786440 | tf_op jit(solution)/shard_map/ppermute | solution.py:50
  56.9 11.0 %collective-permute-start.16 = (bf16[256,512]{1,0:T(8,128)(2,1)S(1)}, bf16[256,512]{1,0:T(8,128)(2,1)S(1)}, u32[]{:S(2)}, u32[]{:S(2)}) collective-permute-start(bf16[256,512]{1,0:T(8,128)(2,1)S(1)} %pack.2.refs_1_.refs_2_), channel_id=1, source_target_pairs={{0,8},{8,16},{16,24},{1,9},{9,17},{17,25},{2,10},{10,18},{18,26},{... | collective-permute-start | bytes 786440 | tf_op jit(solution)/shard_map/ppermute | solution.py:29
  58.8 9.1 %collective-permute-start.17 = (bf16[256,512]{1,0:T(8,128)(2,1)S(1)}, bf16[256,512]{1,0:T(8,128)(2,1)S(1)}, u32[]{:S(2)}, u32[]{:S(2)}) collective-permute-start(bf16[256,512]{1,0:T(8,128)(2,1)S(1)} %pack.2.refs_1_.refs_2_), channel_id=1, source_target_pairs={{0,9},{1,8},{2,11},{3,10},{4,13},{5,12},{6,15},{7,14},{8,17},{9,16... | collective-permute-start | bytes 786440 | tf_op jit(solution)/shard_map/ppermute | solution.py:37
  64.3 3.6 %copy-start.1 = (bf16[1,128,1024]{2,1,0:T(8,128)(2,1)S(1)}, bf16[1,128,1024]{2,1,0:T(8,128)(2,1)}, u32[]{:S(2)}) copy-start(bf16[1,128,1024]{2,1,0:T(8,128)(2,1)} %param.7) | copy-start | bytes 786436
  64.3 3.6 %copy-start.2 = (f32[1,1024]{1,0:T(1,128)S(1)}, f32[1,1024]{1,0:T(1,128)}, u32[]{:S(2)}) copy-start(f32[1,1024]{1,0:T(1,128)} %refs_4_.1) | copy-start | bytes 12292
  69.9 10.8 %collective-permute-start.27 = (bf16[512,512]{1,0:T(8,128)(2,1)S(1)}, bf16[512,512]{1,0:T(8,128)(2,1)S(1)}, u32[]{:S(2)}, u32[]{:S(2)}) collective-permute-start(bf16[512,512]{1,0:T(8,128)(2,1)S(1)} %get-tuple-element.30), channel_id=1, source_target_pairs={{8,0},{16,8},{24,16},{9,1},{17,9},{25,17},{10,2},{18,10},{26,18},{... | collective-permute-start | bytes 1572872 | tf_op jit(solution)/shard_map/ppermute | solution.py:29
  74.0 11.9 %collective-permute-start.23 = (bf16[512,512]{1,0:T(8,128)(2,1)S(1)}, bf16[512,512]{1,0:T(8,128)(2,1)S(1)}, u32[]{:S(2)}, u32[]{:S(2)}) collective-permute-start(bf16[512,512]{1,0:T(8,128)(2,1)S(1)} %get-tuple-element.24), channel_id=1, source_target_pairs={{8,0},{16,8},{24,16},{9,1},{17,9},{25,17},{10,2},{18,10},{26,18},{... | collective-permute-start | bytes 1572872 | tf_op jit(solution)/shard_map/ppermute | solution.py:29
  80.7 8.0 %collective-permute-start.28 = (bf16[256,512]{1,0:T(8,128)(2,1)S(1)}, bf16[256,512]{1,0:T(8,128)(2,1)S(1)}, u32[]{:S(2)}, u32[]{:S(2)}) collective-permute-start(bf16[256,512]{1,0:T(8,128)(2,1)S(1)} %get-tuple-element.32), channel_id=1, source_target_pairs={{0,1},{1,0},{2,3},{3,2},{4,5},{5,4},{6,7},{7,6},{8,9},{9,8},{10,11... | collective-permute-start | bytes 786440 | tf_op jit(solution)/shard_map/ppermute | solution.py:50
  86.1 17.4 %collective-permute-start.24 = (bf16[128,512]{1,0:T(8,128)(2,1)S(1)}, bf16[128,512]{1,0:T(8,128)(2,1)S(1)}, u32[]{:S(2)}, u32[]{:S(2)}) collective-permute-start(bf16[128,512]{1,0:T(8,128)(2,1)S(1)} %get-tuple-element.26), channel_id=1, source_target_pairs={{0,1},{1,0},{2,3},{3,2},{4,5},{5,4},{6,7},{7,6},{8,9},{9,8},{10,11... | collective-permute-start | bytes 393224 | tf_op jit(solution)/shard_map/ppermute | solution.py:50
  86.8 16.7 %collective-permute-start.25 = (bf16[128,512]{1,0:T(8,128)(2,1)S(1)}, bf16[128,512]{1,0:T(8,128)(2,1)S(1)}, u32[]{:S(2)}, u32[]{:S(2)}) collective-permute-start(bf16[128,512]{1,0:T(8,128)(2,1)S(1)} %get-tuple-element.27), channel_id=1, source_target_pairs={{0,2},{1,3},{2,0},{3,1},{4,6},{5,7},{6,4},{7,5},{8,10},{9,11},{10,... | collective-permute-start | bytes 393224 | tf_op jit(solution)/shard_map/ppermute | solution.py:50
  87.1 16.3 %collective-permute-start.26 = (bf16[128,512]{1,0:T(8,128)(2,1)S(1)}, bf16[128,512]{1,0:T(8,128)(2,1)S(1)}, u32[]{:S(2)}, u32[]{:S(2)}) collective-permute-start(bf16[128,512]{1,0:T(8,128)(2,1)S(1)} %get-tuple-element.28), channel_id=1, source_target_pairs={{0,3},{1,2},{2,1},{3,0},{4,7},{5,6},{6,5},{7,4},{8,11},{9,10},{10,... | collective-permute-start | bytes 393224 | tf_op jit(solution)/shard_map/ppermute | solution.py:50
  88.8 14.6 %collective-permute-start.29 = (bf16[128,512]{1,0:T(8,128)(2,1)S(1)}, bf16[128,512]{1,0:T(8,128)(2,1)S(1)}, u32[]{:S(2)}, u32[]{:S(2)}) collective-permute-start(bf16[128,512]{1,0:T(8,128)(2,1)S(1)} %get-tuple-element.33), channel_id=1, source_target_pairs={{0,6},{1,7},{2,4},{3,5},{4,2},{5,3},{6,0},{7,1},{8,14},{9,15},{10,... | collective-permute-start | bytes 393224 | tf_op jit(solution)/shard_map/ppermute | solution.py:50
  90.9 12.5 %collective-permute-start.30 = (bf16[128,512]{1,0:T(8,128)(2,1)S(1)}, bf16[128,512]{1,0:T(8,128)(2,1)S(1)}, u32[]{:S(2)}, u32[]{:S(2)}) collective-permute-start(bf16[128,512]{1,0:T(8,128)(2,1)S(1)} %get-tuple-element.34), channel_id=1, source_target_pairs={{0,4},{1,5},{2,6},{3,7},{4,0},{5,1},{6,2},{7,3},{8,12},{9,13},{10,... | collective-permute-start | bytes 393224 | tf_op jit(solution)/shard_map/ppermute | solution.py:50

commit v8 on v5

--- a/solution.py
+++ b/solution.py
@@ -177,6 +177,14 @@
         total_ref[here, :] = decoded(w_ref, 0, here, parts, BLOCKS, tok, None)
 
 
+def near_recon_kernel(part_ref, before_ref, w_ref, total_ref):
+    tok = total_ref.shape[1]
+    steps, tile = tiles(w_ref.shape[1])
+    for j in range(steps):
+        here = slice(j * tile, (j + 1) * tile)
+        total_ref[here, :] = decoded(w_ref, 1, here, [part_ref], BLOCKS[:1], tok, before_ref[here, :])
+
+
 def products(error_ref, w_ref, slot, masks, out_ref):
     tok = error_ref.shape[0]
     for row, mask in enumerate(masks):
@@ -187,13 +195,14 @@
 
 
 def recon_kernel(scale, *refs):
-    parts, (total_ref, w_ref, b_ref, target_ref, error_ref, far_ref) = refs[: len(BLOCKS)], refs[len(BLOCKS) :]
+    rest = BLOCKS[1:]
+    parts, (total_ref, w_ref, b_ref, target_ref, error_ref, far_ref) = refs[: len(rest)], refs[len(rest) :]
     tok = total_ref.shape[1]
     steps, tile = tiles(w_ref.shape[1])
 
     for j in range(steps):
         here = slice(j * tile, (j + 1) * tile)
-        total = decoded(w_ref, 1, here, parts, BLOCKS, tok, total_ref[here, :])
+        total = decoded(w_ref, 1, here, parts, rest, tok, total_ref[here, :])
         error = total.T + b_ref[:, here] - target_ref[:, here].astype(F32)
         error_ref[:, here] = (error * scale).astype(BF16)
 
@@ -281,15 +290,25 @@
         cost_estimate=cost(matmul, 0),
     )(*own, weights)
 
+    total = pl.pallas_call(
+        near_recon_kernel,
+        name="near_recon",
+        out_shape=struct((width, tok), F32),
+        in_specs=vmem(3),
+        out_specs=vmem(1)[0],
+        compiler_params=params(8),
+        cost_estimate=cost(matmul // 2, 0),
+    )(previous[0], total, weights)
+
     error, sent_far = pl.pallas_call(
         functools.partial(recon_kernel, scale),
         name="recon",
         out_shape=(struct((tok, width), BF16), stack(FAR + CROSSING, BF16)),
-        in_specs=vmem(len(previous) + 4),
+        in_specs=vmem(len(previous) + 3),
         out_specs=tuple(vmem(2)),
         compiler_params=params(8),
         cost_estimate=cost(2 * matmul, 4 * MIB),
-    )(*previous, total, weights, dec_b, targets[0])
+    )(*previous[1:], total, weights, dec_b, targets[0])
     arrived_far = from_behind(sent_far, "section", -1)
 
     sent_near, own_near, own_far = pl.pallas_call(
@@ -346,18 +365,19 @@
     held_grad = pltpu.with_memory_space_constraint(dec_grad, pltpu.HBM)
     dec_grad = dec_grad_slot(1, BLOCKS, previous, held_grad)
 
+    block_rows = tiles(own_features)[1]
     enc_grad = pl.pallas_call(
         enc_grad_kernel,
         name="enc_grad",
-        grid=(own_features // LANES,),
+        grid=(own_features // block_rows,),
         out_shape=struct(enc_w.shape, BF16),
         in_specs=[
-            *[pl.BlockSpec((tok, LANES), lambda j: (0, j))] * len(grads),
+            *[pl.BlockSpec((tok, block_rows), lambda j: (0, j))] * len(grads),
             *[pl.BlockSpec((tok // 2, width), lambda j: (0, 0))] * (2 * count),
-            pl.BlockSpec((tok, LANES), lambda j: (0, j)),
+            pl.BlockSpec((tok, block_rows), lambda j: (0, j)),
         ],
-        out_specs=pl.BlockSpec((1, LANES, model), lambda j: (0, j, 0)),
-        compiler_params=params(16),
+        out_specs=pl.BlockSpec((1, block_rows, model), lambda j: (0, j, 0)),
+        compiler_params=params(24),
         cost_estimate=cost(matmul, 2 * own_features * model),
     )(*grads, *inputs_of, active)
     return enc_grad, dec_grad

time: 99 us -> 98.1 us (level)
  waiting for transfers between devices: 30.5 us -> 23.1 us
  starting transfers between devices: 41.4 us -> 48 us
    ppermute x5, starting transfers between devices: 17 us -> 23.8 us  [from_behind(): lax.ppermute(value, axis, [(source, source + steps) for source in range(i...]
    ppermute x5, waiting for transfers between devices: 14.8 us -> 10.2 us  [from_behind(): lax.ppermute(value, axis, [(source, source + steps) for source in range(i...]
    ppermute x12, waiting for transfers between devices: 5.21 us -> 2.43 us  [exchanged(): return lax.ppermute(value, 'feat', [(i, i ^ mask) for i in range(count)])]
    pallas_call x1, Pallas kernels: 3 us -> 1.94 us  [on_device(): pl.pallas_call(functools.partial(recon_kernel, scale), name='recon', out_...]
    pallas_call x1 -> x2, Pallas kernels: 5.2 us -> 6.13 us  [the longest x1 4.89 us: on_device(): pl.pallas_call(enc_grad_kernel, name='enc_grad', grid=(own_features // bl...]
  transfers between devices with their start and end apart: 31 -> 31, of which waited for: 15 -> 13; matrix products, arithmetic and copies ran while one was open for 0% -> 0% of each run, Pallas kernels for 14% -> 16%
where the time goes in v8:
time: 98.1 us; the launch traced here: 97.9 us
  starting transfers between devices  48 us (49%)
  Pallas kernels  24.8 us (25%)
  waiting for transfers between devices  23.1 us (24%)
  local copies, waits for them, and re-layouts  1.13 us (1%)
    ppermute x5, starting transfers between devices, from_behind(): lax.ppermute(value, axis, [(source, source + steps) for source in range(i...  23.8 us
    ppermute x12, starting transfers between devices, exchanged(): return lax.ppermute(value, 'feat', [(i, i ^ mask) for i in range(count)])  12.8 us
    ppermute x14, starting transfers between devices, passed_on(): lax.ppermute(value, 'feat', [(order[p], order[(p + by) % count]) for p in...  11.4 us
    ppermute x14, waiting for transfers between devices, passed_on(): lax.ppermute(value, 'feat', [(order[p], order[(p + by) % count]) for p in...  10.5 us
    ppermute x5, waiting for transfers between devices, from_behind(): lax.ppermute(value, axis, [(source, source + steps) for source in range(i...  10.2 us
    pallas_call x2, Pallas kernels, dec_grad_slot(): pl.pallas_call(functools.partial(dec_grad_kernel, groups), name='dec_grad...  9.81 us
    pallas_call x1, Pallas kernels, on_device(): pl.pallas_call(enc_grad_kernel, name='enc_grad', grid=(own_features // bl...  4.89 us
    ppermute x12, waiting for transfers between devices, exchanged(): return lax.ppermute(value, 'feat', [(i, i ^ mask) for i in range(count)])  2.43 us
  transfers between devices with their start and end apart: 31, of which 13 were waited for; matrix products, arithmetic and copies ran while one was open for 0% of the time, Pallas kernels for 16%

profile of v8, /device:TPU:1, one launch (start us, length us, event | category | flops | bytes accessed | tf_op | source)
XLA Modules:
  0.0 97.9 jit_solution(9808465160932324778)
XLA Ops:
  0.7 1.1 %copy-done.4 = bf16[1,128,1024]{2,1,0:T(8,128)(2,1)S(1)} copy-done((bf16[1,128,1024]{2,1,0:T(8,128)(2,1)S(1)}, bf16[1,128,1024]{2,1,0:T(8,128)(2,1)}, u32[]{:S(2)}) %copy-start.4) | copy-done | bytes 262168
  1.8 2.2 %collective-permute-start = (bf16[64,1024]{1,0:T(8,128)(2,1)S(1)}, bf16[64,1024]{1,0:T(8,128)(2,1)S(1)}, u32[]{:S(2)}, u32[]{:S(2)}) collective-permute-start(bf16[64,1024]{1,0:T(8,128)(2,1)S(1)} %get-tuple-element.19.refs_0_.refs_6_), channel_id=1, source_target_pairs={{0,2},{2,4},{4,6},{6,7},{7,5},{5,3},{3,1},{1,0},{8,10},{10,12},{12... | collective-permute-start | bytes 393224 | tf_op jit(solution)/shard_map/ppermute | solution.py:51
  4.0 1.4 %collective-permute-start.2 = (bf16[64,1024]{1,0:T(8,128)(2,1)S(1)}, bf16[64,1024]{1,0:T(8,128)(2,1)S(1)}, u32[]{:S(2)}, u32[]{:S(2)}) collective-permute-start(bf16[64,1024]{1,0:T(8,128)(2,1)S(1)} %get-tuple-element.19.refs_0_.refs_6_), channel_id=1, source_target_pairs={{0,1},{2,0},{4,2},{6,4},{7,6},{5,7},{3,5},{1,3},{8,9},{10,8},{12,1... | collective-permute-start | bytes 393224 | tf_op jit(solution)/shard_map/ppermute | solution.py:51
  5.5 1.7 %collective-permute-done.refs_2_.refs_8_ = bf16[64,1024]{1,0:T(8,128)(2,1)S(1)} collective-permute-done((bf16[64,1024]{1,0:T(8,128)(2,1)S(1)}, bf16[64,1024]{1,0:T(8,128)(2,1)S(1)}, u32[]{:S(2)}, u32[]{:S(2)}) %collective-permute-start) | collective-permute-done | bytes 131104 | tf_op jit(solution)/shard_map/ppermute | solution.py:51
  7.1 1.2 %collective-permute-start.4 = (bf16[64,1024]{1,0:T(8,128)(2,1)S(1)}, bf16[64,1024]{1,0:T(8,128)(2,1)S(1)}, u32[]{:S(2)}, u32[]{:S(2)}) collective-permute-start(bf16[64,1024]{1,0:T(8,128)(2,1)S(1)} %collective-permute-done.refs_2_.refs_8_), channel_id=1, source_target_pairs={{0,2},{2,4},{4,6},{6,7},{7,5},{5,3},{3,1},{1,0},{8,10},{10,12},{12... | collective-permute-start | bytes 393224 | tf_op jit(solution)/shard_map/ppermute | solution.py:51
  8.3 0.3 collective-permute-start.7
  8.6 2.2 %collective-permute-done.2.refs_4_.refs_10_ = bf16[64,1024]{1,0:T(8,128)(2,1)S(1)} collective-permute-done((bf16[64,1024]{1,0:T(8,128)(2,1)S(1)}, bf16[64,1024]{1,0:T(8,128)(2,1)S(1)}, u32[]{:S(2)}, u32[]{:S(2)}) %collective-permute-start.2) | collective-permute-done | bytes 131104 | tf_op jit(solution)/shard_map/ppermute | solution.py:51
  10.8 0.3 collective-permute-start.6
  11.2 1.1 %collective-permute-start.5 = (bf16[64,1024]{1,0:T(8,128)(2,1)S(1)}, bf16[64,1024]{1,0:T(8,128)(2,1)S(1)}, u32[]{:S(2)}, u32[]{:S(2)}) collective-permute-start(bf16[64,1024]{1,0:T(8,128)(2,1)S(1)} %collective-permute-done.1.refs_3_.refs_9_), channel_id=1, source_target_pairs={{0,2},{2,4},{4,6},{6,7},{7,5},{5,3},{3,1},{1,0},{8,10},{10,12},{12... | collective-permute-start | bytes 393224 | tf_op jit(solution)/shard_map/ppermute | solution.py:51
  12.3 0.1 collective-permute-done.4.refs_6_.refs_12_
  12.4 1.3 %collective-permute-start.8 = (bf16[64,1024]{1,0:T(8,128)(2,1)S(1)}, bf16[64,1024]{1,0:T(8,128)(2,1)S(1)}, u32[]{:S(2)}, u32[]{:S(2)}) collective-permute-start(bf16[64,1024]{1,0:T(8,128)(2,1)S(1)} %collective-permute-done.4.refs_6_.refs_12_), channel_id=1, source_target_pairs={{0,2},{2,4},{4,6},{6,7},{7,5},{5,3},{3,1},{1,0},{8,10},{10,12},{12... | collective-permute-start | bytes 393224 | tf_op jit(solution)/shard_map/ppermute | solution.py:51
  13.7 0.2 collective-permute-start.11
  13.9 1.8 %collective-permute-done.6.refs_8_.refs_14_ = bf16[64,1024]{1,0:T(8,128)(2,1)S(1)} collective-permute-done((bf16[64,1024]{1,0:T(8,128)(2,1)S(1)}, bf16[64,1024]{1,0:T(8,128)(2,1)S(1)}, u32[]{:S(2)}, u32[]{:S(2)}) %collective-permute-start.6) | collective-permute-done | bytes 131104 | tf_op jit(solution)/shard_map/ppermute | solution.py:51
  15.7 0.7 collective-permute-start.10
  16.3 0.8 collective-permute-start.9
  17.1 1.3 %collective-permute-start.12 = (bf16[64,1024]{1,0:T(8,128)(2,1)S(1)}, bf16[64,1024]{1,0:T(8,128)(2,1)S(1)}, u32[]{:S(2)}, u32[]{:S(2)}) collective-permute-start(bf16[64,1024]{1,0:T(8,128)(2,1)S(1)} %collective-permute-done.8.refs_10_.refs_16_), channel_id=1, source_target_pairs={{0,2},{2,4},{4,6},{6,7},{7,5},{5,3},{3,1},{1,0},{8,10},{10,12},{12... | collective-permute-start | bytes 393224 | tf_op jit(solution)/shard_map/ppermute | solution.py:51
  18.4 0.4 collective-permute-done.11.refs_13_.refs_19_
  18.8 0.5 collective-permute-start.13
  19.4 1.4 %collective-permute-done.10.refs_12_.refs_18_ = bf16[64,1024]{1,0:T(8,128)(2,1)S(1)} collective-permute-done((bf16[64,1024]{1,0:T(8,128)(2,1)S(1)}, bf16[64,1024]{1,0:T(8,128)(2,1)S(1)}, u32[]{:S(2)}, u32[]{:S(2)}) %collective-permute-start.10) | collective-permute-done | bytes 131104 | tf_op jit(solution)/shard_map/ppermute | solution.py:51
  20.7 1.1 %collective-permute-done.9.refs_11_.refs_17_ = bf16[64,1024]{1,0:T(8,128)(2,1)S(1)} collective-permute-done((bf16[64,1024]{1,0:T(8,128)(2,1)S(1)}, bf16[64,1024]{1,0:T(8,128)(2,1)S(1)}, u32[]{:S(2)}, u32[]{:S(2)}) %collective-permute-start.9) | collective-permute-done | bytes 131104 | tf_op jit(solution)/shard_map/ppermute | solution.py:51
  21.8 1.1 %collective-permute-done.12.refs_14_.refs_20_ = bf16[64,1024]{1,0:T(8,128)(2,1)S(1)} collective-permute-done((bf16[64,1024]{1,0:T(8,128)(2,1)S(1)}, bf16[64,1024]{1,0:T(8,128)(2,1)S(1)}, u32[]{:S(2)}, u32[]{:S(2)}) %collective-permute-start.12) | collective-permute-done | bytes 131104 | tf_op jit(solution)/shard_map/ppermute | solution.py:51
  23.0 0.7 collective-permute-done.13.refs_15_.refs_21_
  23.6 2.4 %pre.1 = (bf16[128,512]{1,0:T(8,128)(2,1)S(1)}, f32[128,512]{1,0:T(8,128)S(1)}) custom-call(bf16[64,1024]{1,0:T(8,128)(2,1)S(1)} %get-tuple-element.19.refs_0_.refs_6_, bf16[64,1024]{1,0:T(8,128)(2,1)S(1)} %get-tuple-element.20.refs_1_.refs_7_, bf16[64,1024]{1,0:T(8,128)(2,1)S(1)} %collective-permute-done.refs_2_.refs_8_, ...), custom_call_target="tpu_custom_call" | custom-call | flops 1073741824 | tf_op jit(solution)/shard_map/pre/pallas_call | solution.py:268
  26.1 0.8 collective-permute-start.19
  26.9 1.3 %collective-permute-start.20 = (bf16[128,512]{1,0:T(8,128)(2,1)S(1)}, bf16[128,512]{1,0:T(8,128)(2,1)S(1)}, u32[]{:S(2)}, u32[]{:S(2)}) collective-permute-start(bf16[128,512]{1,0:T(8,128)(2,1)S(1)} %get-tuple-element.21.refs_0_), channel_id=1, source_target_pairs={{0,2},{1,3},{2,0},{3,1},{4,6},{5,7},{6,4},{7,5},{8,10},{9,11},{10,... | collective-permute-start | bytes 393224 | tf_op jit(solution)/shard_map/ppermute | solution.py:41
  28.2 0.6 collective-permute-start.21
  28.8 3.3 %collective-permute-start.14 = (bf16[128,512]{1,0:T(8,128)(2,1)S(1)}, bf16[128,512]{1,0:T(8,128)(2,1)S(1)}, u32[]{:S(2)}, u32[]{:S(2)}) collective-permute-start(bf16[128,512]{1,0:T(8,128)(2,1)S(1)} %get-tuple-element.21.refs_0_), channel_id=1, source_target_pairs={{0,6},{1,7},{2,4},{3,5},{4,2},{5,3},{6,0},{7,1},{8,14},{9,15},{10,... | collective-permute-start | bytes 393224 | tf_op jit(solution)/shard_map/ppermute | solution.py:41
  32.1 0.8 collective-permute-done.21.refs_3_
  32.9 11.3 %collective-permute-start.22 = (bf16[512,512]{1,0:T(8,128)(2,1)S(1)}, bf16[512,512]{1,0:T(8,128)(2,1)S(1)}, u32[]{:S(2)}, u32[]{:S(2)}) collective-permute-start(bf16[512,512]{1,0:T(8,128)(2,1)S(1)} %pack.3.refs_0_.refs_1_), channel_id=1, source_target_pairs={{0,8},{8,16},{16,24},{1,9},{9,17},{17,25},{2,10},{10,18},{18,26},{... | collective-permute-start | bytes 1572872 | tf_op jit(solution)/shard_map/ppermute | solution.py:28
  44.3 0.8 collective-permute-start.17
  45.1 4.1 %collective-permute-start.16 = (bf16[256,512]{1,0:T(8,128)(2,1)S(1)}, bf16[256,512]{1,0:T(8,128)(2,1)S(1)}, u32[]{:S(2)}, u32[]{:S(2)}) collective-permute-start(bf16[256,512]{1,0:T(8,128)(2,1)S(1)} %pack.2.refs_1_.refs_2_), channel_id=1, source_target_pairs={{0,8},{8,16},{16,24},{1,9},{9,17},{17,25},{2,10},{10,18},{18,26},{... | collective-permute-start | bytes 786440 | tf_op jit(solution)/shard_map/ppermute | solution.py:28
  49.2 1.6 %collective-permute-done.17.refs_2_.refs_3_ = bf16[256,512]{1,0:T(8,128)(2,1)S(1)} collective-permute-done((bf16[256,512]{1,0:T(8,128)(2,1)S(1)}, bf16[256,512]{1,0:T(8,128)(2,1)S(1)}, u32[]{:S(2)}, u32[]{:S(2)}) %collective-permute-start.17) | collective-permute-done | bytes 262176 | tf_op jit(solution)/shard_map/ppermute | solution.py:41
  50.8 4.3 %collective-permute-start.18 = (bf16[256,512]{1,0:T(8,128)(2,1)S(1)}, bf16[256,512]{1,0:T(8,128)(2,1)S(1)}, u32[]{:S(2)}, u32[]{:S(2)}) collective-permute-start(bf16[256,512]{1,0:T(8,128)(2,1)S(1)} %collective-permute-done.17.refs_2_.refs_3_), channel_id=1, source_target_pairs={{0,8},{8,16},{16,24},{1,9},{9,17},{17,25},{2,10},{10,18},{18,26},{... | collective-permute-start | bytes 786440 | tf_op jit(solution)/shard_map/ppermute | solution.py:28
  55.2 2.3 %own_recon.1.before_ref = f32[1024,128]{1,0:T(8,128)S(1)} custom-call(bf16[512,512]{1,0:T(8,128)(2,1)S(1)} %pack.3.refs_0_.refs_1_, bf16[256,512]{1,0:T(8,128)(2,1)S(1)} %pack.2.refs_1_.refs_2_, bf16[256,512]{1,0:T(8,128)(2,1)S(1)} %collective-permute-done.17.refs_2_.refs_3_, bf16[2,1024,4096]{2,1,0:T(8,128)(2,1)S(1)} %bitcast.6), custom_call_target="tpu_custom_call" | custom-call | flops 1073741824 | tf_op jit(solution)/shard_map/own_recon/pallas_call | solution.py:283
  57.5 1.2 %near_recon.1.refs_2_ = f32[1024,128]{1,0:T(8,128)S(1)} custom-call(bf16[512,512]{1,0:T(8,128)(2,1)S(1)} %collective-permute-done.22.part_ref.refs_1_, f32[1024,128]{1,0:T(8,128)S(1)} %own_recon.1.before_ref, bf16[2,1024,4096]{2,1,0:T(8,128)(2,1)S(1)} %bitcast.7), custom_call_target="tpu_custom_call" | custom-call | flops 536870912 | tf_op jit(solution)/shard_map/near_recon/pallas_call | solution.py:293
  58.8 1.9 %recon.1 = (bf16[128,1024]{1,0:T(8,128)(2,1)S(1)}, bf16[512,512]{1,0:T(8,128)(2,1)S(1)}) custom-call(bf16[256,512]{1,0:T(8,128)(2,1)S(1)} %collective-permute-done.16.refs_0_.refs_2_, bf16[256,512]{1,0:T(8,128)(2,1)S(1)} %collective-permute-done.18.refs_1_.refs_3_, f32[1024,128]{1,0:T(8,128)S(1)} %near_recon.1.refs_2_, bf16[2,1024,4096]{2,1,0:T(8,128)(2,1)S(1)} %bitcast.8, ...), custom_call_target="tpu_custom_call" | custom-call | flops 2147483648 | bytes 4194304 | tf_op jit(solution)/shard_map/recon/pallas_call | solution.py:303
  60.7 1.9 %collective-permute-start.27 = (bf16[512,512]{1,0:T(8,128)(2,1)S(1)}, bf16[512,512]{1,0:T(8,128)(2,1)S(1)}, u32[]{:S(2)}, u32[]{:S(2)}) collective-permute-start(bf16[512,512]{1,0:T(8,128)(2,1)S(1)} %get-tuple-element.30), channel_id=1, source_target_pairs={{8,0},{16,8},{24,16},{9,1},{17,9},{25,17},{10,2},{18,10},{26,18},{... | collective-permute-start | bytes 1572872 | tf_op jit(solution)/shard_map/ppermute | solution.py:28
  62.7 1.8 %own_grad.1 = (bf16[512,512]{1,0:T(8,128)(2,1)S(1)}, f32[512,512]{1,0:T(8,128)S(1)}, f32[512,512]{1,0:T(8,128)S(1)}) custom-call(bf16[128,1024]{1,0:T(8,128)(2,1)S(1)} %get-tuple-element.22.error_ref.refs_0_, bf16[2,1024,4096]{2,1,0:T(8,128)(2,1)S(1)} %bitcast.9), custom_call_target="tpu_custom_call" | custom-call | flops 1610612736 | bytes 6291456 | tf_op jit(solution)/shard_map/own_grad/pallas_call | solution.py:314
  64.5 2.1 %collective-permute-start.23 = (bf16[512,512]{1,0:T(8,128)(2,1)S(1)}, bf16[512,512]{1,0:T(8,128)(2,1)S(1)}, u32[]{:S(2)}, u32[]{:S(2)}) collective-permute-start(bf16[512,512]{1,0:T(8,128)(2,1)S(1)} %get-tuple-element.24), channel_id=1, source_target_pairs={{8,0},{16,8},{24,16},{9,1},{17,9},{25,17},{10,2},{18,10},{26,18},{... | collective-permute-start | bytes 1572872 | tf_op jit(solution)/shard_map/ppermute | solution.py:28
  66.6 5.3 %collective-permute-done.27.arrived_ref = bf16[512,512]{1,0:T(8,128)(2,1)S(1)} collective-permute-done((bf16[512,512]{1,0:T(8,128)(2,1)S(1)}, bf16[512,512]{1,0:T(8,128)(2,1)S(1)}, u32[]{:S(2)}, u32[]{:S(2)}) %collective-permute-start.27) | collective-permute-done | bytes 524320 | tf_op jit(solution)/shard_map/ppermute | solution.py:28
  72.0 0.3 collective-permute-start.28
  72.2 5.0 %collective-permute-done.23.arrived_ref = bf16[512,512]{1,0:T(8,128)(2,1)S(1)} collective-permute-done((bf16[512,512]{1,0:T(8,128)(2,1)S(1)}, bf16[512,512]{1,0:T(8,128)(2,1)S(1)}, u32[]{:S(2)}, u32[]{:S(2)}) %collective-permute-start.23) | collective-permute-done | bytes 524320 | tf_op jit(solution)/shard_map/ppermute | solution.py:28
  77.3 0.3 collective-permute-start.24
  77.7 2.4 %collective-permute-start.26 = (bf16[128,512]{1,0:T(8,128)(2,1)S(1)}, bf16[128,512]{1,0:T(8,128)(2,1)S(1)}, u32[]{:S(2)}, u32[]{:S(2)}) collective-permute-start(bf16[128,512]{1,0:T(8,128)(2,1)S(1)} %get-tuple-element.28), channel_id=1, source_target_pairs={{0,3},{1,2},{2,1},{3,0},{4,7},{5,6},{6,5},{7,4},{8,11},{9,10},{10,... | collective-permute-start | bytes 393224 | tf_op jit(solution)/shard_map/ppermute | solution.py:41
  80.1 3.1 %collective-permute-start.29 = (bf16[128,512]{1,0:T(8,128)(2,1)S(1)}, bf16[128,512]{1,0:T(8,128)(2,1)S(1)}, u32[]{:S(2)}, u32[]{:S(2)}) collective-permute-start(bf16[128,512]{1,0:T(8,128)(2,1)S(1)} %get-tuple-element.33), channel_id=1, source_target_pairs={{0,6},{1,7},{2,4},{3,5},{4,2},{5,3},{6,0},{7,1},{8,14},{9,15},{10,... | collective-permute-start | bytes 393224 | tf_op jit(solution)/shard_map/ppermute | solution.py:41
  83.2 4.9 %dec_grad.2.refs_4_ = bf16[1,2,1024,4096]{3,2,1,0:T(8,128)(2,1)} custom-call(bf16[128,1024]{1,0:T(8,128)(2,1)S(1)} %get-tuple-element.22.error_ref.refs_0_, bf16[512,512]{1,0:T(8,128)(2,1)S(1)} %pack.3.refs_0_.refs_1_, bf16[256,512]{1,0:T(8,128)(2,1)S(1)} %pack.2.refs_1_.refs_2_, bf16[256,512]{1,0:T(8,128)(2,1)S(1)} %collective-permute-done.17.refs_2_.refs_3_), custom_call_target="tpu_custom_call" | custom-call | flops 1073741824 | bytes 8388608 | tf_op jit(solution)/shard_map/dec_grad/pallas_call | solution.py:328
  88.1 4.9 %dec_grad.3 = bf16[1,2,1024,4096]{3,2,1,0:T(8,128)(2,1)} custom-call(bf16[128,1024]{1,0:T(8,128)(2,1)S(1)} %get-tuple-element.22.error_ref.refs_0_, bf16[512,512]{1,0:T(8,128)(2,1)S(1)} %collective-permute-done.22.part_ref.refs_1_, bf16[256,512]{1,0:T(8,128)(2,1)S(1)} %collective-permute-done.16.refs_0_.refs_2_, ...), custom_call_target="tpu_custom_call", output_to_operand_aliasing={{}: (4, {})} | custom-call | flops 1073741824 | bytes 8388608 | tf_op jit(solution)/shard_map/dec_grad/pallas_call | solution.py:328
  93.0 4.9 %enc_grad.1 = bf16[1,512,8192]{2,1,0:T(8,128)(2,1)} custom-call(f32[128,512]{1,0:T(8,128)S(1)} %get-tuple-element.25.refs_0_, bf16[128,512]{1,0:T(8,128)(2,1)S(1)} %collective-permute-done.24.refs_1_, bf16[128,512]{1,0:T(8,128)(2,1)S(1)} %collective-permute-done.25.refs_2_, bf16[128,512]{1,0:T(8,128)(2,1)S(1)} %collective-permute-done.26.refs_3_, ...), custom_call_target="tpu_custom_call" | custom-call | flops 1073741824 | bytes 8388608 | tf_op jit(solution)/shard_map/enc_grad/pallas_call | solution.py:369
  (47 shorter events, 0.6 us)
Async XLA Ops:
  0.6 54.5 %slice-start = ((s8[16777216]{0:T(1024)(128)(4,1)}), s8[4194304]{0:T(1024)(128)(4,1)S(1)}, s32[]{:S(2)}) async-start(s8[16777216]{0:T(1024)(128)(4,1)} %bitcast.4), calls=%async_computation | async-start | bytes 8388608
  0.6 1.1 %copy-start.4 = (bf16[1,128,1024]{2,1,0:T(8,128)(2,1)S(1)}, bf16[1,128,1024]{2,1,0:T(8,128)(2,1)}, u32[]{:S(2)}) copy-start(bf16[1,128,1024]{2,1,0:T(8,128)(2,1)} %param.6) | copy-start | bytes 786436
  1.7 21.9 %copy-start = (bf16[1,512,8192]{2,1,0:T(8,128)(2,1)S(1)}, bf16[1,512,8192]{2,1,0:T(8,128)(2,1)}, u32[]{:S(2)}) copy-start(bf16[1,512,8192]{2,1,0:T(8,128)(2,1)} %param.8) | copy-start | bytes 25165828
  1.7 21.9 %copy-start.3 = (f32[1,512]{1,0:T(1,128)S(1)}, f32[1,512]{1,0:T(1,128)}, u32[]{:S(2)}) copy-start(f32[1,512]{1,0:T(1,128)} %refs_17_.1) | copy-start | bytes 6148
  1.7 53.4 %slice-start.1 = ((s8[16777216]{0:T(1024)(128)(4,1)}), s8[4194304]{0:T(1024)(128)(4,1)S(1)}, s32[]{:S(2)}) async-start(s8[16777216]{0:T(1024)(128)(4,1)} %bitcast.4), calls=%async_computation.1 | async-start | bytes 8388608
  1.7 53.4 %slice-start.2 = ((s8[16777216]{0:T(1024)(128)(4,1)}), s8[4194304]{0:T(1024)(128)(4,1)S(1)}, s32[]{:S(2)}) async-start(s8[16777216]{0:T(1024)(128)(4,1)} %bitcast.4), calls=%async_computation.2 | async-start | bytes 8388608
  1.8 53.4 %slice-start.3 = ((s8[16777216]{0:T(1024)(128)(4,1)}), s8[4194304]{0:T(1024)(128)(4,1)S(1)}, s32[]{:S(2)}) async-start(s8[16777216]{0:T(1024)(128)(4,1)} %bitcast.4), calls=%async_computation.3 | async-start | bytes 8388608
  1.8 5.3 %collective-permute-start = (bf16[64,1024]{1,0:T(8,128)(2,1)S(1)}, bf16[64,1024]{1,0:T(8,128)(2,1)S(1)}, u32[]{:S(2)}, u32[]{:S(2)}) collective-permute-start(bf16[64,1024]{1,0:T(8,128)(2,1)S(1)} %get-tuple-element.19.refs_0_.refs_6_), channel_id=1, source_target_pairs={{0,2},{2,4},{4,6},{6,7},{7,5},{5,3},{3,1},{1,0},{8,10},{10,12},{12... | collective-permute-start | bytes 393224 | tf_op jit(solution)/shard_map/ppermute | solution.py:51
  4.0 4.4 %collective-permute-start.3 = (bf16[64,1024]{1,0:T(8,128)(2,1)S(1)}, bf16[64,1024]{1,0:T(8,128)(2,1)S(1)}, u32[]{:S(2)}, u32[]{:S(2)}) collective-permute-start(bf16[64,1024]{1,0:T(8,128)(2,1)S(1)} %get-tuple-element.20.refs_1_.refs_7_), channel_id=1, source_target_pairs={{0,1},{2,0},{4,2},{6,4},{7,6},{5,7},{3,5},{1,3},{8,9},{10,8},{12,1... | collective-permute-start | bytes 393224 | tf_op jit(solution)/shard_map/ppermute | solution.py:51
  4.0 6.8 %collective-permute-start.2 = (bf16[64,1024]{1,0:T(8,128)(2,1)S(1)}, bf16[64,1024]{1,0:T(8,128)(2,1)S(1)}, u32[]{:S(2)}, u32[]{:S(2)}) collective-permute-start(bf16[64,1024]{1,0:T(8,128)(2,1)S(1)} %get-tuple-element.19.refs_0_.refs_6_), channel_id=1, source_target_pairs={{0,1},{2,0},{4,2},{6,4},{7,6},{5,7},{3,5},{1,3},{8,9},{10,8},{12,1... | collective-permute-start | bytes 393224 | tf_op jit(solution)/shard_map/ppermute | solution.py:51
  5.4 5.8 %collective-permute-start.1 = (bf16[64,1024]{1,0:T(8,128)(2,1)S(1)}, bf16[64,1024]{1,0:T(8,128)(2,1)S(1)}, u32[]{:S(2)}, u32[]{:S(2)}) collective-permute-start(bf16[64,1024]{1,0:T(8,128)(2,1)S(1)} %get-tuple-element.20.refs_1_.refs_7_), channel_id=1, source_target_pairs={{0,2},{2,4},{4,6},{6,7},{7,5},{5,3},{3,1},{1,0},{8,10},{10,12},{12... | collective-permute-start | bytes 393224 | tf_op jit(solution)/shard_map/ppermute | solution.py:51
  7.1 5.3 %collective-permute-start.4 = (bf16[64,1024]{1,0:T(8,128)(2,1)S(1)}, bf16[64,1024]{1,0:T(8,128)(2,1)S(1)}, u32[]{:S(2)}, u32[]{:S(2)}) collective-permute-start(bf16[64,1024]{1,0:T(8,128)(2,1)S(1)} %collective-permute-done.refs_2_.refs_8_), channel_id=1, source_target_pairs={{0,2},{2,4},{4,6},{6,7},{7,5},{5,3},{3,1},{1,0},{8,10},{10,12},{12... | collective-permute-start | bytes 393224 | tf_op jit(solution)/shard_map/ppermute | solution.py:51
  8.3 5.4 %collective-permute-start.7 = (bf16[64,1024]{1,0:T(8,128)(2,1)S(1)}, bf16[64,1024]{1,0:T(8,128)(2,1)S(1)}, u32[]{:S(2)}, u32[]{:S(2)}) collective-permute-start(bf16[64,1024]{1,0:T(8,128)(2,1)S(1)} %collective-permute-done.3.refs_5_.refs_11_), channel_id=1, source_target_pairs={{0,1},{2,0},{4,2},{6,4},{7,6},{5,7},{3,5},{1,3},{8,9},{10,8},{12,1... | collective-permute-start | bytes 393224 | tf_op jit(solution)/shard_map/ppermute | solution.py:51
  10.8 4.8 %collective-permute-start.6 = (bf16[64,1024]{1,0:T(8,128)(2,1)S(1)}, bf16[64,1024]{1,0:T(8,128)(2,1)S(1)}, u32[]{:S(2)}, u32[]{:S(2)}) collective-permute-start(bf16[64,1024]{1,0:T(8,128)(2,1)S(1)} %collective-permute-done.2.refs_4_.refs_10_), channel_id=1, source_target_pairs={{0,1},{2,0},{4,2},{6,4},{7,6},{5,7},{3,5},{1,3},{8,9},{10,8},{12,1... | collective-permute-start | bytes 393224 | tf_op jit(solution)/shard_map/ppermute | solution.py:51
  11.2 5.2 %collective-permute-start.5 = (bf16[64,1024]{1,0:T(8,128)(2,1)S(1)}, bf16[64,1024]{1,0:T(8,128)(2,1)S(1)}, u32[]{:S(2)}, u32[]{:S(2)}) collective-permute-start(bf16[64,1024]{1,0:T(8,128)(2,1)S(1)} %collective-permute-done.1.refs_3_.refs_9_), channel_id=1, source_target_pairs={{0,2},{2,4},{4,6},{6,7},{7,5},{5,3},{3,1},{1,0},{8,10},{10,12},{12... | collective-permute-start | bytes 393224 | tf_op jit(solution)/shard_map/ppermute | solution.py:51
  12.4 4.7 %collective-permute-start.8 = (bf16[64,1024]{1,0:T(8,128)(2,1)S(1)}, bf16[64,1024]{1,0:T(8,128)(2,1)S(1)}, u32[]{:S(2)}, u32[]{:S(2)}) collective-permute-start(bf16[64,1024]{1,0:T(8,128)(2,1)S(1)} %collective-permute-done.4.refs_6_.refs_12_), channel_id=1, source_target_pairs={{0,2},{2,4},{4,6},{6,7},{7,5},{5,3},{3,1},{1,0},{8,10},{10,12},{12... | collective-permute-start | bytes 393224 | tf_op jit(solution)/shard_map/ppermute | solution.py:51
  13.7 5.1 %collective-permute-start.11 = (bf16[64,1024]{1,0:T(8,128)(2,1)S(1)}, bf16[64,1024]{1,0:T(8,128)(2,1)S(1)}, u32[]{:S(2)}, u32[]{:S(2)}) collective-permute-start(bf16[64,1024]{1,0:T(8,128)(2,1)S(1)} %collective-permute-done.7.refs_9_.refs_15_), channel_id=1, source_target_pairs={{0,1},{2,0},{4,2},{6,4},{7,6},{5,7},{3,5},{1,3},{8,9},{10,8},{12,1... | collective-permute-start | bytes 393224 | tf_op jit(solution)/shard_map/ppermute | solution.py:51
  15.7 5.1 %collective-permute-start.10 = (bf16[64,1024]{1,0:T(8,128)(2,1)S(1)}, bf16[64,1024]{1,0:T(8,128)(2,1)S(1)}, u32[]{:S(2)}, u32[]{:S(2)}) collective-permute-start(bf16[64,1024]{1,0:T(8,128)(2,1)S(1)} %collective-permute-done.6.refs_8_.refs_14_), channel_id=1, source_target_pairs={{0,1},{2,0},{4,2},{6,4},{7,6},{5,7},{3,5},{1,3},{8,9},{10,8},{12,1... | collective-permute-start | bytes 393224 | tf_op jit(solution)/shard_map/ppermute | solution.py:51
  16.3 5.5 %collective-permute-start.9 = (bf16[64,1024]{1,0:T(8,128)(2,1)S(1)}, bf16[64,1024]{1,0:T(8,128)(2,1)S(1)}, u32[]{:S(2)}, u32[]{:S(2)}) collective-permute-start(bf16[64,1024]{1,0:T(8,128)(2,1)S(1)} %collective-permute-done.5.refs_7_.refs_13_), channel_id=1, source_target_pairs={{0,2},{2,4},{4,6},{6,7},{7,5},{5,3},{3,1},{1,0},{8,10},{10,12},{12... | collective-permute-start | bytes 393224 | tf_op jit(solution)/shard_map/ppermute | solution.py:51
  17.1 5.8 %collective-permute-start.12 = (bf16[64,1024]{1,0:T(8,128)(2,1)S(1)}, bf16[64,1024]{1,0:T(8,128)(2,1)S(1)}, u32[]{:S(2)}, u32[]{:S(2)}) collective-permute-start(bf16[64,1024]{1,0:T(8,128)(2,1)S(1)} %collective-permute-done.8.refs_10_.refs_16_), channel_id=1, source_target_pairs={{0,2},{2,4},{4,6},{6,7},{7,5},{5,3},{3,1},{1,0},{8,10},{10,12},{12... | collective-permute-start | bytes 393224 | tf_op jit(solution)/shard_map/ppermute | solution.py:51
  18.8 4.8 %collective-permute-start.13 = (bf16[64,1024]{1,0:T(8,128)(2,1)S(1)}, bf16[64,1024]{1,0:T(8,128)(2,1)S(1)}, u32[]{:S(2)}, u32[]{:S(2)}) collective-permute-start(bf16[64,1024]{1,0:T(8,128)(2,1)S(1)} %collective-permute-done.11.refs_13_.refs_19_), channel_id=1, source_target_pairs={{0,1},{2,0},{4,2},{6,4},{7,6},{5,7},{3,5},{1,3},{8,9},{10,8},{12,1... | collective-permute-start | bytes 393224 | tf_op jit(solution)/shard_map/ppermute | solution.py:51
  26.1 6.0 %collective-permute-start.19 = (bf16[128,512]{1,0:T(8,128)(2,1)S(1)}, bf16[128,512]{1,0:T(8,128)(2,1)S(1)}, u32[]{:S(2)}, u32[]{:S(2)}) collective-permute-start(bf16[128,512]{1,0:T(8,128)(2,1)S(1)} %get-tuple-element.21.refs_0_), channel_id=1, source_target_pairs={{0,1},{1,0},{2,3},{3,2},{4,5},{5,4},{6,7},{7,6},{8,9},{9,8},{10,11... | collective-permute-start | bytes 393224 | tf_op jit(solution)/shard_map/ppermute | solution.py:41
  26.9 5.2 %collective-permute-start.20 = (bf16[128,512]{1,0:T(8,128)(2,1)S(1)}, bf16[128,512]{1,0:T(8,128)(2,1)S(1)}, u32[]{:S(2)}, u32[]{:S(2)}) collective-permute-start(bf16[128,512]{1,0:T(8,128)(2,1)S(1)} %get-tuple-element.21.refs_0_), channel_id=1, source_target_pairs={{0,2},{1,3},{2,0},{3,1},{4,6},{5,7},{6,4},{7,5},{8,10},{9,11},{10,... | collective-permute-start | bytes 393224 | tf_op jit(solution)/shard_map/ppermute | solution.py:41
  28.2 4.7 %collective-permute-start.21 = (bf16[128,512]{1,0:T(8,128)(2,1)S(1)}, bf16[128,512]{1,0:T(8,128)(2,1)S(1)}, u32[]{:S(2)}, u32[]{:S(2)}) collective-permute-start(bf16[128,512]{1,0:T(8,128)(2,1)S(1)} %get-tuple-element.21.refs_0_), channel_id=1, source_target_pairs={{0,3},{1,2},{2,1},{3,0},{4,7},{5,6},{6,5},{7,4},{8,11},{9,10},{10,... | collective-permute-start | bytes 393224 | tf_op jit(solution)/shard_map/ppermute | solution.py:41
  28.8 15.5 %collective-permute-start.14 = (bf16[128,512]{1,0:T(8,128)(2,1)S(1)}, bf16[128,512]{1,0:T(8,128)(2,1)S(1)}, u32[]{:S(2)}, u32[]{:S(2)}) collective-permute-start(bf16[128,512]{1,0:T(8,128)(2,1)S(1)} %get-tuple-element.21.refs_0_), channel_id=1, source_target_pairs={{0,6},{1,7},{2,4},{3,5},{4,2},{5,3},{6,0},{7,1},{8,14},{9,15},{10,... | collective-permute-start | bytes 393224 | tf_op jit(solution)/shard_map/ppermute | solution.py:41
  32.0 12.2 %collective-permute-start.15 = (bf16[128,512]{1,0:T(8,128)(2,1)S(1)}, bf16[128,512]{1,0:T(8,128)(2,1)S(1)}, u32[]{:S(2)}, u32[]{:S(2)}) collective-permute-start(bf16[128,512]{1,0:T(8,128)(2,1)S(1)} %get-tuple-element.21.refs_0_), channel_id=1, source_target_pairs={{0,4},{1,5},{2,6},{3,7},{4,0},{5,1},{6,2},{7,3},{8,12},{9,13},{10,... | collective-permute-start | bytes 393224 | tf_op jit(solution)/shard_map/ppermute | solution.py:41
  32.9 24.6 %collective-permute-start.22 = (bf16[512,512]{1,0:T(8,128)(2,1)S(1)}, bf16[512,512]{1,0:T(8,128)(2,1)S(1)}, u32[]{:S(2)}, u32[]{:S(2)}) collective-permute-start(bf16[512,512]{1,0:T(8,128)(2,1)S(1)} %pack.3.refs_0_.refs_1_), channel_id=1, source_target_pairs={{0,8},{8,16},{16,24},{1,9},{9,17},{17,25},{2,10},{10,18},{18,26},{... | collective-permute-start | bytes 1572872 | tf_op jit(solution)/shard_map/ppermute | solution.py:28
  44.3 6.5 %collective-permute-start.17 = (bf16[256,512]{1,0:T(8,128)(2,1)S(1)}, bf16[256,512]{1,0:T(8,128)(2,1)S(1)}, u32[]{:S(2)}, u32[]{:S(2)}) collective-permute-start(bf16[256,512]{1,0:T(8,128)(2,1)S(1)} %pack.2.refs_1_.refs_2_), channel_id=1, source_target_pairs={{0,1},{1,0},{2,3},{3,2},{4,5},{5,4},{6,7},{7,6},{8,9},{9,8},{10,11... | collective-permute-start | bytes 786440 | tf_op jit(solution)/shard_map/ppermute | solution.py:41
  45.1 13.7 %collective-permute-start.16 = (bf16[256,512]{1,0:T(8,128)(2,1)S(1)}, bf16[256,512]{1,0:T(8,128)(2,1)S(1)}, u32[]{:S(2)}, u32[]{:S(2)}) collective-permute-start(bf16[256,512]{1,0:T(8,128)(2,1)S(1)} %pack.2.refs_1_.refs_2_), channel_id=1, source_target_pairs={{0,8},{8,16},{16,24},{1,9},{9,17},{17,25},{2,10},{10,18},{18,26},{... | collective-permute-start | bytes 786440 | tf_op jit(solution)/shard_map/ppermute | solution.py:28
  50.8 8.0 %collective-permute-start.18 = (bf16[256,512]{1,0:T(8,128)(2,1)S(1)}, bf16[256,512]{1,0:T(8,128)(2,1)S(1)}, u32[]{:S(2)}, u32[]{:S(2)}) collective-permute-start(bf16[256,512]{1,0:T(8,128)(2,1)S(1)} %collective-permute-done.17.refs_2_.refs_3_), channel_id=1, source_target_pairs={{0,8},{8,16},{16,24},{1,9},{9,17},{17,25},{2,10},{10,18},{18,26},{... | collective-permute-start | bytes 786440 | tf_op jit(solution)/shard_map/ppermute | solution.py:28
  55.2 3.6 %copy-start.1 = (bf16[1,128,1024]{2,1,0:T(8,128)(2,1)S(1)}, bf16[1,128,1024]{2,1,0:T(8,128)(2,1)}, u32[]{:S(2)}) copy-start(bf16[1,128,1024]{2,1,0:T(8,128)(2,1)} %param.7) | copy-start | bytes 786436
  55.2 3.6 %copy-start.2 = (f32[1,1024]{1,0:T(1,128)S(1)}, f32[1,1024]{1,0:T(1,128)}, u32[]{:S(2)}) copy-start(f32[1,1024]{1,0:T(1,128)} %refs_4_.1) | copy-start | bytes 12292
  60.7 11.1 %collective-permute-start.27 = (bf16[512,512]{1,0:T(8,128)(2,1)S(1)}, bf16[512,512]{1,0:T(8,128)(2,1)S(1)}, u32[]{:S(2)}, u32[]{:S(2)}) collective-permute-start(bf16[512,512]{1,0:T(8,128)(2,1)S(1)} %get-tuple-element.30), channel_id=1, source_target_pairs={{8,0},{16,8},{24,16},{9,1},{17,9},{25,17},{10,2},{18,10},{26,18},{... | collective-permute-start | bytes 1572872 | tf_op jit(solution)/shard_map/ppermute | solution.py:28
  64.5 12.7 %collective-permute-start.23 = (bf16[512,512]{1,0:T(8,128)(2,1)S(1)}, bf16[512,512]{1,0:T(8,128)(2,1)S(1)}, u32[]{:S(2)}, u32[]{:S(2)}) collective-permute-start(bf16[512,512]{1,0:T(8,128)(2,1)S(1)} %get-tuple-element.24), channel_id=1, source_target_pairs={{8,0},{16,8},{24,16},{9,1},{17,9},{25,17},{10,2},{18,10},{26,18},{... | collective-permute-start | bytes 1572872 | tf_op jit(solution)/shard_map/ppermute | solution.py:28
  72.0 8.0 %collective-permute-start.28 = (bf16[256,512]{1,0:T(8,128)(2,1)S(1)}, bf16[256,512]{1,0:T(8,128)(2,1)S(1)}, u32[]{:S(2)}, u32[]{:S(2)}) collective-permute-start(bf16[256,512]{1,0:T(8,128)(2,1)S(1)} %get-tuple-element.32), channel_id=1, source_target_pairs={{0,1},{1,0},{2,3},{3,2},{4,5},{5,4},{6,7},{7,6},{8,9},{9,8},{10,11... | collective-permute-start | bytes 786440 | tf_op jit(solution)/shard_map/ppermute | solution.py:41
  77.3 15.7 %collective-permute-start.24 = (bf16[128,512]{1,0:T(8,128)(2,1)S(1)}, bf16[128,512]{1,0:T(8,128)(2,1)S(1)}, u32[]{:S(2)}, u32[]{:S(2)}) collective-permute-start(bf16[128,512]{1,0:T(8,128)(2,1)S(1)} %get-tuple-element.26), channel_id=1, source_target_pairs={{0,1},{1,0},{2,3},{3,2},{4,5},{5,4},{6,7},{7,6},{8,9},{9,8},{10,11... | collective-permute-start | bytes 393224 | tf_op jit(solution)/shard_map/ppermute | solution.py:41
  77.6 15.4 %collective-permute-start.25 = (bf16[128,512]{1,0:T(8,128)(2,1)S(1)}, bf16[128,512]{1,0:T(8,128)(2,1)S(1)}, u32[]{:S(2)}, u32[]{:S(2)}) collective-permute-start(bf16[128,512]{1,0:T(8,128)(2,1)S(1)} %get-tuple-element.27), channel_id=1, source_target_pairs={{0,2},{1,3},{2,0},{3,1},{4,6},{5,7},{6,4},{7,5},{8,10},{9,11},{10,... | collective-permute-start | bytes 393224 | tf_op jit(solution)/shard_map/ppermute | solution.py:41
  77.7 15.4 %collective-permute-start.26 = (bf16[128,512]{1,0:T(8,128)(2,1)S(1)}, bf16[128,512]{1,0:T(8,128)(2,1)S(1)}, u32[]{:S(2)}, u32[]{:S(2)}) collective-permute-start(bf16[128,512]{1,0:T(8,128)(2,1)S(1)} %get-tuple-element.28), channel_id=1, source_target_pairs={{0,3},{1,2},{2,1},{3,0},{4,7},{5,6},{6,5},{7,4},{8,11},{9,10},{10,... | collective-permute-start | bytes 393224 | tf_op jit(solution)/shard_map/ppermute | solution.py:41
  80.1 12.9 %collective-permute-start.29 = (bf16[128,512]{1,0:T(8,128)(2,1)S(1)}, bf16[128,512]{1,0:T(8,128)(2,1)S(1)}, u32[]{:S(2)}, u32[]{:S(2)}) collective-permute-start(bf16[128,512]{1,0:T(8,128)(2,1)S(1)} %get-tuple-element.33), channel_id=1, source_target_pairs={{0,6},{1,7},{2,4},{3,5},{4,2},{5,3},{6,0},{7,1},{8,14},{9,15},{10,... | collective-permute-start | bytes 393224 | tf_op jit(solution)/shard_map/ppermute | solution.py:41
  83.2 9.8 %collective-permute-start.30 = (bf16[128,512]{1,0:T(8,128)(2,1)S(1)}, bf16[128,512]{1,0:T(8,128)(2,1)S(1)}, u32[]{:S(2)}, u32[]{:S(2)}) collective-permute-start(bf16[128,512]{1,0:T(8,128)(2,1)S(1)} %get-tuple-element.34), channel_id=1, source_target_pairs={{0,4},{1,5},{2,6},{3,7},{4,0},{5,1},{6,2},{7,3},{8,12},{9,13},{10,... | collective-permute-start | bytes 393224 | tf_op jit(solution)/shard_map/ppermute | solution.py:41

commit v9 on v8

--- a/solution.py
+++ b/solution.py
@@ -224,9 +224,8 @@
         out_ref[0, 0, :, columns(owner(mask), width)] = transposed(error_ref[...], part).astype(BF16)
 
 
-def add_kernel(own_ref, arrived_ref, *outs):
-    first = 0
-    for out_ref in outs:
+def add_kernel(count, first, own_ref, arrived_ref, *refs):
+    for out_ref in refs[-count:]:
         here = slice(first, first + out_ref.shape[0])
         out_ref[...] = (own_ref[here, :] + arrived_ref[here, :].astype(F32)).astype(out_ref.dtype)
         first += out_ref.shape[0]
@@ -324,7 +323,18 @@
 
     rows = 256 if width % 256 == 0 else LANES
 
-    def dec_grad_slot(slot, groups, parts, *held):
+    def sums(outs, own_part, arrived, *after, first=0):
+        return pl.pallas_call(
+            functools.partial(add_kernel, len(outs), first),
+            name="sum",
+            out_shape=tuple(stack(masks, kind) for masks, kind in outs),
+            in_specs=[*vmem(2), *[pl.BlockSpec(memory_space=kind) for _, kind in after]],
+            out_specs=tuple(vmem(len(outs))),
+            compiler_params=params(2),
+            cost_estimate=cost(tok * features, 2 * MIB),
+        )(own_part, arrived, *[value for value, _ in after])
+
+    def dec_grad_slot(slot, groups, parts, before, held):
         return pl.pallas_call(
             functools.partial(dec_grad_kernel, groups),
             name="dec_grad",
@@ -333,37 +343,32 @@
             in_specs=[
                 pl.BlockSpec((tok, rows), lambda j: (0, j)),
                 *[pl.BlockSpec(part.shape, lambda j: (0, 0)) for part in parts],
-                *[pl.BlockSpec(memory_space=pltpu.HBM) for _ in held],
+                pl.BlockSpec(memory_space=pltpu.HBM) if held else pl.BlockSpec(memory_space=pl.ANY),
             ],
             out_specs=pl.BlockSpec((1, 1, rows, features), lambda j: (0, slot, j, 0)),
             input_output_aliases={1 + len(parts): 0} if held else {},
             compiler_params=params(12),
             cost_estimate=cost(matmul, 2 * width * features),
-        )(error, *parts, *held)
-
-    dec_grad = dec_grad_slot(0, BLOCKS, own)
-
-    def sums(outs, own_part, arrived):
-        return pl.pallas_call(
-            add_kernel,
-            name="sum",
-            out_shape=tuple(stack(masks, kind) for masks, kind in outs),
-            in_specs=vmem(2),
-            out_specs=tuple(vmem(len(outs))),
-            compiler_params=params(2),
-            cost_estimate=cost(tok * features, 2 * MIB),
-        )(own_part, arrived)
+        )(error, *parts, before)
 
     kept, crossing = sums(((FAR, F32), (CROSSING, BF16)), own_far, arrived_far)
-    lines = sums([((mask,), BF16) for mask in FAR], kept, exchanged(crossing, 1))
-    near = sums([((mask,), BF16 if mask else F32) for mask in NEAR], own_near, arrived_near)
+    dec_grad = dec_grad_slot(0, BLOCKS, own, crossing, False)
+    held_grad = pltpu.with_memory_space_constraint(dec_grad, pltpu.HBM)
+    lines = sums(
+        [((mask,), BF16) for mask in FAR], kept, exchanged(crossing, 1), (held_grad, pltpu.HBM)
+    )
+    mine, across = sums([((0,), F32), ((1,), BF16)], own_near, arrived_near, (lines[0], pltpu.VMEM))
+    across = exchanged(across, 1)
+    near = sums(
+        [((2,), BF16), ((3,), BF16)], own_near, arrived_near, (across, pltpu.VMEM), first=2 * tok
+    )
     grads = [
-        near[0],
-        *[exchanged(near[mask], mask) for mask in NEAR[1:]],
+        mine,
+        across,
         *[exchanged(line, mask) for mask, line in zip(FAR, lines)],
+        *[exchanged(part, mask) for mask, part in zip((2, 3), near)],
     ]
-    held_grad = pltpu.with_memory_space_constraint(dec_grad, pltpu.HBM)
-    dec_grad = dec_grad_slot(1, BLOCKS, previous, held_grad)
+    dec_grad = dec_grad_slot(1, BLOCKS, previous, held_grad, True)
 
     block_rows = tiles(own_features)[1]
     enc_grad = pl.pallas_call(

time: 98.1 us -> 95.4 us (0.972)
  waiting for transfers between devices: 23.1 us -> 20.5 us
    ppermute x5, waiting for transfers between devices: 10.2 us -> 5.02 us  [from_behind(): lax.ppermute(value, axis, [(source, source + steps) for source in range(i...]
    ppermute x5, starting transfers between devices: 23.8 us -> 19.5 us  [from_behind(): lax.ppermute(value, axis, [(source, source + steps) for source in range(i...]
    ppermute x12, starting transfers between devices: 12.8 us -> 17.1 us  [exchanged(): return lax.ppermute(value, 'feat', [(i, i ^ mask) for i in range(count)])]
    ppermute x12, waiting for transfers between devices: 2.43 us -> 5.05 us  [exchanged(): return lax.ppermute(value, 'feat', [(i, i ^ mask) for i in range(count)])]
  transfers between devices with their start and end apart: 31 -> 31, of which waited for: 13 -> 15; matrix products, arithmetic and copies ran while one was open for 0% -> 0% of each run, Pallas kernels for 16% -> 16%
where the time goes in v9:
time: 95.4 us; the launch traced here: 95.2 us
  starting transfers between devices  47.9 us (50%)
  Pallas kernels  24.7 us (26%)
  waiting for transfers between devices  20.5 us (21%)
  local copies, waits for them, and re-layouts  1.13 us (1%)
    ppermute x5, starting transfers between devices, from_behind(): lax.ppermute(value, axis, [(source, source + steps) for source in range(i...  19.5 us
    ppermute x12, starting transfers between devices, exchanged(): return lax.ppermute(value, 'feat', [(i, i ^ mask) for i in range(count)])  17.1 us
    ppermute x14, starting transfers between devices, passed_on(): lax.ppermute(value, 'feat', [(order[p], order[(p + by) % count]) for p in...  11.4 us
    ppermute x14, waiting for transfers between devices, passed_on(): lax.ppermute(value, 'feat', [(order[p], order[(p + by) % count]) for p in...  10.5 us
    pallas_call x2, Pallas kernels, dec_grad_slot(): pl.pallas_call(functools.partial(dec_grad_kernel, groups), name='dec_grad...  9.81 us
    ppermute x12, waiting for transfers between devices, exchanged(): return lax.ppermute(value, 'feat', [(i, i ^ mask) for i in range(count)])  5.05 us
    ppermute x5, waiting for transfers between devices, from_behind(): lax.ppermute(value, axis, [(source, source + steps) for source in range(i...  5.02 us
    pallas_call x1, Pallas kernels, on_device(): pl.pallas_call(enc_grad_kernel, name='enc_grad', grid=(own_features // bl...  4.86 us
  transfers between devices with their start and end apart: 31, of which 15 were waited for; matrix products, arithmetic and copies ran while one was open for 0% of the time, Pallas kernels for 16%

profile of v9, /device:TPU:1, one launch (start us, length us, event | category | flops | bytes accessed | tf_op | source)
XLA Modules:
  0.0 95.2 jit_solution(12540851294123774403)
XLA Ops:
  0.7 1.1 %copy-done.4 = bf16[1,128,1024]{2,1,0:T(8,128)(2,1)S(1)} copy-done((bf16[1,128,1024]{2,1,0:T(8,128)(2,1)S(1)}, bf16[1,128,1024]{2,1,0:T(8,128)(2,1)}, u32[]{:S(2)}) %copy-start.4) | copy-done | bytes 262168
  1.8 2.2 %collective-permute-start = (bf16[64,1024]{1,0:T(8,128)(2,1)S(1)}, bf16[64,1024]{1,0:T(8,128)(2,1)S(1)}, u32[]{:S(2)}, u32[]{:S(2)}) collective-permute-start(bf16[64,1024]{1,0:T(8,128)(2,1)S(1)} %get-tuple-element.19.refs_0_.refs_6_), channel_id=1, source_target_pairs={{0,2},{2,4},{4,6},{6,7},{7,5},{5,3},{3,1},{1,0},{8,10},{10,12},{12... | collective-permute-start | bytes 393224 | tf_op jit(solution)/shard_map/ppermute | solution.py:51
  4.0 1.4 %collective-permute-start.2 = (bf16[64,1024]{1,0:T(8,128)(2,1)S(1)}, bf16[64,1024]{1,0:T(8,128)(2,1)S(1)}, u32[]{:S(2)}, u32[]{:S(2)}) collective-permute-start(bf16[64,1024]{1,0:T(8,128)(2,1)S(1)} %get-tuple-element.19.refs_0_.refs_6_), channel_id=1, source_target_pairs={{0,1},{2,0},{4,2},{6,4},{7,6},{5,7},{3,5},{1,3},{8,9},{10,8},{12,1... | collective-permute-start | bytes 393224 | tf_op jit(solution)/shard_map/ppermute | solution.py:51
  5.5 1.7 %collective-permute-done.refs_2_.refs_8_ = bf16[64,1024]{1,0:T(8,128)(2,1)S(1)} collective-permute-done((bf16[64,1024]{1,0:T(8,128)(2,1)S(1)}, bf16[64,1024]{1,0:T(8,128)(2,1)S(1)}, u32[]{:S(2)}, u32[]{:S(2)}) %collective-permute-start) | collective-permute-done | bytes 131104 | tf_op jit(solution)/shard_map/ppermute | solution.py:51
  7.1 1.2 %collective-permute-start.4 = (bf16[64,1024]{1,0:T(8,128)(2,1)S(1)}, bf16[64,1024]{1,0:T(8,128)(2,1)S(1)}, u32[]{:S(2)}, u32[]{:S(2)}) collective-permute-start(bf16[64,1024]{1,0:T(8,128)(2,1)S(1)} %collective-permute-done.refs_2_.refs_8_), channel_id=1, source_target_pairs={{0,2},{2,4},{4,6},{6,7},{7,5},{5,3},{3,1},{1,0},{8,10},{10,12},{12... | collective-permute-start | bytes 393224 | tf_op jit(solution)/shard_map/ppermute | solution.py:51
  8.3 0.3 collective-permute-start.7
  8.6 2.2 %collective-permute-done.2.refs_4_.refs_10_ = bf16[64,1024]{1,0:T(8,128)(2,1)S(1)} collective-permute-done((bf16[64,1024]{1,0:T(8,128)(2,1)S(1)}, bf16[64,1024]{1,0:T(8,128)(2,1)S(1)}, u32[]{:S(2)}, u32[]{:S(2)}) %collective-permute-start.2) | collective-permute-done | bytes 131104 | tf_op jit(solution)/shard_map/ppermute | solution.py:51
  10.8 0.3 collective-permute-start.6
  11.2 1.1 %collective-permute-start.5 = (bf16[64,1024]{1,0:T(8,128)(2,1)S(1)}, bf16[64,1024]{1,0:T(8,128)(2,1)S(1)}, u32[]{:S(2)}, u32[]{:S(2)}) collective-permute-start(bf16[64,1024]{1,0:T(8,128)(2,1)S(1)} %collective-permute-done.1.refs_3_.refs_9_), channel_id=1, source_target_pairs={{0,2},{2,4},{4,6},{6,7},{7,5},{5,3},{3,1},{1,0},{8,10},{10,12},{12... | collective-permute-start | bytes 393224 | tf_op jit(solution)/shard_map/ppermute | solution.py:51
  12.4 1.3 %collective-permute-start.8 = (bf16[64,1024]{1,0:T(8,128)(2,1)S(1)}, bf16[64,1024]{1,0:T(8,128)(2,1)S(1)}, u32[]{:S(2)}, u32[]{:S(2)}) collective-permute-start(bf16[64,1024]{1,0:T(8,128)(2,1)S(1)} %collective-permute-done.4.refs_6_.refs_12_), channel_id=1, source_target_pairs={{0,2},{2,4},{4,6},{6,7},{7,5},{5,3},{3,1},{1,0},{8,10},{10,12},{12... | collective-permute-start | bytes 393224 | tf_op jit(solution)/shard_map/ppermute | solution.py:51
  13.9 1.8 %collective-permute-done.6.refs_8_.refs_14_ = bf16[64,1024]{1,0:T(8,128)(2,1)S(1)} collective-permute-done((bf16[64,1024]{1,0:T(8,128)(2,1)S(1)}, bf16[64,1024]{1,0:T(8,128)(2,1)S(1)}, u32[]{:S(2)}, u32[]{:S(2)}) %collective-permute-start.6) | collective-permute-done | bytes 131104 | tf_op jit(solution)/shard_map/ppermute | solution.py:51
  15.7 0.7 collective-permute-start.10
  16.3 0.8 collective-permute-start.9
  17.1 1.3 %collective-permute-start.12 = (bf16[64,1024]{1,0:T(8,128)(2,1)S(1)}, bf16[64,1024]{1,0:T(8,128)(2,1)S(1)}, u32[]{:S(2)}, u32[]{:S(2)}) collective-permute-start(bf16[64,1024]{1,0:T(8,128)(2,1)S(1)} %collective-permute-done.8.refs_10_.refs_16_), channel_id=1, source_target_pairs={{0,2},{2,4},{4,6},{6,7},{7,5},{5,3},{3,1},{1,0},{8,10},{10,12},{12... | collective-permute-start | bytes 393224 | tf_op jit(solution)/shard_map/ppermute | solution.py:51
  18.4 0.4 collective-permute-done.11.refs_13_.refs_19_
  18.8 0.5 collective-permute-start.13
  19.4 1.4 %collective-permute-done.10.refs_12_.refs_18_ = bf16[64,1024]{1,0:T(8,128)(2,1)S(1)} collective-permute-done((bf16[64,1024]{1,0:T(8,128)(2,1)S(1)}, bf16[64,1024]{1,0:T(8,128)(2,1)S(1)}, u32[]{:S(2)}, u32[]{:S(2)}) %collective-permute-start.10) | collective-permute-done | bytes 131104 | tf_op jit(solution)/shard_map/ppermute | solution.py:51
  20.7 1.1 %collective-permute-done.9.refs_11_.refs_17_ = bf16[64,1024]{1,0:T(8,128)(2,1)S(1)} collective-permute-done((bf16[64,1024]{1,0:T(8,128)(2,1)S(1)}, bf16[64,1024]{1,0:T(8,128)(2,1)S(1)}, u32[]{:S(2)}, u32[]{:S(2)}) %collective-permute-start.9) | collective-permute-done | bytes 131104 | tf_op jit(solution)/shard_map/ppermute | solution.py:51
  21.8 1.1 %collective-permute-done.12.refs_14_.refs_20_ = bf16[64,1024]{1,0:T(8,128)(2,1)S(1)} collective-permute-done((bf16[64,1024]{1,0:T(8,128)(2,1)S(1)}, bf16[64,1024]{1,0:T(8,128)(2,1)S(1)}, u32[]{:S(2)}, u32[]{:S(2)}) %collective-permute-start.12) | collective-permute-done | bytes 131104 | tf_op jit(solution)/shard_map/ppermute | solution.py:51
  23.0 0.7 collective-permute-done.13.refs_15_.refs_21_
  23.6 2.4 %pre.1 = (bf16[128,512]{1,0:T(8,128)(2,1)S(1)}, f32[128,512]{1,0:T(8,128)S(1)}) custom-call(bf16[64,1024]{1,0:T(8,128)(2,1)S(1)} %get-tuple-element.19.refs_0_.refs_6_, bf16[64,1024]{1,0:T(8,128)(2,1)S(1)} %get-tuple-element.20.refs_1_.refs_7_, bf16[64,1024]{1,0:T(8,128)(2,1)S(1)} %collective-permute-done.refs_2_.refs_8_, ...), custom_call_target="tpu_custom_call" | custom-call | flops 1073741824 | tf_op jit(solution)/shard_map/pre/pallas_call | solution.py:267
  26.1 1.8 %collective-permute-start.21 = (bf16[128,512]{1,0:T(8,128)(2,1)S(1)}, bf16[128,512]{1,0:T(8,128)(2,1)S(1)}, u32[]{:S(2)}, u32[]{:S(2)}) collective-permute-start(bf16[128,512]{1,0:T(8,128)(2,1)S(1)} %get-tuple-element.21.refs_0_), channel_id=1, source_target_pairs={{0,3},{1,2},{2,1},{3,0},{4,7},{5,6},{6,5},{7,4},{8,11},{9,10},{10,... | collective-permute-start | bytes 393224 | tf_op jit(solution)/shard_map/ppermute | solution.py:41
  28.0 0.8 collective-permute-start.19
  28.8 2.3 %collective-permute-start.15 = (bf16[128,512]{1,0:T(8,128)(2,1)S(1)}, bf16[128,512]{1,0:T(8,128)(2,1)S(1)}, u32[]{:S(2)}, u32[]{:S(2)}) collective-permute-start(bf16[128,512]{1,0:T(8,128)(2,1)S(1)} %get-tuple-element.21.refs_0_), channel_id=1, source_target_pairs={{0,4},{1,5},{2,6},{3,7},{4,0},{5,1},{6,2},{7,3},{8,12},{9,13},{10,... | collective-permute-start | bytes 393224 | tf_op jit(solution)/shard_map/ppermute | solution.py:41
  31.1 1.1 %collective-permute-start.14 = (bf16[128,512]{1,0:T(8,128)(2,1)S(1)}, bf16[128,512]{1,0:T(8,128)(2,1)S(1)}, u32[]{:S(2)}, u32[]{:S(2)}) collective-permute-start(bf16[128,512]{1,0:T(8,128)(2,1)S(1)} %get-tuple-element.21.refs_0_), channel_id=1, source_target_pairs={{0,6},{1,7},{2,4},{3,5},{4,2},{5,3},{6,0},{7,1},{8,14},{9,15},{10,... | collective-permute-start | bytes 393224 | tf_op jit(solution)/shard_map/ppermute | solution.py:41
  32.3 9.9 %collective-permute-start.22 = (bf16[512,512]{1,0:T(8,128)(2,1)S(1)}, bf16[512,512]{1,0:T(8,128)(2,1)S(1)}, u32[]{:S(2)}, u32[]{:S(2)}) collective-permute-start(bf16[512,512]{1,0:T(8,128)(2,1)S(1)} %pack.3.refs_0_.refs_1_), channel_id=1, source_target_pairs={{0,8},{8,16},{16,24},{1,9},{9,17},{17,25},{2,10},{10,18},{18,26},{... | collective-permute-start | bytes 1572872 | tf_op jit(solution)/shard_map/ppermute | solution.py:28
  42.2 2.8 %collective-permute-start.17 = (bf16[256,512]{1,0:T(8,128)(2,1)S(1)}, bf16[256,512]{1,0:T(8,128)(2,1)S(1)}, u32[]{:S(2)}, u32[]{:S(2)}) collective-permute-start(bf16[256,512]{1,0:T(8,128)(2,1)S(1)} %pack.2.refs_1_.refs_2_), channel_id=1, source_target_pairs={{0,1},{1,0},{2,3},{3,2},{4,5},{5,4},{6,7},{7,6},{8,9},{9,8},{10,11... | collective-permute-start | bytes 786440 | tf_op jit(solution)/shard_map/ppermute | solution.py:41
  45.0 2.8 %collective-permute-start.16 = (bf16[256,512]{1,0:T(8,128)(2,1)S(1)}, bf16[256,512]{1,0:T(8,128)(2,1)S(1)}, u32[]{:S(2)}, u32[]{:S(2)}) collective-permute-start(bf16[256,512]{1,0:T(8,128)(2,1)S(1)} %pack.2.refs_1_.refs_2_), channel_id=1, source_target_pairs={{0,8},{8,16},{16,24},{1,9},{9,17},{17,25},{2,10},{10,18},{18,26},{... | collective-permute-start | bytes 786440 | tf_op jit(solution)/shard_map/ppermute | solution.py:28
  47.8 3.3 %collective-permute-done.17.refs_2_.refs_3_ = bf16[256,512]{1,0:T(8,128)(2,1)S(1)} collective-permute-done((bf16[256,512]{1,0:T(8,128)(2,1)S(1)}, bf16[256,512]{1,0:T(8,128)(2,1)S(1)}, u32[]{:S(2)}, u32[]{:S(2)}) %collective-permute-start.17) | collective-permute-done | bytes 262176 | tf_op jit(solution)/shard_map/ppermute | solution.py:41
  51.2 2.7 %collective-permute-start.18 = (bf16[256,512]{1,0:T(8,128)(2,1)S(1)}, bf16[256,512]{1,0:T(8,128)(2,1)S(1)}, u32[]{:S(2)}, u32[]{:S(2)}) collective-permute-start(bf16[256,512]{1,0:T(8,128)(2,1)S(1)} %collective-permute-done.17.refs_2_.refs_3_), channel_id=1, source_target_pairs={{0,8},{8,16},{16,24},{1,9},{9,17},{17,25},{2,10},{10,18},{18,26},{... | collective-permute-start | bytes 786440 | tf_op jit(solution)/shard_map/ppermute | solution.py:28
  54.0 2.3 %own_recon.1.before_ref = f32[1024,128]{1,0:T(8,128)S(1)} custom-call(bf16[512,512]{1,0:T(8,128)(2,1)S(1)} %pack.3.refs_0_.refs_1_, bf16[256,512]{1,0:T(8,128)(2,1)S(1)} %pack.2.refs_1_.refs_2_, bf16[256,512]{1,0:T(8,128)(2,1)S(1)} %collective-permute-done.17.refs_2_.refs_3_, bf16[2,1024,4096]{2,1,0:T(8,128)(2,1)S(1)} %bitcast.6), custom_call_target="tpu_custom_call" | custom-call | flops 1073741824 | tf_op jit(solution)/shard_map/own_recon/pallas_call | solution.py:282
  56.3 1.2 %near_recon.1.refs_2_ = f32[1024,128]{1,0:T(8,128)S(1)} custom-call(bf16[512,512]{1,0:T(8,128)(2,1)S(1)} %collective-permute-done.22.part_ref.refs_1_, f32[1024,128]{1,0:T(8,128)S(1)} %own_recon.1.before_ref, bf16[2,1024,4096]{2,1,0:T(8,128)(2,1)S(1)} %bitcast.7), custom_call_target="tpu_custom_call" | custom-call | flops 536870912 | tf_op jit(solution)/shard_map/near_recon/pallas_call | solution.py:292
  57.6 1.9 %recon.1 = (bf16[128,1024]{1,0:T(8,128)(2,1)S(1)}, bf16[512,512]{1,0:T(8,128)(2,1)S(1)}) custom-call(bf16[256,512]{1,0:T(8,128)(2,1)S(1)} %collective-permute-done.16.refs_0_.refs_2_, bf16[256,512]{1,0:T(8,128)(2,1)S(1)} %collective-permute-done.18.refs_1_.refs_3_, f32[1024,128]{1,0:T(8,128)S(1)} %near_recon.1.refs_2_, bf16[2,1024,4096]{2,1,0:T(8,128)(2,1)S(1)} %bitcast.8, ...), custom_call_target="tpu_custom_call" | custom-call | flops 2147483648 | bytes 4194304 | tf_op jit(solution)/shard_map/recon/pallas_call | solution.py:302
  59.5 1.9 %collective-permute-start.24 = (bf16[512,512]{1,0:T(8,128)(2,1)S(1)}, bf16[512,512]{1,0:T(8,128)(2,1)S(1)}, u32[]{:S(2)}, u32[]{:S(2)}) collective-permute-start(bf16[512,512]{1,0:T(8,128)(2,1)S(1)} %get-tuple-element.26), channel_id=1, source_target_pairs={{8,0},{16,8},{24,16},{9,1},{17,9},{25,17},{10,2},{18,10},{26,18},{... | collective-permute-start | bytes 1572872 | tf_op jit(solution)/shard_map/ppermute | solution.py:28
  61.5 1.8 %own_grad.1 = (bf16[512,512]{1,0:T(8,128)(2,1)S(1)}, f32[512,512]{1,0:T(8,128)S(1)}, f32[512,512]{1,0:T(8,128)S(1)}) custom-call(bf16[128,1024]{1,0:T(8,128)(2,1)S(1)} %get-tuple-element.22.error_ref.refs_0_, bf16[2,1024,4096]{2,1,0:T(8,128)(2,1)S(1)} %bitcast.9), custom_call_target="tpu_custom_call" | custom-call | flops 1610612736 | bytes 6291456 | tf_op jit(solution)/shard_map/own_grad/pallas_call | solution.py:313
  63.3 2.1 %collective-permute-start.23 = (bf16[512,512]{1,0:T(8,128)(2,1)S(1)}, bf16[512,512]{1,0:T(8,128)(2,1)S(1)}, u32[]{:S(2)}, u32[]{:S(2)}) collective-permute-start(bf16[512,512]{1,0:T(8,128)(2,1)S(1)} %get-tuple-element.24), channel_id=1, source_target_pairs={{8,0},{16,8},{24,16},{9,1},{17,9},{25,17},{10,2},{18,10},{26,18},{... | collective-permute-start | bytes 1572872 | tf_op jit(solution)/shard_map/ppermute | solution.py:28
  65.4 5.0 %collective-permute-done.24.arrived_ref = bf16[512,512]{1,0:T(8,128)(2,1)S(1)} collective-permute-done((bf16[512,512]{1,0:T(8,128)(2,1)S(1)}, bf16[512,512]{1,0:T(8,128)(2,1)S(1)}, u32[]{:S(2)}, u32[]{:S(2)}) %collective-permute-start.24) | collective-permute-done | bytes 524320 | tf_op jit(solution)/shard_map/ppermute | solution.py:28
  70.5 1.7 %collective-permute-start.25 = (bf16[256,512]{1,0:T(8,128)(2,1)S(1)}, bf16[256,512]{1,0:T(8,128)(2,1)S(1)}, u32[]{:S(2)}, u32[]{:S(2)}) collective-permute-start(bf16[256,512]{1,0:T(8,128)(2,1)S(1)} %get-tuple-element.28.refs_4_), channel_id=1, source_target_pairs={{0,1},{1,0},{2,3},{3,2},{4,5},{5,4},{6,7},{7,6},{8,9},{9,8},{10,11... | collective-permute-start | bytes 786440 | tf_op jit(solution)/shard_map/ppermute | solution.py:41
  72.2 4.9 %dec_grad.2.refs_0_.refs_4_ = bf16[1,2,1024,4096]{3,2,1,0:T(8,128)(2,1)} custom-call(bf16[128,1024]{1,0:T(8,128)(2,1)S(1)} %get-tuple-element.22.error_ref.refs_0_, bf16[512,512]{1,0:T(8,128)(2,1)S(1)} %pack.3.refs_0_.refs_1_, bf16[256,512]{1,0:T(8,128)(2,1)S(1)} %pack.2.refs_1_.refs_2_, bf16[256,512]{1,0:T(8,128)(2,1)S(1)} %collective-permute-done.17.refs_2_.refs_3_, ...), custom_call_target="tpu_custom_call" | custom-call | flops 1073741824 | bytes 8388608 | tf_op jit(solution)/shard_map/dec_grad/pallas_call | solution.py:338
  77.1 0.5 collective-permute-done.25.arrived_ref
  77.7 1.6 %collective-permute-start.26 = (bf16[128,512]{1,0:T(8,128)(2,1)S(1)}, bf16[128,512]{1,0:T(8,128)(2,1)S(1)}, u32[]{:S(2)}, u32[]{:S(2)}) collective-permute-start(bf16[128,512]{1,0:T(8,128)(2,1)S(1)} %get-tuple-element.31), channel_id=1, source_target_pairs={{0,1},{1,0},{2,3},{3,2},{4,5},{5,4},{6,7},{7,6},{8,9},{9,8},{10,11... | collective-permute-start | bytes 393224 | tf_op jit(solution)/shard_map/ppermute | solution.py:41
  79.3 2.2 %collective-permute-start.27 = (bf16[128,512]{1,0:T(8,128)(2,1)S(1)}, bf16[128,512]{1,0:T(8,128)(2,1)S(1)}, u32[]{:S(2)}, u32[]{:S(2)}) collective-permute-start(bf16[128,512]{1,0:T(8,128)(2,1)S(1)} %get-tuple-element.29.refs_0_), channel_id=1, source_target_pairs={{0,6},{1,7},{2,4},{3,5},{4,2},{5,3},{6,0},{7,1},{8,14},{9,15},{10,... | collective-permute-start | bytes 393224 | tf_op jit(solution)/shard_map/ppermute | solution.py:41
  81.5 0.4 collective-permute-done.26.refs_0_.refs_1_
  82.0 1.0 %collective-permute-start.29 = (bf16[128,512]{1,0:T(8,128)(2,1)S(1)}, bf16[128,512]{1,0:T(8,128)(2,1)S(1)}, u32[]{:S(2)}, u32[]{:S(2)}) collective-permute-start(bf16[128,512]{1,0:T(8,128)(2,1)S(1)} %get-tuple-element.33), channel_id=1, source_target_pairs={{0,2},{1,3},{2,0},{3,1},{4,6},{5,7},{6,4},{7,5},{8,10},{9,11},{10,... | collective-permute-start | bytes 393224 | tf_op jit(solution)/shard_map/ppermute | solution.py:41
  83.0 1.7 %collective-permute-start.30 = (bf16[128,512]{1,0:T(8,128)(2,1)S(1)}, bf16[128,512]{1,0:T(8,128)(2,1)S(1)}, u32[]{:S(2)}, u32[]{:S(2)}) collective-permute-start(bf16[128,512]{1,0:T(8,128)(2,1)S(1)} %get-tuple-element.34), channel_id=1, source_target_pairs={{0,3},{1,2},{2,1},{3,0},{4,7},{5,6},{6,5},{7,4},{8,11},{9,10},{10,... | collective-permute-start | bytes 393224 | tf_op jit(solution)/shard_map/ppermute | solution.py:41
  84.7 4.9 %dec_grad.3 = bf16[1,2,1024,4096]{3,2,1,0:T(8,128)(2,1)} custom-call(bf16[128,1024]{1,0:T(8,128)(2,1)S(1)} %get-tuple-element.22.error_ref.refs_0_, bf16[512,512]{1,0:T(8,128)(2,1)S(1)} %collective-permute-done.22.part_ref.refs_1_, bf16[256,512]{1,0:T(8,128)(2,1)S(1)} %collective-permute-done.16.refs_0_.refs_2_, ...), custom_call_target="tpu_custom_call", output_to_operand_aliasing={{}: (4, {})} | custom-call | flops 1073741824 | bytes 8388608 | tf_op jit(solution)/shard_map/dec_grad/pallas_call | solution.py:338
  89.6 0.7 collective-permute-done.30.refs_5_
  90.3 4.9 %enc_grad.1 = bf16[1,512,8192]{2,1,0:T(8,128)(2,1)} custom-call(f32[128,512]{1,0:T(8,128)S(1)} %get-tuple-element.30.refs_0_, bf16[128,512]{1,0:T(8,128)(2,1)S(1)} %collective-permute-done.26.refs_0_.refs_1_, bf16[128,512]{1,0:T(8,128)(2,1)S(1)} %collective-permute-done.27.refs_2_, bf16[128,512]{1,0:T(8,128)(2,1)S(1)} %collective-permute-done.28.refs_3_, ...), custom_call_target="tpu_custom_call" | custom-call | flops 1073741824 | bytes 8388608 | tf_op jit(solution)/shard_map/enc_grad/pallas_call | solution.py:374
  (48 shorter events, 1.1 us)
Async XLA Ops:
  0.6 53.3 %slice-start = ((s8[16777216]{0:T(1024)(128)(4,1)}), s8[4194304]{0:T(1024)(128)(4,1)S(1)}, s32[]{:S(2)}) async-start(s8[16777216]{0:T(1024)(128)(4,1)} %bitcast.4), calls=%async_computation | async-start | bytes 8388608
  0.6 1.1 %copy-start.4 = (bf16[1,128,1024]{2,1,0:T(8,128)(2,1)S(1)}, bf16[1,128,1024]{2,1,0:T(8,128)(2,1)}, u32[]{:S(2)}) copy-start(bf16[1,128,1024]{2,1,0:T(8,128)(2,1)} %param.6) | copy-start | bytes 786436
  1.7 21.9 %copy-start = (bf16[1,512,8192]{2,1,0:T(8,128)(2,1)S(1)}, bf16[1,512,8192]{2,1,0:T(8,128)(2,1)}, u32[]{:S(2)}) copy-start(bf16[1,512,8192]{2,1,0:T(8,128)(2,1)} %param.8) | copy-start | bytes 25165828
  1.7 21.9 %copy-start.3 = (f32[1,512]{1,0:T(1,128)S(1)}, f32[1,512]{1,0:T(1,128)}, u32[]{:S(2)}) copy-start(f32[1,512]{1,0:T(1,128)} %refs_17_.1) | copy-start | bytes 6148
  1.7 52.2 %slice-start.1 = ((s8[16777216]{0:T(1024)(128)(4,1)}), s8[4194304]{0:T(1024)(128)(4,1)S(1)}, s32[]{:S(2)}) async-start(s8[16777216]{0:T(1024)(128)(4,1)} %bitcast.4), calls=%async_computation.1 | async-start | bytes 8388608
  1.7 52.2 %slice-start.2 = ((s8[16777216]{0:T(1024)(128)(4,1)}), s8[4194304]{0:T(1024)(128)(4,1)S(1)}, s32[]{:S(2)}) async-start(s8[16777216]{0:T(1024)(128)(4,1)} %bitcast.4), calls=%async_computation.2 | async-start | bytes 8388608
  1.8 52.2 %slice-start.3 = ((s8[16777216]{0:T(1024)(128)(4,1)}), s8[4194304]{0:T(1024)(128)(4,1)S(1)}, s32[]{:S(2)}) async-start(s8[16777216]{0:T(1024)(128)(4,1)} %bitcast.4), calls=%async_computation.3 | async-start | bytes 8388608
  1.8 5.3 %collective-permute-start = (bf16[64,1024]{1,0:T(8,128)(2,1)S(1)}, bf16[64,1024]{1,0:T(8,128)(2,1)S(1)}, u32[]{:S(2)}, u32[]{:S(2)}) collective-permute-start(bf16[64,1024]{1,0:T(8,128)(2,1)S(1)} %get-tuple-element.19.refs_0_.refs_6_), channel_id=1, source_target_pairs={{0,2},{2,4},{4,6},{6,7},{7,5},{5,3},{3,1},{1,0},{8,10},{10,12},{12... | collective-permute-start | bytes 393224 | tf_op jit(solution)/shard_map/ppermute | solution.py:51
  4.0 4.4 %collective-permute-start.3 = (bf16[64,1024]{1,0:T(8,128)(2,1)S(1)}, bf16[64,1024]{1,0:T(8,128)(2,1)S(1)}, u32[]{:S(2)}, u32[]{:S(2)}) collective-permute-start(bf16[64,1024]{1,0:T(8,128)(2,1)S(1)} %get-tuple-element.20.refs_1_.refs_7_), channel_id=1, source_target_pairs={{0,1},{2,0},{4,2},{6,4},{7,6},{5,7},{3,5},{1,3},{8,9},{10,8},{12,1... | collective-permute-start | bytes 393224 | tf_op jit(solution)/shard_map/ppermute | solution.py:51
  4.0 6.8 %collective-permute-start.2 = (bf16[64,1024]{1,0:T(8,128)(2,1)S(1)}, bf16[64,1024]{1,0:T(8,128)(2,1)S(1)}, u32[]{:S(2)}, u32[]{:S(2)}) collective-permute-start(bf16[64,1024]{1,0:T(8,128)(2,1)S(1)} %get-tuple-element.19.refs_0_.refs_6_), channel_id=1, source_target_pairs={{0,1},{2,0},{4,2},{6,4},{7,6},{5,7},{3,5},{1,3},{8,9},{10,8},{12,1... | collective-permute-start | bytes 393224 | tf_op jit(solution)/shard_map/ppermute | solution.py:51
  5.4 5.8 %collective-permute-start.1 = (bf16[64,1024]{1,0:T(8,128)(2,1)S(1)}, bf16[64,1024]{1,0:T(8,128)(2,1)S(1)}, u32[]{:S(2)}, u32[]{:S(2)}) collective-permute-start(bf16[64,1024]{1,0:T(8,128)(2,1)S(1)} %get-tuple-element.20.refs_1_.refs_7_), channel_id=1, source_target_pairs={{0,2},{2,4},{4,6},{6,7},{7,5},{5,3},{3,1},{1,0},{8,10},{10,12},{12... | collective-permute-start | bytes 393224 | tf_op jit(solution)/shard_map/ppermute | solution.py:51
  7.1 5.3 %collective-permute-start.4 = (bf16[64,1024]{1,0:T(8,128)(2,1)S(1)}, bf16[64,1024]{1,0:T(8,128)(2,1)S(1)}, u32[]{:S(2)}, u32[]{:S(2)}) collective-permute-start(bf16[64,1024]{1,0:T(8,128)(2,1)S(1)} %collective-permute-done.refs_2_.refs_8_), channel_id=1, source_target_pairs={{0,2},{2,4},{4,6},{6,7},{7,5},{5,3},{3,1},{1,0},{8,10},{10,12},{12... | collective-permute-start | bytes 393224 | tf_op jit(solution)/shard_map/ppermute | solution.py:51
  8.3 5.4 %collective-permute-start.7 = (bf16[64,1024]{1,0:T(8,128)(2,1)S(1)}, bf16[64,1024]{1,0:T(8,128)(2,1)S(1)}, u32[]{:S(2)}, u32[]{:S(2)}) collective-permute-start(bf16[64,1024]{1,0:T(8,128)(2,1)S(1)} %collective-permute-done.3.refs_5_.refs_11_), channel_id=1, source_target_pairs={{0,1},{2,0},{4,2},{6,4},{7,6},{5,7},{3,5},{1,3},{8,9},{10,8},{12,1... | collective-permute-start | bytes 393224 | tf_op jit(solution)/shard_map/ppermute | solution.py:51
  10.8 4.8 %collective-permute-start.6 = (bf16[64,1024]{1,0:T(8,128)(2,1)S(1)}, bf16[64,1024]{1,0:T(8,128)(2,1)S(1)}, u32[]{:S(2)}, u32[]{:S(2)}) collective-permute-start(bf16[64,1024]{1,0:T(8,128)(2,1)S(1)} %collective-permute-done.2.refs_4_.refs_10_), channel_id=1, source_target_pairs={{0,1},{2,0},{4,2},{6,4},{7,6},{5,7},{3,5},{1,3},{8,9},{10,8},{12,1... | collective-permute-start | bytes 393224 | tf_op jit(solution)/shard_map/ppermute | solution.py:51
  11.2 5.2 %collective-permute-start.5 = (bf16[64,1024]{1,0:T(8,128)(2,1)S(1)}, bf16[64,1024]{1,0:T(8,128)(2,1)S(1)}, u32[]{:S(2)}, u32[]{:S(2)}) collective-permute-start(bf16[64,1024]{1,0:T(8,128)(2,1)S(1)} %collective-permute-done.1.refs_3_.refs_9_), channel_id=1, source_target_pairs={{0,2},{2,4},{4,6},{6,7},{7,5},{5,3},{3,1},{1,0},{8,10},{10,12},{12... | collective-permute-start | bytes 393224 | tf_op jit(solution)/shard_map/ppermute | solution.py:51
  12.4 4.7 %collective-permute-start.8 = (bf16[64,1024]{1,0:T(8,128)(2,1)S(1)}, bf16[64,1024]{1,0:T(8,128)(2,1)S(1)}, u32[]{:S(2)}, u32[]{:S(2)}) collective-permute-start(bf16[64,1024]{1,0:T(8,128)(2,1)S(1)} %collective-permute-done.4.refs_6_.refs_12_), channel_id=1, source_target_pairs={{0,2},{2,4},{4,6},{6,7},{7,5},{5,3},{3,1},{1,0},{8,10},{10,12},{12... | collective-permute-start | bytes 393224 | tf_op jit(solution)/shard_map/ppermute | solution.py:51
  13.7 5.1 %collective-permute-start.11 = (bf16[64,1024]{1,0:T(8,128)(2,1)S(1)}, bf16[64,1024]{1,0:T(8,128)(2,1)S(1)}, u32[]{:S(2)}, u32[]{:S(2)}) collective-permute-start(bf16[64,1024]{1,0:T(8,128)(2,1)S(1)} %collective-permute-done.7.refs_9_.refs_15_), channel_id=1, source_target_pairs={{0,1},{2,0},{4,2},{6,4},{7,6},{5,7},{3,5},{1,3},{8,9},{10,8},{12,1... | collective-permute-start | bytes 393224 | tf_op jit(solution)/shard_map/ppermute | solution.py:51
  15.7 5.1 %collective-permute-start.10 = (bf16[64,1024]{1,0:T(8,128)(2,1)S(1)}, bf16[64,1024]{1,0:T(8,128)(2,1)S(1)}, u32[]{:S(2)}, u32[]{:S(2)}) collective-permute-start(bf16[64,1024]{1,0:T(8,128)(2,1)S(1)} %collective-permute-done.6.refs_8_.refs_14_), channel_id=1, source_target_pairs={{0,1},{2,0},{4,2},{6,4},{7,6},{5,7},{3,5},{1,3},{8,9},{10,8},{12,1... | collective-permute-start | bytes 393224 | tf_op jit(solution)/shard_map/ppermute | solution.py:51
  16.3 5.5 %collective-permute-start.9 = (bf16[64,1024]{1,0:T(8,128)(2,1)S(1)}, bf16[64,1024]{1,0:T(8,128)(2,1)S(1)}, u32[]{:S(2)}, u32[]{:S(2)}) collective-permute-start(bf16[64,1024]{1,0:T(8,128)(2,1)S(1)} %collective-permute-done.5.refs_7_.refs_13_), channel_id=1, source_target_pairs={{0,2},{2,4},{4,6},{6,7},{7,5},{5,3},{3,1},{1,0},{8,10},{10,12},{12... | collective-permute-start | bytes 393224 | tf_op jit(solution)/shard_map/ppermute | solution.py:51
  17.1 5.8 %collective-permute-start.12 = (bf16[64,1024]{1,0:T(8,128)(2,1)S(1)}, bf16[64,1024]{1,0:T(8,128)(2,1)S(1)}, u32[]{:S(2)}, u32[]{:S(2)}) collective-permute-start(bf16[64,1024]{1,0:T(8,128)(2,1)S(1)} %collective-permute-done.8.refs_10_.refs_16_), channel_id=1, source_target_pairs={{0,2},{2,4},{4,6},{6,7},{7,5},{5,3},{3,1},{1,0},{8,10},{10,12},{12... | collective-permute-start | bytes 393224 | tf_op jit(solution)/shard_map/ppermute | solution.py:51
  18.8 4.8 %collective-permute-start.13 = (bf16[64,1024]{1,0:T(8,128)(2,1)S(1)}, bf16[64,1024]{1,0:T(8,128)(2,1)S(1)}, u32[]{:S(2)}, u32[]{:S(2)}) collective-permute-start(bf16[64,1024]{1,0:T(8,128)(2,1)S(1)} %collective-permute-done.11.refs_13_.refs_19_), channel_id=1, source_target_pairs={{0,1},{2,0},{4,2},{6,4},{7,6},{5,7},{3,5},{1,3},{8,9},{10,8},{12,1... | collective-permute-start | bytes 393224 | tf_op jit(solution)/shard_map/ppermute | solution.py:51
  26.1 6.1 %collective-permute-start.21 = (bf16[128,512]{1,0:T(8,128)(2,1)S(1)}, bf16[128,512]{1,0:T(8,128)(2,1)S(1)}, u32[]{:S(2)}, u32[]{:S(2)}) collective-permute-start(bf16[128,512]{1,0:T(8,128)(2,1)S(1)} %get-tuple-element.21.refs_0_), channel_id=1, source_target_pairs={{0,3},{1,2},{2,1},{3,0},{4,7},{5,6},{6,5},{7,4},{8,11},{9,10},{10,... | collective-permute-start | bytes 393224 | tf_op jit(solution)/shard_map/ppermute | solution.py:41
  27.9 4.3 %collective-permute-start.20 = (bf16[128,512]{1,0:T(8,128)(2,1)S(1)}, bf16[128,512]{1,0:T(8,128)(2,1)S(1)}, u32[]{:S(2)}, u32[]{:S(2)}) collective-permute-start(bf16[128,512]{1,0:T(8,128)(2,1)S(1)} %get-tuple-element.21.refs_0_), channel_id=1, source_target_pairs={{0,2},{1,3},{2,0},{3,1},{4,6},{5,7},{6,4},{7,5},{8,10},{9,11},{10,... | collective-permute-start | bytes 393224 | tf_op jit(solution)/shard_map/ppermute | solution.py:41
  28.0 4.2 %collective-permute-start.19 = (bf16[128,512]{1,0:T(8,128)(2,1)S(1)}, bf16[128,512]{1,0:T(8,128)(2,1)S(1)}, u32[]{:S(2)}, u32[]{:S(2)}) collective-permute-start(bf16[128,512]{1,0:T(8,128)(2,1)S(1)} %get-tuple-element.21.refs_0_), channel_id=1, source_target_pairs={{0,1},{1,0},{2,3},{3,2},{4,5},{5,4},{6,7},{7,6},{8,9},{9,8},{10,11... | collective-permute-start | bytes 393224 | tf_op jit(solution)/shard_map/ppermute | solution.py:41
  28.8 13.4 %collective-permute-start.15 = (bf16[128,512]{1,0:T(8,128)(2,1)S(1)}, bf16[128,512]{1,0:T(8,128)(2,1)S(1)}, u32[]{:S(2)}, u32[]{:S(2)}) collective-permute-start(bf16[128,512]{1,0:T(8,128)(2,1)S(1)} %get-tuple-element.21.refs_0_), channel_id=1, source_target_pairs={{0,4},{1,5},{2,6},{3,7},{4,0},{5,1},{6,2},{7,3},{8,12},{9,13},{10,... | collective-permute-start | bytes 393224 | tf_op jit(solution)/shard_map/ppermute | solution.py:41
  31.1 11.1 %collective-permute-start.14 = (bf16[128,512]{1,0:T(8,128)(2,1)S(1)}, bf16[128,512]{1,0:T(8,128)(2,1)S(1)}, u32[]{:S(2)}, u32[]{:S(2)}) collective-permute-start(bf16[128,512]{1,0:T(8,128)(2,1)S(1)} %get-tuple-element.21.refs_0_), channel_id=1, source_target_pairs={{0,6},{1,7},{2,4},{3,5},{4,2},{5,3},{6,0},{7,1},{8,14},{9,15},{10,... | collective-permute-start | bytes 393224 | tf_op jit(solution)/shard_map/ppermute | solution.py:41
  32.3 24.0 %collective-permute-start.22 = (bf16[512,512]{1,0:T(8,128)(2,1)S(1)}, bf16[512,512]{1,0:T(8,128)(2,1)S(1)}, u32[]{:S(2)}, u32[]{:S(2)}) collective-permute-start(bf16[512,512]{1,0:T(8,128)(2,1)S(1)} %pack.3.refs_0_.refs_1_), channel_id=1, source_target_pairs={{0,8},{8,16},{16,24},{1,9},{9,17},{17,25},{2,10},{10,18},{18,26},{... | collective-permute-start | bytes 1572872 | tf_op jit(solution)/shard_map/ppermute | solution.py:28
  42.2 8.9 %collective-permute-start.17 = (bf16[256,512]{1,0:T(8,128)(2,1)S(1)}, bf16[256,512]{1,0:T(8,128)(2,1)S(1)}, u32[]{:S(2)}, u32[]{:S(2)}) collective-permute-start(bf16[256,512]{1,0:T(8,128)(2,1)S(1)} %pack.2.refs_1_.refs_2_), channel_id=1, source_target_pairs={{0,1},{1,0},{2,3},{3,2},{4,5},{5,4},{6,7},{7,6},{8,9},{9,8},{10,11... | collective-permute-start | bytes 786440 | tf_op jit(solution)/shard_map/ppermute | solution.py:41
  45.0 12.5 %collective-permute-start.16 = (bf16[256,512]{1,0:T(8,128)(2,1)S(1)}, bf16[256,512]{1,0:T(8,128)(2,1)S(1)}, u32[]{:S(2)}, u32[]{:S(2)}) collective-permute-start(bf16[256,512]{1,0:T(8,128)(2,1)S(1)} %pack.2.refs_1_.refs_2_), channel_id=1, source_target_pairs={{0,8},{8,16},{16,24},{1,9},{9,17},{17,25},{2,10},{10,18},{18,26},{... | collective-permute-start | bytes 786440 | tf_op jit(solution)/shard_map/ppermute | solution.py:28
  51.2 6.4 %collective-permute-start.18 = (bf16[256,512]{1,0:T(8,128)(2,1)S(1)}, bf16[256,512]{1,0:T(8,128)(2,1)S(1)}, u32[]{:S(2)}, u32[]{:S(2)}) collective-permute-start(bf16[256,512]{1,0:T(8,128)(2,1)S(1)} %collective-permute-done.17.refs_2_.refs_3_), channel_id=1, source_target_pairs={{0,8},{8,16},{16,24},{1,9},{9,17},{17,25},{2,10},{10,18},{18,26},{... | collective-permute-start | bytes 786440 | tf_op jit(solution)/shard_map/ppermute | solution.py:28
  54.0 3.6 %copy-start.1 = (bf16[1,128,1024]{2,1,0:T(8,128)(2,1)S(1)}, bf16[1,128,1024]{2,1,0:T(8,128)(2,1)}, u32[]{:S(2)}) copy-start(bf16[1,128,1024]{2,1,0:T(8,128)(2,1)} %param.7) | copy-start | bytes 786436
  54.0 3.6 %copy-start.2 = (f32[1,1024]{1,0:T(1,128)S(1)}, f32[1,1024]{1,0:T(1,128)}, u32[]{:S(2)}) copy-start(f32[1,1024]{1,0:T(1,128)} %refs_4_.1) | copy-start | bytes 12292
  59.5 10.9 %collective-permute-start.24 = (bf16[512,512]{1,0:T(8,128)(2,1)S(1)}, bf16[512,512]{1,0:T(8,128)(2,1)S(1)}, u32[]{:S(2)}, u32[]{:S(2)}) collective-permute-start(bf16[512,512]{1,0:T(8,128)(2,1)S(1)} %get-tuple-element.26), channel_id=1, source_target_pairs={{8,0},{16,8},{24,16},{9,1},{17,9},{25,17},{10,2},{18,10},{26,18},{... | collective-permute-start | bytes 1572872 | tf_op jit(solution)/shard_map/ppermute | solution.py:28
  63.3 14.3 %collective-permute-start.23 = (bf16[512,512]{1,0:T(8,128)(2,1)S(1)}, bf16[512,512]{1,0:T(8,128)(2,1)S(1)}, u32[]{:S(2)}, u32[]{:S(2)}) collective-permute-start(bf16[512,512]{1,0:T(8,128)(2,1)S(1)} %get-tuple-element.24), channel_id=1, source_target_pairs={{8,0},{16,8},{24,16},{9,1},{17,9},{25,17},{10,2},{18,10},{26,18},{... | collective-permute-start | bytes 1572872 | tf_op jit(solution)/shard_map/ppermute | solution.py:28
  70.5 7.1 %collective-permute-start.25 = (bf16[256,512]{1,0:T(8,128)(2,1)S(1)}, bf16[256,512]{1,0:T(8,128)(2,1)S(1)}, u32[]{:S(2)}, u32[]{:S(2)}) collective-permute-start(bf16[256,512]{1,0:T(8,128)(2,1)S(1)} %get-tuple-element.28.refs_4_), channel_id=1, source_target_pairs={{0,1},{1,0},{2,3},{3,2},{4,5},{5,4},{6,7},{7,6},{8,9},{9,8},{10,11... | collective-permute-start | bytes 786440 | tf_op jit(solution)/shard_map/ppermute | solution.py:41
  77.7 4.3 %collective-permute-start.26 = (bf16[128,512]{1,0:T(8,128)(2,1)S(1)}, bf16[128,512]{1,0:T(8,128)(2,1)S(1)}, u32[]{:S(2)}, u32[]{:S(2)}) collective-permute-start(bf16[128,512]{1,0:T(8,128)(2,1)S(1)} %get-tuple-element.31), channel_id=1, source_target_pairs={{0,1},{1,0},{2,3},{3,2},{4,5},{5,4},{6,7},{7,6},{8,9},{9,8},{10,11... | collective-permute-start | bytes 393224 | tf_op jit(solution)/shard_map/ppermute | solution.py:41
  79.3 10.3 %collective-permute-start.27 = (bf16[128,512]{1,0:T(8,128)(2,1)S(1)}, bf16[128,512]{1,0:T(8,128)(2,1)S(1)}, u32[]{:S(2)}, u32[]{:S(2)}) collective-permute-start(bf16[128,512]{1,0:T(8,128)(2,1)S(1)} %get-tuple-element.29.refs_0_), channel_id=1, source_target_pairs={{0,6},{1,7},{2,4},{3,5},{4,2},{5,3},{6,0},{7,1},{8,14},{9,15},{10,... | collective-permute-start | bytes 393224 | tf_op jit(solution)/shard_map/ppermute | solution.py:41
  81.5 8.1 %collective-permute-start.28 = (bf16[128,512]{1,0:T(8,128)(2,1)S(1)}, bf16[128,512]{1,0:T(8,128)(2,1)S(1)}, u32[]{:S(2)}, u32[]{:S(2)}) collective-permute-start(bf16[128,512]{1,0:T(8,128)(2,1)S(1)} %get-tuple-element.32), channel_id=1, source_target_pairs={{0,4},{1,5},{2,6},{3,7},{4,0},{5,1},{6,2},{7,3},{8,12},{9,13},{10,... | collective-permute-start | bytes 393224 | tf_op jit(solution)/shard_map/ppermute | solution.py:41
  82.0 7.6 %collective-permute-start.29 = (bf16[128,512]{1,0:T(8,128)(2,1)S(1)}, bf16[128,512]{1,0:T(8,128)(2,1)S(1)}, u32[]{:S(2)}, u32[]{:S(2)}) collective-permute-start(bf16[128,512]{1,0:T(8,128)(2,1)S(1)} %get-tuple-element.33), channel_id=1, source_target_pairs={{0,2},{1,3},{2,0},{3,1},{4,6},{5,7},{6,4},{7,5},{8,10},{9,11},{10,... | collective-permute-start | bytes 393224 | tf_op jit(solution)/shard_map/ppermute | solution.py:41
  83.0 7.4 %collective-permute-start.30 = (bf16[128,512]{1,0:T(8,128)(2,1)S(1)}, bf16[128,512]{1,0:T(8,128)(2,1)S(1)}, u32[]{:S(2)}, u32[]{:S(2)}) collective-permute-start(bf16[128,512]{1,0:T(8,128)(2,1)S(1)} %get-tuple-element.34), channel_id=1, source_target_pairs={{0,3},{1,2},{2,1},{3,0},{4,7},{5,6},{6,5},{7,4},{8,11},{9,10},{10,... | collective-permute-start | bytes 393224 | tf_op jit(solution)/shard_map/ppermute | solution.py:41

commit v10 on v9

--- a/solution.py
+++ b/solution.py
@@ -60,10 +60,16 @@
     return jnp.where(place < count // 2, 2 * place, 2 * (count - 1 - place) + 1)
 
 
-def split_kernel(in_ref, first_ref, last_ref):
+def split_kernel(in_ref, first_ref, last_ref, sems):
     middle = first_ref.shape[0]
-    first_ref[...] = in_ref[:middle, :]
-    last_ref[...] = in_ref[middle:, :]
+    copies = [
+        pltpu.make_async_copy(in_ref.at[:middle, :], first_ref, sems.at[0]),
+        pltpu.make_async_copy(in_ref.at[middle:, :], last_ref, sems.at[1]),
+    ]
+    for copy in copies:
+        copy.start()
+    for copy in copies:
+        copy.wait()
 
 
 def ring_gather(own):
@@ -75,11 +81,12 @@
             split_kernel,
             name="split",
             out_shape=(part, part),
-            in_specs=vmem(1),
+            in_specs=[pl.BlockSpec(memory_space=pltpu.HBM)],
             out_specs=tuple(vmem(2)),
+            scratch_shapes=[pltpu.SemaphoreType.DMA((2,))],
             compiler_params=params(2),
             cost_estimate=cost(SPLIT_FLOPS, 0),
-        )(own)
+        )(pltpu.with_memory_space_constraint(own, pltpu.HBM))
     )
     for step in range(1, count // 2):
         for held in (first, last):

time: 95.4 us -> 95.5 us (level)
  Pallas kernels: 24.7 us -> 25.8 us
  local copies, waits for them, and re-layouts: 1.13 us -> 0.04 us
    pallas_call x1, Pallas kernels: 0.02 us -> 1.14 us  [ring_gather(): pl.pallas_call(split_kernel, name='split', out_shape=(part, part), in_spe...]
    unnamed x18 -> x16, local copies, waits for them, and re-layouts: 1.13 us -> 0.04 us
where the time goes in v10:
time: 95.5 us; the launch traced here: 95.2 us
  starting transfers between devices  47.9 us (50%)
  Pallas kernels  25.8 us (27%)
  waiting for transfers between devices  20.5 us (21%)
    ppermute x5, starting transfers between devices, from_behind(): lax.ppermute(value, axis, [(source, source + steps) for source in range(i...  19.5 us
    ppermute x12, starting transfers between devices, exchanged(): return lax.ppermute(value, 'feat', [(i, i ^ mask) for i in range(count)])  17.1 us
    ppermute x14, starting transfers between devices, passed_on(): lax.ppermute(value, 'feat', [(order[p], order[(p + by) % count]) for p in...  11.4 us
    ppermute x14, waiting for transfers between devices, passed_on(): lax.ppermute(value, 'feat', [(order[p], order[(p + by) % count]) for p in...  10.5 us
    pallas_call x2, Pallas kernels, dec_grad_slot(): pl.pallas_call(functools.partial(dec_grad_kernel, groups), name='dec_grad...  9.81 us
    ppermute x12, waiting for transfers between devices, exchanged(): return lax.ppermute(value, 'feat', [(i, i ^ mask) for i in range(count)])  5.02 us
    ppermute x5, waiting for transfers between devices, from_behind(): lax.ppermute(value, axis, [(source, source + steps) for source in range(i...  5.01 us
    pallas_call x1, Pallas kernels, on_device(): pl.pallas_call(enc_grad_kernel, name='enc_grad', grid=(own_features // bl...  4.86 us
  transfers between devices with their start and end apart: 31, of which 15 were waited for; matrix products, arithmetic and copies ran while one was open for 0% of the time, Pallas kernels for 16%

profile of v10, /device:TPU:1, one launch (start us, length us, event | category | flops | bytes accessed | tf_op | source)
XLA Modules:
  0.0 95.2 jit_solution(13740049494831401160)
XLA Ops:
  0.7 1.1 %split.1 = (bf16[64,1024]{1,0:T(8,128)(2,1)S(1)}, bf16[64,1024]{1,0:T(8,128)(2,1)S(1)}) custom-call(bf16[128,1024]{1,0:T(8,128)(2,1)} %bitcast.12), custom_call_target="tpu_custom_call" | custom-call | flops 10000000000 | tf_op jit(solution)/shard_map/split/pallas_call | solution.py:80
  1.8 2.2 %collective-permute-start = (bf16[64,1024]{1,0:T(8,128)(2,1)S(1)}, bf16[64,1024]{1,0:T(8,128)(2,1)S(1)}, u32[]{:S(2)}, u32[]{:S(2)}) collective-permute-start(bf16[64,1024]{1,0:T(8,128)(2,1)S(1)} %get-tuple-element.19.refs_0_.refs_6_), channel_id=1, source_target_pairs={{0,2},{2,4},{4,6},{6,7},{7,5},{5,3},{3,1},{1,0},{8,10},{10,12},{12... | collective-permute-start | bytes 393224 | tf_op jit(solution)/shard_map/ppermute | solution.py:51
  4.0 1.4 %collective-permute-start.2 = (bf16[64,1024]{1,0:T(8,128)(2,1)S(1)}, bf16[64,1024]{1,0:T(8,128)(2,1)S(1)}, u32[]{:S(2)}, u32[]{:S(2)}) collective-permute-start(bf16[64,1024]{1,0:T(8,128)(2,1)S(1)} %get-tuple-element.19.refs_0_.refs_6_), channel_id=1, source_target_pairs={{0,1},{2,0},{4,2},{6,4},{7,6},{5,7},{3,5},{1,3},{8,9},{10,8},{12,1... | collective-permute-start | bytes 393224 | tf_op jit(solution)/shard_map/ppermute | solution.py:51
  5.5 1.7 %collective-permute-done.refs_2_.refs_8_ = bf16[64,1024]{1,0:T(8,128)(2,1)S(1)} collective-permute-done((bf16[64,1024]{1,0:T(8,128)(2,1)S(1)}, bf16[64,1024]{1,0:T(8,128)(2,1)S(1)}, u32[]{:S(2)}, u32[]{:S(2)}) %collective-permute-start) | collective-permute-done | bytes 131104 | tf_op jit(solution)/shard_map/ppermute | solution.py:51
  7.2 1.2 %collective-permute-start.4 = (bf16[64,1024]{1,0:T(8,128)(2,1)S(1)}, bf16[64,1024]{1,0:T(8,128)(2,1)S(1)}, u32[]{:S(2)}, u32[]{:S(2)}) collective-permute-start(bf16[64,1024]{1,0:T(8,128)(2,1)S(1)} %collective-permute-done.refs_2_.refs_8_), channel_id=1, source_target_pairs={{0,2},{2,4},{4,6},{6,7},{7,5},{5,3},{3,1},{1,0},{8,10},{10,12},{12... | collective-permute-start | bytes 393224 | tf_op jit(solution)/shard_map/ppermute | solution.py:51
  8.4 0.3 collective-permute-start.7
  8.7 2.2 %collective-permute-done.2.refs_4_.refs_10_ = bf16[64,1024]{1,0:T(8,128)(2,1)S(1)} collective-permute-done((bf16[64,1024]{1,0:T(8,128)(2,1)S(1)}, bf16[64,1024]{1,0:T(8,128)(2,1)S(1)}, u32[]{:S(2)}, u32[]{:S(2)}) %collective-permute-start.2) | collective-permute-done | bytes 131104 | tf_op jit(solution)/shard_map/ppermute | solution.py:51
  10.9 0.3 collective-permute-start.6
  11.2 1.1 %collective-permute-start.5 = (bf16[64,1024]{1,0:T(8,128)(2,1)S(1)}, bf16[64,1024]{1,0:T(8,128)(2,1)S(1)}, u32[]{:S(2)}, u32[]{:S(2)}) collective-permute-start(bf16[64,1024]{1,0:T(8,128)(2,1)S(1)} %collective-permute-done.1.refs_3_.refs_9_), channel_id=1, source_target_pairs={{0,2},{2,4},{4,6},{6,7},{7,5},{5,3},{3,1},{1,0},{8,10},{10,12},{12... | collective-permute-start | bytes 393224 | tf_op jit(solution)/shard_map/ppermute | solution.py:51
  12.5 1.3 %collective-permute-start.8 = (bf16[64,1024]{1,0:T(8,128)(2,1)S(1)}, bf16[64,1024]{1,0:T(8,128)(2,1)S(1)}, u32[]{:S(2)}, u32[]{:S(2)}) collective-permute-start(bf16[64,1024]{1,0:T(8,128)(2,1)S(1)} %collective-permute-done.4.refs_6_.refs_12_), channel_id=1, source_target_pairs={{0,2},{2,4},{4,6},{6,7},{7,5},{5,3},{3,1},{1,0},{8,10},{10,12},{12... | collective-permute-start | bytes 393224 | tf_op jit(solution)/shard_map/ppermute | solution.py:51
  13.9 1.8 %collective-permute-done.6.refs_8_.refs_14_ = bf16[64,1024]{1,0:T(8,128)(2,1)S(1)} collective-permute-done((bf16[64,1024]{1,0:T(8,128)(2,1)S(1)}, bf16[64,1024]{1,0:T(8,128)(2,1)S(1)}, u32[]{:S(2)}, u32[]{:S(2)}) %collective-permute-start.6) | collective-permute-done | bytes 131104 | tf_op jit(solution)/shard_map/ppermute | solution.py:51
  15.7 0.7 collective-permute-start.10
  16.4 0.8 collective-permute-start.9
  17.2 1.3 %collective-permute-start.12 = (bf16[64,1024]{1,0:T(8,128)(2,1)S(1)}, bf16[64,1024]{1,0:T(8,128)(2,1)S(1)}, u32[]{:S(2)}, u32[]{:S(2)}) collective-permute-start(bf16[64,1024]{1,0:T(8,128)(2,1)S(1)} %collective-permute-done.8.refs_10_.refs_16_), channel_id=1, source_target_pairs={{0,2},{2,4},{4,6},{6,7},{7,5},{5,3},{3,1},{1,0},{8,10},{10,12},{12... | collective-permute-start | bytes 393224 | tf_op jit(solution)/shard_map/ppermute | solution.py:51
  18.5 0.4 collective-permute-done.11.refs_13_.refs_19_
  18.9 0.5 collective-permute-start.13
  19.4 1.4 %collective-permute-done.10.refs_12_.refs_18_ = bf16[64,1024]{1,0:T(8,128)(2,1)S(1)} collective-permute-done((bf16[64,1024]{1,0:T(8,128)(2,1)S(1)}, bf16[64,1024]{1,0:T(8,128)(2,1)S(1)}, u32[]{:S(2)}, u32[]{:S(2)}) %collective-permute-start.10) | collective-permute-done | bytes 131104 | tf_op jit(solution)/shard_map/ppermute | solution.py:51
  20.8 1.1 %collective-permute-done.9.refs_11_.refs_17_ = bf16[64,1024]{1,0:T(8,128)(2,1)S(1)} collective-permute-done((bf16[64,1024]{1,0:T(8,128)(2,1)S(1)}, bf16[64,1024]{1,0:T(8,128)(2,1)S(1)}, u32[]{:S(2)}, u32[]{:S(2)}) %collective-permute-start.9) | collective-permute-done | bytes 131104 | tf_op jit(solution)/shard_map/ppermute | solution.py:51
  21.9 1.1 %collective-permute-done.12.refs_14_.refs_20_ = bf16[64,1024]{1,0:T(8,128)(2,1)S(1)} collective-permute-done((bf16[64,1024]{1,0:T(8,128)(2,1)S(1)}, bf16[64,1024]{1,0:T(8,128)(2,1)S(1)}, u32[]{:S(2)}, u32[]{:S(2)}) %collective-permute-start.12) | collective-permute-done | bytes 131104 | tf_op jit(solution)/shard_map/ppermute | solution.py:51
  23.0 0.7 collective-permute-done.13.refs_15_.refs_21_
  23.7 2.4 %pre.1 = (bf16[128,512]{1,0:T(8,128)(2,1)S(1)}, f32[128,512]{1,0:T(8,128)S(1)}) custom-call(bf16[64,1024]{1,0:T(8,128)(2,1)S(1)} %get-tuple-element.19.refs_0_.refs_6_, bf16[64,1024]{1,0:T(8,128)(2,1)S(1)} %get-tuple-element.20.refs_1_.refs_7_, bf16[64,1024]{1,0:T(8,128)(2,1)S(1)} %collective-permute-done.refs_2_.refs_8_, ...), custom_call_target="tpu_custom_call" | custom-call | flops 1073741824 | tf_op jit(solution)/shard_map/pre/pallas_call | solution.py:274
  26.1 1.8 %collective-permute-start.21 = (bf16[128,512]{1,0:T(8,128)(2,1)S(1)}, bf16[128,512]{1,0:T(8,128)(2,1)S(1)}, u32[]{:S(2)}, u32[]{:S(2)}) collective-permute-start(bf16[128,512]{1,0:T(8,128)(2,1)S(1)} %get-tuple-element.21.refs_0_), channel_id=1, source_target_pairs={{0,3},{1,2},{2,1},{3,0},{4,7},{5,6},{6,5},{7,4},{8,11},{9,10},{10,... | collective-permute-start | bytes 393224 | tf_op jit(solution)/shard_map/ppermute | solution.py:41
  28.1 0.7 collective-permute-start.19
  28.8 2.3 %collective-permute-start.15 = (bf16[128,512]{1,0:T(8,128)(2,1)S(1)}, bf16[128,512]{1,0:T(8,128)(2,1)S(1)}, u32[]{:S(2)}, u32[]{:S(2)}) collective-permute-start(bf16[128,512]{1,0:T(8,128)(2,1)S(1)} %get-tuple-element.21.refs_0_), channel_id=1, source_target_pairs={{0,4},{1,5},{2,6},{3,7},{4,0},{5,1},{6,2},{7,3},{8,12},{9,13},{10,... | collective-permute-start | bytes 393224 | tf_op jit(solution)/shard_map/ppermute | solution.py:41
  31.1 1.1 %collective-permute-start.14 = (bf16[128,512]{1,0:T(8,128)(2,1)S(1)}, bf16[128,512]{1,0:T(8,128)(2,1)S(1)}, u32[]{:S(2)}, u32[]{:S(2)}) collective-permute-start(bf16[128,512]{1,0:T(8,128)(2,1)S(1)} %get-tuple-element.21.refs_0_), channel_id=1, source_target_pairs={{0,6},{1,7},{2,4},{3,5},{4,2},{5,3},{6,0},{7,1},{8,14},{9,15},{10,... | collective-permute-start | bytes 393224 | tf_op jit(solution)/shard_map/ppermute | solution.py:41
  32.3 9.9 %collective-permute-start.22 = (bf16[512,512]{1,0:T(8,128)(2,1)S(1)}, bf16[512,512]{1,0:T(8,128)(2,1)S(1)}, u32[]{:S(2)}, u32[]{:S(2)}) collective-permute-start(bf16[512,512]{1,0:T(8,128)(2,1)S(1)} %pack.3.refs_0_.refs_1_), channel_id=1, source_target_pairs={{0,8},{8,16},{16,24},{1,9},{9,17},{17,25},{2,10},{10,18},{18,26},{... | collective-permute-start | bytes 1572872 | tf_op jit(solution)/shard_map/ppermute | solution.py:28
  42.3 2.8 %collective-permute-start.17 = (bf16[256,512]{1,0:T(8,128)(2,1)S(1)}, bf16[256,512]{1,0:T(8,128)(2,1)S(1)}, u32[]{:S(2)}, u32[]{:S(2)}) collective-permute-start(bf16[256,512]{1,0:T(8,128)(2,1)S(1)} %pack.2.refs_1_.refs_2_), channel_id=1, source_target_pairs={{0,1},{1,0},{2,3},{3,2},{4,5},{5,4},{6,7},{7,6},{8,9},{9,8},{10,11... | collective-permute-start | bytes 786440 | tf_op jit(solution)/shard_map/ppermute | solution.py:41
  45.1 2.8 %collective-permute-start.16 = (bf16[256,512]{1,0:T(8,128)(2,1)S(1)}, bf16[256,512]{1,0:T(8,128)(2,1)S(1)}, u32[]{:S(2)}, u32[]{:S(2)}) collective-permute-start(bf16[256,512]{1,0:T(8,128)(2,1)S(1)} %pack.2.refs_1_.refs_2_), channel_id=1, source_target_pairs={{0,8},{8,16},{16,24},{1,9},{9,17},{17,25},{2,10},{10,18},{18,26},{... | collective-permute-start | bytes 786440 | tf_op jit(solution)/shard_map/ppermute | solution.py:28
  47.9 3.3 %collective-permute-done.17.refs_2_.refs_3_ = bf16[256,512]{1,0:T(8,128)(2,1)S(1)} collective-permute-done((bf16[256,512]{1,0:T(8,128)(2,1)S(1)}, bf16[256,512]{1,0:T(8,128)(2,1)S(1)}, u32[]{:S(2)}, u32[]{:S(2)}) %collective-permute-start.17) | collective-permute-done | bytes 262176 | tf_op jit(solution)/shard_map/ppermute | solution.py:41
  51.2 2.7 %collective-permute-start.18 = (bf16[256,512]{1,0:T(8,128)(2,1)S(1)}, bf16[256,512]{1,0:T(8,128)(2,1)S(1)}, u32[]{:S(2)}, u32[]{:S(2)}) collective-permute-start(bf16[256,512]{1,0:T(8,128)(2,1)S(1)} %collective-permute-done.17.refs_2_.refs_3_), channel_id=1, source_target_pairs={{0,8},{8,16},{16,24},{1,9},{9,17},{17,25},{2,10},{10,18},{18,26},{... | collective-permute-start | bytes 786440 | tf_op jit(solution)/shard_map/ppermute | solution.py:28
  54.0 2.3 %own_recon.1.before_ref = f32[1024,128]{1,0:T(8,128)S(1)} custom-call(bf16[512,512]{1,0:T(8,128)(2,1)S(1)} %pack.3.refs_0_.refs_1_, bf16[256,512]{1,0:T(8,128)(2,1)S(1)} %pack.2.refs_1_.refs_2_, bf16[256,512]{1,0:T(8,128)(2,1)S(1)} %collective-permute-done.17.refs_2_.refs_3_, bf16[2,1024,4096]{2,1,0:T(8,128)(2,1)S(1)} %bitcast.6), custom_call_target="tpu_custom_call" | custom-call | flops 1073741824 | tf_op jit(solution)/shard_map/own_recon/pallas_call | solution.py:289
  56.4 1.2 %near_recon.1.refs_2_ = f32[1024,128]{1,0:T(8,128)S(1)} custom-call(bf16[512,512]{1,0:T(8,128)(2,1)S(1)} %collective-permute-done.22.part_ref.refs_1_, f32[1024,128]{1,0:T(8,128)S(1)} %own_recon.1.before_ref, bf16[2,1024,4096]{2,1,0:T(8,128)(2,1)S(1)} %bitcast.7), custom_call_target="tpu_custom_call" | custom-call | flops 536870912 | tf_op jit(solution)/shard_map/near_recon/pallas_call | solution.py:299
  57.6 1.9 %recon.1 = (bf16[128,1024]{1,0:T(8,128)(2,1)S(1)}, bf16[512,512]{1,0:T(8,128)(2,1)S(1)}) custom-call(bf16[256,512]{1,0:T(8,128)(2,1)S(1)} %collective-permute-done.16.refs_0_.refs_2_, bf16[256,512]{1,0:T(8,128)(2,1)S(1)} %collective-permute-done.18.refs_1_.refs_3_, f32[1024,128]{1,0:T(8,128)S(1)} %near_recon.1.refs_2_, bf16[2,1024,4096]{2,1,0:T(8,128)(2,1)S(1)} %bitcast.8, ...), custom_call_target="tpu_custom_call" | custom-call | flops 2147483648 | bytes 4194304 | tf_op jit(solution)/shard_map/recon/pallas_call | solution.py:309
  59.6 1.9 %collective-permute-start.24 = (bf16[512,512]{1,0:T(8,128)(2,1)S(1)}, bf16[512,512]{1,0:T(8,128)(2,1)S(1)}, u32[]{:S(2)}, u32[]{:S(2)}) collective-permute-start(bf16[512,512]{1,0:T(8,128)(2,1)S(1)} %get-tuple-element.26), channel_id=1, source_target_pairs={{8,0},{16,8},{24,16},{9,1},{17,9},{25,17},{10,2},{18,10},{26,18},{... | collective-permute-start | bytes 1572872 | tf_op jit(solution)/shard_map/ppermute | solution.py:28
  61.5 1.8 %own_grad.1 = (bf16[512,512]{1,0:T(8,128)(2,1)S(1)}, f32[512,512]{1,0:T(8,128)S(1)}, f32[512,512]{1,0:T(8,128)S(1)}) custom-call(bf16[128,1024]{1,0:T(8,128)(2,1)S(1)} %get-tuple-element.22.error_ref.refs_0_, bf16[2,1024,4096]{2,1,0:T(8,128)(2,1)S(1)} %bitcast.9), custom_call_target="tpu_custom_call" | custom-call | flops 1610612736 | bytes 6291456 | tf_op jit(solution)/shard_map/own_grad/pallas_call | solution.py:320
  63.4 2.1 %collective-permute-start.23 = (bf16[512,512]{1,0:T(8,128)(2,1)S(1)}, bf16[512,512]{1,0:T(8,128)(2,1)S(1)}, u32[]{:S(2)}, u32[]{:S(2)}) collective-permute-start(bf16[512,512]{1,0:T(8,128)(2,1)S(1)} %get-tuple-element.24), channel_id=1, source_target_pairs={{8,0},{16,8},{24,16},{9,1},{17,9},{25,17},{10,2},{18,10},{26,18},{... | collective-permute-start | bytes 1572872 | tf_op jit(solution)/shard_map/ppermute | solution.py:28
  65.5 5.0 %collective-permute-done.24.arrived_ref = bf16[512,512]{1,0:T(8,128)(2,1)S(1)} collective-permute-done((bf16[512,512]{1,0:T(8,128)(2,1)S(1)}, bf16[512,512]{1,0:T(8,128)(2,1)S(1)}, u32[]{:S(2)}, u32[]{:S(2)}) %collective-permute-start.24) | collective-permute-done | bytes 524320 | tf_op jit(solution)/shard_map/ppermute | solution.py:28
  70.6 1.7 %collective-permute-start.25 = (bf16[256,512]{1,0:T(8,128)(2,1)S(1)}, bf16[256,512]{1,0:T(8,128)(2,1)S(1)}, u32[]{:S(2)}, u32[]{:S(2)}) collective-permute-start(bf16[256,512]{1,0:T(8,128)(2,1)S(1)} %get-tuple-element.28.refs_4_), channel_id=1, source_target_pairs={{0,1},{1,0},{2,3},{3,2},{4,5},{5,4},{6,7},{7,6},{8,9},{9,8},{10,11... | collective-permute-start | bytes 786440 | tf_op jit(solution)/shard_map/ppermute | solution.py:41
  72.2 4.9 %dec_grad.2.refs_0_.refs_4_ = bf16[1,2,1024,4096]{3,2,1,0:T(8,128)(2,1)} custom-call(bf16[128,1024]{1,0:T(8,128)(2,1)S(1)} %get-tuple-element.22.error_ref.refs_0_, bf16[512,512]{1,0:T(8,128)(2,1)S(1)} %pack.3.refs_0_.refs_1_, bf16[256,512]{1,0:T(8,128)(2,1)S(1)} %pack.2.refs_1_.refs_2_, bf16[256,512]{1,0:T(8,128)(2,1)S(1)} %collective-permute-done.17.refs_2_.refs_3_, ...), custom_call_target="tpu_custom_call" | custom-call | flops 1073741824 | bytes 8388608 | tf_op jit(solution)/shard_map/dec_grad/pallas_call | solution.py:345
  77.2 0.5 collective-permute-done.25.arrived_ref
  77.7 1.6 %collective-permute-start.26 = (bf16[128,512]{1,0:T(8,128)(2,1)S(1)}, bf16[128,512]{1,0:T(8,128)(2,1)S(1)}, u32[]{:S(2)}, u32[]{:S(2)}) collective-permute-start(bf16[128,512]{1,0:T(8,128)(2,1)S(1)} %get-tuple-element.31), channel_id=1, source_target_pairs={{0,1},{1,0},{2,3},{3,2},{4,5},{5,4},{6,7},{7,6},{8,9},{9,8},{10,11... | collective-permute-start | bytes 393224 | tf_op jit(solution)/shard_map/ppermute | solution.py:41
  79.3 2.2 %collective-permute-start.27 = (bf16[128,512]{1,0:T(8,128)(2,1)S(1)}, bf16[128,512]{1,0:T(8,128)(2,1)S(1)}, u32[]{:S(2)}, u32[]{:S(2)}) collective-permute-start(bf16[128,512]{1,0:T(8,128)(2,1)S(1)} %get-tuple-element.29.refs_0_), channel_id=1, source_target_pairs={{0,6},{1,7},{2,4},{3,5},{4,2},{5,3},{6,0},{7,1},{8,14},{9,15},{10,... | collective-permute-start | bytes 393224 | tf_op jit(solution)/shard_map/ppermute | solution.py:41
  81.6 0.4 collective-permute-done.26.refs_0_.refs_1_
  82.1 1.0 %collective-permute-start.29 = (bf16[128,512]{1,0:T(8,128)(2,1)S(1)}, bf16[128,512]{1,0:T(8,128)(2,1)S(1)}, u32[]{:S(2)}, u32[]{:S(2)}) collective-permute-start(bf16[128,512]{1,0:T(8,128)(2,1)S(1)} %get-tuple-element.33), channel_id=1, source_target_pairs={{0,2},{1,3},{2,0},{3,1},{4,6},{5,7},{6,4},{7,5},{8,10},{9,11},{10,... | collective-permute-start | bytes 393224 | tf_op jit(solution)/shard_map/ppermute | solution.py:41
  83.0 1.7 %collective-permute-start.30 = (bf16[128,512]{1,0:T(8,128)(2,1)S(1)}, bf16[128,512]{1,0:T(8,128)(2,1)S(1)}, u32[]{:S(2)}, u32[]{:S(2)}) collective-permute-start(bf16[128,512]{1,0:T(8,128)(2,1)S(1)} %get-tuple-element.34), channel_id=1, source_target_pairs={{0,3},{1,2},{2,1},{3,0},{4,7},{5,6},{6,5},{7,4},{8,11},{9,10},{10,... | collective-permute-start | bytes 393224 | tf_op jit(solution)/shard_map/ppermute | solution.py:41
  84.8 4.9 %dec_grad.3 = bf16[1,2,1024,4096]{3,2,1,0:T(8,128)(2,1)} custom-call(bf16[128,1024]{1,0:T(8,128)(2,1)S(1)} %get-tuple-element.22.error_ref.refs_0_, bf16[512,512]{1,0:T(8,128)(2,1)S(1)} %collective-permute-done.22.part_ref.refs_1_, bf16[256,512]{1,0:T(8,128)(2,1)S(1)} %collective-permute-done.16.refs_0_.refs_2_, ...), custom_call_target="tpu_custom_call", output_to_operand_aliasing={{}: (4, {})} | custom-call | flops 1073741824 | bytes 8388608 | tf_op jit(solution)/shard_map/dec_grad/pallas_call | solution.py:345
  89.7 0.7 collective-permute-done.30.refs_5_
  90.4 4.9 %enc_grad.1 = bf16[1,512,8192]{2,1,0:T(8,128)(2,1)} custom-call(f32[128,512]{1,0:T(8,128)S(1)} %get-tuple-element.30.refs_0_, bf16[128,512]{1,0:T(8,128)(2,1)S(1)} %collective-permute-done.26.refs_0_.refs_1_, bf16[128,512]{1,0:T(8,128)(2,1)S(1)} %collective-permute-done.27.refs_2_, bf16[128,512]{1,0:T(8,128)(2,1)S(1)} %collective-permute-done.28.refs_3_, ...), custom_call_target="tpu_custom_call" | custom-call | flops 1073741824 | bytes 8388608 | tf_op jit(solution)/shard_map/enc_grad/pallas_call | solution.py:381
  (46 shorter events, 1.1 us)
Async XLA Ops:
  0.6 53.3 %slice-start = ((s8[16777216]{0:T(1024)(128)(4,1)}), s8[4194304]{0:T(1024)(128)(4,1)S(1)}, s32[]{:S(2)}) async-start(s8[16777216]{0:T(1024)(128)(4,1)} %bitcast.4), calls=%async_computation | async-start | bytes 8388608
  0.6 23.0 %copy-start = (bf16[1,512,8192]{2,1,0:T(8,128)(2,1)S(1)}, bf16[1,512,8192]{2,1,0:T(8,128)(2,1)}, u32[]{:S(2)}) copy-start(bf16[1,512,8192]{2,1,0:T(8,128)(2,1)} %param.8) | copy-start | bytes 25165828
  0.7 23.0 %copy-start.3 = (f32[1,512]{1,0:T(1,128)S(1)}, f32[1,512]{1,0:T(1,128)}, u32[]{:S(2)}) copy-start(f32[1,512]{1,0:T(1,128)} %refs_17_.1) | copy-start | bytes 6148
  0.7 53.3 %slice-start.1 = ((s8[16777216]{0:T(1024)(128)(4,1)}), s8[4194304]{0:T(1024)(128)(4,1)S(1)}, s32[]{:S(2)}) async-start(s8[16777216]{0:T(1024)(128)(4,1)} %bitcast.4), calls=%async_computation.1 | async-start | bytes 8388608
  0.7 53.3 %slice-start.2 = ((s8[16777216]{0:T(1024)(128)(4,1)}), s8[4194304]{0:T(1024)(128)(4,1)S(1)}, s32[]{:S(2)}) async-start(s8[16777216]{0:T(1024)(128)(4,1)} %bitcast.4), calls=%async_computation.2 | async-start | bytes 8388608
  0.7 53.3 %slice-start.3 = ((s8[16777216]{0:T(1024)(128)(4,1)}), s8[4194304]{0:T(1024)(128)(4,1)S(1)}, s32[]{:S(2)}) async-start(s8[16777216]{0:T(1024)(128)(4,1)} %bitcast.4), calls=%async_computation.3 | async-start | bytes 8388608
  1.8 5.3 %collective-permute-start = (bf16[64,1024]{1,0:T(8,128)(2,1)S(1)}, bf16[64,1024]{1,0:T(8,128)(2,1)S(1)}, u32[]{:S(2)}, u32[]{:S(2)}) collective-permute-start(bf16[64,1024]{1,0:T(8,128)(2,1)S(1)} %get-tuple-element.19.refs_0_.refs_6_), channel_id=1, source_target_pairs={{0,2},{2,4},{4,6},{6,7},{7,5},{5,3},{3,1},{1,0},{8,10},{10,12},{12... | collective-permute-start | bytes 393224 | tf_op jit(solution)/shard_map/ppermute | solution.py:51
  4.0 4.4 %collective-permute-start.3 = (bf16[64,1024]{1,0:T(8,128)(2,1)S(1)}, bf16[64,1024]{1,0:T(8,128)(2,1)S(1)}, u32[]{:S(2)}, u32[]{:S(2)}) collective-permute-start(bf16[64,1024]{1,0:T(8,128)(2,1)S(1)} %get-tuple-element.20.refs_1_.refs_7_), channel_id=1, source_target_pairs={{0,1},{2,0},{4,2},{6,4},{7,6},{5,7},{3,5},{1,3},{8,9},{10,8},{12,1... | collective-permute-start | bytes 393224 | tf_op jit(solution)/shard_map/ppermute | solution.py:51
  4.0 6.8 %collective-permute-start.2 = (bf16[64,1024]{1,0:T(8,128)(2,1)S(1)}, bf16[64,1024]{1,0:T(8,128)(2,1)S(1)}, u32[]{:S(2)}, u32[]{:S(2)}) collective-permute-start(bf16[64,1024]{1,0:T(8,128)(2,1)S(1)} %get-tuple-element.19.refs_0_.refs_6_), channel_id=1, source_target_pairs={{0,1},{2,0},{4,2},{6,4},{7,6},{5,7},{3,5},{1,3},{8,9},{10,8},{12,1... | collective-permute-start | bytes 393224 | tf_op jit(solution)/shard_map/ppermute | solution.py:51
  5.4 5.8 %collective-permute-start.1 = (bf16[64,1024]{1,0:T(8,128)(2,1)S(1)}, bf16[64,1024]{1,0:T(8,128)(2,1)S(1)}, u32[]{:S(2)}, u32[]{:S(2)}) collective-permute-start(bf16[64,1024]{1,0:T(8,128)(2,1)S(1)} %get-tuple-element.20.refs_1_.refs_7_), channel_id=1, source_target_pairs={{0,2},{2,4},{4,6},{6,7},{7,5},{5,3},{3,1},{1,0},{8,10},{10,12},{12... | collective-permute-start | bytes 393224 | tf_op jit(solution)/shard_map/ppermute | solution.py:51
  7.2 5.3 %collective-permute-start.4 = (bf16[64,1024]{1,0:T(8,128)(2,1)S(1)}, bf16[64,1024]{1,0:T(8,128)(2,1)S(1)}, u32[]{:S(2)}, u32[]{:S(2)}) collective-permute-start(bf16[64,1024]{1,0:T(8,128)(2,1)S(1)} %collective-permute-done.refs_2_.refs_8_), channel_id=1, source_target_pairs={{0,2},{2,4},{4,6},{6,7},{7,5},{5,3},{3,1},{1,0},{8,10},{10,12},{12... | collective-permute-start | bytes 393224 | tf_op jit(solution)/shard_map/ppermute | solution.py:51
  8.4 5.4 %collective-permute-start.7 = (bf16[64,1024]{1,0:T(8,128)(2,1)S(1)}, bf16[64,1024]{1,0:T(8,128)(2,1)S(1)}, u32[]{:S(2)}, u32[]{:S(2)}) collective-permute-start(bf16[64,1024]{1,0:T(8,128)(2,1)S(1)} %collective-permute-done.3.refs_5_.refs_11_), channel_id=1, source_target_pairs={{0,1},{2,0},{4,2},{6,4},{7,6},{5,7},{3,5},{1,3},{8,9},{10,8},{12,1... | collective-permute-start | bytes 393224 | tf_op jit(solution)/shard_map/ppermute | solution.py:51
  10.9 4.8 %collective-permute-start.6 = (bf16[64,1024]{1,0:T(8,128)(2,1)S(1)}, bf16[64,1024]{1,0:T(8,128)(2,1)S(1)}, u32[]{:S(2)}, u32[]{:S(2)}) collective-permute-start(bf16[64,1024]{1,0:T(8,128)(2,1)S(1)} %collective-permute-done.2.refs_4_.refs_10_), channel_id=1, source_target_pairs={{0,1},{2,0},{4,2},{6,4},{7,6},{5,7},{3,5},{1,3},{8,9},{10,8},{12,1... | collective-permute-start | bytes 393224 | tf_op jit(solution)/shard_map/ppermute | solution.py:51
  11.2 5.2 %collective-permute-start.5 = (bf16[64,1024]{1,0:T(8,128)(2,1)S(1)}, bf16[64,1024]{1,0:T(8,128)(2,1)S(1)}, u32[]{:S(2)}, u32[]{:S(2)}) collective-permute-start(bf16[64,1024]{1,0:T(8,128)(2,1)S(1)} %collective-permute-done.1.refs_3_.refs_9_), channel_id=1, source_target_pairs={{0,2},{2,4},{4,6},{6,7},{7,5},{5,3},{3,1},{1,0},{8,10},{10,12},{12... | collective-permute-start | bytes 393224 | tf_op jit(solution)/shard_map/ppermute | solution.py:51
  12.5 4.7 %collective-permute-start.8 = (bf16[64,1024]{1,0:T(8,128)(2,1)S(1)}, bf16[64,1024]{1,0:T(8,128)(2,1)S(1)}, u32[]{:S(2)}, u32[]{:S(2)}) collective-permute-start(bf16[64,1024]{1,0:T(8,128)(2,1)S(1)} %collective-permute-done.4.refs_6_.refs_12_), channel_id=1, source_target_pairs={{0,2},{2,4},{4,6},{6,7},{7,5},{5,3},{3,1},{1,0},{8,10},{10,12},{12... | collective-permute-start | bytes 393224 | tf_op jit(solution)/shard_map/ppermute | solution.py:51
  13.7 5.1 %collective-permute-start.11 = (bf16[64,1024]{1,0:T(8,128)(2,1)S(1)}, bf16[64,1024]{1,0:T(8,128)(2,1)S(1)}, u32[]{:S(2)}, u32[]{:S(2)}) collective-permute-start(bf16[64,1024]{1,0:T(8,128)(2,1)S(1)} %collective-permute-done.7.refs_9_.refs_15_), channel_id=1, source_target_pairs={{0,1},{2,0},{4,2},{6,4},{7,6},{5,7},{3,5},{1,3},{8,9},{10,8},{12,1... | collective-permute-start | bytes 393224 | tf_op jit(solution)/shard_map/ppermute | solution.py:51
  15.7 5.1 %collective-permute-start.10 = (bf16[64,1024]{1,0:T(8,128)(2,1)S(1)}, bf16[64,1024]{1,0:T(8,128)(2,1)S(1)}, u32[]{:S(2)}, u32[]{:S(2)}) collective-permute-start(bf16[64,1024]{1,0:T(8,128)(2,1)S(1)} %collective-permute-done.6.refs_8_.refs_14_), channel_id=1, source_target_pairs={{0,1},{2,0},{4,2},{6,4},{7,6},{5,7},{3,5},{1,3},{8,9},{10,8},{12,1... | collective-permute-start | bytes 393224 | tf_op jit(solution)/shard_map/ppermute | solution.py:51
  16.4 5.5 %collective-permute-start.9 = (bf16[64,1024]{1,0:T(8,128)(2,1)S(1)}, bf16[64,1024]{1,0:T(8,128)(2,1)S(1)}, u32[]{:S(2)}, u32[]{:S(2)}) collective-permute-start(bf16[64,1024]{1,0:T(8,128)(2,1)S(1)} %collective-permute-done.5.refs_7_.refs_13_), channel_id=1, source_target_pairs={{0,2},{2,4},{4,6},{6,7},{7,5},{5,3},{3,1},{1,0},{8,10},{10,12},{12... | collective-permute-start | bytes 393224 | tf_op jit(solution)/shard_map/ppermute | solution.py:51
  17.2 5.8 %collective-permute-start.12 = (bf16[64,1024]{1,0:T(8,128)(2,1)S(1)}, bf16[64,1024]{1,0:T(8,128)(2,1)S(1)}, u32[]{:S(2)}, u32[]{:S(2)}) collective-permute-start(bf16[64,1024]{1,0:T(8,128)(2,1)S(1)} %collective-permute-done.8.refs_10_.refs_16_), channel_id=1, source_target_pairs={{0,2},{2,4},{4,6},{6,7},{7,5},{5,3},{3,1},{1,0},{8,10},{10,12},{12... | collective-permute-start | bytes 393224 | tf_op jit(solution)/shard_map/ppermute | solution.py:51
  18.9 4.8 %collective-permute-start.13 = (bf16[64,1024]{1,0:T(8,128)(2,1)S(1)}, bf16[64,1024]{1,0:T(8,128)(2,1)S(1)}, u32[]{:S(2)}, u32[]{:S(2)}) collective-permute-start(bf16[64,1024]{1,0:T(8,128)(2,1)S(1)} %collective-permute-done.11.refs_13_.refs_19_), channel_id=1, source_target_pairs={{0,1},{2,0},{4,2},{6,4},{7,6},{5,7},{3,5},{1,3},{8,9},{10,8},{12,1... | collective-permute-start | bytes 393224 | tf_op jit(solution)/shard_map/ppermute | solution.py:51
  26.1 6.1 %collective-permute-start.21 = (bf16[128,512]{1,0:T(8,128)(2,1)S(1)}, bf16[128,512]{1,0:T(8,128)(2,1)S(1)}, u32[]{:S(2)}, u32[]{:S(2)}) collective-permute-start(bf16[128,512]{1,0:T(8,128)(2,1)S(1)} %get-tuple-element.21.refs_0_), channel_id=1, source_target_pairs={{0,3},{1,2},{2,1},{3,0},{4,7},{5,6},{6,5},{7,4},{8,11},{9,10},{10,... | collective-permute-start | bytes 393224 | tf_op jit(solution)/shard_map/ppermute | solution.py:41
  27.9 4.3 %collective-permute-start.20 = (bf16[128,512]{1,0:T(8,128)(2,1)S(1)}, bf16[128,512]{1,0:T(8,128)(2,1)S(1)}, u32[]{:S(2)}, u32[]{:S(2)}) collective-permute-start(bf16[128,512]{1,0:T(8,128)(2,1)S(1)} %get-tuple-element.21.refs_0_), channel_id=1, source_target_pairs={{0,2},{1,3},{2,0},{3,1},{4,6},{5,7},{6,4},{7,5},{8,10},{9,11},{10,... | collective-permute-start | bytes 393224 | tf_op jit(solution)/shard_map/ppermute | solution.py:41
  28.1 4.2 %collective-permute-start.19 = (bf16[128,512]{1,0:T(8,128)(2,1)S(1)}, bf16[128,512]{1,0:T(8,128)(2,1)S(1)}, u32[]{:S(2)}, u32[]{:S(2)}) collective-permute-start(bf16[128,512]{1,0:T(8,128)(2,1)S(1)} %get-tuple-element.21.refs_0_), channel_id=1, source_target_pairs={{0,1},{1,0},{2,3},{3,2},{4,5},{5,4},{6,7},{7,6},{8,9},{9,8},{10,11... | collective-permute-start | bytes 393224 | tf_op jit(solution)/shard_map/ppermute | solution.py:41
  28.8 13.4 %collective-permute-start.15 = (bf16[128,512]{1,0:T(8,128)(2,1)S(1)}, bf16[128,512]{1,0:T(8,128)(2,1)S(1)}, u32[]{:S(2)}, u32[]{:S(2)}) collective-permute-start(bf16[128,512]{1,0:T(8,128)(2,1)S(1)} %get-tuple-element.21.refs_0_), channel_id=1, source_target_pairs={{0,4},{1,5},{2,6},{3,7},{4,0},{5,1},{6,2},{7,3},{8,12},{9,13},{10,... | collective-permute-start | bytes 393224 | tf_op jit(solution)/shard_map/ppermute | solution.py:41
  31.1 11.1 %collective-permute-start.14 = (bf16[128,512]{1,0:T(8,128)(2,1)S(1)}, bf16[128,512]{1,0:T(8,128)(2,1)S(1)}, u32[]{:S(2)}, u32[]{:S(2)}) collective-permute-start(bf16[128,512]{1,0:T(8,128)(2,1)S(1)} %get-tuple-element.21.refs_0_), channel_id=1, source_target_pairs={{0,6},{1,7},{2,4},{3,5},{4,2},{5,3},{6,0},{7,1},{8,14},{9,15},{10,... | collective-permute-start | bytes 393224 | tf_op jit(solution)/shard_map/ppermute | solution.py:41
  32.3 24.0 %collective-permute-start.22 = (bf16[512,512]{1,0:T(8,128)(2,1)S(1)}, bf16[512,512]{1,0:T(8,128)(2,1)S(1)}, u32[]{:S(2)}, u32[]{:S(2)}) collective-permute-start(bf16[512,512]{1,0:T(8,128)(2,1)S(1)} %pack.3.refs_0_.refs_1_), channel_id=1, source_target_pairs={{0,8},{8,16},{16,24},{1,9},{9,17},{17,25},{2,10},{10,18},{18,26},{... | collective-permute-start | bytes 1572872 | tf_op jit(solution)/shard_map/ppermute | solution.py:28
  42.3 8.9 %collective-permute-start.17 = (bf16[256,512]{1,0:T(8,128)(2,1)S(1)}, bf16[256,512]{1,0:T(8,128)(2,1)S(1)}, u32[]{:S(2)}, u32[]{:S(2)}) collective-permute-start(bf16[256,512]{1,0:T(8,128)(2,1)S(1)} %pack.2.refs_1_.refs_2_), channel_id=1, source_target_pairs={{0,1},{1,0},{2,3},{3,2},{4,5},{5,4},{6,7},{7,6},{8,9},{9,8},{10,11... | collective-permute-start | bytes 786440 | tf_op jit(solution)/shard_map/ppermute | solution.py:41
  45.1 12.5 %collective-permute-start.16 = (bf16[256,512]{1,0:T(8,128)(2,1)S(1)}, bf16[256,512]{1,0:T(8,128)(2,1)S(1)}, u32[]{:S(2)}, u32[]{:S(2)}) collective-permute-start(bf16[256,512]{1,0:T(8,128)(2,1)S(1)} %pack.2.refs_1_.refs_2_), channel_id=1, source_target_pairs={{0,8},{8,16},{16,24},{1,9},{9,17},{17,25},{2,10},{10,18},{18,26},{... | collective-permute-start | bytes 786440 | tf_op jit(solution)/shard_map/ppermute | solution.py:28
  51.2 6.4 %collective-permute-start.18 = (bf16[256,512]{1,0:T(8,128)(2,1)S(1)}, bf16[256,512]{1,0:T(8,128)(2,1)S(1)}, u32[]{:S(2)}, u32[]{:S(2)}) collective-permute-start(bf16[256,512]{1,0:T(8,128)(2,1)S(1)} %collective-permute-done.17.refs_2_.refs_3_), channel_id=1, source_target_pairs={{0,8},{8,16},{16,24},{1,9},{9,17},{17,25},{2,10},{10,18},{18,26},{... | collective-permute-start | bytes 786440 | tf_op jit(solution)/shard_map/ppermute | solution.py:28
  54.0 3.6 %copy-start.1 = (bf16[1,128,1024]{2,1,0:T(8,128)(2,1)S(1)}, bf16[1,128,1024]{2,1,0:T(8,128)(2,1)}, u32[]{:S(2)}) copy-start(bf16[1,128,1024]{2,1,0:T(8,128)(2,1)} %param.7) | copy-start | bytes 786436
  54.0 3.6 %copy-start.2 = (f32[1,1024]{1,0:T(1,128)S(1)}, f32[1,1024]{1,0:T(1,128)}, u32[]{:S(2)}) copy-start(f32[1,1024]{1,0:T(1,128)} %refs_4_.1) | copy-start | bytes 12292
  59.6 10.9 %collective-permute-start.24 = (bf16[512,512]{1,0:T(8,128)(2,1)S(1)}, bf16[512,512]{1,0:T(8,128)(2,1)S(1)}, u32[]{:S(2)}, u32[]{:S(2)}) collective-permute-start(bf16[512,512]{1,0:T(8,128)(2,1)S(1)} %get-tuple-element.26), channel_id=1, source_target_pairs={{8,0},{16,8},{24,16},{9,1},{17,9},{25,17},{10,2},{18,10},{26,18},{... | collective-permute-start | bytes 1572872 | tf_op jit(solution)/shard_map/ppermute | solution.py:28
  63.4 14.3 %collective-permute-start.23 = (bf16[512,512]{1,0:T(8,128)(2,1)S(1)}, bf16[512,512]{1,0:T(8,128)(2,1)S(1)}, u32[]{:S(2)}, u32[]{:S(2)}) collective-permute-start(bf16[512,512]{1,0:T(8,128)(2,1)S(1)} %get-tuple-element.24), channel_id=1, source_target_pairs={{8,0},{16,8},{24,16},{9,1},{17,9},{25,17},{10,2},{18,10},{26,18},{... | collective-permute-start | bytes 1572872 | tf_op jit(solution)/shard_map/ppermute | solution.py:28
  70.6 7.1 %collective-permute-start.25 = (bf16[256,512]{1,0:T(8,128)(2,1)S(1)}, bf16[256,512]{1,0:T(8,128)(2,1)S(1)}, u32[]{:S(2)}, u32[]{:S(2)}) collective-permute-start(bf16[256,512]{1,0:T(8,128)(2,1)S(1)} %get-tuple-element.28.refs_4_), channel_id=1, source_target_pairs={{0,1},{1,0},{2,3},{3,2},{4,5},{5,4},{6,7},{7,6},{8,9},{9,8},{10,11... | collective-permute-start | bytes 786440 | tf_op jit(solution)/shard_map/ppermute | solution.py:41
  77.7 4.3 %collective-permute-start.26 = (bf16[128,512]{1,0:T(8,128)(2,1)S(1)}, bf16[128,512]{1,0:T(8,128)(2,1)S(1)}, u32[]{:S(2)}, u32[]{:S(2)}) collective-permute-start(bf16[128,512]{1,0:T(8,128)(2,1)S(1)} %get-tuple-element.31), channel_id=1, source_target_pairs={{0,1},{1,0},{2,3},{3,2},{4,5},{5,4},{6,7},{7,6},{8,9},{9,8},{10,11... | collective-permute-start | bytes 393224 | tf_op jit(solution)/shard_map/ppermute | solution.py:41
  79.3 10.3 %collective-permute-start.27 = (bf16[128,512]{1,0:T(8,128)(2,1)S(1)}, bf16[128,512]{1,0:T(8,128)(2,1)S(1)}, u32[]{:S(2)}, u32[]{:S(2)}) collective-permute-start(bf16[128,512]{1,0:T(8,128)(2,1)S(1)} %get-tuple-element.29.refs_0_), channel_id=1, source_target_pairs={{0,6},{1,7},{2,4},{3,5},{4,2},{5,3},{6,0},{7,1},{8,14},{9,15},{10,... | collective-permute-start | bytes 393224 | tf_op jit(solution)/shard_map/ppermute | solution.py:41
  81.6 8.1 %collective-permute-start.28 = (bf16[128,512]{1,0:T(8,128)(2,1)S(1)}, bf16[128,512]{1,0:T(8,128)(2,1)S(1)}, u32[]{:S(2)}, u32[]{:S(2)}) collective-permute-start(bf16[128,512]{1,0:T(8,128)(2,1)S(1)} %get-tuple-element.32), channel_id=1, source_target_pairs={{0,4},{1,5},{2,6},{3,7},{4,0},{5,1},{6,2},{7,3},{8,12},{9,13},{10,... | collective-permute-start | bytes 393224 | tf_op jit(solution)/shard_map/ppermute | solution.py:41
  82.1 7.6 %collective-permute-start.29 = (bf16[128,512]{1,0:T(8,128)(2,1)S(1)}, bf16[128,512]{1,0:T(8,128)(2,1)S(1)}, u32[]{:S(2)}, u32[]{:S(2)}) collective-permute-start(bf16[128,512]{1,0:T(8,128)(2,1)S(1)} %get-tuple-element.33), channel_id=1, source_target_pairs={{0,2},{1,3},{2,0},{3,1},{4,6},{5,7},{6,4},{7,5},{8,10},{9,11},{10,... | collective-permute-start | bytes 393224 | tf_op jit(solution)/shard_map/ppermute | solution.py:41
  83.0 7.4 %collective-permute-start.30 = (bf16[128,512]{1,0:T(8,128)(2,1)S(1)}, bf16[128,512]{1,0:T(8,128)(2,1)S(1)}, u32[]{:S(2)}, u32[]{:S(2)}) collective-permute-start(bf16[128,512]{1,0:T(8,128)(2,1)S(1)} %get-tuple-element.34), channel_id=1, source_target_pairs={{0,3},{1,2},{2,1},{3,0},{4,7},{5,6},{6,5},{7,4},{8,11},{9,10},{10,... | collective-permute-start | bytes 393224 | tf_op jit(solution)/shard_map/ppermute | solution.py:41
